TPU v7x, 256 devices: a whole 4x4x8 slice. The times are simulated.
256 devices in a mesh: patch: 64 (over x, z, core), feat: 4 (over y).
Axes of the slice: x: 4, y: 4, z: 8, core: 2. Of those that a mesh axis runs over, the one named last changes fastest.
Arguments:
- nodes: bfloat16 [40960, 512], P(('patch', 'feat')), may hold values from -6 to 6
- edges: bfloat16 [327680, 512], P(('patch', 'feat')), may hold values from -6 to 6
- receivers: int32 [327680], P(('patch', 'feat')), may hold values from 0 to 639
- sender_slot: int32 [327680], P(('patch', 'feat')), may hold values from 0 to 2175
- send_rows: int32 [64, 4, 64, 24], P('patch', 'feat'), may hold values from 0 to 159
- live_edges: int32 [256], P(('patch', 'feat')), may hold values from 1 to 1280, 245760 in all
- edge_w1: bfloat16 [1536, 512], replicated, may hold values from -0.15625 to 0.15625
- edge_b1: float32 [512], replicated, may hold values from -3 to 3
- edge_w2: bfloat16 [512, 512], replicated, may hold values from -0.25 to 0.25
- edge_gain: float32 [512], replicated, may hold values from 0.5 to 1.5
- node_w1: bfloat16 [1024, 512], replicated, may hold values from -0.1875 to 0.1875
- node_b1: float32 [512], replicated, may hold values from -3 to 3
- node_w2: bfloat16 [512, 512], replicated, may hold values from -0.25 to 0.25
- node_gain: float32 [512], replicated, may hold values from 0.5 to 1.5
Outputs:
- edges_out: bfloat16 [327680, 512], P(('patch', 'feat'))
- nodes_out: bfloat16 [40960, 512], P(('patch', 'feat'))
Inputs may be any that keep to these rules, and one draw needn't show every extreme that they name: `live_edges`: edge slots at or past a device's count are padding.
All inputs are finite; a program needn't handle non-finite values.
Results may differ from a plain program's by a relative error of at most 0.0052.
Values may be sent and summed in bfloat16 or wider, within the bound.
No kernel may reach another device: no remote copies, remote signals or barrier semaphores. Data moves between devices by JAX's collectives and lax.ppermute only.
A program may use at most 64 MiB of HBM per device.

v0:
```python
import jax
import jax.numpy as jnp
from jax import lax
from jax.sharding import PartitionSpec as P

epsilon = 1e-05


def cut_along(value, dim, size):
    lengths = value.shape
    tiles = value.reshape(*lengths[:dim], size, lengths[dim] // size, *lengths[dim + 1 :])
    return jnp.moveaxis(tiles, dim, 0)


def sum_at_owner(value, axis, dim):
    size = lax.axis_size(axis)
    tiles = lax.all_to_all(cut_along(value, dim, size), axis, 0, 0, tiled=True)
    return jnp.sum(tiles, axis=0)


def layer_norm(values, scales):
    average = jnp.mean(values, axis=-1, keepdims=True)
    centred = values - average
    variance = jnp.mean(centred * centred, axis=-1, keepdims=True)
    return centred * lax.rsqrt(variance + epsilon) * scales


def edge_change(edge_rows, sender_feat, receiver_feat, edge_w1, edge_b1, edge_w2, edge_gain):
    latent = edge_rows.shape[1]
    first = jnp.dot(edge_rows, edge_w1[:latent], preferred_element_type=jnp.float32)
    first = first + jnp.dot(
        sender_feat, edge_w1[latent : 2 * latent], preferred_element_type=jnp.float32
    )
    first = first + jnp.dot(
        receiver_feat, edge_w1[2 * latent :], preferred_element_type=jnp.float32
    )
    hidden = jax.nn.silu(first + edge_b1).astype(jnp.bfloat16)
    return layer_norm(jnp.dot(hidden, edge_w2, preferred_element_type=jnp.float32), edge_gain)


def node_change(node_rows, incoming, node_w1, node_b1, node_w2, node_gain):
    latent = node_rows.shape[1]
    first = jnp.dot(node_rows, node_w1[:latent], preferred_element_type=jnp.float32)
    first = first + jnp.dot(incoming, node_w1[latent:], preferred_element_type=jnp.float32)
    hidden = jax.nn.silu(first + node_b1).astype(jnp.bfloat16)
    return layer_norm(jnp.dot(hidden, node_w2, preferred_element_type=jnp.float32), node_gain)


def local(
    nodes,
    edges,
    receivers,
    sender_slot,
    send_rows,
    live_edges,
    edge_w1,
    edge_b1,
    edge_w2,
    edge_gain,
    node_w1,
    node_b1,
    node_w2,
    node_gain,
):
    latent = nodes.shape[1]
    edge_count = edges.shape[0]
    patch_rows = lax.all_gather(nodes, "feat", axis=0, tiled=True)
    patch_count = patch_rows.shape[0]
    outgoing = send_rows[0, 0]
    packed = jnp.take(nodes, outgoing.reshape(-1), axis=0).reshape(
        outgoing.shape[0], outgoing.shape[1], latent
    )
    remote = lax.all_to_all(packed, "patch", split_axis=0, concat_axis=0, tiled=True).reshape(
        -1, latent
    )
    lookup_rows = jnp.concatenate([patch_rows, remote], axis=0)
    sender_feat = jnp.take(lookup_rows, sender_slot, axis=0)
    receiver_feat = jnp.take(patch_rows, receivers, axis=0)
    alive_count = live_edges[0]
    alive = lax.broadcasted_iota(jnp.int32, (edge_count,), 0) < alive_count
    change = edge_change(edges, sender_feat, receiver_feat, edge_w1, edge_b1, edge_w2, edge_gain)
    edges_out = (edges.astype(jnp.float32) + jnp.where(alive[:, None], change, 0.0)).astype(
        jnp.bfloat16
    )
    owner_rows = lax.broadcasted_iota(jnp.int32, (patch_count, edge_count), 0)
    one_hot = ((receivers[None, :] == owner_rows) & alive[None, :]).astype(jnp.bfloat16)
    partial_sums = jnp.dot(one_hot, edges_out, preferred_element_type=jnp.float32)
    summed = sum_at_owner(partial_sums, "feat", 0)
    incoming = summed.astype(jnp.bfloat16)
    change = node_change(nodes, incoming, node_w1, node_b1, node_w2, node_gain)
    nodes_out = (nodes.astype(jnp.float32) + change).astype(jnp.bfloat16)
    return (edges_out, nodes_out)


def solution(mesh):
    placed = (
        P(("patch", "feat"), None),
        P(("patch", "feat"), None),
        P(("patch", "feat")),
        P(("patch", "feat")),
        P("patch", "feat", None, None),
        P(("patch", "feat")),
        P(),
        P(),
        P(),
        P(),
        P(),
        P(),
        P(),
        P(),
    )
    return jax.shard_map(
        local,
        mesh=mesh,
        in_specs=placed,
        out_specs=(P(("patch", "feat"), None), P(("patch", "feat"), None)),
        check_vma=False,
    )
```

profile of v0, /device:TPU:1, one launch (start us, length us, event | category | flops | bytes accessed | tf_op | source)
XLA Modules:
  0.0 107.9 jit_solution(567308543703744715)
XLA Ops:
  0.6 0.0 copy-start
  0.6 0.8 copy.21
  1.5 0.7 compare_and_fusion
  2.2 0.1 reshape_squeeze.6
  2.3 0.1 copy.20
  2.5 5.8 %gather_fusion = bf16[1536,512]{1,0:T(8,128)(2,1)S(1)} fusion(bf16[160,512]{1,0:T(8,128)(2,1)} %param.14, s32[2048]{0:T(1024)S(1)} %pad_clamp_fusion.2), kind=kCustom, calls=%fused_computation | custom fusion | bytes 3151872 | tf_op jit(solution)/shard_map/jit(_take)/gather | solution.py:70
  8.3 1.4 %broadcast_select_fusion = bf16[64,24,512]{2,1,0:T(8,128)(2,1)} fusion(bf16[64,24,512]{2,1,0:T(8,128)(2,1)S(1)} %bitcast.18, pred[64,24]{1,0:T(8,128)(4,1)S(1)} %copy.20), kind=kLoop, calls=%fused_computation.15 | loop fusion | flops 786432 | bytes 3147264 | tf_op jit(solution)/shard_map/jit(_take)/select_n | solution.py:70
  9.7 13.0 %all-to-all-start = ((bf16[64,24,512]{2,1,0:T(8,128)(2,1)}), bf16[64,24,512]{2,1,0:T(8,128)(2,1)S(1)}, u32[]{:S(2)}, u32[]{:S(2)}) async-start(bf16[64,24,512]{2,1,0:T(8,128)(2,1)} %broadcast_select_fusion), calls=%async_computation | async-start | bytes 3145728 | tf_op jit(solution)/shard_map/all_to_all | solution.py:73
  22.7 0.0 copy-start.7
  22.7 0.0 copy-start.1
  23.4 2.4 %copy.19 = bf16[1280,512]{0,1:T(8,128)(2,1)} copy(bf16[1280,512]{1,0:T(8,128)(2,1)} %param.15) | data formatting | bytes 2621440 | tf_op args[1]
  25.8 0.0 copy-done.7
  25.8 0.0 copy-done.1
  25.8 12.0 %all_gather.3 = bf16[640,512]{1,0:T(8,128)(2,1)S(1)} all-gather(bf16[160,512]{1,0:T(8,128)(2,1)S(1)} %copy-done.1), channel_id=1, replica_groups=mesh['patch'=64,'feat'=4] {'feat'}, dimensions={0}, use_global_device_ids=true | all-gather | bytes 819200 | tf_op jit(solution)/shard_map/all_gather | solution.py:67
  37.8 0.0 copy-start.6
  37.8 4.7 %gather_fusion.2 = bf16[1280,512]{1,0:T(8,128)(2,1)} fusion(bf16[640,512]{1,0:T(8,128)(2,1)S(1)} %all_gather.3, s32[2048]{0:T(1024)S(1)} %pad_clamp_fusion), kind=kCustom, calls=%fused_computation.2 | custom fusion | bytes 2626560 | tf_op jit(solution)/shard_map/jit(_take)/gather | solution.py:78
  42.6 0.0 copy-done.6
  42.6 3.8 %fusion.25 = f32[1280,512]{1,0:T(8,128)} fusion(bf16[1280,512]{1,0:T(8,128)(2,1)} %param.15, bf16[1536,512]{1,0:T(8,128)(2,1)} %param.20), kind=kOutput, calls=%fused_computation.32 | convolution fusion | flops 671088640 | bytes 4456448 | tf_op jit(solution)/shard_map/dot_general | solution.py:30
  46.4 16.0 %all-to-all-done = bf16[64,24,512]{2,1,0:T(8,128)(2,1)S(1)} async-done(((bf16[64,24,512]{2,1,0:T(8,128)(2,1)}), bf16[64,24,512]{2,1,0:T(8,128)(2,1)S(1)}, u32[]{:S(2)}, u32[]{:S(2)}) %all-to-all-start) | async-done | bytes 1572896 | tf_op jit(solution)/shard_map/all_to_all | solution.py:73
  62.5 1.5 %pad_maximum_fusion = bf16[2176,512]{1,0:T(8,128)(2,1)} fusion(bf16[1536,512]{1,0:T(8,128)(2,1)S(1)} %bitcast.17, bf16[640,512]{1,0:T(8,128)(2,1)S(1)} %all_gather.3), kind=kLoop, calls=%fused_computation.12 | loop fusion | flops 4456448 | bytes 4456448 | tf_op jit(solution)/shard_map/concatenate | solution.py:76
  64.0 0.0 copy-start.2
  64.0 6.9 %gather_fusion.1 = bf16[1280,512]{1,0:T(8,128)(2,1)} fusion(bf16[2176,512]{1,0:T(8,128)(2,1)} %pad_maximum_fusion, s32[2048]{0:T(1024)S(1)} %pad_clamp_fusion.1), kind=kCustom, calls=%fused_computation.1 | custom fusion | bytes 2626560 | tf_op jit(solution)/shard_map/jit(_take)/gather | solution.py:77
  70.9 0.0 copy-done.2
  70.9 0.0 copy-start.10
  70.9 3.9 %convolution_add_fusion.1 = f32[1280,512]{1,0:T(8,128)} fusion(f32[1280,512]{1,0:T(8,128)S(1)} %copy-done.2, bf16[1280,512]{1,0:T(8,128)(2,1)} %gather_fusion.1, pred[1280]{0:T(1024)(128)(4,1)S(1)} %compare_and_fusion.2, bf16[1536,512]{1,0:T(8,128)(2,1)} %param.20), kind=kOutput, calls=%fused_computation.5 | convolution fusion | flops 672399360 | bytes 7079168 | tf_op jit(solution)/shard_map/dot_general | solution.py:31
  74.7 0.0 copy-done
  74.7 0.0 copy-done.10
  74.7 4.1 %fusion.42 = (f32[1280]{0:T(1024)S(1)}, f32[1280,512]{0,1:T(8,128)S(1)}) fusion(bf16[512,512]{1,0:T(8,128)(2,1)S(1)} %copy-done, f32[1280,512]{1,0:T(8,128)} %convolution_add_fusion.1, f32[512]{0:T(512)S(1)} %copy-done.10, bf16[1280,512]{1,0:T(8,128)(2,1)} %gather_fusion.2, pred[1280]{0:T(1024)(128)(4,1)S(1)} %compare_and_fusion.1, bf16[1536,512]{1,0:T(8,128)(2,1)} %param.20), kind=kOutput, calls=%fused_computation.61 | convolution fusion | flops 1348074240 | bytes 7610624 | tf_op jit(solution)/shard_map/dot_general | solution.py:38
  78.8 0.0 copy-start.3
  78.8 0.0 copy-start.8
  78.9 0.3 multiply_reduce_fusion
  79.2 1.0 copy-done.3
  80.1 0.0 copy-done.8
  80.2 0.6 add_convert_fusion
  80.8 0.0 copy-start.4
  80.8 2.1 %fusion.2 = f32[640,512]{1,0:T(8,128)} fusion(bf16[1280,512]{0,1:T(8,128)(2,1)S(1)} %add_convert_fusion, s32[1280]{0:T(1024)S(1)} %copy-done.7, pred[1280]{0:T(1024)(128)(4,1)S(1)} %iota_compare_fusion.1), kind=kOutput, calls=%fused_computation.8 | convolution fusion | flops 840499200 | bytes 2627840 | tf_op jit(solution)/shard_map/dot_general | solution.py:87
  82.9 0.0 copy-done.4
  82.9 0.0 copy-start.5
  82.9 4.3 %all-to-all-start.1 = ((f32[4,160,512]{2,1,0:T(8,128)}), f32[4,160,512]{2,1,0:T(8,128)S(1)}, u32[]{:S(2)}, u32[]{:S(2)}) async-start(f32[4,160,512]{2,1,0:T(8,128)} %bitcast.19), calls=%async_computation.1 | async-start | bytes 2621440 | tf_op jit(solution)/shard_map/all_to_all | solution.py:17
  87.2 2.0 %fusion.20 = f32[160,512]{1,0:T(8,128)} fusion(bf16[160,512]{1,0:T(8,128)(2,1)S(1)} %copy-done.1, bf16[1024,512]{1,0:T(8,128)(2,1)} %param.24), kind=kOutput, calls=%fused_computation.28 | convolution fusion | flops 83886080 | bytes 1015808 | tf_op jit(solution)/shard_map/dot_general | solution.py:43
  89.3 0.0 copy-done.5
  89.3 0.0 copy-start.11
  89.3 1.5 %copy.22 = bf16[1280,512]{1,0:T(8,128)(2,1)} copy(bf16[1280,512]{0,1:T(8,128)(2,1)S(1)} %copy-done.5) | data formatting | bytes 2621440
  90.8 14.1 %all-to-all-done.1 = f32[4,160,512]{2,1,0:T(8,128)S(1)} async-done(((f32[4,160,512]{2,1,0:T(8,128)}), f32[4,160,512]{2,1,0:T(8,128)S(1)}, u32[]{:S(2)}, u32[]{:S(2)}) %all-to-all-start.1) | async-done | bytes 1310752 | tf_op jit(solution)/shard_map/all_to_all | solution.py:17
  104.8 0.1 reduce_sum.47
  104.9 0.0 copy-done.11
  105.0 0.0 copy-start.9
  105.0 1.9 %fusion.47 = (f32[160]{0:T(256)S(1)}, f32[160,512]{1,0:T(8,128)S(1)}) fusion(bf16[512,512]{1,0:T(8,128)(2,1)} %param.26, f32[160,512]{1,0:T(8,128)} %fusion.20, bf16[1024,512]{1,0:T(8,128)(2,1)} %param.24, f32[512]{0:T(512)S(1)} %copy-done.11, bf16[160,512]{1,0:T(8,128)(2,1)S(1)} %reduce_sum.47), kind=kOutput, calls=%fused_computation.62 | convolution fusion | flops 168427360 | bytes 1870464 | tf_op jit(solution)/shard_map/dot_general | solution.py:46
  106.9 0.2 multiply_reduce_fusion.1
  107.1 0.0 copy-done.9
  107.1 0.8 add_convert_fusion.1
  (13 shorter events, 0.1 us)
Async XLA Ops:
  0.6 74.1 %copy-start = (bf16[512,512]{1,0:T(8,128)(2,1)S(1)}, bf16[512,512]{1,0:T(8,128)(2,1)}, u32[]{:S(2)}) copy-start(bf16[512,512]{1,0:T(8,128)(2,1)} %param.22) | copy-start | bytes 1572868
  9.7 52.8 %all-to-all-start = ((bf16[64,24,512]{2,1,0:T(8,128)(2,1)}), bf16[64,24,512]{2,1,0:T(8,128)(2,1)S(1)}, u32[]{:S(2)}, u32[]{:S(2)}) async-start(bf16[64,24,512]{2,1,0:T(8,128)(2,1)} %broadcast_select_fusion), calls=%async_computation | async-start | bytes 3145728 | tf_op jit(solution)/shard_map/all_to_all | solution.py:73
  22.7 3.1 %copy-start.7 = (s32[1280]{0:T(1024)S(1)}, s32[1280]{0:T(1024)}, u32[]{:S(2)}) copy-start(s32[1280]{0:T(1024)} %param.16) | copy-start | bytes 15364
  22.7 3.1 %copy-start.1 = (bf16[160,512]{1,0:T(8,128)(2,1)S(1)}, bf16[160,512]{1,0:T(8,128)(2,1)}, u32[]{:S(2)}) copy-start(bf16[160,512]{1,0:T(8,128)(2,1)} %param.14) | copy-start | bytes 491524
  37.8 4.7 %copy-start.6 = (s32[1280]{0:T(1024)S(1)}, s32[1280]{0:T(1024)}, u32[]{:S(2)}) copy-start(s32[1280]{0:T(1024)} %param.17) | copy-start | bytes 15364
  64.0 6.9 %copy-start.2 = (f32[1280,512]{1,0:T(8,128)S(1)}, f32[1280,512]{1,0:T(8,128)}, u32[]{:S(2)}) copy-start(f32[1280,512]{1,0:T(8,128)} %fusion.25) | copy-start | bytes 7864324
  70.9 3.9 %copy-start.10 = (f32[512]{0:T(512)S(1)}, f32[512]{0:T(512)}, u32[]{:S(2)}) copy-start(f32[512]{0:T(512)} %param.21) | copy-start | bytes 6148
  78.8 1.3 %copy-start.3 = (bf16[1280,512]{0,1:T(8,128)(2,1)S(1)}, bf16[1280,512]{0,1:T(8,128)(2,1)}, u32[]{:S(2)}) copy-start(bf16[1280,512]{0,1:T(8,128)(2,1)} %copy.19) | copy-start | bytes 3932164
  78.8 1.3 %copy-start.8 = (f32[512]{0:T(512)S(1)}, f32[512]{0:T(512)}, u32[]{:S(2)}) copy-start(f32[512]{0:T(512)} %param.23) | copy-start | bytes 6148
  80.8 2.1 %copy-start.4 = (bf16[1280,512]{0,1:T(8,128)(2,1)}, bf16[1280,512]{0,1:T(8,128)(2,1)S(1)}, u32[]{:S(2)}) copy-start(bf16[1280,512]{0,1:T(8,128)(2,1)S(1)} %add_convert_fusion) | copy-start | bytes 3932164
  82.9 6.3 %copy-start.5 = (bf16[1280,512]{0,1:T(8,128)(2,1)S(1)}, bf16[1280,512]{0,1:T(8,128)(2,1)}, u32[]{:S(2)}) copy-start(bf16[1280,512]{0,1:T(8,128)(2,1)} %copy-done.4) | copy-start | bytes 3932164
  82.9 21.9 %all-to-all-start.1 = ((f32[4,160,512]{2,1,0:T(8,128)}), f32[4,160,512]{2,1,0:T(8,128)S(1)}, u32[]{:S(2)}, u32[]{:S(2)}) async-start(f32[4,160,512]{2,1,0:T(8,128)} %bitcast.19), calls=%async_computation.1 | async-start | bytes 2621440 | tf_op jit(solution)/shard_map/all_to_all | solution.py:17
  89.3 15.7 %copy-start.11 = (f32[512]{0:T(512)S(1)}, f32[512]{0:T(512)}, u32[]{:S(2)}) copy-start(f32[512]{0:T(512)} %param.25) | copy-start | bytes 6148
  105.0 2.1 %copy-start.9 = (f32[512]{0:T(512)S(1)}, f32[512]{0:T(512)}, u32[]{:S(2)}) copy-start(f32[512]{0:T(512)} %param.27) | copy-start | bytes 6148
where the time goes:
time: 108 us
  waiting for transfers between devices  30.1 us (28%)
  local copies, waits for them, and re-layouts  23.4 us (22%)
  matrix products  17.8 us (16%)
  starting transfers between devices  17.3 us (16%)
  blocking collectives  12 us (11%)
  other arithmetic  5.84 us (5%)
  between operations  1.51 us (1%)
    all_to_all x1, waiting for transfers between devices, local(): lax.all_to_all(packed, 'patch', split_axis=0, concat_axis=0, tiled=True)  16 us
    all_to_all x1, waiting for transfers between devices, sum_at_owner(): tiles = lax.all_to_all(cut_along(value, dim, size), axis, 0, 0, tiled=True)  14.1 us
    all_to_all x1, starting transfers between devices, local(): lax.all_to_all(packed, 'patch', split_axis=0, concat_axis=0, tiled=True)  13 us
    all_gather x1, blocking collectives, local(): patch_rows = lax.all_gather(nodes, 'feat', axis=0, tiled=True)  12 us
    gather x1, local copies, waits for them, and re-layouts, local(): sender_feat = jnp.take(lookup_rows, sender_slot, axis=0)  6.87 us
    gather x1, local copies, waits for them, and re-layouts, local(): jnp.take(nodes, outgoing.reshape(-1), axis=0)  5.8 us
    unnamed x27, local copies, waits for them, and re-layouts  5.78 us
    gather x1, local copies, waits for them, and re-layouts, local(): receiver_feat = jnp.take(patch_rows, receivers, axis=0)  4.72 us
  transfers between devices with their start and end apart: 2, of which 2 were waited for; matrix products, arithmetic and copies ran while one was open for 13% of the time, Pallas kernels for 0%

commit v1 on v0

v1 whole, which is shorter than its diff:
```python
import functools

import jax
import jax.numpy as jnp
from jax import lax
from jax.experimental import pallas as pl
from jax.experimental.pallas import tpu as pltpu
from jax.sharding import PartitionSpec as P

epsilon = 1e-05
f32 = jnp.float32
bf16 = jnp.bfloat16
TILE = 256
LIMIT = 48 << 20


def dot(left, right):
    return jnp.dot(left, right, preferred_element_type=f32)


def silu(value):
    return value / (1.0 + jnp.exp(-value))


def layer_norm(values, scales):
    average = jnp.mean(values, axis=-1, keepdims=True)
    centred = values - average
    variance = jnp.mean(centred * centred, axis=-1, keepdims=True)
    return centred * lax.rsqrt(variance + epsilon) * scales


def one_hot_rows(column, count, first=0):
    ids = lax.broadcasted_iota(jnp.int32, (column.shape[0], count), 1) + first
    return (column == ids).astype(f32).astype(bf16)


def one_hot_columns(row, count):
    ids = lax.broadcasted_iota(jnp.int32, (count, row.shape[1]), 0)
    return row == ids


def whole(*shape):
    return pl.BlockSpec(shape, lambda i: (0,) * len(shape))


def rows_of(tile, width):
    return pl.BlockSpec((tile, width), lambda i: (i, 0))


def select_kernel(index_ref, table_ref, out_ref):
    hot = one_hot_columns(index_ref[...], table_ref.shape[0]).astype(f32).astype(bf16)
    rows = lax.dot_general(
        hot, table_ref[...], (((0,), (0,)), ((), ())), preferred_element_type=f32
    )
    out_ref[...] = rows.astype(bf16)


def select(index, table):
    count, width = index.shape[1], table.shape[1]
    tile = 512
    return pl.pallas_call(
        select_kernel,
        grid=(count // tile,),
        in_specs=[
            pl.BlockSpec((1, tile), lambda i: (0, i)),
            whole(*table.shape),
        ],
        out_specs=rows_of(tile, width),
        out_shape=jax.ShapeDtypeStruct((count, width), bf16),
        compiler_params=pltpu.CompilerParams(vmem_limit_bytes=LIMIT),
        name="select",
    )(index, table)


def before_kernel(patch_ref, edges_ref, recv_ref, send_ref, w1_ref, b1_ref, out_ref):
    latent = edges_ref.shape[1]
    count = patch_ref.shape[0]
    patch = patch_ref[...]
    own = dot(one_hot_rows(recv_ref[...], count), patch).astype(bf16)
    near = dot(one_hot_rows(send_ref[...], count), patch).astype(bf16)
    total = dot(edges_ref[...], w1_ref[:latent])
    total = total + dot(near, w1_ref[latent : 2 * latent])
    total = total + dot(own, w1_ref[2 * latent :])
    out_ref[...] = total + b1_ref[...]


def edge_before(patch_rows, edges, recv, send, w1, b1):
    count, latent = edges.shape
    return pl.pallas_call(
        before_kernel,
        grid=(count // TILE,),
        in_specs=[
            whole(*patch_rows.shape),
            rows_of(TILE, latent),
            rows_of(TILE, 1),
            rows_of(TILE, 1),
            whole(*w1.shape),
            whole(1, latent),
        ],
        out_specs=rows_of(TILE, latent),
        out_shape=jax.ShapeDtypeStruct((count, latent), f32),
        compiler_params=pltpu.CompilerParams(vmem_limit_bytes=LIMIT),
        cost_estimate=pl.CostEstimate(
            flops=2 * count * latent * (3 * latent + 2 * patch_rows.shape[0]),
            bytes_accessed=8 << 20,
            transcendentals=0,
        ),
        name="edge_before",
    )(patch_rows, edges, recv, send, w1, b1)


def after_kernel(
    live_ref, before_ref, remote_ref, edges_ref, send_ref, recv_ref, w1_ref, w2_ref, gain_ref,
    out_ref, sums_ref, total_ref,
):
    step = pl.program_id(0)
    tile = edges_ref.shape[0]
    nodes = sums_ref.shape[0]
    hot = one_hot_rows(send_ref[...], remote_ref.shape[0], nodes)
    far = dot(hot, remote_ref[...]).astype(bf16)
    hidden = silu(before_ref[...] + dot(far, w1_ref[...])).astype(bf16)
    change = layer_norm(dot(hidden, w2_ref[...]), gain_ref[...])
    live = live_ref[0] - step * tile
    alive = lax.broadcasted_iota(jnp.int32, (tile, 1), 0) < live
    edge = edges_ref[...].astype(f32) + jnp.where(alive, change, 0.0)
    edge = edge.astype(bf16)
    out_ref[...] = edge
    alive_row = lax.broadcasted_iota(jnp.int32, (1, tile), 1) < live
    receiver = jnp.where(alive_row, recv_ref[...], -1)
    hot = one_hot_columns(receiver, nodes).astype(f32).astype(bf16)
    part = dot(hot, edge)

    @pl.when(step == 0)
    def _():
        total_ref[...] = part

    @pl.when(step > 0)
    def _():
        total_ref[...] += part

    @pl.when(step == pl.num_programs(0) - 1)
    def _():
        sums_ref[...] = total_ref[...].astype(bf16)


def edge_after(live, before, remote, edges, send, recv, w1, w2, gain, nodes):
    count, latent = edges.shape
    return pl.pallas_call(
        after_kernel,
        grid=(count // TILE,),
        in_specs=[
            pl.BlockSpec(memory_space=pltpu.SMEM),
            rows_of(TILE, latent),
            whole(*remote.shape),
            rows_of(TILE, latent),
            rows_of(TILE, 1),
            pl.BlockSpec((1, TILE), lambda i: (0, i)),
            pl.BlockSpec((latent, latent), lambda i: (1, 0)),
            whole(*w2.shape),
            whole(1, latent),
        ],
        out_specs=[rows_of(TILE, latent), whole(nodes, latent)],
        out_shape=[
            jax.ShapeDtypeStruct((count, latent), bf16),
            jax.ShapeDtypeStruct((nodes, latent), bf16),
        ],
        scratch_shapes=[pltpu.VMEM((nodes, latent), f32)],
        compiler_params=pltpu.CompilerParams(vmem_limit_bytes=LIMIT),
        name="edge_after",
    )(live, before, remote, edges, send, recv, w1, w2, gain)


def node_kernel(nodes_ref, p0_ref, p1_ref, p2_ref, p3_ref, w1_ref, b1_ref, w2_ref, gain_ref, out_ref):
    latent = nodes_ref.shape[1]
    total = p0_ref[...].astype(f32) + p1_ref[...].astype(f32)
    total = total + p2_ref[...].astype(f32) + p3_ref[...].astype(f32)
    incoming = total.astype(bf16)
    nodes = nodes_ref[...]
    first = dot(nodes, w1_ref[:latent]) + dot(incoming, w1_ref[latent:])
    hidden = silu(first + b1_ref[...]).astype(bf16)
    change = layer_norm(dot(hidden, w2_ref[...]), gain_ref[...])
    out_ref[...] = (nodes.astype(f32) + change).astype(bf16)


def node_update(nodes, parts, w1, b1, w2, gain):
    return pl.pallas_call(
        node_kernel,
        out_shape=jax.ShapeDtypeStruct(nodes.shape, bf16),
        compiler_params=pltpu.CompilerParams(vmem_limit_bytes=LIMIT),
        name="node_update",
    )(nodes, *parts, w1, b1, w2, gain)


def local(
    nodes,
    edges,
    receivers,
    sender_slot,
    send_rows,
    live_edges,
    edge_w1,
    edge_b1,
    edge_w2,
    edge_gain,
    node_w1,
    node_b1,
    node_w2,
    node_gain,
):
    rows, latent = nodes.shape
    outgoing = send_rows[0, 0]
    packed = select(outgoing.reshape(1, -1), nodes).reshape(*outgoing.shape, latent)
    remote = lax.all_to_all(packed, "patch", split_axis=0, concat_axis=0, tiled=True)
    remote = remote.reshape(-1, latent)
    patch_rows = lax.all_gather(nodes, "feat", axis=0, tiled=True)
    recv = receivers.reshape(-1, 1)
    send = sender_slot.reshape(-1, 1)
    before = edge_before(patch_rows, edges, recv, send, edge_w1, edge_b1.reshape(1, -1))
    edges_out, sums = edge_after(
        live_edges, before, remote, edges, send, receivers.reshape(1, -1), edge_w1, edge_w2,
        edge_gain.reshape(1, -1), patch_rows.shape[0],
    )
    size = lax.axis_size("feat")
    me = lax.axis_index("feat")
    parts = []
    for k in range(size):
        part = lax.dynamic_slice_in_dim(sums, lax.rem(me + k, size) * rows, rows)
        if k:
            part = lax.ppermute(part, "feat", [(i, (i + k) % size) for i in range(size)])
        parts.append(part)
    nodes_out = node_update(
        nodes, parts, node_w1, node_b1.reshape(1, -1), node_w2, node_gain.reshape(1, -1)
    )
    return (edges_out, nodes_out)


def solution(mesh):
    placed = (
        P(("patch", "feat"), None),
        P(("patch", "feat"), None),
        P(("patch", "feat")),
        P(("patch", "feat")),
        P("patch", "feat", None, None),
        P(("patch", "feat")),
    ) + (P(),) * 8
    return jax.shard_map(
        local,
        mesh=mesh,
        in_specs=placed,
        out_specs=(P(("patch", "feat"), None), P(("patch", "feat"), None)),
        check_vma=False,
    )
```

time: 108 us -> 84.6 us (0.78)
  Pallas kernels: 0 us -> 21.2 us
  matrix products: 17.8 us -> 0 us
  local copies, waits for them, and re-layouts: 23.4 us -> 7.41 us
  waiting for transfers between devices: 30.1 us -> 23.9 us
  other arithmetic: 5.84 us -> 0 us
    pallas_call x0 -> x4, Pallas kernels: none -> 21.2 us  [the longest x1 11 us: edge_after(): pl.pallas_call(after_kernel, grid=(count // TILE,), in_specs=[pl.BlockSpe...]
    dot_general x6 -> x0, matrix products: 17.8 us -> none  [the longest x1 4.09 us: edge_change(): jnp.dot(hidden, edge_w2, preferred_element_type=jnp.float32)]
    gather x3 -> x0, local copies, waits for them, and re-layouts: 17.4 us -> none  [the longest x1 6.87 us: local(): sender_feat = jnp.take(lookup_rows, sender_slot, axis=0)]
    all_to_all x1 -> x0, waiting for transfers between devices: 14.1 us -> none  [sum_at_owner(): tiles = lax.all_to_all(cut_along(value, dim, size), axis, 0, 0, tiled=True)]
    ppermute x0 -> x3, waiting for transfers between devices: none -> 6.62 us  [local(): lax.ppermute(part, 'feat', [(i, (i + k) % size) for i in range(size)])]
    ppermute x0 -> x3, starting transfers between devices: none -> 5.05 us  [local(): lax.ppermute(part, 'feat', [(i, (i + k) % size) for i in range(size)])]
    all_to_all x1 -> x0, starting transfers between devices: 4.3 us -> none  [sum_at_owner(): tiles = lax.all_to_all(cut_along(value, dim, size), axis, 0, 0, tiled=True)]
    concatenate x1 -> x0, other arithmetic: 1.52 us -> none  [local(): lookup_rows = jnp.concatenate([patch_rows, remote], axis=0)]
  transfers between devices with their start and end apart: 2 -> 4, of which waited for: 2 -> 3; matrix products, arithmetic and copies ran while one was open for 13% -> 1% of each run, Pallas kernels for 0% -> 8%
where the time goes in v1:
time: 84.6 us; the launch traced here: 84.2 us
  waiting for transfers between devices  23.9 us (28%)
  Pallas kernels  21.2 us (25%)
  starting transfers between devices  18.2 us (22%)
  blocking collectives  12 us (14%)
  local copies, waits for them, and re-layouts  7.41 us (9%)
  between operations  1.44 us (2%)
    all_to_all x1, waiting for transfers between devices, local(): lax.all_to_all(packed, 'patch', split_axis=0, concat_axis=0, tiled=True)  17.3 us
    all_to_all x1, starting transfers between devices, local(): lax.all_to_all(packed, 'patch', split_axis=0, concat_axis=0, tiled=True)  13.1 us
    all_gather x1, blocking collectives, local(): patch_rows = lax.all_gather(nodes, 'feat', axis=0, tiled=True)  12 us
    pallas_call x1, Pallas kernels, edge_after(): pl.pallas_call(after_kernel, grid=(count // TILE,), in_specs=[pl.BlockSpe...  11 us
    unnamed x29, local copies, waits for them, and re-layouts  6.82 us
    ppermute x3, waiting for transfers between devices, local(): lax.ppermute(part, 'feat', [(i, (i + k) % size) for i in range(size)])  6.62 us
    pallas_call x1, Pallas kernels, edge_before(): pl.pallas_call(before_kernel, grid=(count // TILE,), in_specs=[whole(*pat...  6.52 us
    ppermute x3, starting transfers between devices, local(): lax.ppermute(part, 'feat', [(i, (i + k) % size) for i in range(size)])  5.05 us
  transfers between devices with their start and end apart: 4, of which 3 were waited for; matrix products, arithmetic and copies ran while one was open for 1% of the time, Pallas kernels for 8%

profile of v1, /device:TPU:1, one launch (start us, length us, event | category | flops | bytes accessed | tf_op | source)
XLA Modules:
  0.0 84.2 jit_solution(8456751476985194437)
XLA Ops:
  0.6 0.8 copy.19
  1.4 0.1 reshape_squeeze.3.index_ref
  1.5 0.0 copy-start.1
  1.5 0.9 %copy-done.1 = bf16[160,512]{1,0:T(8,128)(2,1)S(1)} copy-done((bf16[160,512]{1,0:T(8,128)(2,1)S(1)}, bf16[160,512]{1,0:T(8,128)(2,1)}, u32[]{:S(2)}) %copy-start.1) | copy-done | bytes 163864
  2.4 2.3 %select.9 = bf16[1536,512]{1,0:T(8,128)(2,1)} custom-call(s32[1,1536]{1,0:T(1,128)S(1)} %reshape_squeeze.3.index_ref, bf16[160,512]{1,0:T(8,128)(2,1)S(1)} %copy-done.1), custom_call_target="tpu_custom_call" | custom-call | tf_op jit(solution)/shard_map/select/pallas_call | solution.py:61
  4.7 0.0 copy-start.12
  4.7 0.0 copy-start.13
  4.7 0.0 copy-start.2
  4.7 13.1 %all-to-all-start = ((bf16[64,24,512]{2,1,0:T(8,128)(2,1)}), bf16[64,24,512]{2,1,0:T(8,128)(2,1)S(1)}, u32[]{:S(2)}, u32[]{:S(2)}) async-start(bf16[64,24,512]{2,1,0:T(8,128)(2,1)} %bitcast.1), calls=%async_computation | async-start | bytes 3145728 | tf_op jit(solution)/shard_map/all_to_all | solution.py:213
  17.8 0.0 copy-done.12
  17.9 0.0 copy-start.11
  17.9 0.2 reshape.40.recv_ref
  18.8 0.0 copy-done.13
  18.8 0.2 reshape.41.send_ref
  19.0 0.0 copy-done.2
  19.1 12.0 %all_gather.3.patch_ref = bf16[640,512]{1,0:T(8,128)(2,1)S(1)} all-gather(bf16[160,512]{1,0:T(8,128)(2,1)S(1)} %copy-done.2), channel_id=1, replica_groups=mesh['patch'=64,'feat'=4] {'feat'}, dimensions={0}, use_global_device_ids=true | all-gather | bytes 819200 | tf_op jit(solution)/shard_map/all_gather | solution.py:215
  31.1 0.0 copy-done.11
  31.1 0.0 copy-start
  31.1 1.4 %copy-done = bf16[1536,512]{1,0:T(8,128)(2,1)S(1)} copy-done((bf16[1536,512]{1,0:T(8,128)(2,1)S(1)}, bf16[1536,512]{1,0:T(8,128)(2,1)}, u32[]{:S(2)}) %copy-start) | copy-done | bytes 1572888
  32.5 0.0 copy-start.3
  32.5 1.3 %copy-done.3 = bf16[1280,512]{1,0:T(8,128)(2,1)S(1)} copy-done((bf16[1280,512]{1,0:T(8,128)(2,1)S(1)}, bf16[1280,512]{1,0:T(8,128)(2,1)}, u32[]{:S(2)}) %copy-start.3) | copy-done | bytes 1310744
  33.8 0.0 copy-start.8
  33.8 6.5 %edge_before.1.before_ref = f32[1280,512]{1,0:T(8,128)} custom-call(bf16[640,512]{1,0:T(8,128)(2,1)S(1)} %all_gather.3.patch_ref, bf16[1280,512]{1,0:T(8,128)(2,1)S(1)} %copy-done.3, s32[1280,1]{1,0:T(8,128)S(1)} %reshape.40.recv_ref, s32[1280,1]{1,0:T(8,128)S(1)} %reshape.41.send_ref, bf16[1536,512]{1,0:T(8,128)(2,1)S(1)} %copy-done, f32[1,512]{1,0:T(1,128)S(1)} %bitcast.12), custom_call_target="tpu_custom_call" | custom-call | flops 3690987520 | bytes 8388608 | tf_op jit(solution)/shard_map/edge_before/pallas_call | solution.py:89
  40.3 17.3 %all-to-all-done = bf16[64,24,512]{2,1,0:T(8,128)(2,1)S(1)} async-done(((bf16[64,24,512]{2,1,0:T(8,128)(2,1)}), bf16[64,24,512]{2,1,0:T(8,128)(2,1)S(1)}, u32[]{:S(2)}, u32[]{:S(2)}) %all-to-all-start) | async-done | bytes 1572896 | tf_op jit(solution)/shard_map/all_to_all | solution.py:213
  57.6 0.0 copy-done.8
  57.6 0.0 copy-start.4
  57.6 1.3 %copy-done.4 = bf16[1280,512]{1,0:T(8,128)(2,1)S(1)} copy-done((bf16[1280,512]{1,0:T(8,128)(2,1)S(1)}, bf16[1280,512]{1,0:T(8,128)(2,1)}, u32[]{:S(2)}) %copy-start.4) | copy-done | bytes 1310744
  59.0 0.0 copy-start.6
  59.0 1.0 %copy-done.6 = bf16[512,512]{1,0:T(8,128)(2,1)S(1)} copy-done((bf16[512,512]{1,0:T(8,128)(2,1)S(1)}, bf16[512,512]{1,0:T(8,128)(2,1)}, u32[]{:S(2)}) %copy-start.6) | copy-done | bytes 524312
  60.0 0.0 copy-start.7
  60.0 0.0 copy-start.9
  60.0 0.0 copy-start.10
  60.0 11.0 %edge_after.1 = (bf16[1280,512]{1,0:T(8,128)(2,1)}, bf16[640,512]{1,0:T(8,128)(2,1)S(1)}) custom-call(s32[1]{0:T(128)S(6)} %copy.21.live_ref, f32[1280,512]{1,0:T(8,128)} %edge_before.1.before_ref, bf16[1536,512]{1,0:T(8,128)(2,1)S(1)} %bitcast.8, bf16[1280,512]{1,0:T(8,128)(2,1)S(1)} %copy-done.4, s32[1280,1]{1,0:T(8,128)S(1)} %reshape.41.send_ref, ...), custom_call_target="tpu_custom_call" | custom-call | tf_op jit(solution)/shard_map/edge_after/pallas_call | solution.py:148
  71.0 0.0 copy-start.5
  71.0 1.4 %collective-permute-start = (bf16[160,512]{1,0:T(8,128)(2,1)S(1)}, bf16[160,512]{1,0:T(8,128)(2,1)S(1)}, u32[]{:S(2)}, u32[]{:S(2)}) collective-permute-start(bf16[160,512]{1,0:T(8,128)(2,1)S(1)} %get-tuple-element.8), channel_id=1, source_target_pairs={{0,1},{1,2},{2,3},{3,0},{4,5},{5,6},{6,7},{7,4},{8,9},{9,10},{10,1... | collective-permute-start | bytes 491528 | tf_op jit(solution)/shard_map/ppermute | solution.py:229
  72.4 2.6 %collective-permute-start.1 = (bf16[160,512]{1,0:T(8,128)(2,1)S(1)}, bf16[160,512]{1,0:T(8,128)(2,1)S(1)}, u32[]{:S(2)}, u32[]{:S(2)}) collective-permute-start(bf16[160,512]{1,0:T(8,128)(2,1)S(1)} %get-tuple-element.7), channel_id=1, source_target_pairs={{0,2},{1,3},{2,0},{3,1},{4,6},{5,7},{6,4},{7,5},{8,10},{9,11},{10,... | collective-permute-start | bytes 491528 | tf_op jit(solution)/shard_map/ppermute | solution.py:229
  75.0 1.1 %collective-permute-start.2 = (bf16[160,512]{1,0:T(8,128)(2,1)S(1)}, bf16[160,512]{1,0:T(8,128)(2,1)S(1)}, u32[]{:S(2)}, u32[]{:S(2)}) collective-permute-start(bf16[160,512]{1,0:T(8,128)(2,1)S(1)} %get-tuple-element.6), channel_id=1, source_target_pairs={{0,3},{1,0},{2,1},{3,2},{4,7},{5,4},{6,5},{7,6},{8,11},{9,8},{10,9... | collective-permute-start | bytes 491528 | tf_op jit(solution)/shard_map/ppermute | solution.py:229
  76.1 2.0 %collective-permute-done.p1_ref = bf16[160,512]{1,0:T(8,128)(2,1)S(1)} collective-permute-done((bf16[160,512]{1,0:T(8,128)(2,1)S(1)}, bf16[160,512]{1,0:T(8,128)(2,1)S(1)}, u32[]{:S(2)}, u32[]{:S(2)}) %collective-permute-start) | collective-permute-done | bytes 163872 | tf_op jit(solution)/shard_map/ppermute | solution.py:229
  78.1 4.6 %collective-permute-done.1.p2_ref = bf16[160,512]{1,0:T(8,128)(2,1)S(1)} collective-permute-done((bf16[160,512]{1,0:T(8,128)(2,1)S(1)}, bf16[160,512]{1,0:T(8,128)(2,1)S(1)}, u32[]{:S(2)}, u32[]{:S(2)}) %collective-permute-start.1) | collective-permute-done | bytes 163872 | tf_op jit(solution)/shard_map/ppermute | solution.py:229
  82.7 0.0 collective-permute-done.2.p3_ref
  82.7 0.0 copy-done.7
  82.7 0.0 copy-done.9
  82.7 0.0 copy-done.10
  82.7 0.0 copy-done.5
  82.7 1.4 %node_update.1 = bf16[160,512]{1,0:T(8,128)(2,1)} custom-call(bf16[160,512]{1,0:T(8,128)(2,1)S(1)} %copy-done.2, bf16[160,512]{1,0:T(8,128)(2,1)S(1)} %get-tuple-element.9.p0_ref, bf16[160,512]{1,0:T(8,128)(2,1)S(1)} %collective-permute-done.p1_ref, bf16[160,512]{1,0:T(8,128)(2,1)S(1)} %collective-permute-done.1.p2_ref, ...), custom_call_target="tpu_custom_call" | custom-call | tf_op jit(solution)/shard_map/node_update/pallas_call | solution.py:186
  (2 shorter events, 0.1 us)
Async XLA Ops:
  1.5 0.9 %copy-start.1 = (bf16[160,512]{1,0:T(8,128)(2,1)S(1)}, bf16[160,512]{1,0:T(8,128)(2,1)}, u32[]{:S(2)}) copy-start(bf16[160,512]{1,0:T(8,128)(2,1)} %nodes_ref.1) | copy-start | bytes 491524
  4.7 13.1 %copy-start.12 = (s32[1280]{0:T(1024)S(1)}, s32[1280]{0:T(1024)}, u32[]{:S(2)}) copy-start(s32[1280]{0:T(1024)} %param.16) | copy-start | bytes 15364
  4.7 14.1 %copy-start.13 = (s32[1280]{0:T(1024)S(1)}, s32[1280]{0:T(1024)}, u32[]{:S(2)}) copy-start(s32[1280]{0:T(1024)} %param.17) | copy-start | bytes 15364
  4.7 14.3 %copy-start.2 = (bf16[160,512]{1,0:T(8,128)(2,1)S(1)}, bf16[160,512]{1,0:T(8,128)(2,1)}, u32[]{:S(2)}) copy-start(bf16[160,512]{1,0:T(8,128)(2,1)} %nodes_ref.1) | copy-start | bytes 491524
  4.7 52.9 %all-to-all-start = ((bf16[64,24,512]{2,1,0:T(8,128)(2,1)}), bf16[64,24,512]{2,1,0:T(8,128)(2,1)S(1)}, u32[]{:S(2)}, u32[]{:S(2)}) async-start(bf16[64,24,512]{2,1,0:T(8,128)(2,1)} %bitcast.1), calls=%async_computation | async-start | bytes 3145728 | tf_op jit(solution)/shard_map/all_to_all | solution.py:213
  17.9 13.2 %copy-start.11 = (f32[512]{0:T(512)S(1)}, f32[512]{0:T(512)}, u32[]{:S(2)}) copy-start(f32[512]{0:T(512)} %param.21) | copy-start | bytes 6148
  31.1 1.4 %copy-start = (bf16[1536,512]{1,0:T(8,128)(2,1)S(1)}, bf16[1536,512]{1,0:T(8,128)(2,1)}, u32[]{:S(2)}) copy-start(bf16[1536,512]{1,0:T(8,128)(2,1)} %w1_ref.4) | copy-start | bytes 4718596
  32.5 1.3 %copy-start.3 = (bf16[1280,512]{1,0:T(8,128)(2,1)S(1)}, bf16[1280,512]{1,0:T(8,128)(2,1)}, u32[]{:S(2)}) copy-start(bf16[1280,512]{1,0:T(8,128)(2,1)} %edges_ref.3) | copy-start | bytes 3932164
  33.8 23.8 %copy-start.8 = (f32[512]{0:T(512)S(1)}, f32[512]{0:T(512)}, u32[]{:S(2)}) copy-start(f32[512]{0:T(512)} %param.23) | copy-start | bytes 6148
  57.6 1.3 %copy-start.4 = (bf16[1280,512]{1,0:T(8,128)(2,1)S(1)}, bf16[1280,512]{1,0:T(8,128)(2,1)}, u32[]{:S(2)}) copy-start(bf16[1280,512]{1,0:T(8,128)(2,1)} %edges_ref.3) | copy-start | bytes 3932164
  59.0 1.0 %copy-start.6 = (bf16[512,512]{1,0:T(8,128)(2,1)S(1)}, bf16[512,512]{1,0:T(8,128)(2,1)}, u32[]{:S(2)}) copy-start(bf16[512,512]{1,0:T(8,128)(2,1)} %w2_ref.2) | copy-start | bytes 1572868
  60.0 22.7 %copy-start.7 = (bf16[512,512]{1,0:T(8,128)(2,1)S(1)}, bf16[512,512]{1,0:T(8,128)(2,1)}, u32[]{:S(2)}) copy-start(bf16[512,512]{1,0:T(8,128)(2,1)} %w2_ref.3) | copy-start | bytes 1572868
  60.0 22.7 %copy-start.9 = (f32[512]{0:T(512)S(1)}, f32[512]{0:T(512)}, u32[]{:S(2)}) copy-start(f32[512]{0:T(512)} %param.25) | copy-start | bytes 6148
  60.0 22.7 %copy-start.10 = (f32[512]{0:T(512)S(1)}, f32[512]{0:T(512)}, u32[]{:S(2)}) copy-start(f32[512]{0:T(512)} %param.27) | copy-start | bytes 6148
  71.0 11.8 %copy-start.5 = (bf16[1024,512]{1,0:T(8,128)(2,1)S(1)}, bf16[1024,512]{1,0:T(8,128)(2,1)}, u32[]{:S(2)}) copy-start(bf16[1024,512]{1,0:T(8,128)(2,1)} %w1_ref.5) | copy-start | bytes 3145732
  71.0 7.1 %collective-permute-start = (bf16[160,512]{1,0:T(8,128)(2,1)S(1)}, bf16[160,512]{1,0:T(8,128)(2,1)S(1)}, u32[]{:S(2)}, u32[]{:S(2)}) collective-permute-start(bf16[160,512]{1,0:T(8,128)(2,1)S(1)} %get-tuple-element.8), channel_id=1, source_target_pairs={{0,1},{1,2},{2,3},{3,0},{4,5},{5,6},{6,7},{7,4},{8,9},{9,10},{10,1... | collective-permute-start | bytes 491528 | tf_op jit(solution)/shard_map/ppermute | solution.py:229
  72.4 10.3 %collective-permute-start.1 = (bf16[160,512]{1,0:T(8,128)(2,1)S(1)}, bf16[160,512]{1,0:T(8,128)(2,1)S(1)}, u32[]{:S(2)}, u32[]{:S(2)}) collective-permute-start(bf16[160,512]{1,0:T(8,128)(2,1)S(1)} %get-tuple-element.7), channel_id=1, source_target_pairs={{0,2},{1,3},{2,0},{3,1},{4,6},{5,7},{6,4},{7,5},{8,10},{9,11},{10,... | collective-permute-start | bytes 491528 | tf_op jit(solution)/shard_map/ppermute | solution.py:229
  75.0 7.7 %collective-permute-start.2 = (bf16[160,512]{1,0:T(8,128)(2,1)S(1)}, bf16[160,512]{1,0:T(8,128)(2,1)S(1)}, u32[]{:S(2)}, u32[]{:S(2)}) collective-permute-start(bf16[160,512]{1,0:T(8,128)(2,1)S(1)} %get-tuple-element.6), channel_id=1, source_target_pairs={{0,3},{1,0},{2,1},{3,2},{4,7},{5,4},{6,5},{7,6},{8,11},{9,8},{10,9... | collective-permute-start | bytes 491528 | tf_op jit(solution)/shard_map/ppermute | solution.py:229

commit v2 on v1

v2 whole, which is shorter than its diff:
```python
import jax
import jax.numpy as jnp
from jax import lax
from jax.experimental import pallas as pl
from jax.experimental.pallas import tpu as pltpu
from jax.sharding import PartitionSpec as P

epsilon = 1e-05
f32 = jnp.float32
bf16 = jnp.bfloat16
i32 = jnp.int32
TILE = 256
LIMIT = 48 << 20
X, Z, C = 4, 8, 2
TAIL = 16
BATCHES = (((0, 1), (7, 2)), ((6, 3),), ((5, 4),))


def dot(left, right):
    return jnp.dot(left, right, preferred_element_type=f32)


def dot_first(left, right):
    return lax.dot_general(left, right, (((0,), (0,)), ((), ())), preferred_element_type=f32)


def silu(value):
    return value / (1.0 + jnp.exp(-value))


def layer_norm(values, scales):
    average = jnp.mean(values, axis=-1, keepdims=True)
    centred = values - average
    variance = jnp.mean(centred * centred, axis=-1, keepdims=True)
    return centred * lax.rsqrt(variance + epsilon) * scales


def as_bf16(mask):
    return mask.astype(f32).astype(bf16)


def hot_rows(column, count, first=0):
    ids = lax.broadcasted_iota(i32, (column.shape[0], count), 1) + first
    return as_bf16(column == ids)


def hot_columns(row, count):
    return as_bf16(row == lax.broadcasted_iota(i32, (count, row.shape[1]), 0))


def whole(*shape):
    return pl.BlockSpec(shape, lambda i: (0,) * len(shape))


def rows_of(tile, width):
    return pl.BlockSpec((tile, width), lambda i: (i, 0))


def odd(dz):
    return (dz >= 1) & (dz <= 4)


def pack_kernel(where_ref, lists_ref, nodes_ref, out_ref):
    rows, latent = nodes_ref.shape
    cap, peers = lists_ref.shape
    out_ref[:rows] = nodes_ref[...]
    me = where_ref[0]
    x, z, c = me // (Z * C), me // C % Z, me % C
    lane = lax.broadcasted_iota(i32, (cap, latent), 1)
    spread = as_bf16(lane % cap == lax.broadcasted_iota(i32, (cap, latent), 0))
    listed = dot_first(lists_ref[...].astype(f32).astype(bf16), spread)
    peer = lax.broadcasted_iota(i32, (peers, latent), 0)
    lane = lax.broadcasted_iota(i32, (peers, latent), 1)
    k = (peer // (Z * C) - x) & (X - 1)
    dz = (peer // C % Z - z) & (Z - 1)
    s = (peer % C - c) & (C - 1)
    slot = (k * C + s) * 2 + jnp.where(odd(dz), 1, 0)
    listed = jnp.where(lane // cap == slot, listed + 1.0, 0.0).astype(bf16)
    row = lax.broadcasted_iota(i32, (TAIL, peers), 0)
    peer = lax.broadcasted_iota(i32, (TAIL, peers), 1)
    pick = as_bf16(row == ((peer // C % Z - z) & (Z - 1)))
    out_ref[rows:] = (dot(pick, listed) - 1.0).astype(bf16)


def pack(me, lists, nodes):
    return pl.pallas_call(
        pack_kernel,
        in_specs=[
            pl.BlockSpec(memory_space=pltpu.SMEM),
            pl.BlockSpec(memory_space=pltpu.VMEM),
            pl.BlockSpec(memory_space=pltpu.VMEM),
        ],
        out_shape=jax.ShapeDtypeStruct((nodes.shape[0] + TAIL, nodes.shape[1]), bf16),
        name="pack",
    )(me, lists, nodes)


def select_kernel(pairs, cap, *refs):
    blocks, outs = refs[: 2 * len(pairs)], refs[2 * len(pairs) :]
    rows = blocks[0].shape[0] - TAIL
    lanes = X * C * 2 * cap
    for at, pair in enumerate(pairs):
        total = None
        for side, dz in enumerate(pair):
            block = blocks[2 * at + side]
            wanted = block[rows:].astype(f32)[dz : dz + 1, :lanes].astype(i32)
            part = dot_first(hot_columns(wanted, rows), block[:rows])
            total = part if total is None else total + part
        total = total.astype(bf16)
        size = 2 * cap
        for k in range(X):
            for s in range(C):
                first = (k * C + s) * size
                put = (s * len(pairs) + at) * size
                outs[k][put : put + size] = total[first : first + size]


def select(pairs, cap, blocks):
    latent = blocks[0].shape[1]
    shape = jax.ShapeDtypeStruct((C * len(pairs) * 2 * cap, latent), bf16)
    rows = blocks[0].shape[0]
    return pl.pallas_call(
        lambda *refs: select_kernel(pairs, cap, *refs),
        out_shape=[shape] * X,
        cost_estimate=pl.CostEstimate(
            flops=len(pairs) * 2 * 384 * rows * latent * 4,
            bytes_accessed=len(pairs) * 2 << 20,
            transcendentals=0,
        ),
        name="select",
    )(*blocks)


def before_kernel(
    n0_ref, n1_ref, n2_ref, n3_ref, edges_ref, recv_ref, send_ref, w1_ref, b1_ref, out_ref, patch_ref
):
    latent = edges_ref.shape[1]
    rows = n0_ref.shape[0]
    count = patch_ref.shape[0]

    @pl.when(pl.program_id(0) == 0)
    def _():
        for k, ref in enumerate((n0_ref, n1_ref, n2_ref, n3_ref)):
            patch_ref[k * rows : (k + 1) * rows] = ref[...]

    patch = patch_ref[...]
    own = dot(hot_rows(recv_ref[...], count), patch).astype(bf16)
    near = dot(hot_rows(send_ref[...], count), patch).astype(bf16)
    total = dot(edges_ref[...], w1_ref[:latent])
    total = total + dot(near, w1_ref[latent : 2 * latent])
    total = total + dot(own, w1_ref[2 * latent :])
    out_ref[...] = total + b1_ref[...]


def edge_before(parts, edges, recv, send, w1, b1):
    count, latent = edges.shape
    rows = parts[0].shape[0]
    return pl.pallas_call(
        before_kernel,
        grid=(count // TILE,),
        in_specs=[whole(rows, latent)] * 4
        + [
            rows_of(TILE, latent),
            rows_of(TILE, 1),
            rows_of(TILE, 1),
            whole(*w1.shape),
            whole(1, latent),
        ],
        out_specs=rows_of(TILE, latent),
        out_shape=jax.ShapeDtypeStruct((count, latent), f32),
        scratch_shapes=[pltpu.VMEM((4 * rows, latent), bf16)],
        compiler_params=pltpu.CompilerParams(vmem_limit_bytes=LIMIT),
        cost_estimate=pl.CostEstimate(
            flops=2 * count * latent * (3 * latent + 8 * rows),
            bytes_accessed=8 << 20,
            transcendentals=0,
        ),
        name="edge_before",
    )(*parts, edges, recv, send, w1, b1)


def after_kernel(cap, *refs):
    live_ref, before_ref, edges_ref, send_ref, recv_ref, w1_ref, w2_ref, gain_ref = refs[:8]
    count = len(BATCHES) * (X + 1)
    remote_refs = refs[8 : 8 + count]
    out_ref, s0_ref, s1_ref, s2_ref, s3_ref, total_ref, table_ref = refs[8 + count :]
    step = pl.program_id(0)
    tile = edges_ref.shape[0]
    rows = s0_ref.shape[0]
    nodes = 4 * rows

    @pl.when(step == 0)
    def _():
        total_ref[...] = jnp.zeros_like(total_ref)
        put = 0
        for at, pairs in enumerate(BATCHES):
            size = len(pairs) * 2 * cap
            group = remote_refs[at * (X + 1) : (at + 1) * (X + 1)]
            for k in range(X):
                table_ref[put : put + size] = group[k][:size]
                put += size
            table_ref[put : put + X * size] = group[X][...]
            put += X * size

    hot = hot_rows(send_ref[...], table_ref.shape[0], nodes)
    far = dot(hot, table_ref[...]).astype(bf16)
    hidden = silu(before_ref[...] + dot(far, w1_ref[...])).astype(bf16)
    change = layer_norm(dot(hidden, w2_ref[...]), gain_ref[...])
    live = live_ref[0] - step * tile
    alive = lax.broadcasted_iota(i32, (tile, 1), 0) < live
    edge = edges_ref[...].astype(f32) + jnp.where(alive, change, 0.0)
    edge = edge.astype(bf16)
    out_ref[...] = edge
    alive_row = lax.broadcasted_iota(i32, (1, tile), 1) < live
    receiver = jnp.where(alive_row, recv_ref[...], -1)
    total_ref[...] += dot(hot_columns(receiver, nodes), edge)

    @pl.when(step == pl.num_programs(0) - 1)
    def _():
        for k, ref in enumerate((s0_ref, s1_ref, s2_ref, s3_ref)):
            ref[...] = total_ref[k * rows : (k + 1) * rows].astype(ref.dtype)


def edge_after(cap, rows, live, before, edges, send, recv, w1, w2, gain, remote):
    count, latent = edges.shape
    slots = X * Z * C * cap
    sums = jax.ShapeDtypeStruct((rows, latent), bf16)
    return pl.pallas_call(
        lambda *refs: after_kernel(cap, *refs),
        grid=(count // TILE,),
        in_specs=[
            pl.BlockSpec(memory_space=pltpu.SMEM),
            rows_of(TILE, latent),
            rows_of(TILE, latent),
            rows_of(TILE, 1),
            pl.BlockSpec((1, TILE), lambda i: (0, i)),
            pl.BlockSpec((latent, latent), lambda i: (1, 0)),
            whole(*w2.shape),
            whole(1, latent),
        ]
        + [whole(*part.shape) for part in remote],
        out_specs=[rows_of(TILE, latent)] + [whole(rows, latent)] * 4,
        out_shape=[
            jax.ShapeDtypeStruct((count, latent), bf16),
            jax.ShapeDtypeStruct((rows, latent), f32),
            sums,
            sums,
            sums,
        ],
        scratch_shapes=[pltpu.VMEM((4 * rows, latent), f32), pltpu.VMEM((slots, latent), bf16)],
        compiler_params=pltpu.CompilerParams(vmem_limit_bytes=LIMIT),
        name="edge_after",
    )(live, before, edges, send, recv, w1, w2, gain, *remote)


def node_kernel(nodes_ref, p0_ref, p1_ref, p2_ref, p3_ref, w1_ref, b1_ref, w2_ref, gain_ref, out_ref):
    latent = nodes_ref.shape[1]
    total = p0_ref[...].astype(f32) + p1_ref[...].astype(f32)
    total = total + p2_ref[...].astype(f32) + p3_ref[...].astype(f32)
    incoming = total.astype(bf16)
    nodes = nodes_ref[...]
    first = dot(nodes, w1_ref[:latent]) + dot(incoming, w1_ref[latent:])
    hidden = silu(first + b1_ref[...]).astype(bf16)
    change = layer_norm(dot(hidden, w2_ref[...]), gain_ref[...])
    out_ref[...] = (nodes.astype(f32) + change).astype(bf16)


def node_update(nodes, parts, w1, b1, w2, gain):
    return pl.pallas_call(
        node_kernel,
        out_shape=jax.ShapeDtypeStruct(nodes.shape, bf16),
        compiler_params=pltpu.CompilerParams(vmem_limit_bytes=LIMIT),
        name="node_update",
    )(nodes, *parts, w1, b1, w2, gain)


def pairs_of(move):
    found = []
    for x in range(X):
        for z in range(Z):
            for c in range(C):
                tx, tz, tc = move(x, z, c)
                found.append(((x * Z + z) * C + c, ((tx % X) * Z + tz % Z) * C + tc % C))
    return found


def moved(value, move):
    return lax.ppermute(value, "patch", pairs_of(move))


def local(
    nodes,
    edges,
    receivers,
    sender_slot,
    send_rows,
    live_edges,
    edge_w1,
    edge_b1,
    edge_w2,
    edge_gain,
    node_w1,
    node_b1,
    node_w2,
    node_gain,
):
    rows, latent = nodes.shape
    cap = send_rows.shape[3]
    me = lax.axis_index("patch")
    mine = lax.axis_index("feat")
    x, z, c = me // (Z * C), me // C % Z, me % C
    feat = lax.axis_size("feat")

    block = pack(me.reshape(1), send_rows[0, 0].T, nodes)
    up = lambda a: moved(a, lambda x, z, c: (x, z + 1, c))
    down = lambda a: moved(a, lambda x, z, c: (x, z - 1, c))
    held = {0: block}
    forth = back = block
    for hop in range(1, 4):
        forth, back = up(forth), down(back)
        held[hop], held[Z - hop] = forth, back
    last = jnp.where(c == 0, forth, back)
    held[4] = moved(last, lambda x, z, c: (x, z + 1 - 2 * c, c))

    remote = []
    for pairs in BATCHES:
        picked = select(pairs, cap, [held[dz] for pair in pairs for dz in pair])
        group = [picked[0]]
        for k in range(1, X):
            group.append(moved(picked[k], lambda x, z, c: (x + k, z, c)))
        size = len(pairs) * 2 * cap
        crossing = jnp.concatenate([part[size:] for part in group], axis=0)
        group.append(moved(crossing, lambda x, z, c: (x, z, c + 1)))
        remote += group

    parts = [nodes]
    for k in range(1, feat):
        parts.append(lax.ppermute(nodes, "feat", [(i, (i + k) % feat) for i in range(feat)]))

    def near_row(row):
        return ((mine - row // rows) & (feat - 1)) * rows + row % rows

    patch_rows = feat * rows
    slot = jnp.maximum(sender_slot - patch_rows, 0)
    source, entry = slot // cap, slot % cap
    k = (x - source // (Z * C)) & (X - 1)
    dz = (z - source // C % Z) & (Z - 1)
    s = (source - c) & (C - 1)
    place = jnp.zeros_like(slot)
    base = 0
    for pairs in BATCHES:
        for at, pair in enumerate(pairs):
            for side, value in enumerate(pair):
                size = len(pairs) * 2 * cap
                here = base + (s * X + k) * size + at * 2 * cap + side * cap
                place = jnp.where(dz == value, here, place)
        base += X * C * len(pairs) * 2 * cap
    far_row = patch_rows + place + entry
    send = jnp.where(sender_slot < patch_rows, near_row(sender_slot), far_row).reshape(-1, 1)
    recv = near_row(receivers)

    before = edge_before(
        parts, edges, recv.reshape(-1, 1), send, edge_w1, edge_b1.reshape(1, -1)
    )
    edges_out, *sums = edge_after(
        cap, rows, live_edges, before, edges, send, recv.reshape(1, -1), edge_w1, edge_w2,
        edge_gain.reshape(1, -1), remote,
    )
    parts = [sums[0]]
    for k in range(1, feat):
        parts.append(lax.ppermute(sums[k], "feat", [(i, (i - k) % feat) for i in range(feat)]))
    nodes_out = node_update(
        nodes, parts, node_w1, node_b1.reshape(1, -1), node_w2, node_gain.reshape(1, -1)
    )
    return (edges_out, nodes_out)


def solution(mesh):
    placed = (
        P(("patch", "feat"), None),
        P(("patch", "feat"), None),
        P(("patch", "feat")),
        P(("patch", "feat")),
        P("patch", "feat", None, None),
        P(("patch", "feat")),
    ) + (P(),) * 8
    return jax.shard_map(
        local,
        mesh=mesh,
        in_specs=placed,
        out_specs=(P(("patch", "feat"), None), P(("patch", "feat"), None)),
        check_vma=False,
    )
```

time: 84.6 us -> 99.4 us (1.17)
  starting transfers between devices: 18.2 us -> 39.4 us
  blocking collectives: 12 us -> 0 us
  waiting for transfers between devices: 23.9 us -> 15.9 us
  Pallas kernels: 21.2 us -> 28.8 us
  local copies, waits for them, and re-layouts: 7.41 us -> 10.4 us
  other arithmetic: 0 us -> 2.7 us
    ppermute x3 -> x25, starting transfers between devices: 5.05 us -> 39.4 us  [the longest x19 32.1 us: moved(): return lax.ppermute(value, 'patch', pairs_of(move))]
    all_to_all x1 -> x0, waiting for transfers between devices: 17.3 us -> none  [local(): lax.all_to_all(packed, 'patch', split_axis=0, concat_axis=0, tiled=True)]
    all_to_all x1 -> x0, starting transfers between devices: 13.1 us -> none  [local(): lax.all_to_all(packed, 'patch', split_axis=0, concat_axis=0, tiled=True)]
    all_gather x1 -> x0, blocking collectives: 12 us -> none  [local(): patch_rows = lax.all_gather(nodes, 'feat', axis=0, tiled=True)]
    ppermute x3 -> x25, waiting for transfers between devices: 6.62 us -> 15.9 us  [the longest x3 9.88 us: local(): lax.ppermute(sums[k], 'feat', [(i, (i - k) % feat) for i in range(feat)])]
    pallas_call x3 -> x6, Pallas kernels: 19.8 us -> 27.3 us  [the longest x1 10.8 us: edge_after(): pl.pallas_call(lambda *refs: after_kernel(cap, *refs), grid=(count // TIL...]
    slice x0 -> x12, local copies, waits for them, and re-layouts: none -> 7.24 us  [local(): crossing = jnp.concatenate([part[size:] for part in group], axis=0)]
    unnamed x29 -> x58, local copies, waits for them, and re-layouts: 6.82 us -> 1.87 us
  transfers between devices with their start and end apart: 4 -> 25, of which waited for: 3 -> 5; matrix products, arithmetic and copies ran while one was open for 1% -> 11% of each run, Pallas kernels for 8% -> 15%
where the time goes in v2:
time: 99.4 us; the launch traced here: 98.8 us
  starting transfers between devices  39.4 us (40%)
  Pallas kernels  28.8 us (29%)
  waiting for transfers between devices  15.9 us (16%)
  local copies, waits for them, and re-layouts  10.4 us (10%)
  other arithmetic  2.7 us (3%)
  between operations  1.63 us (2%)
    ppermute x19, starting transfers between devices, moved(): return lax.ppermute(value, 'patch', pairs_of(move))  32.1 us
    pallas_call x1, Pallas kernels, edge_after(): pl.pallas_call(lambda *refs: after_kernel(cap, *refs), grid=(count // TIL...  10.8 us
    ppermute x3, waiting for transfers between devices, local(): lax.ppermute(sums[k], 'feat', [(i, (i - k) % feat) for i in range(feat)])  9.88 us
    pallas_call x1, Pallas kernels, edge_before(): pl.pallas_call(before_kernel, grid=(count // TILE,), in_specs=[whole(rows...  7.63 us
    slice x12, local copies, waits for them, and re-layouts, local(): crossing = jnp.concatenate([part[size:] for part in group], axis=0)  7.24 us
    pallas_call x3, Pallas kernels, select(): pl.pallas_call(lambda *refs: select_kernel(pairs, cap, *refs), out_shape=...  6.98 us
    ppermute x19, waiting for transfers between devices, moved(): return lax.ppermute(value, 'patch', pairs_of(move))  6.01 us
    ppermute x3, starting transfers between devices, local(): lax.ppermute(nodes, 'feat', [(i, (i + k) % feat) for i in range(feat)])  3.94 us
  transfers between devices with their start and end apart: 25, of which 5 were waited for; matrix products, arithmetic and copies ran while one was open for 11% of the time, Pallas kernels for 15%

profile of v2, /device:TPU:1, one launch (start us, length us, event | category | flops | bytes accessed | tf_op | source)
XLA Modules:
  0.0 98.8 jit_solution(13278321235208331709)
XLA Ops:
  0.7 1.9 %pack.1.refs_0_ = bf16[176,512]{1,0:T(8,128)(2,1)} custom-call(s32[1]{0:T(128)} %bitcast.2.where_ref, s32[24,64]{1,0:T(8,128)} %bitcast.12, bf16[160,512]{1,0:T(8,128)(2,1)} %nodes_ref.3), custom_call_target="tpu_custom_call" | custom-call | tf_op jit(solution)/shard_map/pack/pallas_call | solution.py:86
  2.6 6.4 %collective-permute-start.4 = (bf16[176,512]{1,0:T(8,128)(2,1)}, bf16[176,512]{1,0:T(8,128)(2,1)S(1)}, u32[]{:S(2)}, u32[]{:S(2)}) collective-permute-start(bf16[176,512]{1,0:T(8,128)(2,1)} %pack.1.refs_0_), channel_id=1, source_target_pairs={{0,56},{4,60},{8,0},{12,4},{16,8},{20,12},{24,16},{28,20},{32,24},... | collective-permute-start | bytes 540680 | tf_op jit(solution)/shard_map/ppermute | solution.py:288
  9.0 3.5 %collective-permute-done.4.refs_2_ = bf16[176,512]{1,0:T(8,128)(2,1)S(1)} collective-permute-done((bf16[176,512]{1,0:T(8,128)(2,1)}, bf16[176,512]{1,0:T(8,128)(2,1)S(1)}, u32[]{:S(2)}, u32[]{:S(2)}) %collective-permute-start.4) | collective-permute-done | bytes 180256 | tf_op jit(solution)/shard_map/ppermute | solution.py:288
  12.5 3.3 %collective-permute-start.10 = (bf16[176,512]{1,0:T(8,128)(2,1)S(1)}, bf16[176,512]{1,0:T(8,128)(2,1)S(1)}, u32[]{:S(2)}, u32[]{:S(2)}) collective-permute-start(bf16[176,512]{1,0:T(8,128)(2,1)S(1)} %collective-permute-done.4.refs_2_), channel_id=1, source_target_pairs={{0,56},{4,60},{8,0},{12,4},{16,8},{20,12},{24,16},{28,20},{32,24},... | collective-permute-start | bytes 540680 | tf_op jit(solution)/shard_map/ppermute | solution.py:288
  15.8 0.0 collective-permute-done.3.refs_1_
  15.8 2.4 %collective-permute-done.10.refs_0_ = bf16[176,512]{1,0:T(8,128)(2,1)S(1)} collective-permute-done((bf16[176,512]{1,0:T(8,128)(2,1)S(1)}, bf16[176,512]{1,0:T(8,128)(2,1)S(1)}, u32[]{:S(2)}, u32[]{:S(2)}) %collective-permute-start.10) | collective-permute-done | bytes 180256 | tf_op jit(solution)/shard_map/ppermute | solution.py:288
  18.3 3.1 %collective-permute-start.16 = (bf16[176,512]{1,0:T(8,128)(2,1)S(1)}, bf16[176,512]{1,0:T(8,128)(2,1)S(1)}, u32[]{:S(2)}, u32[]{:S(2)}) collective-permute-start(bf16[176,512]{1,0:T(8,128)(2,1)S(1)} %collective-permute-done.10.refs_0_), channel_id=1, source_target_pairs={{0,56},{4,60},{8,0},{12,4},{16,8},{20,12},{24,16},{28,20},{32,24},... | collective-permute-start | bytes 540680 | tf_op jit(solution)/shard_map/ppermute | solution.py:288
  21.4 0.0 collective-permute-done.5.refs_3_
  21.4 0.0 collective-permute-start.11
  21.4 2.8 %collective-permute-start.2 = (bf16[160,512]{1,0:T(8,128)(2,1)}, bf16[160,512]{1,0:T(8,128)(2,1)}, u32[]{:S(2)}, u32[]{:S(2)}) collective-permute-start(bf16[160,512]{1,0:T(8,128)(2,1)} %nodes_ref.3), channel_id=1, source_target_pairs={{0,3},{1,0},{2,1},{3,2},{4,7},{5,4},{6,5},{7,6},{8,11},{9,8},{10,9... | collective-permute-start | bytes 491528 | tf_op jit(solution)/shard_map/ppermute | solution.py:338
  24.2 2.6 %select.25 = (bf16[192,512]{1,0:T(8,128)(2,1)}, bf16[192,512]{1,0:T(8,128)(2,1)}, bf16[192,512]{1,0:T(8,128)(2,1)}, bf16[192,512]{1,0:T(8,128)(2,1)}) custom-call(bf16[176,512]{1,0:T(8,128)(2,1)} %pack.1.refs_0_, bf16[176,512]{1,0:T(8,128)(2,1)} %copy-done.28, bf16[176,512]{1,0:T(8,128)(2,1)} %copy-done.26, bf16[176,512]{1,0:T(8,128)(2,1)} %copy-done.27), custom_call_target="tpu_custom_call" | custom-call | flops 553648128 | bytes 4194304 | tf_op jit(solution)/shard_map/select/pallas_call | solution.py:122
  26.8 1.2 %collective-permute-start.6 = (bf16[192,512]{1,0:T(8,128)(2,1)}, bf16[192,512]{1,0:T(8,128)(2,1)S(1)}, u32[]{:S(2)}, u32[]{:S(2)}) collective-permute-start(bf16[192,512]{1,0:T(8,128)(2,1)} %get-tuple-element.20), channel_id=1, source_target_pairs={{0,64},{4,68},{8,72},{12,76},{16,80},{20,84},{24,88},{28,92},{32,9... | collective-permute-start | bytes 589832 | tf_op jit(solution)/shard_map/ppermute | solution.py:288
  28.1 2.4 %collective-permute-start.7 = (bf16[192,512]{1,0:T(8,128)(2,1)}, bf16[192,512]{1,0:T(8,128)(2,1)S(1)}, u32[]{:S(2)}, u32[]{:S(2)}) collective-permute-start(bf16[192,512]{1,0:T(8,128)(2,1)} %get-tuple-element.21), channel_id=1, source_target_pairs={{0,128},{4,132},{8,136},{12,140},{16,144},{20,148},{24,152},{28,15... | collective-permute-start | bytes 589832 | tf_op jit(solution)/shard_map/ppermute | solution.py:288
  30.5 1.2 %collective-permute-start.8 = (bf16[192,512]{1,0:T(8,128)(2,1)}, bf16[192,512]{1,0:T(8,128)(2,1)S(1)}, u32[]{:S(2)}, u32[]{:S(2)}) collective-permute-start(bf16[192,512]{1,0:T(8,128)(2,1)} %get-tuple-element.22), channel_id=1, source_target_pairs={{0,192},{4,196},{8,200},{12,204},{16,208},{20,212},{24,216},{28,22... | collective-permute-start | bytes 589832 | tf_op jit(solution)/shard_map/ppermute | solution.py:288
  31.7 0.0 collective-permute-done.11.refs_1_
  31.7 0.7 broadcast_select_fusion
  32.4 2.6 %collective-permute-start.17 = (bf16[176,512]{1,0:T(8,128)(2,1)}, bf16[176,512]{1,0:T(8,128)(2,1)}, u32[]{:S(2)}, u32[]{:S(2)}) collective-permute-start(bf16[176,512]{1,0:T(8,128)(2,1)} %broadcast_select_fusion), channel_id=1, source_target_pairs={{0,8},{4,60},{8,16},{12,4},{16,24},{20,12},{24,32},{28,20},{32,40}... | collective-permute-start | bytes 540680 | tf_op jit(solution)/shard_map/ppermute | solution.py:288
  35.0 0.1 fusion.3
  35.1 1.1 %reshape.36.recv_ref = s32[1280,1]{1,0:T(8,128)} reshape(s32[1280]{0:T(1024)S(1)} %get-tuple-element.36) | data formatting | bytes 10240 | tf_op jit(solution)/shard_map/reshape | solution.py:363
  36.8 0.2 reshape.37.send_ref.refs_3_
  37.1 0.6 slice.36
  37.7 2.1 %select.26 = (bf16[96,512]{1,0:T(8,128)(2,1)}, bf16[96,512]{1,0:T(8,128)(2,1)}, bf16[96,512]{1,0:T(8,128)(2,1)}, bf16[96,512]{1,0:T(8,128)(2,1)}) custom-call(bf16[176,512]{1,0:T(8,128)(2,1)} %copy-done.25, bf16[176,512]{1,0:T(8,128)(2,1)} %copy-done.22), custom_call_target="tpu_custom_call" | custom-call | flops 276824064 | bytes 2097152 | tf_op jit(solution)/shard_map/select/pallas_call | solution.py:122
  39.8 1.4 %slice.40 = bf16[48,512]{1,0:T(8,128)(2,1)} slice(bf16[96,512]{1,0:T(8,128)(2,1)} %get-tuple-element.23.refs_13_), slice={[48:96], [0:512]} | slice | bytes 98304 | tf_op jit(solution)/shard_map/slice | solution.py:332
  41.2 0.0 collective-permute-done.6.refs_9_
  41.2 0.3 collective-permute-start.12
  41.6 0.7 slice.48
  42.2 0.0 collective-permute-done.7.refs_10_
  42.2 0.9 collective-permute-start.13
  43.2 0.7 slice.49
  43.8 0.0 collective-permute-done.8.refs_11_
  43.8 1.5 %collective-permute-start.14 = (bf16[96,512]{1,0:T(8,128)(2,1)}, bf16[96,512]{1,0:T(8,128)(2,1)}, u32[]{:S(2)}, u32[]{:S(2)}) collective-permute-start(bf16[96,512]{1,0:T(8,128)(2,1)} %get-tuple-element.26), channel_id=1, source_target_pairs={{0,192},{4,196},{8,200},{12,204},{16,208},{20,212},{24,216},{28,22... | collective-permute-start | bytes 294920 | tf_op jit(solution)/shard_map/ppermute | solution.py:288
  45.3 0.6 slice.50
  46.0 0.7 copy-done.13
  46.7 2.3 %select.27 = (bf16[96,512]{1,0:T(8,128)(2,1)}, bf16[96,512]{1,0:T(8,128)(2,1)}, bf16[96,512]{1,0:T(8,128)(2,1)}, bf16[96,512]{1,0:T(8,128)(2,1)}) custom-call(bf16[176,512]{1,0:T(8,128)(2,1)} %copy-done.21, bf16[176,512]{1,0:T(8,128)(2,1)} %collective-permute-done.17.refs_1_), custom_call_target="tpu_custom_call" | custom-call | flops 276824064 | bytes 2097152 | tf_op jit(solution)/shard_map/select/pallas_call | solution.py:122
  48.9 0.5 collective-permute-start.18
  49.4 1.1 %pad_maximum_fusion = bf16[384,512]{1,0:T(8,128)(2,1)S(1)} fusion(bf16[96,512]{1,0:T(8,128)(2,1)} %slice.50, bf16[96,512]{1,0:T(8,128)(2,1)} %slice.49, bf16[96,512]{1,0:T(8,128)(2,1)} %slice.48, bf16[96,512]{1,0:T(8,128)(2,1)} %slice.36), kind=kLoop, calls=%fused_computation | loop fusion | flops 1572864 | bytes 786432 | tf_op jit(solution)/shard_map/concatenate | solution.py:332
  50.5 0.4 collective-permute-start.1
  50.9 0.8 slice.51
  51.8 0.7 collective-permute-start
  52.5 0.8 slice.52
  53.3 0.8 slice.53
  54.1 1.8 %collective-permute-start.19 = (bf16[96,512]{1,0:T(8,128)(2,1)}, bf16[96,512]{1,0:T(8,128)(2,1)S(1)}, u32[]{:S(2)}, u32[]{:S(2)}) collective-permute-start(bf16[96,512]{1,0:T(8,128)(2,1)} %get-tuple-element.29), channel_id=1, source_target_pairs={{0,128},{4,132},{8,136},{12,140},{16,144},{20,148},{24,152},{28,15... | collective-permute-start | bytes 294920 | tf_op jit(solution)/shard_map/ppermute | solution.py:288
  55.9 2.0 %collective-permute-start.20 = (bf16[96,512]{1,0:T(8,128)(2,1)}, bf16[96,512]{1,0:T(8,128)(2,1)S(1)}, u32[]{:S(2)}, u32[]{:S(2)}) collective-permute-start(bf16[96,512]{1,0:T(8,128)(2,1)} %get-tuple-element.30), channel_id=1, source_target_pairs={{0,192},{4,196},{8,200},{12,204},{16,208},{20,212},{24,216},{28,22... | collective-permute-start | bytes 294920 | tf_op jit(solution)/shard_map/ppermute | solution.py:288
  57.9 0.8 pad_maximum_fusion.1
  58.7 0.8 slice.44
  59.5 0.0 collective-permute-done.19.refs_20_
  59.5 3.8 %collective-permute-start.9 = (bf16[384,512]{1,0:T(8,128)(2,1)S(1)}, bf16[384,512]{1,0:T(8,128)(2,1)S(1)}, u32[]{:S(2)}, u32[]{:S(2)}) collective-permute-start(bf16[384,512]{1,0:T(8,128)(2,1)S(1)} %pad_maximum_fusion), channel_id=1, source_target_pairs={{0,4},{4,0},{8,12},{12,8},{16,20},{20,16},{24,28},{28,24},{32,36},... | collective-permute-start | bytes 1179656 | tf_op jit(solution)/shard_map/ppermute | solution.py:288
  63.4 0.8 collective-permute-start.15
  64.2 0.1 collective-permute-start.21
  64.4 0.0 copy-start.3
  64.4 1.1 %copy-done.3 = s32[1280,1]{1,0:T(8,128)S(1)} copy-done((s32[1280,1]{1,0:T(8,128)S(1)}, s32[1280,1]{1,0:T(8,128)}, u32[]{:S(2)}) %copy-start.3) | copy-done | bytes 5144
  65.5 0.0 copy-start.17
  65.5 7.6 %edge_before.1.refs_1_ = f32[1280,512]{1,0:T(8,128)} custom-call(bf16[160,512]{1,0:T(8,128)(2,1)S(1)} %copy-done.4, bf16[160,512]{1,0:T(8,128)(2,1)S(1)} %collective-permute-done.n1_ref, bf16[160,512]{1,0:T(8,128)(2,1)S(1)} %collective-permute-done.1.n2_ref, bf16[160,512]{1,0:T(8,128)(2,1)} %collective-permute-done.2.n3_ref, ...), custom_call_target="tpu_custom_call" | custom-call | flops 3690987520 | bytes 8388608 | tf_op jit(solution)/shard_map/edge_before/pallas_call | solution.py:158
  73.3 0.0 copy-start.2
  73.3 0.0 copy-start.6
  73.3 0.0 copy-start.18
  73.3 0.0 copy-start.19
  73.3 10.8 %edge_after.1 = (bf16[1280,512]{1,0:T(8,128)(2,1)}, f32[160,512]{1,0:T(8,128)S(1)}, bf16[160,512]{1,0:T(8,128)(2,1)S(1)}, bf16[160,512]{1,0:T(8,128)(2,1)S(1)}, bf16[160,512]{1,0:T(8,128)(2,1)S(1)}) custom-call(s32[1]{0:T(128)S(6)} %copy.19.refs_0_, f32[1280,512]{1,0:T(8,128)} %edge_before.1.refs_1_, bf16[1280,512]{1,0:T(8,128)(2,1)S(1)} %copy-done.1, ...), custom_call_target="tpu_custom_call" | custom-call | tf_op jit(solution)/shard_map/edge_after/pallas_call | solution.py:228
  84.1 2.1 %collective-permute-start.22 = (bf16[160,512]{1,0:T(8,128)(2,1)S(1)}, bf16[160,512]{1,0:T(8,128)(2,1)S(1)}, u32[]{:S(2)}, u32[]{:S(2)}) collective-permute-start(bf16[160,512]{1,0:T(8,128)(2,1)S(1)} %get-tuple-element.33), channel_id=1, source_target_pairs={{0,3},{1,0},{2,1},{3,2},{4,7},{5,4},{6,5},{7,6},{8,11},{9,8},{10,9... | collective-permute-start | bytes 491528 | tf_op jit(solution)/shard_map/ppermute | solution.py:371
  86.2 1.2 %collective-permute-start.23 = (bf16[160,512]{1,0:T(8,128)(2,1)S(1)}, bf16[160,512]{1,0:T(8,128)(2,1)S(1)}, u32[]{:S(2)}, u32[]{:S(2)}) collective-permute-start(bf16[160,512]{1,0:T(8,128)(2,1)S(1)} %get-tuple-element.34), channel_id=1, source_target_pairs={{0,2},{1,3},{2,0},{3,1},{4,6},{5,7},{6,4},{7,5},{8,10},{9,11},{10,... | collective-permute-start | bytes 491528 | tf_op jit(solution)/shard_map/ppermute | solution.py:371
  87.5 2.2 %collective-permute-done.22.p1_ref = bf16[160,512]{1,0:T(8,128)(2,1)S(1)} collective-permute-done((bf16[160,512]{1,0:T(8,128)(2,1)S(1)}, bf16[160,512]{1,0:T(8,128)(2,1)S(1)}, u32[]{:S(2)}, u32[]{:S(2)}) %collective-permute-start.22) | collective-permute-done | bytes 163872 | tf_op jit(solution)/shard_map/ppermute | solution.py:371
  89.6 3.0 %collective-permute-done.23.p2_ref = bf16[160,512]{1,0:T(8,128)(2,1)S(1)} collective-permute-done((bf16[160,512]{1,0:T(8,128)(2,1)S(1)}, bf16[160,512]{1,0:T(8,128)(2,1)S(1)}, u32[]{:S(2)}, u32[]{:S(2)}) %collective-permute-start.23) | collective-permute-done | bytes 163872 | tf_op jit(solution)/shard_map/ppermute | solution.py:371
  92.7 4.7 %collective-permute-done.24.p3_ref = bf16[160,512]{1,0:T(8,128)(2,1)S(1)} collective-permute-done((bf16[160,512]{1,0:T(8,128)(2,1)S(1)}, bf16[160,512]{1,0:T(8,128)(2,1)S(1)}, u32[]{:S(2)}, u32[]{:S(2)}) %collective-permute-start.24) | collective-permute-done | bytes 163872 | tf_op jit(solution)/shard_map/ppermute | solution.py:371
  97.4 1.5 %node_update.1 = bf16[160,512]{1,0:T(8,128)(2,1)} custom-call(bf16[160,512]{1,0:T(8,128)(2,1)S(1)} %copy-done.4, f32[160,512]{1,0:T(8,128)S(1)} %get-tuple-element.32.p0_ref, bf16[160,512]{1,0:T(8,128)(2,1)S(1)} %collective-permute-done.22.p1_ref, bf16[160,512]{1,0:T(8,128)(2,1)S(1)} %collective-permute-done.23.p2_ref, ...), custom_call_target="tpu_custom_call" | custom-call | tf_op jit(solution)/shard_map/node_update/pallas_call | solution.py:269
  (71 shorter events, 0.2 us)
Async XLA Ops:
  0.6 34.4 %copy-start.24 = (s32[1280]{0:T(1024)S(1)}, s32[1280]{0:T(1024)}, u32[]{:S(2)}) copy-start(s32[1280]{0:T(1024)} %param.17) | copy-start | bytes 15364
  0.6 34.4 %copy-start.23 = (s32[1280]{0:T(1024)S(1)}, s32[1280]{0:T(1024)}, u32[]{:S(2)}) copy-start(s32[1280]{0:T(1024)} %param.16) | copy-start | bytes 15364
  2.6 9.9 %collective-permute-start.4 = (bf16[176,512]{1,0:T(8,128)(2,1)}, bf16[176,512]{1,0:T(8,128)(2,1)S(1)}, u32[]{:S(2)}, u32[]{:S(2)}) collective-permute-start(bf16[176,512]{1,0:T(8,128)(2,1)} %pack.1.refs_0_), channel_id=1, source_target_pairs={{0,56},{4,60},{8,0},{12,4},{16,8},{20,12},{24,16},{28,20},{32,24},... | collective-permute-start | bytes 540680 | tf_op jit(solution)/shard_map/ppermute | solution.py:288
  9.0 6.8 %collective-permute-start.3 = (bf16[176,512]{1,0:T(8,128)(2,1)}, bf16[176,512]{1,0:T(8,128)(2,1)S(1)}, u32[]{:S(2)}, u32[]{:S(2)}) collective-permute-start(bf16[176,512]{1,0:T(8,128)(2,1)} %pack.1.refs_0_), channel_id=1, source_target_pairs={{0,8},{4,12},{8,16},{12,20},{16,24},{20,28},{24,32},{28,36},{32,40... | collective-permute-start | bytes 540680 | tf_op jit(solution)/shard_map/ppermute | solution.py:288
  12.5 11.7 %copy-start.26 = (bf16[176,512]{1,0:T(8,128)(2,1)}, bf16[176,512]{1,0:T(8,128)(2,1)S(1)}, u32[]{:S(2)}) copy-start(bf16[176,512]{1,0:T(8,128)(2,1)S(1)} %collective-permute-done.4.refs_2_) | copy-start | bytes 540676
  12.5 5.7 %collective-permute-start.10 = (bf16[176,512]{1,0:T(8,128)(2,1)S(1)}, bf16[176,512]{1,0:T(8,128)(2,1)S(1)}, u32[]{:S(2)}, u32[]{:S(2)}) collective-permute-start(bf16[176,512]{1,0:T(8,128)(2,1)S(1)} %collective-permute-done.4.refs_2_), channel_id=1, source_target_pairs={{0,56},{4,60},{8,0},{12,4},{16,8},{20,12},{24,16},{28,20},{32,24},... | collective-permute-start | bytes 540680 | tf_op jit(solution)/shard_map/ppermute | solution.py:288
  15.8 8.4 %copy-start.28 = (bf16[176,512]{1,0:T(8,128)(2,1)}, bf16[176,512]{1,0:T(8,128)(2,1)S(1)}, u32[]{:S(2)}) copy-start(bf16[176,512]{1,0:T(8,128)(2,1)S(1)} %collective-permute-done.3.refs_1_) | copy-start | bytes 540676
  15.8 5.6 %collective-permute-start.5 = (bf16[176,512]{1,0:T(8,128)(2,1)S(1)}, bf16[176,512]{1,0:T(8,128)(2,1)S(1)}, u32[]{:S(2)}, u32[]{:S(2)}) collective-permute-start(bf16[176,512]{1,0:T(8,128)(2,1)S(1)} %collective-permute-done.3.refs_1_), channel_id=1, source_target_pairs={{0,8},{4,12},{8,16},{12,20},{16,24},{20,28},{24,32},{28,36},{32,40... | collective-permute-start | bytes 540680 | tf_op jit(solution)/shard_map/ppermute | solution.py:288
  18.3 17.9 %copy-start.25 = (bf16[176,512]{1,0:T(8,128)(2,1)}, bf16[176,512]{1,0:T(8,128)(2,1)S(1)}, u32[]{:S(2)}) copy-start(bf16[176,512]{1,0:T(8,128)(2,1)S(1)} %collective-permute-done.10.refs_0_) | copy-start | bytes 540676
  18.3 12.2 %collective-permute-start.16 = (bf16[176,512]{1,0:T(8,128)(2,1)S(1)}, bf16[176,512]{1,0:T(8,128)(2,1)S(1)}, u32[]{:S(2)}, u32[]{:S(2)}) collective-permute-start(bf16[176,512]{1,0:T(8,128)(2,1)S(1)} %collective-permute-done.10.refs_0_), channel_id=1, source_target_pairs={{0,56},{4,60},{8,0},{12,4},{16,8},{20,12},{24,16},{28,20},{32,24},... | collective-permute-start | bytes 540680 | tf_op jit(solution)/shard_map/ppermute | solution.py:288
  21.4 2.8 %copy-start.27 = (bf16[176,512]{1,0:T(8,128)(2,1)}, bf16[176,512]{1,0:T(8,128)(2,1)S(1)}, u32[]{:S(2)}) copy-start(bf16[176,512]{1,0:T(8,128)(2,1)S(1)} %collective-permute-done.5.refs_3_) | copy-start | bytes 540676
  21.4 10.3 %collective-permute-start.11 = (bf16[176,512]{1,0:T(8,128)(2,1)S(1)}, bf16[176,512]{1,0:T(8,128)(2,1)S(1)}, u32[]{:S(2)}, u32[]{:S(2)}) collective-permute-start(bf16[176,512]{1,0:T(8,128)(2,1)S(1)} %collective-permute-done.5.refs_3_), channel_id=1, source_target_pairs={{0,8},{4,12},{8,16},{12,20},{16,24},{20,28},{24,32},{28,36},{32,40... | collective-permute-start | bytes 540680 | tf_op jit(solution)/shard_map/ppermute | solution.py:288
  21.4 42.8 %collective-permute-start.2 = (bf16[160,512]{1,0:T(8,128)(2,1)}, bf16[160,512]{1,0:T(8,128)(2,1)}, u32[]{:S(2)}, u32[]{:S(2)}) collective-permute-start(bf16[160,512]{1,0:T(8,128)(2,1)} %nodes_ref.3), channel_id=1, source_target_pairs={{0,3},{1,0},{2,1},{3,2},{4,7},{5,4},{6,5},{7,6},{8,11},{9,8},{10,9... | collective-permute-start | bytes 491528 | tf_op jit(solution)/shard_map/ppermute | solution.py:338
  26.8 10.2 %copy-start.7 = (bf16[192,512]{1,0:T(8,128)(2,1)S(1)}, bf16[192,512]{1,0:T(8,128)(2,1)}, u32[]{:S(2)}) copy-start(bf16[192,512]{1,0:T(8,128)(2,1)} %get-tuple-element.19.refs_8_) | copy-start | bytes 589828
  26.8 14.4 %collective-permute-start.6 = (bf16[192,512]{1,0:T(8,128)(2,1)}, bf16[192,512]{1,0:T(8,128)(2,1)S(1)}, u32[]{:S(2)}, u32[]{:S(2)}) collective-permute-start(bf16[192,512]{1,0:T(8,128)(2,1)} %get-tuple-element.20), channel_id=1, source_target_pairs={{0,64},{4,68},{8,72},{12,76},{16,80},{20,84},{24,88},{28,92},{32,9... | collective-permute-start | bytes 589832 | tf_op jit(solution)/shard_map/ppermute | solution.py:288
  28.1 14.2 %collective-permute-start.7 = (bf16[192,512]{1,0:T(8,128)(2,1)}, bf16[192,512]{1,0:T(8,128)(2,1)S(1)}, u32[]{:S(2)}, u32[]{:S(2)}) collective-permute-start(bf16[192,512]{1,0:T(8,128)(2,1)} %get-tuple-element.21), channel_id=1, source_target_pairs={{0,128},{4,132},{8,136},{12,140},{16,144},{20,148},{24,152},{28,15... | collective-permute-start | bytes 589832 | tf_op jit(solution)/shard_map/ppermute | solution.py:288
  30.5 4.6 %copy-start.21 = (bf16[176,512]{1,0:T(8,128)(2,1)}, bf16[176,512]{1,0:T(8,128)(2,1)S(1)}, u32[]{:S(2)}) copy-start(bf16[176,512]{1,0:T(8,128)(2,1)S(1)} %collective-permute-done.16.refs_0_) | copy-start | bytes 540676
  30.5 13.3 %collective-permute-start.8 = (bf16[192,512]{1,0:T(8,128)(2,1)}, bf16[192,512]{1,0:T(8,128)(2,1)S(1)}, u32[]{:S(2)}, u32[]{:S(2)}) collective-permute-start(bf16[192,512]{1,0:T(8,128)(2,1)} %get-tuple-element.22), channel_id=1, source_target_pairs={{0,192},{4,196},{8,200},{12,204},{16,208},{20,212},{24,216},{28,22... | collective-permute-start | bytes 589832 | tf_op jit(solution)/shard_map/ppermute | solution.py:288
  31.7 6.1 %copy-start.22 = (bf16[176,512]{1,0:T(8,128)(2,1)}, bf16[176,512]{1,0:T(8,128)(2,1)S(1)}, u32[]{:S(2)}) copy-start(bf16[176,512]{1,0:T(8,128)(2,1)S(1)} %collective-permute-done.11.refs_1_) | copy-start | bytes 540676
  32.4 14.2 %collective-permute-start.17 = (bf16[176,512]{1,0:T(8,128)(2,1)}, bf16[176,512]{1,0:T(8,128)(2,1)}, u32[]{:S(2)}, u32[]{:S(2)}) collective-permute-start(bf16[176,512]{1,0:T(8,128)(2,1)} %broadcast_select_fusion), channel_id=1, source_target_pairs={{0,8},{4,60},{8,16},{12,4},{16,24},{20,12},{24,32},{28,20},{32,40}... | collective-permute-start | bytes 540680 | tf_op jit(solution)/shard_map/ppermute | solution.py:288
  41.2 4.1 %copy-start.9 = (bf16[192,512]{1,0:T(8,128)(2,1)}, bf16[192,512]{1,0:T(8,128)(2,1)S(1)}, u32[]{:S(2)}) copy-start(bf16[192,512]{1,0:T(8,128)(2,1)S(1)} %collective-permute-done.6.refs_9_) | copy-start | bytes 589828
  41.2 9.3 %collective-permute-start.12 = (bf16[96,512]{1,0:T(8,128)(2,1)}, bf16[96,512]{1,0:T(8,128)(2,1)}, u32[]{:S(2)}, u32[]{:S(2)}) collective-permute-start(bf16[96,512]{1,0:T(8,128)(2,1)} %get-tuple-element.24), channel_id=1, source_target_pairs={{0,64},{4,68},{8,72},{12,76},{16,80},{20,84},{24,88},{28,92},{32,9... | collective-permute-start | bytes 294920 | tf_op jit(solution)/shard_map/ppermute | solution.py:288
  42.2 3.1 %copy-start.11 = (bf16[192,512]{1,0:T(8,128)(2,1)}, bf16[192,512]{1,0:T(8,128)(2,1)S(1)}, u32[]{:S(2)}) copy-start(bf16[192,512]{1,0:T(8,128)(2,1)S(1)} %collective-permute-done.7.refs_10_) | copy-start | bytes 589828
  42.2 9.5 %collective-permute-start.13 = (bf16[96,512]{1,0:T(8,128)(2,1)}, bf16[96,512]{1,0:T(8,128)(2,1)}, u32[]{:S(2)}, u32[]{:S(2)}) collective-permute-start(bf16[96,512]{1,0:T(8,128)(2,1)} %get-tuple-element.25), channel_id=1, source_target_pairs={{0,128},{4,132},{8,136},{12,140},{16,144},{20,148},{24,152},{28,15... | collective-permute-start | bytes 294920 | tf_op jit(solution)/shard_map/ppermute | solution.py:288
  43.8 9.4 %collective-permute-start.14 = (bf16[96,512]{1,0:T(8,128)(2,1)}, bf16[96,512]{1,0:T(8,128)(2,1)}, u32[]{:S(2)}, u32[]{:S(2)}) collective-permute-start(bf16[96,512]{1,0:T(8,128)(2,1)} %get-tuple-element.26), channel_id=1, source_target_pairs={{0,192},{4,196},{8,200},{12,204},{16,208},{20,212},{24,216},{28,22... | collective-permute-start | bytes 294920 | tf_op jit(solution)/shard_map/ppermute | solution.py:288
  46.0 0.7 copy-start.13
  46.7 17.7 %copy-start = (bf16[1536,512]{1,0:T(8,128)(2,1)S(1)}, bf16[1536,512]{1,0:T(8,128)(2,1)}, u32[]{:S(2)}) copy-start(bf16[1536,512]{1,0:T(8,128)(2,1)} %refs_5_.1) | copy-start | bytes 4718596
  46.7 17.7 %copy-start.1 = (bf16[1280,512]{1,0:T(8,128)(2,1)S(1)}, bf16[1280,512]{1,0:T(8,128)(2,1)}, u32[]{:S(2)}) copy-start(bf16[1280,512]{1,0:T(8,128)(2,1)} %refs_2_.1) | copy-start | bytes 3932164
  46.7 17.7 %copy-start.20 = (f32[512]{0:T(512)S(1)}, f32[512]{0:T(512)}, u32[]{:S(2)}) copy-start(f32[512]{0:T(512)} %param.21) | copy-start | bytes 6148
  48.9 15.4 %copy-start.4 = (bf16[160,512]{1,0:T(8,128)(2,1)S(1)}, bf16[160,512]{1,0:T(8,128)(2,1)}, u32[]{:S(2)}) copy-start(bf16[160,512]{1,0:T(8,128)(2,1)} %nodes_ref.3) | copy-start | bytes 491524
  48.9 6.9 %collective-permute-start.18 = (bf16[96,512]{1,0:T(8,128)(2,1)}, bf16[96,512]{1,0:T(8,128)(2,1)S(1)}, u32[]{:S(2)}, u32[]{:S(2)}) collective-permute-start(bf16[96,512]{1,0:T(8,128)(2,1)} %get-tuple-element.28), channel_id=1, source_target_pairs={{0,64},{4,68},{8,72},{12,76},{16,80},{20,84},{24,88},{28,92},{32,9... | collective-permute-start | bytes 294920 | tf_op jit(solution)/shard_map/ppermute | solution.py:288
  50.5 13.8 %collective-permute-start.1 = (bf16[160,512]{1,0:T(8,128)(2,1)}, bf16[160,512]{1,0:T(8,128)(2,1)S(1)}, u32[]{:S(2)}, u32[]{:S(2)}) collective-permute-start(bf16[160,512]{1,0:T(8,128)(2,1)} %nodes_ref.3), channel_id=1, source_target_pairs={{0,2},{1,3},{2,0},{3,1},{4,6},{5,7},{6,4},{7,5},{8,10},{9,11},{10,... | collective-permute-start | bytes 491528 | tf_op jit(solution)/shard_map/ppermute | solution.py:338
  51.8 12.6 %collective-permute-start = (bf16[160,512]{1,0:T(8,128)(2,1)}, bf16[160,512]{1,0:T(8,128)(2,1)S(1)}, u32[]{:S(2)}, u32[]{:S(2)}) collective-permute-start(bf16[160,512]{1,0:T(8,128)(2,1)} %nodes_ref.3), channel_id=1, source_target_pairs={{0,1},{1,2},{2,3},{3,0},{4,5},{5,6},{6,7},{7,4},{8,9},{9,10},{10,1... | collective-permute-start | bytes 491528 | tf_op jit(solution)/shard_map/ppermute | solution.py:338
  54.1 5.5 %collective-permute-start.19 = (bf16[96,512]{1,0:T(8,128)(2,1)}, bf16[96,512]{1,0:T(8,128)(2,1)S(1)}, u32[]{:S(2)}, u32[]{:S(2)}) collective-permute-start(bf16[96,512]{1,0:T(8,128)(2,1)} %get-tuple-element.29), channel_id=1, source_target_pairs={{0,128},{4,132},{8,136},{12,140},{16,144},{20,148},{24,152},{28,15... | collective-permute-start | bytes 294920 | tf_op jit(solution)/shard_map/ppermute | solution.py:288
  55.9 7.5 %collective-permute-start.20 = (bf16[96,512]{1,0:T(8,128)(2,1)}, bf16[96,512]{1,0:T(8,128)(2,1)S(1)}, u32[]{:S(2)}, u32[]{:S(2)}) collective-permute-start(bf16[96,512]{1,0:T(8,128)(2,1)} %get-tuple-element.30), channel_id=1, source_target_pairs={{0,192},{4,196},{8,200},{12,204},{16,208},{20,212},{24,216},{28,22... | collective-permute-start | bytes 294920 | tf_op jit(solution)/shard_map/ppermute | solution.py:288
  59.5 13.6 %collective-permute-start.9 = (bf16[384,512]{1,0:T(8,128)(2,1)S(1)}, bf16[384,512]{1,0:T(8,128)(2,1)S(1)}, u32[]{:S(2)}, u32[]{:S(2)}) collective-permute-start(bf16[384,512]{1,0:T(8,128)(2,1)S(1)} %pad_maximum_fusion), channel_id=1, source_target_pairs={{0,4},{4,0},{8,12},{12,8},{16,20},{20,16},{24,28},{28,24},{32,36},... | collective-permute-start | bytes 1179656 | tf_op jit(solution)/shard_map/ppermute | solution.py:288
  63.4 9.8 %collective-permute-start.15 = (bf16[192,512]{1,0:T(8,128)(2,1)S(1)}, bf16[192,512]{1,0:T(8,128)(2,1)S(1)}, u32[]{:S(2)}, u32[]{:S(2)}) collective-permute-start(bf16[192,512]{1,0:T(8,128)(2,1)S(1)} %pad_maximum_fusion.1), channel_id=1, source_target_pairs={{0,4},{4,0},{8,12},{12,8},{16,20},{20,16},{24,28},{28,24},{32,36},... | collective-permute-start | bytes 589832 | tf_op jit(solution)/shard_map/ppermute | solution.py:288
  64.2 8.9 %collective-permute-start.21 = (bf16[192,512]{1,0:T(8,128)(2,1)S(1)}, bf16[192,512]{1,0:T(8,128)(2,1)S(1)}, u32[]{:S(2)}, u32[]{:S(2)}) collective-permute-start(bf16[192,512]{1,0:T(8,128)(2,1)S(1)} %pad_maximum_fusion.2), channel_id=1, source_target_pairs={{0,4},{4,0},{8,12},{12,8},{16,20},{20,16},{24,28},{28,24},{32,36},... | collective-permute-start | bytes 589832 | tf_op jit(solution)/shard_map/ppermute | solution.py:288
  64.4 1.1 %copy-start.3 = (s32[1280,1]{1,0:T(8,128)S(1)}, s32[1280,1]{1,0:T(8,128)}, u32[]{:S(2)}) copy-start(s32[1280,1]{1,0:T(8,128)} %reshape.36.recv_ref) | copy-start | bytes 15364
  65.5 7.7 %copy-start.5 = (bf16[512,512]{1,0:T(8,128)(2,1)S(1)}, bf16[512,512]{1,0:T(8,128)(2,1)}, u32[]{:S(2)}) copy-start(bf16[512,512]{1,0:T(8,128)(2,1)} %refs_6_.1) | copy-start | bytes 1572868
  65.5 7.7 %copy-start.8 = (bf16[192,512]{1,0:T(8,128)(2,1)S(1)}, bf16[192,512]{1,0:T(8,128)(2,1)}, u32[]{:S(2)}) copy-start(bf16[192,512]{1,0:T(8,128)(2,1)} %get-tuple-element.19.refs_8_) | copy-start | bytes 589828
  65.5 7.7 %copy-start.10 = (bf16[192,512]{1,0:T(8,128)(2,1)S(1)}, bf16[192,512]{1,0:T(8,128)(2,1)}, u32[]{:S(2)}) copy-start(bf16[192,512]{1,0:T(8,128)(2,1)} %copy-done.9) | copy-start | bytes 589828
  65.5 7.7 %copy-start.12 = (bf16[192,512]{1,0:T(8,128)(2,1)S(1)}, bf16[192,512]{1,0:T(8,128)(2,1)}, u32[]{:S(2)}) copy-start(bf16[192,512]{1,0:T(8,128)(2,1)} %copy-done.11) | copy-start | bytes 589828
  65.5 7.7 %copy-start.14 = (bf16[192,512]{1,0:T(8,128)(2,1)S(1)}, bf16[192,512]{1,0:T(8,128)(2,1)}, u32[]{:S(2)}) copy-start(bf16[192,512]{1,0:T(8,128)(2,1)} %copy-done.13) | copy-start | bytes 589828
  65.5 7.7 %copy-start.15 = (bf16[96,512]{1,0:T(8,128)(2,1)S(1)}, bf16[96,512]{1,0:T(8,128)(2,1)}, u32[]{:S(2)}) copy-start(bf16[96,512]{1,0:T(8,128)(2,1)} %get-tuple-element.23.refs_13_) | copy-start | bytes 294916
  65.5 7.7 %copy-start.16 = (bf16[96,512]{1,0:T(8,128)(2,1)S(1)}, bf16[96,512]{1,0:T(8,128)(2,1)}, u32[]{:S(2)}) copy-start(bf16[96,512]{1,0:T(8,128)(2,1)} %get-tuple-element.27.refs_18_) | copy-start | bytes 294916
  65.5 7.7 %copy-start.17 = (f32[512]{0:T(512)S(1)}, f32[512]{0:T(512)}, u32[]{:S(2)}) copy-start(f32[512]{0:T(512)} %param.23) | copy-start | bytes 6148
  73.3 24.1 %copy-start.2 = (bf16[1024,512]{1,0:T(8,128)(2,1)S(1)}, bf16[1024,512]{1,0:T(8,128)(2,1)}, u32[]{:S(2)}) copy-start(bf16[1024,512]{1,0:T(8,128)(2,1)} %w1_ref.3) | copy-start | bytes 3145732
  73.3 24.1 %copy-start.6 = (bf16[512,512]{1,0:T(8,128)(2,1)S(1)}, bf16[512,512]{1,0:T(8,128)(2,1)}, u32[]{:S(2)}) copy-start(bf16[512,512]{1,0:T(8,128)(2,1)} %w2_ref.1) | copy-start | bytes 1572868
  73.3 24.1 %copy-start.18 = (f32[512]{0:T(512)S(1)}, f32[512]{0:T(512)}, u32[]{:S(2)}) copy-start(f32[512]{0:T(512)} %param.25) | copy-start | bytes 6148
  73.3 24.1 %copy-start.19 = (f32[512]{0:T(512)S(1)}, f32[512]{0:T(512)}, u32[]{:S(2)}) copy-start(f32[512]{0:T(512)} %param.27) | copy-start | bytes 6148
  84.1 5.6 %collective-permute-start.22 = (bf16[160,512]{1,0:T(8,128)(2,1)S(1)}, bf16[160,512]{1,0:T(8,128)(2,1)S(1)}, u32[]{:S(2)}, u32[]{:S(2)}) collective-permute-start(bf16[160,512]{1,0:T(8,128)(2,1)S(1)} %get-tuple-element.33), channel_id=1, source_target_pairs={{0,3},{1,0},{2,1},{3,2},{4,7},{5,4},{6,5},{7,6},{8,11},{9,8},{10,9... | collective-permute-start | bytes 491528 | tf_op jit(solution)/shard_map/ppermute | solution.py:371
  86.2 6.5 %collective-permute-start.23 = (bf16[160,512]{1,0:T(8,128)(2,1)S(1)}, bf16[160,512]{1,0:T(8,128)(2,1)S(1)}, u32[]{:S(2)}, u32[]{:S(2)}) collective-permute-start(bf16[160,512]{1,0:T(8,128)(2,1)S(1)} %get-tuple-element.34), channel_id=1, source_target_pairs={{0,2},{1,3},{2,0},{3,1},{4,6},{5,7},{6,4},{7,5},{8,10},{9,11},{10,... | collective-permute-start | bytes 491528 | tf_op jit(solution)/shard_map/ppermute | solution.py:371
  87.5 9.9 %collective-permute-start.24 = (bf16[160,512]{1,0:T(8,128)(2,1)S(1)}, bf16[160,512]{1,0:T(8,128)(2,1)S(1)}, u32[]{:S(2)}, u32[]{:S(2)}) collective-permute-start(bf16[160,512]{1,0:T(8,128)(2,1)S(1)} %get-tuple-element.35), channel_id=1, source_target_pairs={{0,1},{1,2},{2,3},{3,0},{4,5},{5,6},{6,7},{7,4},{8,9},{9,10},{10,1... | collective-permute-start | bytes 491528 | tf_op jit(solution)/shard_map/ppermute | solution.py:371

commit v3 on v1

v3 whole, which is shorter than its diff:
```python
import jax
import jax.numpy as jnp
from jax import lax
from jax.experimental import pallas as pl
from jax.experimental.pallas import tpu as pltpu
from jax.sharding import PartitionSpec as P

epsilon = 1e-05
f32 = jnp.float32
bf16 = jnp.bfloat16
TILES = 2
LIMIT = 16 << 20
VMEM = pl.BlockSpec(memory_space=pltpu.VMEM)
SMEM = pl.BlockSpec(memory_space=pltpu.SMEM)


def dot(left, right):
    return jnp.dot(left, right, preferred_element_type=f32)


def silu(value):
    return value / (1.0 + jnp.exp(-value))


def layer_norm(values, scales):
    average = jnp.mean(values, axis=-1, keepdims=True)
    centred = values - average
    variance = jnp.mean(centred * centred, axis=-1, keepdims=True)
    return centred * lax.rsqrt(variance + epsilon) * scales


def dot_first(left, right):
    return lax.dot_general(left, right, (((0,), (0,)), ((), ())), preferred_element_type=f32)


def as_bf16(mask):
    return mask.astype(f32).astype(bf16)


def hot_rows(column, count, first=0):
    ids = lax.broadcasted_iota(jnp.int32, (column.shape[0], count), 1) + first
    return as_bf16(column == ids)


def hot_columns(row, count, first=0):
    ids = lax.broadcasted_iota(jnp.int32, (count, row.shape[1]), 0) + first
    return as_bf16(row == ids)


def select_kernel(lists_ref, table_ref, out_ref):
    cap, peers = lists_ref.shape
    table = table_ref[...]
    lists = lists_ref[...].astype(f32).astype(bf16)
    size = 512
    for at in range(cap * peers // size):
        lane = lax.broadcasted_iota(jnp.int32, (cap, size), 1) + at * size
        spread = as_bf16(lane % cap == lax.broadcasted_iota(jnp.int32, (cap, size), 0))
        listed = dot_first(lists, spread)
        lane = lax.broadcasted_iota(jnp.int32, (peers, size), 1) + at * size
        own = lane // cap == lax.broadcasted_iota(jnp.int32, (peers, size), 0)
        wanted = jnp.sum(jnp.where(own, listed, 0.0), axis=0, keepdims=True)
        hot = hot_columns(wanted.astype(jnp.int32), table.shape[0])
        out_ref[at * size : (at + 1) * size] = dot_first(hot, table).astype(bf16)


def select(lists, table):
    return pl.pallas_call(
        select_kernel,
        in_specs=[VMEM] * 2,
        out_shape=jax.ShapeDtypeStruct((lists.size, table.shape[1]), bf16),
        compiler_params=pltpu.CompilerParams(vmem_limit_bytes=LIMIT),
        name="select",
    )(lists, table)


def before_kernel(patch_ref, edges_ref, recv_ref, send_ref, w1_ref, b1_ref, out_ref):
    count, latent = edges_ref.shape
    tile = count // TILES
    nodes = patch_ref.shape[0]
    for at in range(TILES):
        rows = slice(at * tile, (at + 1) * tile)
        own = dot(hot_rows(recv_ref[rows], nodes), patch_ref[...]).astype(bf16)
        near = dot(hot_rows(send_ref[rows], nodes), patch_ref[...]).astype(bf16)
        total = dot(edges_ref[rows], w1_ref[:latent])
        total = total + dot(near, w1_ref[latent : 2 * latent])
        total = total + dot(own, w1_ref[2 * latent :])
        out_ref[rows] = total + b1_ref[...]


def edge_before(patch_rows, edges, recv, send, w1, b1):
    count, latent = edges.shape
    return pl.pallas_call(
        before_kernel,
        in_specs=[VMEM] * 6,
        out_shape=jax.ShapeDtypeStruct((count, latent), f32),
        compiler_params=pltpu.CompilerParams(vmem_limit_bytes=LIMIT),
        cost_estimate=pl.CostEstimate(
            flops=2 * count * latent * (3 * latent + 2 * patch_rows.shape[0]),
            bytes_accessed=8 << 20,
            transcendentals=0,
        ),
        name="edge_before",
    )(patch_rows, edges, recv, send, w1, b1)


def after_kernel(
    live_ref, before_ref, remote_ref, edges_ref, send_ref, recv_ref, w1_ref, w2_ref, gain_ref,
    out_ref, sums_ref,
):
    count, latent = edges_ref.shape
    tile = count // TILES
    nodes = sums_ref.shape[0]
    live = live_ref[0]
    for at in range(TILES):
        rows = slice(at * tile, (at + 1) * tile)
        hot = hot_rows(send_ref[rows], remote_ref.shape[0], nodes)
        far = dot(hot, remote_ref[...]).astype(bf16)
        first = before_ref[rows] + dot(far, w1_ref[latent : 2 * latent])
        hidden = silu(first).astype(bf16)
        change = layer_norm(dot(hidden, w2_ref[...]), gain_ref[...])
        alive = lax.broadcasted_iota(jnp.int32, (tile, 1), 0) + at * tile < live
        edge = edges_ref[rows].astype(f32) + jnp.where(alive, change, 0.0)
        out_ref[rows] = edge.astype(bf16)
    alive = lax.broadcasted_iota(jnp.int32, (1, count), 1) < live
    receiver = jnp.where(alive, recv_ref[...], -1)
    size = nodes // 4
    for at in range(4):
        hot = hot_columns(receiver, size, at * size)
        sums_ref[at * size : (at + 1) * size] = dot(hot, out_ref[...]).astype(bf16)


def edge_after(live, before, remote, edges, send, recv, w1, w2, gain, nodes):
    count, latent = edges.shape
    return pl.pallas_call(
        after_kernel,
        in_specs=[SMEM] + [VMEM] * 8,
        out_shape=[
            jax.ShapeDtypeStruct((count, latent), bf16),
            jax.ShapeDtypeStruct((nodes, latent), bf16),
        ],
        compiler_params=pltpu.CompilerParams(vmem_limit_bytes=LIMIT),
        name="edge_after",
    )(live, before, remote, edges, send, recv, w1, w2, gain)


def node_kernel(nodes_ref, p0_ref, p1_ref, p2_ref, p3_ref, w1_ref, b1_ref, w2_ref, gain_ref, out_ref):
    latent = nodes_ref.shape[1]
    total = p0_ref[...].astype(f32) + p1_ref[...].astype(f32)
    total = total + p2_ref[...].astype(f32) + p3_ref[...].astype(f32)
    incoming = total.astype(bf16)
    nodes = nodes_ref[...]
    first = dot(nodes, w1_ref[:latent]) + dot(incoming, w1_ref[latent:])
    hidden = silu(first + b1_ref[...]).astype(bf16)
    change = layer_norm(dot(hidden, w2_ref[...]), gain_ref[...])
    out_ref[...] = (nodes.astype(f32) + change).astype(bf16)


def node_update(nodes, parts, w1, b1, w2, gain):
    return pl.pallas_call(
        node_kernel,
        out_shape=jax.ShapeDtypeStruct(nodes.shape, bf16),
        compiler_params=pltpu.CompilerParams(vmem_limit_bytes=LIMIT),
        name="node_update",
    )(nodes, *parts, w1, b1, w2, gain)


def local(
    nodes,
    edges,
    receivers,
    sender_slot,
    send_rows,
    live_edges,
    edge_w1,
    edge_b1,
    edge_w2,
    edge_gain,
    node_w1,
    node_b1,
    node_w2,
    node_gain,
):
    rows, latent = nodes.shape
    outgoing = send_rows[0, 0]
    packed = select(outgoing.T, nodes).reshape(*outgoing.shape, latent)
    remote = lax.all_to_all(packed, "patch", split_axis=0, concat_axis=0, tiled=True)
    remote = remote.reshape(-1, latent)
    patch_rows = lax.all_gather(nodes, "feat", axis=0, tiled=True)
    recv = receivers.reshape(-1, 1)
    send = sender_slot.reshape(-1, 1)
    before = edge_before(patch_rows, edges, recv, send, edge_w1, edge_b1.reshape(1, -1))
    edges_out, sums = edge_after(
        live_edges, before, remote, edges, send, receivers.reshape(1, -1), edge_w1, edge_w2,
        edge_gain.reshape(1, -1), patch_rows.shape[0],
    )
    size = lax.axis_size("feat")
    me = lax.axis_index("feat")
    parts = []
    for k in range(size):
        part = lax.dynamic_slice_in_dim(sums, lax.rem(me + k, size) * rows, rows)
        if k:
            part = lax.ppermute(part, "feat", [(i, (i + k) % size) for i in range(size)])
        parts.append(part)
    nodes_out = node_update(
        nodes, parts, node_w1, node_b1.reshape(1, -1), node_w2, node_gain.reshape(1, -1)
    )
    return (edges_out, nodes_out)


def solution(mesh):
    placed = (
        P(("patch", "feat"), None),
        P(("patch", "feat"), None),
        P(("patch", "feat")),
        P(("patch", "feat")),
        P("patch", "feat", None, None),
        P(("patch", "feat")),
    ) + (P(),) * 8
    return jax.shard_map(
        local,
        mesh=mesh,
        in_specs=placed,
        out_specs=(P(("patch", "feat"), None), P(("patch", "feat"), None)),
        check_vma=False,
    )
```

time: 84.6 us -> 82.3 us (0.973)
  Pallas kernels: 21.2 us -> 13.6 us
  local copies, waits for them, and re-layouts: 7.41 us -> 11.9 us
    pallas_call x3, Pallas kernels: 19.8 us -> 12.2 us  [the longest x1 5.5 us: edge_after(): pl.pallas_call(after_kernel, in_specs=[SMEM] + [VMEM] * 8, out_shape=[jax...]
    unnamed x29 -> x36, local copies, waits for them, and re-layouts: 6.82 us -> 11.4 us
  transfers between devices with their start and end apart: 4 -> 4, of which waited for: 3 -> 3; matrix products, arithmetic and copies ran while one was open for 1% -> 1% of each run, Pallas kernels for 8% -> 5%
where the time goes in v3:
time: 82.3 us; the launch traced here: 81.9 us
  waiting for transfers between devices  24.7 us (30%)
  starting transfers between devices  18.2 us (22%)
  Pallas kernels  13.6 us (17%)
  blocking collectives  12 us (15%)
  local copies, waits for them, and re-layouts  11.9 us (14%)
  between operations  1.45 us (2%)
    all_to_all x1, waiting for transfers between devices, local(): lax.all_to_all(packed, 'patch', split_axis=0, concat_axis=0, tiled=True)  18.1 us
    all_to_all x1, starting transfers between devices, local(): lax.all_to_all(packed, 'patch', split_axis=0, concat_axis=0, tiled=True)  13.1 us
    all_gather x1, blocking collectives, local(): patch_rows = lax.all_gather(nodes, 'feat', axis=0, tiled=True)  12 us
    unnamed x36, local copies, waits for them, and re-layouts  11.4 us
    ppermute x3, waiting for transfers between devices, local(): lax.ppermute(part, 'feat', [(i, (i + k) % size) for i in range(size)])  6.63 us
    pallas_call x1, Pallas kernels, edge_after(): pl.pallas_call(after_kernel, in_specs=[SMEM] + [VMEM] * 8, out_shape=[jax...  5.5 us
    ppermute x3, starting transfers between devices, local(): lax.ppermute(part, 'feat', [(i, (i + k) % size) for i in range(size)])  5.08 us
    pallas_call x1, Pallas kernels, edge_before(): pl.pallas_call(before_kernel, in_specs=[VMEM] * 6, out_shape=jax.ShapeDty...  4.27 us
  transfers between devices with their start and end apart: 4, of which 3 were waited for; matrix products, arithmetic and copies ran while one was open for 1% of the time, Pallas kernels for 5%

profile of v3, /device:TPU:1, one launch (start us, length us, event | category | flops | bytes accessed | tf_op | source)
XLA Modules:
  0.0 81.9 jit_solution(13029614979313879549)
XLA Ops:
  0.6 0.0 copy-start.4
  0.6 0.9 %copy-done.4 = bf16[160,512]{1,0:T(8,128)(2,1)S(1)} copy-done((bf16[160,512]{1,0:T(8,128)(2,1)S(1)}, bf16[160,512]{1,0:T(8,128)(2,1)}, u32[]{:S(2)}) %copy-start.4) | copy-done | bytes 163864
  1.5 0.0 copy-start.11
  1.6 0.7 copy-done.11
  2.3 2.4 %select.9 = bf16[1536,512]{1,0:T(8,128)(2,1)} custom-call(s32[24,64]{1,0:T(8,128)S(1)} %bitcast.10, bf16[160,512]{1,0:T(8,128)(2,1)S(1)} %copy-done.4), custom_call_target="tpu_custom_call" | custom-call | tf_op jit(solution)/shard_map/select/pallas_call | solution.py:67
  4.7 0.0 copy-start.16
  4.7 0.0 copy-start.17
  4.7 0.0 copy-start.5
  4.7 13.1 %all-to-all-start = ((bf16[64,24,512]{2,1,0:T(8,128)(2,1)}), bf16[64,24,512]{2,1,0:T(8,128)(2,1)S(1)}, u32[]{:S(2)}, u32[]{:S(2)}) async-start(bf16[64,24,512]{2,1,0:T(8,128)(2,1)} %bitcast.3), calls=%async_computation | async-start | bytes 3145728 | tf_op jit(solution)/shard_map/all_to_all | solution.py:186
  17.8 0.0 copy-done.16
  17.8 0.0 copy-start.15
  17.8 0.2 reshape.40.recv_ref
  18.8 0.0 copy-done.17
  18.8 0.2 reshape.41.send_ref
  19.0 0.0 copy-done.5
  19.0 12.0 %all_gather.3.patch_ref = bf16[640,512]{1,0:T(8,128)(2,1)S(1)} all-gather(bf16[160,512]{1,0:T(8,128)(2,1)S(1)} %copy-done.5), channel_id=1, replica_groups=mesh['patch'=64,'feat'=4] {'feat'}, dimensions={0}, use_global_device_ids=true | all-gather | bytes 819200 | tf_op jit(solution)/shard_map/all_gather | solution.py:188
  31.0 0.0 copy-done.15
  31.0 0.0 copy-start.2
  31.0 1.4 %copy-done.2 = bf16[1536,512]{1,0:T(8,128)(2,1)S(1)} copy-done((bf16[1536,512]{1,0:T(8,128)(2,1)S(1)}, bf16[1536,512]{1,0:T(8,128)(2,1)}, u32[]{:S(2)}) %copy-start.2) | copy-done | bytes 1572888
  32.4 0.0 copy-start.6
  32.4 1.3 %copy-done.6 = bf16[1280,512]{1,0:T(8,128)(2,1)S(1)} copy-done((bf16[1280,512]{1,0:T(8,128)(2,1)S(1)}, bf16[1280,512]{1,0:T(8,128)(2,1)}, u32[]{:S(2)}) %copy-start.6) | copy-done | bytes 1310744
  33.8 0.0 copy-start.12
  33.8 4.3 %edge_before.1.before_ref = f32[1280,512]{1,0:T(8,128)S(1)} custom-call(bf16[640,512]{1,0:T(8,128)(2,1)S(1)} %all_gather.3.patch_ref, bf16[1280,512]{1,0:T(8,128)(2,1)S(1)} %copy-done.6, s32[1280,1]{1,0:T(8,128)S(1)} %reshape.40.recv_ref, s32[1280,1]{1,0:T(8,128)S(1)} %reshape.41.send_ref, bf16[1536,512]{1,0:T(8,128)(2,1)S(1)} %copy-done.2, ...), custom_call_target="tpu_custom_call" | custom-call | flops 3690987520 | bytes 8388608 | tf_op jit(solution)/shard_map/edge_before/pallas_call | solution.py:92
  38.0 0.0 copy-start
  38.1 1.5 %copy-done = f32[1280,512]{1,0:T(8,128)} copy-done((f32[1280,512]{1,0:T(8,128)}, f32[1280,512]{1,0:T(8,128)S(1)}, u32[]{:S(2)}) %copy-start) | copy-done | bytes 2621464
  39.6 18.1 %all-to-all-done = bf16[64,24,512]{2,1,0:T(8,128)(2,1)S(1)} async-done(((bf16[64,24,512]{2,1,0:T(8,128)(2,1)}), bf16[64,24,512]{2,1,0:T(8,128)(2,1)S(1)}, u32[]{:S(2)}, u32[]{:S(2)}) %all-to-all-start) | async-done | bytes 1572896 | tf_op jit(solution)/shard_map/all_to_all | solution.py:186
  57.6 0.0 copy-done.12
  57.6 0.0 copy-start.1
  57.6 1.7 %copy-done.1 = f32[1280,512]{1,0:T(8,128)S(1)} copy-done((f32[1280,512]{1,0:T(8,128)S(1)}, f32[1280,512]{1,0:T(8,128)}, u32[]{:S(2)}) %copy-start.1) | copy-done | bytes 2621464
  59.4 0.0 copy-start.3
  59.4 1.4 %copy-done.3 = bf16[1536,512]{1,0:T(8,128)(2,1)S(1)} copy-done((bf16[1536,512]{1,0:T(8,128)(2,1)S(1)}, bf16[1536,512]{1,0:T(8,128)(2,1)}, u32[]{:S(2)}) %copy-start.3) | copy-done | bytes 1572888
  60.8 0.0 copy-start.7
  60.8 1.3 %copy-done.7 = bf16[1280,512]{1,0:T(8,128)(2,1)S(1)} copy-done((bf16[1280,512]{1,0:T(8,128)(2,1)S(1)}, bf16[1280,512]{1,0:T(8,128)(2,1)}, u32[]{:S(2)}) %copy-start.7) | copy-done | bytes 1310744
  62.1 0.0 copy-start.9
  62.1 1.0 %copy-done.9 = bf16[512,512]{1,0:T(8,128)(2,1)S(1)} copy-done((bf16[512,512]{1,0:T(8,128)(2,1)S(1)}, bf16[512,512]{1,0:T(8,128)(2,1)}, u32[]{:S(2)}) %copy-start.9) | copy-done | bytes 524312
  63.1 0.0 copy-start.10
  63.1 0.0 copy-start.13
  63.1 0.0 copy-start.14
  63.1 5.5 %edge_after.1 = (bf16[1280,512]{1,0:T(8,128)(2,1)}, bf16[640,512]{1,0:T(8,128)(2,1)S(1)}) custom-call(s32[1]{0:T(128)S(6)} %copy.19.live_ref, f32[1280,512]{1,0:T(8,128)S(1)} %copy-done.1, bf16[1536,512]{1,0:T(8,128)(2,1)S(1)} %bitcast.9, bf16[1280,512]{1,0:T(8,128)(2,1)S(1)} %copy-done.7, s32[1280,1]{1,0:T(8,128)S(1)} %reshape.41.send_ref, ...), custom_call_target="tpu_custom_call" | custom-call | tf_op jit(solution)/shard_map/edge_after/pallas_call | solution.py:134
  68.6 0.0 copy-start.8
  68.7 1.4 %collective-permute-start = (bf16[160,512]{1,0:T(8,128)(2,1)S(1)}, bf16[160,512]{1,0:T(8,128)(2,1)S(1)}, u32[]{:S(2)}, u32[]{:S(2)}) collective-permute-start(bf16[160,512]{1,0:T(8,128)(2,1)S(1)} %get-tuple-element.8), channel_id=1, source_target_pairs={{0,1},{1,2},{2,3},{3,0},{4,5},{5,6},{6,7},{7,4},{8,9},{9,10},{10,1... | collective-permute-start | bytes 491528 | tf_op jit(solution)/shard_map/ppermute | solution.py:202
  70.1 2.6 %collective-permute-start.1 = (bf16[160,512]{1,0:T(8,128)(2,1)S(1)}, bf16[160,512]{1,0:T(8,128)(2,1)S(1)}, u32[]{:S(2)}, u32[]{:S(2)}) collective-permute-start(bf16[160,512]{1,0:T(8,128)(2,1)S(1)} %get-tuple-element.7), channel_id=1, source_target_pairs={{0,2},{1,3},{2,0},{3,1},{4,6},{5,7},{6,4},{7,5},{8,10},{9,11},{10,... | collective-permute-start | bytes 491528 | tf_op jit(solution)/shard_map/ppermute | solution.py:202
  72.7 1.1 %collective-permute-start.2 = (bf16[160,512]{1,0:T(8,128)(2,1)S(1)}, bf16[160,512]{1,0:T(8,128)(2,1)S(1)}, u32[]{:S(2)}, u32[]{:S(2)}) collective-permute-start(bf16[160,512]{1,0:T(8,128)(2,1)S(1)} %get-tuple-element.6), channel_id=1, source_target_pairs={{0,3},{1,0},{2,1},{3,2},{4,7},{5,4},{6,5},{7,6},{8,11},{9,8},{10,9... | collective-permute-start | bytes 491528 | tf_op jit(solution)/shard_map/ppermute | solution.py:202
  73.8 2.0 %collective-permute-done.p1_ref = bf16[160,512]{1,0:T(8,128)(2,1)S(1)} collective-permute-done((bf16[160,512]{1,0:T(8,128)(2,1)S(1)}, bf16[160,512]{1,0:T(8,128)(2,1)S(1)}, u32[]{:S(2)}, u32[]{:S(2)}) %collective-permute-start) | collective-permute-done | bytes 163872 | tf_op jit(solution)/shard_map/ppermute | solution.py:202
  75.8 4.6 %collective-permute-done.1.p2_ref = bf16[160,512]{1,0:T(8,128)(2,1)S(1)} collective-permute-done((bf16[160,512]{1,0:T(8,128)(2,1)S(1)}, bf16[160,512]{1,0:T(8,128)(2,1)S(1)}, u32[]{:S(2)}, u32[]{:S(2)}) %collective-permute-start.1) | collective-permute-done | bytes 163872 | tf_op jit(solution)/shard_map/ppermute | solution.py:202
  80.4 0.0 collective-permute-done.2.p3_ref
  80.4 0.0 copy-done.10
  80.4 0.0 copy-done.13
  80.4 0.0 copy-done.14
  80.4 0.0 copy-done.8
  80.4 1.4 %node_update.1 = bf16[160,512]{1,0:T(8,128)(2,1)} custom-call(bf16[160,512]{1,0:T(8,128)(2,1)S(1)} %copy-done.5, bf16[160,512]{1,0:T(8,128)(2,1)S(1)} %get-tuple-element.9.p0_ref, bf16[160,512]{1,0:T(8,128)(2,1)S(1)} %collective-permute-done.p1_ref, bf16[160,512]{1,0:T(8,128)(2,1)S(1)} %collective-permute-done.1.p2_ref, ...), custom_call_target="tpu_custom_call" | custom-call | tf_op jit(solution)/shard_map/node_update/pallas_call | solution.py:159
  (2 shorter events, 0.0 us)
Async XLA Ops:
  0.6 0.9 %copy-start.4 = (bf16[160,512]{1,0:T(8,128)(2,1)S(1)}, bf16[160,512]{1,0:T(8,128)(2,1)}, u32[]{:S(2)}) copy-start(bf16[160,512]{1,0:T(8,128)(2,1)} %nodes_ref.1) | copy-start | bytes 491524
  1.5 0.7 copy-start.11
  4.7 13.1 %copy-start.16 = (s32[1280]{0:T(1024)S(1)}, s32[1280]{0:T(1024)}, u32[]{:S(2)}) copy-start(s32[1280]{0:T(1024)} %param.16) | copy-start | bytes 15364
  4.7 14.1 %copy-start.17 = (s32[1280]{0:T(1024)S(1)}, s32[1280]{0:T(1024)}, u32[]{:S(2)}) copy-start(s32[1280]{0:T(1024)} %param.17) | copy-start | bytes 15364
  4.7 14.3 %copy-start.5 = (bf16[160,512]{1,0:T(8,128)(2,1)S(1)}, bf16[160,512]{1,0:T(8,128)(2,1)}, u32[]{:S(2)}) copy-start(bf16[160,512]{1,0:T(8,128)(2,1)} %nodes_ref.1) | copy-start | bytes 491524
  4.7 52.9 %all-to-all-start = ((bf16[64,24,512]{2,1,0:T(8,128)(2,1)}), bf16[64,24,512]{2,1,0:T(8,128)(2,1)S(1)}, u32[]{:S(2)}, u32[]{:S(2)}) async-start(bf16[64,24,512]{2,1,0:T(8,128)(2,1)} %bitcast.3), calls=%async_computation | async-start | bytes 3145728 | tf_op jit(solution)/shard_map/all_to_all | solution.py:186
  17.8 13.2 %copy-start.15 = (f32[512]{0:T(512)S(1)}, f32[512]{0:T(512)}, u32[]{:S(2)}) copy-start(f32[512]{0:T(512)} %param.21) | copy-start | bytes 6148
  31.0 1.4 %copy-start.2 = (bf16[1536,512]{1,0:T(8,128)(2,1)S(1)}, bf16[1536,512]{1,0:T(8,128)(2,1)}, u32[]{:S(2)}) copy-start(bf16[1536,512]{1,0:T(8,128)(2,1)} %w1_ref.4) | copy-start | bytes 4718596
  32.4 1.3 %copy-start.6 = (bf16[1280,512]{1,0:T(8,128)(2,1)S(1)}, bf16[1280,512]{1,0:T(8,128)(2,1)}, u32[]{:S(2)}) copy-start(bf16[1280,512]{1,0:T(8,128)(2,1)} %edges_ref.3) | copy-start | bytes 3932164
  33.8 23.9 %copy-start.12 = (f32[512]{0:T(512)S(1)}, f32[512]{0:T(512)}, u32[]{:S(2)}) copy-start(f32[512]{0:T(512)} %param.23) | copy-start | bytes 6148
  38.0 1.5 %copy-start = (f32[1280,512]{1,0:T(8,128)}, f32[1280,512]{1,0:T(8,128)S(1)}, u32[]{:S(2)}) copy-start(f32[1280,512]{1,0:T(8,128)S(1)} %edge_before.1.before_ref) | copy-start | bytes 7864324
  57.6 1.7 %copy-start.1 = (f32[1280,512]{1,0:T(8,128)S(1)}, f32[1280,512]{1,0:T(8,128)}, u32[]{:S(2)}) copy-start(f32[1280,512]{1,0:T(8,128)} %copy-done) | copy-start | bytes 7864324
  59.4 1.4 %copy-start.3 = (bf16[1536,512]{1,0:T(8,128)(2,1)S(1)}, bf16[1536,512]{1,0:T(8,128)(2,1)}, u32[]{:S(2)}) copy-start(bf16[1536,512]{1,0:T(8,128)(2,1)} %w1_ref.4) | copy-start | bytes 4718596
  60.8 1.3 %copy-start.7 = (bf16[1280,512]{1,0:T(8,128)(2,1)S(1)}, bf16[1280,512]{1,0:T(8,128)(2,1)}, u32[]{:S(2)}) copy-start(bf16[1280,512]{1,0:T(8,128)(2,1)} %edges_ref.3) | copy-start | bytes 3932164
  62.1 1.0 %copy-start.9 = (bf16[512,512]{1,0:T(8,128)(2,1)S(1)}, bf16[512,512]{1,0:T(8,128)(2,1)}, u32[]{:S(2)}) copy-start(bf16[512,512]{1,0:T(8,128)(2,1)} %w2_ref.2) | copy-start | bytes 1572868
  63.1 17.3 %copy-start.10 = (bf16[512,512]{1,0:T(8,128)(2,1)S(1)}, bf16[512,512]{1,0:T(8,128)(2,1)}, u32[]{:S(2)}) copy-start(bf16[512,512]{1,0:T(8,128)(2,1)} %w2_ref.3) | copy-start | bytes 1572868
  63.1 17.3 %copy-start.13 = (f32[512]{0:T(512)S(1)}, f32[512]{0:T(512)}, u32[]{:S(2)}) copy-start(f32[512]{0:T(512)} %param.25) | copy-start | bytes 6148
  63.1 17.3 %copy-start.14 = (f32[512]{0:T(512)S(1)}, f32[512]{0:T(512)}, u32[]{:S(2)}) copy-start(f32[512]{0:T(512)} %param.27) | copy-start | bytes 6148
  68.6 11.8 %copy-start.8 = (bf16[1024,512]{1,0:T(8,128)(2,1)S(1)}, bf16[1024,512]{1,0:T(8,128)(2,1)}, u32[]{:S(2)}) copy-start(bf16[1024,512]{1,0:T(8,128)(2,1)} %w1_ref.5) | copy-start | bytes 3145732
  68.7 7.1 %collective-permute-start = (bf16[160,512]{1,0:T(8,128)(2,1)S(1)}, bf16[160,512]{1,0:T(8,128)(2,1)S(1)}, u32[]{:S(2)}, u32[]{:S(2)}) collective-permute-start(bf16[160,512]{1,0:T(8,128)(2,1)S(1)} %get-tuple-element.8), channel_id=1, source_target_pairs={{0,1},{1,2},{2,3},{3,0},{4,5},{5,6},{6,7},{7,4},{8,9},{9,10},{10,1... | collective-permute-start | bytes 491528 | tf_op jit(solution)/shard_map/ppermute | solution.py:202
  70.1 10.3 %collective-permute-start.1 = (bf16[160,512]{1,0:T(8,128)(2,1)S(1)}, bf16[160,512]{1,0:T(8,128)(2,1)S(1)}, u32[]{:S(2)}, u32[]{:S(2)}) collective-permute-start(bf16[160,512]{1,0:T(8,128)(2,1)S(1)} %get-tuple-element.7), channel_id=1, source_target_pairs={{0,2},{1,3},{2,0},{3,1},{4,6},{5,7},{6,4},{7,5},{8,10},{9,11},{10,... | collective-permute-start | bytes 491528 | tf_op jit(solution)/shard_map/ppermute | solution.py:202
  72.7 7.7 %collective-permute-start.2 = (bf16[160,512]{1,0:T(8,128)(2,1)S(1)}, bf16[160,512]{1,0:T(8,128)(2,1)S(1)}, u32[]{:S(2)}, u32[]{:S(2)}) collective-permute-start(bf16[160,512]{1,0:T(8,128)(2,1)S(1)} %get-tuple-element.6), channel_id=1, source_target_pairs={{0,3},{1,0},{2,1},{3,2},{4,7},{5,4},{6,5},{7,6},{8,11},{9,8},{10,9... | collective-permute-start | bytes 491528 | tf_op jit(solution)/shard_map/ppermute | solution.py:202

commit v4 on v3

--- a/solution.py
+++ b/solution.py
@@ -9,6 +9,7 @@
 f32 = jnp.float32
 bf16 = jnp.bfloat16
 TILES = 2
+GATHERS = 1
 LIMIT = 16 << 20
 VMEM = pl.BlockSpec(memory_space=pltpu.VMEM)
 SMEM = pl.BlockSpec(memory_space=pltpu.SMEM)
@@ -103,44 +104,81 @@
     )(patch_rows, edges, recv, send, w1, b1)
 
 
+def in_hbm(value):
+    return pltpu.with_memory_space_constraint(value, pltpu.HBM)
+
+
 def after_kernel(
-    live_ref, before_ref, remote_ref, edges_ref, send_ref, recv_ref, w1_ref, w2_ref, gain_ref,
-    out_ref, sums_ref,
+    live_ref, remote_ref, send_ref, recv_ref, gain_ref, before_hbm, w1_hbm, w2_hbm, edges_hbm,
+    out_hbm, sums_ref, before_ref, w1_ref, w2_ref, edges_ref, out_ref, load_sems, store_sems,
 ):
     count, latent = edges_ref.shape
     tile = count // TILES
     nodes = sums_ref.shape[0]
+    loads = [
+        pltpu.make_async_copy(w1_hbm.at[pl.ds(latent, latent)], w1_ref, load_sems.at[0]),
+        pltpu.make_async_copy(before_hbm, before_ref, load_sems.at[1]),
+        pltpu.make_async_copy(w2_hbm, w2_ref, load_sems.at[2]),
+        pltpu.make_async_copy(edges_hbm, edges_ref, load_sems.at[3]),
+    ]
+    for load in loads:
+        load.start()
+    stores = []
     live = live_ref[0]
+    for at in range(GATHERS):
+        rows = slice(at * count // GATHERS, (at + 1) * count // GATHERS)
+        hot = hot_rows(send_ref[rows], remote_ref.shape[0], nodes)
+        out_ref[rows] = dot(hot, remote_ref[...]).astype(bf16)
+    for load in loads:
+        load.wait()
     for at in range(TILES):
         rows = slice(at * tile, (at + 1) * tile)
-        hot = hot_rows(send_ref[rows], remote_ref.shape[0], nodes)
-        far = dot(hot, remote_ref[...]).astype(bf16)
-        first = before_ref[rows] + dot(far, w1_ref[latent : 2 * latent])
+        first = before_ref[rows] + dot(out_ref[rows], w1_ref[...])
         hidden = silu(first).astype(bf16)
         change = layer_norm(dot(hidden, w2_ref[...]), gain_ref[...])
         alive = lax.broadcasted_iota(jnp.int32, (tile, 1), 0) + at * tile < live
         edge = edges_ref[rows].astype(f32) + jnp.where(alive, change, 0.0)
-        out_ref[rows] = edge.astype(bf16)
+        edges_ref[rows] = edge.astype(bf16)
+        part = pl.ds(at * tile, tile)
+        stores.append(
+            pltpu.make_async_copy(edges_ref.at[part], out_hbm.at[part], store_sems.at[at])
+        )
+        stores[-1].start()
     alive = lax.broadcasted_iota(jnp.int32, (1, count), 1) < live
     receiver = jnp.where(alive, recv_ref[...], -1)
     size = nodes // 4
     for at in range(4):
         hot = hot_columns(receiver, size, at * size)
-        sums_ref[at * size : (at + 1) * size] = dot(hot, out_ref[...]).astype(bf16)
+        sums_ref[at * size : (at + 1) * size] = dot(hot, edges_ref[...]).astype(bf16)
+    for store in stores:
+        store.wait()
 
 
 def edge_after(live, before, remote, edges, send, recv, w1, w2, gain, nodes):
     count, latent = edges.shape
+    hbm = pl.BlockSpec(memory_space=pltpu.HBM)
     return pl.pallas_call(
         after_kernel,
-        in_specs=[SMEM] + [VMEM] * 8,
+        in_specs=[SMEM] + [VMEM] * 4 + [hbm] * 4,
+        out_specs=[hbm, VMEM],
         out_shape=[
             jax.ShapeDtypeStruct((count, latent), bf16),
             jax.ShapeDtypeStruct((nodes, latent), bf16),
         ],
-        compiler_params=pltpu.CompilerParams(vmem_limit_bytes=LIMIT),
+        scratch_shapes=[
+            pltpu.VMEM((count, latent), f32),
+            pltpu.VMEM((latent, latent), bf16),
+            pltpu.VMEM((latent, latent), bf16),
+            pltpu.VMEM((count, latent), bf16),
+            pltpu.VMEM((count, latent), bf16),
+            pltpu.SemaphoreType.DMA((4,)),
+            pltpu.SemaphoreType.DMA((TILES,)),
+        ],
+        compiler_params=pltpu.CompilerParams(vmem_limit_bytes=32 << 20),
         name="edge_after",
-    )(live, before, remote, edges, send, recv, w1, w2, gain)
+    )(
+        live, remote, send, recv, gain, in_hbm(before), in_hbm(w1), in_hbm(w2), in_hbm(edges)
+    )
 
 
 def node_kernel(nodes_ref, p0_ref, p1_ref, p2_ref, p3_ref, w1_ref, b1_ref, w2_ref, gain_ref, out_ref):

time: 82.3 us -> 77.1 us (0.937)
  local copies, waits for them, and re-layouts: 11.9 us -> 6.37 us
    unnamed x36 -> x28, local copies, waits for them, and re-layouts: 11.4 us -> 5.87 us
  transfers between devices with their start and end apart: 4 -> 4, of which waited for: 3 -> 3; matrix products, arithmetic and copies ran while one was open for 1% -> 1% of each run, Pallas kernels for 5% -> 6%
where the time goes in v4:
time: 77.1 us; the launch traced here: 76.8 us
  waiting for transfers between devices  24.7 us (32%)
  starting transfers between devices  18.2 us (24%)
  Pallas kernels  14.1 us (18%)
  blocking collectives  12 us (16%)
  local copies, waits for them, and re-layouts  6.37 us (8%)
  between operations  1.47 us (2%)
    all_to_all x1, waiting for transfers between devices, local(): lax.all_to_all(packed, 'patch', split_axis=0, concat_axis=0, tiled=True)  18.1 us
    all_to_all x1, starting transfers between devices, local(): lax.all_to_all(packed, 'patch', split_axis=0, concat_axis=0, tiled=True)  13.1 us
    all_gather x1, blocking collectives, local(): patch_rows = lax.all_gather(nodes, 'feat', axis=0, tiled=True)  12 us
    ppermute x3, waiting for transfers between devices, local(): lax.ppermute(part, 'feat', [(i, (i + k) % size) for i in range(size)])  6.63 us
    pallas_call x1, Pallas kernels, edge_after(): pl.pallas_call(after_kernel, in_specs=[SMEM] + [VMEM] * 4 + [hbm] * 4, ou...  5.9 us
    unnamed x28, local copies, waits for them, and re-layouts  5.87 us
    ppermute x3, starting transfers between devices, local(): lax.ppermute(part, 'feat', [(i, (i + k) % size) for i in range(size)])  5.05 us
    pallas_call x1, Pallas kernels, edge_before(): pl.pallas_call(before_kernel, in_specs=[VMEM] * 6, out_shape=jax.ShapeDty...  4.28 us
  transfers between devices with their start and end apart: 4, of which 3 were waited for; matrix products, arithmetic and copies ran while one was open for 1% of the time, Pallas kernels for 6%

profile of v4, /device:TPU:1, one launch (start us, length us, event | category | flops | bytes accessed | tf_op | source)
XLA Modules:
  0.0 76.8 jit_solution(10303406966522450689)
XLA Ops:
  0.6 0.0 copy-start.2
  0.6 0.9 %copy-done.2 = bf16[160,512]{1,0:T(8,128)(2,1)S(1)} copy-done((bf16[160,512]{1,0:T(8,128)(2,1)S(1)}, bf16[160,512]{1,0:T(8,128)(2,1)}, u32[]{:S(2)}) %copy-start.2) | copy-done | bytes 163864
  1.5 0.0 copy-start.7
  1.6 0.7 copy-done.7
  2.3 2.4 %select.9 = bf16[1536,512]{1,0:T(8,128)(2,1)} custom-call(s32[24,64]{1,0:T(8,128)S(1)} %bitcast.10, bf16[160,512]{1,0:T(8,128)(2,1)S(1)} %copy-done.2), custom_call_target="tpu_custom_call" | custom-call | tf_op jit(solution)/shard_map/select/pallas_call | solution.py:68
  4.7 0.0 copy-start.12
  4.7 0.0 copy-start.13
  4.7 0.0 copy-start.3
  4.7 13.1 %all-to-all-start = ((bf16[64,24,512]{2,1,0:T(8,128)(2,1)}), bf16[64,24,512]{2,1,0:T(8,128)(2,1)S(1)}, u32[]{:S(2)}, u32[]{:S(2)}) async-start(bf16[64,24,512]{2,1,0:T(8,128)(2,1)} %bitcast.2), calls=%async_computation | async-start | bytes 3145728 | tf_op jit(solution)/shard_map/all_to_all | solution.py:224
  17.8 0.0 copy-done.12
  17.8 0.0 copy-start.11
  17.9 0.2 reshape.41.recv_ref
  18.8 0.0 copy-done.13
  18.8 0.2 reshape.40.send_ref
  19.0 0.0 copy-done.3
  19.0 12.0 %all_gather.3.patch_ref = bf16[640,512]{1,0:T(8,128)(2,1)S(1)} all-gather(bf16[160,512]{1,0:T(8,128)(2,1)S(1)} %copy-done.3), channel_id=1, replica_groups=mesh['patch'=64,'feat'=4] {'feat'}, dimensions={0}, use_global_device_ids=true | all-gather | bytes 819200 | tf_op jit(solution)/shard_map/all_gather | solution.py:226
  31.0 0.0 copy-done.11
  31.0 0.0 copy-start.1
  31.0 1.4 %copy-done.1 = bf16[1536,512]{1,0:T(8,128)(2,1)S(1)} copy-done((bf16[1536,512]{1,0:T(8,128)(2,1)S(1)}, bf16[1536,512]{1,0:T(8,128)(2,1)}, u32[]{:S(2)}) %copy-start.1) | copy-done | bytes 1572888
  32.4 0.0 copy-start.4
  32.4 1.3 %copy-done.4 = bf16[1280,512]{1,0:T(8,128)(2,1)S(1)} copy-done((bf16[1280,512]{1,0:T(8,128)(2,1)S(1)}, bf16[1280,512]{1,0:T(8,128)(2,1)}, u32[]{:S(2)}) %copy-start.4) | copy-done | bytes 1310744
  33.8 0.0 copy-start.8
  33.8 4.3 %edge_before.1.before_hbm = f32[1280,512]{1,0:T(8,128)S(1)} custom-call(bf16[640,512]{1,0:T(8,128)(2,1)S(1)} %all_gather.3.patch_ref, bf16[1280,512]{1,0:T(8,128)(2,1)S(1)} %copy-done.4, s32[1280,1]{1,0:T(8,128)S(1)} %reshape.41.recv_ref, s32[1280,1]{1,0:T(8,128)S(1)} %reshape.40.send_ref, bf16[1536,512]{1,0:T(8,128)(2,1)S(1)} %copy-done.1, ...), custom_call_target="tpu_custom_call" | custom-call | flops 3690987520 | bytes 8388608 | tf_op jit(solution)/shard_map/edge_before/pallas_call | solution.py:93
  38.1 0.0 copy-start
  38.1 1.5 %copy-done = f32[1280,512]{1,0:T(8,128)} copy-done((f32[1280,512]{1,0:T(8,128)}, f32[1280,512]{1,0:T(8,128)S(1)}, u32[]{:S(2)}) %copy-start) | copy-done | bytes 2621464
  39.6 18.1 %all-to-all-done = bf16[64,24,512]{2,1,0:T(8,128)(2,1)S(1)} async-done(((bf16[64,24,512]{2,1,0:T(8,128)(2,1)}), bf16[64,24,512]{2,1,0:T(8,128)(2,1)S(1)}, u32[]{:S(2)}, u32[]{:S(2)}) %all-to-all-start) | async-done | bytes 1572896 | tf_op jit(solution)/shard_map/all_to_all | solution.py:224
  57.6 0.0 copy-done.8
  57.6 0.0 copy-start.6
  57.6 0.0 copy-start.9
  57.6 0.0 copy-start.10
  57.6 5.9 %edge_after.1 = (bf16[1280,512]{1,0:T(8,128)(2,1)}, bf16[640,512]{1,0:T(8,128)(2,1)S(1)}) custom-call(s32[1]{0:T(128)S(6)} %copy.19.live_ref, bf16[1536,512]{1,0:T(8,128)(2,1)S(1)} %bitcast.9, s32[1280,1]{1,0:T(8,128)S(1)} %reshape.40.send_ref, s32[1,1280]{1,0:T(1,128)S(1)} %reshape.34.recv_ref, f32[1,512]{1,0:T(1,128)S(1)} %bitcast.11, ...), custom_call_target="tpu_custom_call" | custom-call | tf_op jit(solution)/shard_map/edge_after/pallas_call | solution.py:160
  63.5 0.0 copy-start.5
  63.6 0.1 constant_dynamic-slice_fusion
  63.6 1.4 %collective-permute-start = (bf16[160,512]{1,0:T(8,128)(2,1)S(1)}, bf16[160,512]{1,0:T(8,128)(2,1)S(1)}, u32[]{:S(2)}, u32[]{:S(2)}) collective-permute-start(bf16[160,512]{1,0:T(8,128)(2,1)S(1)} %get-tuple-element.8), channel_id=1, source_target_pairs={{0,1},{1,2},{2,3},{3,0},{4,5},{5,6},{6,7},{7,4},{8,9},{9,10},{10,1... | collective-permute-start | bytes 491528 | tf_op jit(solution)/shard_map/ppermute | solution.py:240
  65.0 2.6 %collective-permute-start.1 = (bf16[160,512]{1,0:T(8,128)(2,1)S(1)}, bf16[160,512]{1,0:T(8,128)(2,1)S(1)}, u32[]{:S(2)}, u32[]{:S(2)}) collective-permute-start(bf16[160,512]{1,0:T(8,128)(2,1)S(1)} %get-tuple-element.7), channel_id=1, source_target_pairs={{0,2},{1,3},{2,0},{3,1},{4,6},{5,7},{6,4},{7,5},{8,10},{9,11},{10,... | collective-permute-start | bytes 491528 | tf_op jit(solution)/shard_map/ppermute | solution.py:240
  67.6 1.1 %collective-permute-start.2 = (bf16[160,512]{1,0:T(8,128)(2,1)S(1)}, bf16[160,512]{1,0:T(8,128)(2,1)S(1)}, u32[]{:S(2)}, u32[]{:S(2)}) collective-permute-start(bf16[160,512]{1,0:T(8,128)(2,1)S(1)} %get-tuple-element.6), channel_id=1, source_target_pairs={{0,3},{1,0},{2,1},{3,2},{4,7},{5,4},{6,5},{7,6},{8,11},{9,8},{10,9... | collective-permute-start | bytes 491528 | tf_op jit(solution)/shard_map/ppermute | solution.py:240
  68.7 2.0 %collective-permute-done.p1_ref = bf16[160,512]{1,0:T(8,128)(2,1)S(1)} collective-permute-done((bf16[160,512]{1,0:T(8,128)(2,1)S(1)}, bf16[160,512]{1,0:T(8,128)(2,1)S(1)}, u32[]{:S(2)}, u32[]{:S(2)}) %collective-permute-start) | collective-permute-done | bytes 163872 | tf_op jit(solution)/shard_map/ppermute | solution.py:240
  70.7 4.6 %collective-permute-done.1.p2_ref = bf16[160,512]{1,0:T(8,128)(2,1)S(1)} collective-permute-done((bf16[160,512]{1,0:T(8,128)(2,1)S(1)}, bf16[160,512]{1,0:T(8,128)(2,1)S(1)}, u32[]{:S(2)}, u32[]{:S(2)}) %collective-permute-start.1) | collective-permute-done | bytes 163872 | tf_op jit(solution)/shard_map/ppermute | solution.py:240
  75.3 0.0 collective-permute-done.2.p3_ref
  75.3 0.0 copy-done.6
  75.3 0.0 copy-done.9
  75.3 0.0 copy-done.10
  75.3 0.0 copy-done.5
  75.3 1.4 %node_update.1 = bf16[160,512]{1,0:T(8,128)(2,1)} custom-call(bf16[160,512]{1,0:T(8,128)(2,1)S(1)} %copy-done.3, bf16[160,512]{1,0:T(8,128)(2,1)S(1)} %get-tuple-element.9.p0_ref, bf16[160,512]{1,0:T(8,128)(2,1)S(1)} %collective-permute-done.p1_ref, bf16[160,512]{1,0:T(8,128)(2,1)S(1)} %collective-permute-done.1.p2_ref, ...), custom_call_target="tpu_custom_call" | custom-call | tf_op jit(solution)/shard_map/node_update/pallas_call | solution.py:197
  (1 shorter events, 0.0 us)
Async XLA Ops:
  0.6 0.9 %copy-start.2 = (bf16[160,512]{1,0:T(8,128)(2,1)S(1)}, bf16[160,512]{1,0:T(8,128)(2,1)}, u32[]{:S(2)}) copy-start(bf16[160,512]{1,0:T(8,128)(2,1)} %nodes_ref.1) | copy-start | bytes 491524
  1.5 0.7 copy-start.7
  4.7 13.1 %copy-start.12 = (s32[1280]{0:T(1024)S(1)}, s32[1280]{0:T(1024)}, u32[]{:S(2)}) copy-start(s32[1280]{0:T(1024)} %param.16) | copy-start | bytes 15364
  4.7 14.1 %copy-start.13 = (s32[1280]{0:T(1024)S(1)}, s32[1280]{0:T(1024)}, u32[]{:S(2)}) copy-start(s32[1280]{0:T(1024)} %param.17) | copy-start | bytes 15364
  4.7 14.3 %copy-start.3 = (bf16[160,512]{1,0:T(8,128)(2,1)S(1)}, bf16[160,512]{1,0:T(8,128)(2,1)}, u32[]{:S(2)}) copy-start(bf16[160,512]{1,0:T(8,128)(2,1)} %nodes_ref.1) | copy-start | bytes 491524
  4.7 52.9 %all-to-all-start = ((bf16[64,24,512]{2,1,0:T(8,128)(2,1)}), bf16[64,24,512]{2,1,0:T(8,128)(2,1)S(1)}, u32[]{:S(2)}, u32[]{:S(2)}) async-start(bf16[64,24,512]{2,1,0:T(8,128)(2,1)} %bitcast.2), calls=%async_computation | async-start | bytes 3145728 | tf_op jit(solution)/shard_map/all_to_all | solution.py:224
  17.8 13.2 %copy-start.11 = (f32[512]{0:T(512)S(1)}, f32[512]{0:T(512)}, u32[]{:S(2)}) copy-start(f32[512]{0:T(512)} %param.21) | copy-start | bytes 6148
  31.0 1.4 %copy-start.1 = (bf16[1536,512]{1,0:T(8,128)(2,1)S(1)}, bf16[1536,512]{1,0:T(8,128)(2,1)}, u32[]{:S(2)}) copy-start(bf16[1536,512]{1,0:T(8,128)(2,1)} %w1_hbm.1) | copy-start | bytes 4718596
  32.4 1.3 %copy-start.4 = (bf16[1280,512]{1,0:T(8,128)(2,1)S(1)}, bf16[1280,512]{1,0:T(8,128)(2,1)}, u32[]{:S(2)}) copy-start(bf16[1280,512]{1,0:T(8,128)(2,1)} %edges_hbm.1) | copy-start | bytes 3932164
  33.8 23.9 %copy-start.8 = (f32[512]{0:T(512)S(1)}, f32[512]{0:T(512)}, u32[]{:S(2)}) copy-start(f32[512]{0:T(512)} %param.23) | copy-start | bytes 6148
  38.1 1.5 %copy-start = (f32[1280,512]{1,0:T(8,128)}, f32[1280,512]{1,0:T(8,128)S(1)}, u32[]{:S(2)}) copy-start(f32[1280,512]{1,0:T(8,128)S(1)} %edge_before.1.before_hbm) | copy-start | bytes 7864324
  57.6 17.7 %copy-start.6 = (bf16[512,512]{1,0:T(8,128)(2,1)S(1)}, bf16[512,512]{1,0:T(8,128)(2,1)}, u32[]{:S(2)}) copy-start(bf16[512,512]{1,0:T(8,128)(2,1)} %w2_ref.1) | copy-start | bytes 1572868
  57.6 17.7 %copy-start.9 = (f32[512]{0:T(512)S(1)}, f32[512]{0:T(512)}, u32[]{:S(2)}) copy-start(f32[512]{0:T(512)} %param.25) | copy-start | bytes 6148
  57.6 17.7 %copy-start.10 = (f32[512]{0:T(512)S(1)}, f32[512]{0:T(512)}, u32[]{:S(2)}) copy-start(f32[512]{0:T(512)} %param.27) | copy-start | bytes 6148
  63.5 11.8 %copy-start.5 = (bf16[1024,512]{1,0:T(8,128)(2,1)S(1)}, bf16[1024,512]{1,0:T(8,128)(2,1)}, u32[]{:S(2)}) copy-start(bf16[1024,512]{1,0:T(8,128)(2,1)} %w1_ref.3) | copy-start | bytes 3145732
  63.6 7.1 %collective-permute-start = (bf16[160,512]{1,0:T(8,128)(2,1)S(1)}, bf16[160,512]{1,0:T(8,128)(2,1)S(1)}, u32[]{:S(2)}, u32[]{:S(2)}) collective-permute-start(bf16[160,512]{1,0:T(8,128)(2,1)S(1)} %get-tuple-element.8), channel_id=1, source_target_pairs={{0,1},{1,2},{2,3},{3,0},{4,5},{5,6},{6,7},{7,4},{8,9},{9,10},{10,1... | collective-permute-start | bytes 491528 | tf_op jit(solution)/shard_map/ppermute | solution.py:240
  65.0 10.3 %collective-permute-start.1 = (bf16[160,512]{1,0:T(8,128)(2,1)S(1)}, bf16[160,512]{1,0:T(8,128)(2,1)S(1)}, u32[]{:S(2)}, u32[]{:S(2)}) collective-permute-start(bf16[160,512]{1,0:T(8,128)(2,1)S(1)} %get-tuple-element.7), channel_id=1, source_target_pairs={{0,2},{1,3},{2,0},{3,1},{4,6},{5,7},{6,4},{7,5},{8,10},{9,11},{10,... | collective-permute-start | bytes 491528 | tf_op jit(solution)/shard_map/ppermute | solution.py:240
  67.6 7.7 %collective-permute-start.2 = (bf16[160,512]{1,0:T(8,128)(2,1)S(1)}, bf16[160,512]{1,0:T(8,128)(2,1)S(1)}, u32[]{:S(2)}, u32[]{:S(2)}) collective-permute-start(bf16[160,512]{1,0:T(8,128)(2,1)S(1)} %get-tuple-element.6), channel_id=1, source_target_pairs={{0,3},{1,0},{2,1},{3,2},{4,7},{5,4},{6,5},{7,6},{8,11},{9,8},{10,9... | collective-permute-start | bytes 491528 | tf_op jit(solution)/shard_map/ppermute | solution.py:240

commit v5 on v2

v5 whole, which is shorter than its diff:
```python
import jax
import jax.numpy as jnp
from jax import lax
from jax.experimental import pallas as pl
from jax.experimental.pallas import tpu as pltpu
from jax.sharding import PartitionSpec as P

epsilon = 1e-05
f32 = jnp.float32
bf16 = jnp.bfloat16
i32 = jnp.int32
TILES = 2
LIMIT = 16 << 20
VMEM = pl.BlockSpec(memory_space=pltpu.VMEM)
SMEM = pl.BlockSpec(memory_space=pltpu.SMEM)
HBM = pl.BlockSpec(memory_space=pltpu.HBM)
X, Z, C = 4, 8, 2
TAIL = 16
COST = 1 << 20
BATCHES = (((0, 1), (7, 2)), ((6, 3), (5, 4)))


def dot(left, right):
    return jnp.dot(left, right, preferred_element_type=f32)


def dot_first(left, right):
    return lax.dot_general(left, right, (((0,), (0,)), ((), ())), preferred_element_type=f32)


def silu(value):
    return value / (1.0 + jnp.exp(-value))


def layer_norm(values, scales):
    average = jnp.mean(values, axis=-1, keepdims=True)
    centred = values - average
    variance = jnp.mean(centred * centred, axis=-1, keepdims=True)
    return centred * lax.rsqrt(variance + epsilon) * scales


def as_bf16(mask):
    return mask.astype(f32).astype(bf16)


def hot_columns(row, count, first=0):
    ids = lax.broadcasted_iota(i32, (count, row.shape[1]), 0) + first
    return as_bf16(row == ids)


def in_hbm(value):
    return pltpu.with_memory_space_constraint(value, pltpu.HBM)


def odd(dz):
    return (dz >= 1) & (dz <= 4)


def pack_kernel(where_ref, lists_ref, nodes_ref, out_ref):
    rows, latent = nodes_ref.shape
    cap, peers = lists_ref.shape
    out_ref[:rows] = nodes_ref[...]
    me = where_ref[0]
    x, z, c = me // (Z * C), me // C % Z, me % C
    lane = lax.broadcasted_iota(i32, (cap, latent), 1)
    spread = as_bf16(lane % cap == lax.broadcasted_iota(i32, (cap, latent), 0))
    listed = dot_first(lists_ref[...].astype(f32).astype(bf16), spread)
    peer = lax.broadcasted_iota(i32, (peers, latent), 0)
    lane = lax.broadcasted_iota(i32, (peers, latent), 1)
    k = (peer // (Z * C) - x) & (X - 1)
    dz = (peer // C % Z - z) & (Z - 1)
    s = (peer % C - c) & (C - 1)
    slot = (k * C + s) * 2 + jnp.where(odd(dz), 1, 0)
    listed = jnp.where(lane // cap == slot, listed + 1.0, 0.0).astype(bf16)
    row = lax.broadcasted_iota(i32, (TAIL, peers), 0)
    peer = lax.broadcasted_iota(i32, (TAIL, peers), 1)
    pick = as_bf16(row == ((peer // C % Z - z) & (Z - 1)))
    out_ref[rows:] = (dot(pick, listed) - 1.0).astype(bf16)


def pack(me, lists, nodes):
    return pl.pallas_call(
        pack_kernel,
        in_specs=[SMEM, VMEM, VMEM],
        out_shape=jax.ShapeDtypeStruct((nodes.shape[0] + TAIL, nodes.shape[1]), bf16),
        name="pack",
    )(me, lists, nodes)


def select_kernel(pairs, cap, *refs):
    blocks, outs = refs[: 2 * len(pairs)], refs[2 * len(pairs) :]
    rows = blocks[0].shape[0] - TAIL
    lanes = X * C * 2 * cap
    for at, pair in enumerate(pairs):
        total = None
        for side, dz in enumerate(pair):
            block = blocks[2 * at + side]
            wanted = block[rows:].astype(f32)[dz : dz + 1, :lanes].astype(i32)
            part = dot_first(hot_columns(wanted, rows), block[:rows])
            total = part if total is None else total + part
        total = total.astype(bf16)
        size = 2 * cap
        for k in range(X):
            for s in range(C):
                first = (k * C + s) * size
                put = (s * len(pairs) + at) * size
                outs[k][put : put + size] = total[first : first + size]


def select(pairs, cap, blocks):
    latent = blocks[0].shape[1]
    shape = jax.ShapeDtypeStruct((C * len(pairs) * 2 * cap, latent), bf16)
    rows = blocks[0].shape[0]
    return pl.pallas_call(
        lambda *refs: select_kernel(pairs, cap, *refs),
        in_specs=[VMEM] * len(blocks),
        out_shape=[shape] * X,
        compiler_params=pltpu.CompilerParams(vmem_limit_bytes=LIMIT),
        cost_estimate=pl.CostEstimate(flops=COST, bytes_accessed=0, transcendentals=0),
        name="select",
    )(*blocks)


def cross_kernel(*refs):
    out_ref = refs[-1]
    size = refs[0].shape[0] // C
    for k in range(X):
        out_ref[k * size : (k + 1) * size] = refs[k][size:]


def crossing(parts, *earlier):
    rows, latent = parts[0].shape
    return pl.pallas_call(
        cross_kernel,
        in_specs=[VMEM] * X + [HBM] * len(earlier),
        out_shape=jax.ShapeDtypeStruct((rows // C * X, latent), bf16),
        compiler_params=pltpu.CompilerParams(vmem_limit_bytes=LIMIT),
        name="crossing",
    )(*parts, *[in_hbm(part) for part in earlier])


def fill(table_ref, put, group):
    size = group[0].shape[0] // C
    for k in range(X):
        table_ref[put : put + size] = group[k][:size]
        put += size
    table_ref[put : put + X * size] = group[X][...]


def before_kernel(*refs):
    recv_ref, send_ref, b1_ref = refs[:3]
    group = refs[3 : 4 + X]
    patch_hbm, edges_hbm, w1_hbm, out_hbm = refs[4 + X : 8 + X]
    patch_ref, table_ref, edges_ref, w1_ref, out_ref, sems = refs[8 + X :]
    fetch = pltpu.make_async_copy(patch_hbm, patch_ref, sems.at[2 + TILES])
    fetch.start()
    loads = [
        pltpu.make_async_copy(edges_hbm, edges_ref, sems.at[0]),
        pltpu.make_async_copy(w1_hbm, w1_ref, sems.at[1]),
    ]
    for load in loads:
        load.start()
    count, latent = edges_ref.shape
    nodes = patch_ref.shape[0]
    tile = count // TILES
    fill(table_ref, nodes, group)
    fetch.wait()
    table_ref[:nodes] = patch_ref[...].astype(bf16)
    stores = []
    for at in range(TILES):
        rows = slice(at * tile, (at + 1) * tile)
        own = dot_first(hot_columns(recv_ref[:, rows], nodes), table_ref[:nodes]).astype(bf16)
        hot = hot_columns(send_ref[:, rows], table_ref.shape[0])
        near = dot_first(hot, table_ref[...]).astype(bf16)
        if at == 0:
            for load in loads:
                load.wait()
        total = dot(edges_ref[rows], w1_ref[:latent])
        total = total + dot(near, w1_ref[latent : 2 * latent])
        total = total + dot(own, w1_ref[2 * latent :])
        out_ref[rows] = total + b1_ref[...]
        part = pl.ds(at * tile, tile)
        stores.append(pltpu.make_async_copy(out_ref.at[part], out_hbm.at[part], sems.at[2 + at]))
        stores[-1].start()
    for store in stores:
        store.wait()


def edge_before(patch_rows, recv, send, b1, group, edges, w1):
    count, latent = edges.shape
    table = patch_rows.shape[0] + sum(part.shape[0] for part in group[:X]) // C + group[X].shape[0]
    return pl.pallas_call(
        before_kernel,
        in_specs=[VMEM] * (4 + X) + [HBM] * 3,
        out_specs=HBM,
        out_shape=pltpu.HBM((count, latent), f32),
        scratch_shapes=[
            pltpu.VMEM(patch_rows.shape, f32),
            pltpu.VMEM((table, latent), bf16),
            pltpu.VMEM((count, latent), bf16),
            pltpu.VMEM(w1.shape, bf16),
            pltpu.VMEM((count, latent), f32),
            pltpu.SemaphoreType.DMA((3 + TILES,)),
        ],
        compiler_params=pltpu.CompilerParams(vmem_limit_bytes=32 << 20),
        cost_estimate=pl.CostEstimate(flops=COST, bytes_accessed=0, transcendentals=0),
        name="edge_before",
    )(recv, send, b1, *group, in_hbm(patch_rows), in_hbm(edges), in_hbm(w1))


def after_kernel(first_row, *refs):
    live_ref, send_ref, recv_ref, gain_ref = refs[:4]
    group = refs[4 : 5 + X]
    before_hbm, w1_hbm, w2_hbm, edges_hbm, out_hbm = refs[5 + X : 10 + X]
    sums_refs = refs[10 + X : 14 + X]
    table_ref, before_ref, w1_ref, w2_ref, edges_ref, far_ref, load_sems, store_sems = refs[14 + X :]
    count, latent = edges_ref.shape
    tile = count // TILES
    loads = [
        pltpu.make_async_copy(w1_hbm.at[pl.ds(latent, latent)], w1_ref, load_sems.at[0]),
        pltpu.make_async_copy(before_hbm, before_ref, load_sems.at[1]),
        pltpu.make_async_copy(w2_hbm, w2_ref, load_sems.at[2]),
        pltpu.make_async_copy(edges_hbm, edges_ref, load_sems.at[3]),
    ]
    for load in loads:
        load.start()
    fill(table_ref, 0, group)
    stores = []
    live = live_ref[0]
    hot = hot_columns(send_ref[...], table_ref.shape[0], first_row)
    far_ref[...] = dot_first(hot, table_ref[...]).astype(bf16)
    for load in loads:
        load.wait()
    for at in range(TILES):
        rows = slice(at * tile, (at + 1) * tile)
        first = before_ref[rows] + dot(far_ref[rows], w1_ref[...])
        hidden = silu(first).astype(bf16)
        change = layer_norm(dot(hidden, w2_ref[...]), gain_ref[...])
        alive = lax.broadcasted_iota(i32, (tile, 1), 0) + at * tile < live
        edge = edges_ref[rows].astype(f32) + jnp.where(alive, change, 0.0)
        edges_ref[rows] = edge.astype(bf16)
        part = pl.ds(at * tile, tile)
        stores.append(
            pltpu.make_async_copy(edges_ref.at[part], out_hbm.at[part], store_sems.at[at])
        )
        stores[-1].start()
    alive = lax.broadcasted_iota(i32, (1, count), 1) < live
    receiver = jnp.where(alive, recv_ref[...], -1)
    size = sums_refs[0].shape[0]
    for at, ref in enumerate(sums_refs):
        hot = hot_columns(receiver, size, at * size)
        ref[...] = dot(hot, edges_ref[...]).astype(ref.dtype)
    for store in stores:
        store.wait()


def edge_after(first_row, live, send, recv, gain, group, before, w1, w2, edges, rows):
    count, latent = edges.shape
    table = sum(part.shape[0] for part in group[:X]) // C + group[X].shape[0]
    return pl.pallas_call(
        lambda *refs: after_kernel(first_row, *refs),
        in_specs=[SMEM] + [VMEM] * (4 + X) + [HBM] * 4,
        out_specs=[HBM] + [VMEM] * 4,
        out_shape=[jax.ShapeDtypeStruct((count, latent), bf16)]
        + [jax.ShapeDtypeStruct((rows, latent), f32 if k == 0 else bf16) for k in range(4)],
        scratch_shapes=[
            pltpu.VMEM((table, latent), bf16),
            pltpu.VMEM((count, latent), f32),
            pltpu.VMEM((latent, latent), bf16),
            pltpu.VMEM((latent, latent), bf16),
            pltpu.VMEM((count, latent), bf16),
            pltpu.VMEM((count, latent), bf16),
            pltpu.SemaphoreType.DMA((4,)),
            pltpu.SemaphoreType.DMA((TILES,)),
        ],
        compiler_params=pltpu.CompilerParams(vmem_limit_bytes=32 << 20),
        name="edge_after",
    )(live, send, recv, gain, *group, *[in_hbm(part) for part in (before, w1, w2, edges)])


def node_kernel(nodes_ref, p0_ref, p1_ref, p2_ref, p3_ref, w1_ref, b1_ref, w2_ref, gain_ref, out_ref):
    latent = nodes_ref.shape[1]
    total = p0_ref[...].astype(f32) + p1_ref[...].astype(f32)
    total = total + p2_ref[...].astype(f32) + p3_ref[...].astype(f32)
    incoming = total.astype(bf16)
    nodes = nodes_ref[...]
    first = dot(nodes, w1_ref[:latent]) + dot(incoming, w1_ref[latent:])
    hidden = silu(first + b1_ref[...]).astype(bf16)
    change = layer_norm(dot(hidden, w2_ref[...]), gain_ref[...])
    out_ref[...] = (nodes.astype(f32) + change).astype(bf16)


def node_update(nodes, parts, w1, b1, w2, gain):
    return pl.pallas_call(
        node_kernel,
        in_specs=[VMEM] * 9,
        out_shape=jax.ShapeDtypeStruct(nodes.shape, bf16),
        compiler_params=pltpu.CompilerParams(vmem_limit_bytes=LIMIT),
        name="node_update",
    )(nodes, *parts, w1, b1, w2, gain)


def pairs_of(move):
    found = []
    for x in range(X):
        for z in range(Z):
            for c in range(C):
                tx, tz, tc = move(x, z, c)
                found.append(((x * Z + z) * C + c, ((tx % X) * Z + tz % Z) * C + tc % C))
    return found


def moved(value, move):
    return lax.ppermute(value, "patch", pairs_of(move))


def local(
    nodes,
    edges,
    receivers,
    sender_slot,
    send_rows,
    live_edges,
    edge_w1,
    edge_b1,
    edge_w2,
    edge_gain,
    node_w1,
    node_b1,
    node_w2,
    node_gain,
):
    rows, latent = nodes.shape
    cap = send_rows.shape[3]
    me = lax.axis_index("patch")
    mine = lax.axis_index("feat")
    x, z, c = me // (Z * C), me // C % Z, me % C
    feat = lax.axis_size("feat")

    block = pack(me.reshape(1), send_rows[0, 0].T, nodes)
    patch_rows = lax.all_gather(nodes.astype(f32), "feat", axis=0, tiled=True)
    up = lambda a: moved(a, lambda x, z, c: (x, z + 1, c))
    down = lambda a: moved(a, lambda x, z, c: (x, z - 1, c))
    held = {0: block}
    forth = back = block
    for hop in range(1, 4):
        forth, back = up(forth), down(back)
        held[hop], held[Z - hop] = forth, back
    held[4] = up(forth)

    groups = []
    for pairs in BATCHES:
        picked = select(pairs, cap, [held[dz] for pair in pairs for dz in pair])
        group = [picked[0]]
        for k in range(1, X):
            group.append(moved(picked[k], lambda x, z, c: (x + k, z, c)))
        groups.append(group)
    swap = lambda a: moved(a, lambda x, z, c: (x, z, c + 1))
    groups[0].append(swap(crossing(groups[0])))

    def near_row(row):
        return ((mine - row // rows) & (feat - 1)) * rows + row % rows

    patch = feat * rows
    slot = jnp.maximum(sender_slot - patch, 0)
    source, entry = slot // cap, slot % cap
    k = (x - source // (Z * C)) & (X - 1)
    dz = (z - source // C % Z) & (Z - 1)
    s = (source - c) & (C - 1)
    place = jnp.zeros_like(slot)
    base = 0
    for pairs in BATCHES:
        for at, pair in enumerate(pairs):
            for side, value in enumerate(pair):
                size = len(pairs) * 2 * cap
                here = base + (s * X + k) * size + at * 2 * cap + side * cap
                place = jnp.where(dz == value, here, place)
        base += X * C * len(pairs) * 2 * cap
    send = jnp.where(sender_slot < patch, sender_slot, patch + place + entry).reshape(1, -1)
    first_row = patch + len(BATCHES[0]) * 2 * cap * X * C
    before = edge_before(
        patch_rows, receivers.reshape(1, -1), send, edge_b1.reshape(1, -1), groups[0], edges, edge_w1
    )
    groups[1].append(swap(crossing(groups[1], before)))
    edges_out, *sums = edge_after(
        first_row, live_edges, send, near_row(receivers).reshape(1, -1), edge_gain.reshape(1, -1),
        groups[1], before, edge_w1, edge_w2, edges, rows,
    )
    parts = [sums[0]]
    for k in range(1, feat):
        parts.append(lax.ppermute(sums[k], "feat", [(i, (i - k) % feat) for i in range(feat)]))
    nodes_out = node_update(
        nodes, parts, node_w1, node_b1.reshape(1, -1), node_w2, node_gain.reshape(1, -1)
    )
    return (edges_out, nodes_out)


def solution(mesh):
    placed = (
        P(("patch", "feat"), None),
        P(("patch", "feat"), None),
        P(("patch", "feat")),
        P(("patch", "feat")),
        P("patch", "feat", None, None),
        P(("patch", "feat")),
    ) + (P(),) * 8
    return jax.shard_map(
        local,
        mesh=mesh,
        in_specs=placed,
        out_specs=(P(("patch", "feat"), None), P(("patch", "feat"), None)),
        check_vma=False,
    )
```

time: 99.4 us -> 93.5 us (0.941)
  between operations: 1.63 us -> 14.9 us
  Pallas kernels: 28.8 us -> 19 us
  local copies, waits for them, and re-layouts: 10.4 us -> 0.98 us
  waiting for transfers between devices: 15.9 us -> 24.6 us
  starting transfers between devices: 39.4 us -> 32.1 us
    pallas_call x7 -> x8, Pallas kernels: 28.8 us -> 19 us  [the longest x1 7.88 us: edge_before(): pl.pallas_call(before_kernel, in_specs=[VMEM] * (4 + X) + [HBM] * 3, out_...]
    ppermute x19 -> x15, waiting for transfers between devices: 6.01 us -> 14.5 us  [moved(): return lax.ppermute(value, 'patch', pairs_of(move))]
    slice x12 -> x0, local copies, waits for them, and re-layouts: 7.24 us -> none  [local(): crossing = jnp.concatenate([part[size:] for part in group], axis=0)]
    ppermute x3 -> x0, starting transfers between devices: 3.94 us -> none  [local(): lax.ppermute(nodes, 'feat', [(i, (i + k) % feat) for i in range(feat)])]
    ppermute x19 -> x15, starting transfers between devices: 32.1 us -> 28.2 us  [moved(): return lax.ppermute(value, 'patch', pairs_of(move))]
    concatenate x3 -> x0, other arithmetic: 1.89 us -> none  [local(): crossing = jnp.concatenate([part[size:] for part in group], axis=0)]
    convert_element_type x0 -> x1, other arithmetic: none -> 1.68 us  [local(): patch_rows = lax.all_gather(nodes.astype(f32), 'feat', axis=0, tiled=True)]
    reshape x3, local copies, waits for them, and re-layouts: 1.3 us -> 0.01 us  [the longest x1 0.01 us: local(): jnp.where(sender_slot < patch, sender_slot, patch + place + entry)]
  transfers between devices with their start and end apart: 25 -> 19, of which waited for: 5 -> 7; matrix products, arithmetic and copies ran while one was open for 11% -> 0% of each run, Pallas kernels for 15% -> 12%
where the time goes in v5:
time: 93.5 us; the launch traced here: 93.3 us
  starting transfers between devices  32.1 us (34%)
  waiting for transfers between devices  24.6 us (26%)
  Pallas kernels  19 us (20%)
  between operations  14.9 us (16%)
  other arithmetic  1.74 us (2%)
  local copies, waits for them, and re-layouts  0.98 us (1%)
    ppermute x15, starting transfers between devices, moved(): return lax.ppermute(value, 'patch', pairs_of(move))  28.2 us
    ppermute x15, waiting for transfers between devices, moved(): return lax.ppermute(value, 'patch', pairs_of(move))  14.5 us
    ppermute x3, waiting for transfers between devices, local(): lax.ppermute(sums[k], 'feat', [(i, (i - k) % feat) for i in range(feat)])  10.1 us
    pallas_call x1, Pallas kernels, edge_before(): pl.pallas_call(before_kernel, in_specs=[VMEM] * (4 + X) + [HBM] * 3, out_...  7.88 us
    pallas_call x1, Pallas kernels, edge_after(): pl.pallas_call(lambda *refs: after_kernel(first_row, *refs), in_specs=[SM...  6.5 us
    ppermute x3, starting transfers between devices, local(): lax.ppermute(sums[k], 'feat', [(i, (i - k) % feat) for i in range(feat)])  3.85 us
    pallas_call x1, Pallas kernels, pack(): pl.pallas_call(pack_kernel, in_specs=[SMEM, VMEM, VMEM], out_shape=jax.Sh...  1.93 us
  transfers between devices with their start and end apart: 19, of which 7 were waited for; matrix products, arithmetic and copies ran while one was open for 0% of the time, Pallas kernels for 12%

profile of v5, /device:TPU:1, one launch (start us, length us, event | category | flops | bytes accessed | tf_op | source)
XLA Modules:
  0.0 93.3 jit_solution(10575455803759099876)
XLA Ops:
  7.2 0.0 all-gather.2.cloned.1.call-start
  7.2 1.7 %convert_element_type.3 = f32[160,512]{1,0:T(8,128)} convert(bf16[160,512]{1,0:T(8,128)(2,1)} %nodes_ref.3) | non-fusion elementwise | flops 81920 | bytes 491520 | tf_op jit(solution)/shard_map/convert_element_type | solution.py:341
  8.9 0.0 copy-start.8
  8.9 0.0 all-gather.2.cloned.1.call-update
  8.9 0.0 copy-start.9
  8.9 0.0 copy-start.4
  8.9 1.9 %pack.1.refs_0_ = bf16[176,512]{1,0:T(8,128)(2,1)} custom-call(s32[1]{0:T(128)} %bitcast.1.where_ref, s32[24,64]{1,0:T(8,128)} %bitcast.12, bf16[160,512]{1,0:T(8,128)(2,1)} %nodes_ref.3), custom_call_target="tpu_custom_call" | custom-call | tf_op jit(solution)/shard_map/pack/pallas_call | solution.py:82
  10.9 2.5 %collective-permute-start.2 = (bf16[176,512]{1,0:T(8,128)(2,1)}, bf16[176,512]{1,0:T(8,128)(2,1)S(1)}, u32[]{:S(2)}, u32[]{:S(2)}) collective-permute-start(bf16[176,512]{1,0:T(8,128)(2,1)} %pack.1.refs_0_), channel_id=1, source_target_pairs={{0,8},{4,12},{8,16},{12,20},{16,24},{20,28},{24,32},{28,36},{32,40... | collective-permute-start | bytes 540680 | tf_op jit(solution)/shard_map/ppermute | solution.py:314
  13.3 3.9 %collective-permute-start = (bf16[176,512]{1,0:T(8,128)(2,1)}, bf16[176,512]{1,0:T(8,128)(2,1)S(1)}, u32[]{:S(2)}, u32[]{:S(2)}) collective-permute-start(bf16[176,512]{1,0:T(8,128)(2,1)} %pack.1.refs_0_), channel_id=1, source_target_pairs={{0,56},{4,60},{8,0},{12,4},{16,8},{20,12},{24,16},{28,20},{32,24},... | collective-permute-start | bytes 540680 | tf_op jit(solution)/shard_map/ppermute | solution.py:314
  17.3 4.5 %collective-permute-done.2.refs_1_ = bf16[176,512]{1,0:T(8,128)(2,1)S(1)} collective-permute-done((bf16[176,512]{1,0:T(8,128)(2,1)}, bf16[176,512]{1,0:T(8,128)(2,1)S(1)}, u32[]{:S(2)}, u32[]{:S(2)}) %collective-permute-start.2) | collective-permute-done | bytes 180256 | tf_op jit(solution)/shard_map/ppermute | solution.py:314
  21.8 0.0 collective-permute-start.3
  21.8 0.0 collective-permute-done.refs_2_
  21.8 6.0 %collective-permute-done.3.refs_3_ = bf16[176,512]{1,0:T(8,128)(2,1)S(1)} collective-permute-done((bf16[176,512]{1,0:T(8,128)(2,1)S(1)}, bf16[176,512]{1,0:T(8,128)(2,1)S(1)}, u32[]{:S(2)}, u32[]{:S(2)}) %collective-permute-start.3) | collective-permute-done | bytes 180256 | tf_op jit(solution)/shard_map/ppermute | solution.py:314
  27.8 0.0 copy-start.2
  27.8 0.9 copy-done.2
  28.7 0.6 select.25
  29.3 1.3 %collective-permute-start.10 = (bf16[192,512]{1,0:T(8,128)(2,1)S(1)}, bf16[192,512]{1,0:T(8,128)(2,1)S(1)}, u32[]{:S(2)}, u32[]{:S(2)}) collective-permute-start(bf16[192,512]{1,0:T(8,128)(2,1)S(1)} %get-tuple-element.20), channel_id=1, source_target_pairs={{0,64},{4,68},{8,72},{12,76},{16,80},{20,84},{24,88},{28,92},{32,9... | collective-permute-start | bytes 589832 | tf_op jit(solution)/shard_map/ppermute | solution.py:314
  30.6 2.4 %collective-permute-start.11 = (bf16[192,512]{1,0:T(8,128)(2,1)S(1)}, bf16[192,512]{1,0:T(8,128)(2,1)S(1)}, u32[]{:S(2)}, u32[]{:S(2)}) collective-permute-start(bf16[192,512]{1,0:T(8,128)(2,1)S(1)} %get-tuple-element.21), channel_id=1, source_target_pairs={{0,128},{4,132},{8,136},{12,140},{16,144},{20,148},{24,152},{28,15... | collective-permute-start | bytes 589832 | tf_op jit(solution)/shard_map/ppermute | solution.py:314
  33.1 1.2 %collective-permute-start.12 = (bf16[192,512]{1,0:T(8,128)(2,1)S(1)}, bf16[192,512]{1,0:T(8,128)(2,1)S(1)}, u32[]{:S(2)}, u32[]{:S(2)}) collective-permute-start(bf16[192,512]{1,0:T(8,128)(2,1)S(1)} %get-tuple-element.22), channel_id=1, source_target_pairs={{0,192},{4,196},{8,200},{12,204},{16,208},{20,212},{24,216},{28,22... | collective-permute-start | bytes 589832 | tf_op jit(solution)/shard_map/ppermute | solution.py:314
  34.2 0.0 collective-permute-start.1
  34.2 1.5 %collective-permute-start.4 = (bf16[176,512]{1,0:T(8,128)(2,1)S(1)}, bf16[176,512]{1,0:T(8,128)(2,1)S(1)}, u32[]{:S(2)}, u32[]{:S(2)}) collective-permute-start(bf16[176,512]{1,0:T(8,128)(2,1)S(1)} %collective-permute-done.3.refs_3_), channel_id=1, source_target_pairs={{0,8},{4,12},{8,16},{12,20},{16,24},{20,28},{24,32},{28,36},{32,40... | collective-permute-start | bytes 540680 | tf_op jit(solution)/shard_map/ppermute | solution.py:314
  35.7 3.3 %collective-permute-done.1.refs_0_ = bf16[176,512]{1,0:T(8,128)(2,1)S(1)} collective-permute-done((bf16[176,512]{1,0:T(8,128)(2,1)S(1)}, bf16[176,512]{1,0:T(8,128)(2,1)S(1)}, u32[]{:S(2)}, u32[]{:S(2)}) %collective-permute-start.1) | collective-permute-done | bytes 180256 | tf_op jit(solution)/shard_map/ppermute | solution.py:314
  39.0 1.2 %collective-permute-start.5 = (bf16[176,512]{1,0:T(8,128)(2,1)S(1)}, bf16[176,512]{1,0:T(8,128)(2,1)S(1)}, u32[]{:S(2)}, u32[]{:S(2)}) collective-permute-start(bf16[176,512]{1,0:T(8,128)(2,1)S(1)} %collective-permute-done.1.refs_0_), channel_id=1, source_target_pairs={{0,56},{4,60},{8,0},{12,4},{16,8},{20,12},{24,16},{28,20},{32,24},... | collective-permute-start | bytes 540680 | tf_op jit(solution)/shard_map/ppermute | solution.py:314
  40.2 0.0 collective-permute-done.4.refs_1_
  40.2 0.3 collective-permute-start.6
  40.4 0.0 collective-permute-done.10.refs_1_.refs_4_
  40.4 0.0 collective-permute-done.11.refs_2_.refs_5_
  40.4 0.0 collective-permute-done.12.refs_3_.refs_6_
  40.5 5.3 %collective-permute-start.13 = (bf16[384,512]{1,0:T(8,128)(2,1)S(1)}, bf16[384,512]{1,0:T(8,128)(2,1)S(1)}, u32[]{:S(2)}, u32[]{:S(2)}) collective-permute-start(bf16[384,512]{1,0:T(8,128)(2,1)S(1)} %crossing.2), channel_id=1, source_target_pairs={{0,4},{4,0},{8,12},{12,8},{16,20},{20,16},{24,28},{28,24},{32,36},... | collective-permute-start | bytes 1179656 | tf_op jit(solution)/shard_map/ppermute | solution.py:314
  45.8 0.0 copy-done.8
  45.8 0.0 collective-permute-done.5.refs_2_
  45.8 0.0 collective-permute-done.6.refs_3_
  45.8 0.6 select.24
  46.4 0.4 collective-permute-start.7
  46.8 0.8 collective-permute-start.8
  47.6 1.7 %collective-permute-start.9 = (bf16[192,512]{1,0:T(8,128)(2,1)S(1)}, bf16[192,512]{1,0:T(8,128)(2,1)S(1)}, u32[]{:S(2)}, u32[]{:S(2)}) collective-permute-start(bf16[192,512]{1,0:T(8,128)(2,1)S(1)} %get-tuple-element.18), channel_id=1, source_target_pairs={{0,192},{4,196},{8,200},{12,204},{16,208},{20,212},{24,216},{28,22... | collective-permute-start | bytes 589832 | tf_op jit(solution)/shard_map/ppermute | solution.py:314
  49.3 0.0 copy-done.9
  49.4 0.0 collective-permute-done.13.refs_7_
  49.4 0.0 all-gather.2.cloned.1.call-done.refs_8_
  49.4 0.0 copy-done.4
  49.4 7.9 %edge_before.1.refs_4_.refs_9_ = f32[1280,512]{1,0:T(8,128)} custom-call(s32[1,1280]{1,0:T(1,128)S(1)} %reshape.32.refs_0_, s32[1,1280]{1,0:T(1,128)S(1)} %reshape.28.refs_1_, f32[1,512]{1,0:T(1,128)S(1)} %bitcast.8, bf16[192,512]{1,0:T(8,128)(2,1)S(1)} %get-tuple-element.19.refs_0_.refs_3_, bf16[192,512]{1,0:T(8,128)(2,1)S(1)} %collective-permute-done.10.refs_1_.refs_4_, ...), custom_call_target="tpu_custom_call" | custom-call | flops 1048576 | tf_op jit(solution)/shard_map/edge_before/pallas_call | solution.py:192
  57.3 0.0 collective-permute-done.7.refs_1_.refs_5_
  57.3 0.0 collective-permute-done.8.refs_2_.refs_6_
  57.3 0.0 collective-permute-done.9.refs_3_.refs_7_
  57.3 0.0 copy-start.7
  57.4 5.8 %collective-permute-start.14 = (bf16[384,512]{1,0:T(8,128)(2,1)S(1)}, bf16[384,512]{1,0:T(8,128)(2,1)S(1)}, u32[]{:S(2)}, u32[]{:S(2)}) collective-permute-start(bf16[384,512]{1,0:T(8,128)(2,1)S(1)} %crossing.3), channel_id=1, source_target_pairs={{0,4},{4,0},{8,12},{12,8},{16,20},{20,16},{24,28},{28,24},{32,36},... | collective-permute-start | bytes 1179656 | tf_op jit(solution)/shard_map/ppermute | solution.py:314
  63.8 0.7 collective-permute-done.14.refs_8_
  64.5 0.0 copy-done.7
  64.5 0.0 copy-start
  64.5 0.0 copy-start.5
  64.5 0.0 copy-start.6
  64.5 6.5 %edge_after.1 = (bf16[1280,512]{1,0:T(8,128)(2,1)}, f32[160,512]{1,0:T(8,128)S(1)}, bf16[160,512]{1,0:T(8,128)(2,1)S(1)}, bf16[160,512]{1,0:T(8,128)(2,1)S(1)}, bf16[160,512]{1,0:T(8,128)(2,1)S(1)}) custom-call(s32[1]{0:T(128)S(6)} %copy.16.refs_0_, s32[1,1280]{1,0:T(1,128)S(1)} %reshape.28.refs_1_, s32[1,1280]{1,0:T(1,128)S(1)} %reshape.29.refs_2_, ...), custom_call_target="tpu_custom_call" | custom-call | tf_op jit(solution)/shard_map/edge_after/pallas_call | solution.py:260
  71.0 2.8 %collective-permute-start.15 = (bf16[160,512]{1,0:T(8,128)(2,1)S(1)}, bf16[160,512]{1,0:T(8,128)(2,1)S(1)}, u32[]{:S(2)}, u32[]{:S(2)}) collective-permute-start(bf16[160,512]{1,0:T(8,128)(2,1)S(1)} %get-tuple-element.25), channel_id=1, source_target_pairs={{0,3},{1,0},{2,1},{3,2},{4,7},{5,4},{6,5},{7,6},{8,11},{9,8},{10,9... | collective-permute-start | bytes 491528 | tf_op jit(solution)/shard_map/ppermute | solution.py:391
  73.8 0.4 collective-permute-start.16
  74.2 0.7 collective-permute-start.17
  74.9 5.5 %collective-permute-done.15.p1_ref = bf16[160,512]{1,0:T(8,128)(2,1)S(1)} collective-permute-done((bf16[160,512]{1,0:T(8,128)(2,1)S(1)}, bf16[160,512]{1,0:T(8,128)(2,1)S(1)}, u32[]{:S(2)}, u32[]{:S(2)}) %collective-permute-start.15) | collective-permute-done | bytes 163872 | tf_op jit(solution)/shard_map/ppermute | solution.py:391
  80.4 0.1 collective-permute-done.16.p2_ref
  80.5 4.5 %collective-permute-done.17.p3_ref = bf16[160,512]{1,0:T(8,128)(2,1)S(1)} collective-permute-done((bf16[160,512]{1,0:T(8,128)(2,1)S(1)}, bf16[160,512]{1,0:T(8,128)(2,1)S(1)}, u32[]{:S(2)}, u32[]{:S(2)}) %collective-permute-start.17) | collective-permute-done | bytes 163872 | tf_op jit(solution)/shard_map/ppermute | solution.py:391
  85.0 0.0 copy-done
  85.0 0.0 copy-done.1
  85.0 0.0 copy-done.3
  85.0 0.0 copy-done.5
  85.0 0.0 copy-done.6
  85.0 1.4 %node_update.1 = bf16[160,512]{1,0:T(8,128)(2,1)} custom-call(bf16[160,512]{1,0:T(8,128)(2,1)S(1)} %copy-done, f32[160,512]{1,0:T(8,128)S(1)} %get-tuple-element.24.p0_ref, bf16[160,512]{1,0:T(8,128)(2,1)S(1)} %collective-permute-done.15.p1_ref, bf16[160,512]{1,0:T(8,128)(2,1)S(1)} %collective-permute-done.16.p2_ref, ...), custom_call_target="tpu_custom_call" | custom-call | tf_op jit(solution)/shard_map/node_update/pallas_call | solution.py:294
  (9 shorter events, 0.1 us)
Async XLA Ops:
  7.2 42.2 %all-gather.2.cloned.1.call-start = ((), (), s32[]{:S(2)}) async-start(), calls=%async_computation | async-start | bytes 1638400 | tf_op jit(solution)/shard_map/all_gather | solution.py:341
  8.9 36.9 %copy-start.8 = (s32[1280]{0:T(1024)S(1)}, s32[1280]{0:T(1024)}, u32[]{:S(2)}) copy-start(s32[1280]{0:T(1024)} %param.16) | copy-start | bytes 15364
  8.9 40.4 %copy-start.9 = (s32[1280]{0:T(1024)S(1)}, s32[1280]{0:T(1024)}, u32[]{:S(2)}) copy-start(s32[1280]{0:T(1024)} %param.17) | copy-start | bytes 15364
  8.9 40.5 %copy-start.4 = (f32[512]{0:T(512)S(1)}, f32[512]{0:T(512)}, u32[]{:S(2)}) copy-start(f32[512]{0:T(512)} %param.21) | copy-start | bytes 6148
  10.9 10.9 %collective-permute-start.2 = (bf16[176,512]{1,0:T(8,128)(2,1)}, bf16[176,512]{1,0:T(8,128)(2,1)S(1)}, u32[]{:S(2)}, u32[]{:S(2)}) collective-permute-start(bf16[176,512]{1,0:T(8,128)(2,1)} %pack.1.refs_0_), channel_id=1, source_target_pairs={{0,8},{4,12},{8,16},{12,20},{16,24},{20,28},{24,32},{28,36},{32,40... | collective-permute-start | bytes 540680 | tf_op jit(solution)/shard_map/ppermute | solution.py:314
  13.3 8.4 %collective-permute-start = (bf16[176,512]{1,0:T(8,128)(2,1)}, bf16[176,512]{1,0:T(8,128)(2,1)S(1)}, u32[]{:S(2)}, u32[]{:S(2)}) collective-permute-start(bf16[176,512]{1,0:T(8,128)(2,1)} %pack.1.refs_0_), channel_id=1, source_target_pairs={{0,56},{4,60},{8,0},{12,4},{16,8},{20,12},{24,16},{28,20},{32,24},... | collective-permute-start | bytes 540680 | tf_op jit(solution)/shard_map/ppermute | solution.py:314
  21.8 6.0 %collective-permute-start.3 = (bf16[176,512]{1,0:T(8,128)(2,1)S(1)}, bf16[176,512]{1,0:T(8,128)(2,1)S(1)}, u32[]{:S(2)}, u32[]{:S(2)}) collective-permute-start(bf16[176,512]{1,0:T(8,128)(2,1)S(1)} %collective-permute-done.2.refs_1_), channel_id=1, source_target_pairs={{0,8},{4,12},{8,16},{12,20},{16,24},{20,28},{24,32},{28,36},{32,40... | collective-permute-start | bytes 540680 | tf_op jit(solution)/shard_map/ppermute | solution.py:314
  27.8 0.9 copy-start.2
  29.3 11.1 %collective-permute-start.10 = (bf16[192,512]{1,0:T(8,128)(2,1)S(1)}, bf16[192,512]{1,0:T(8,128)(2,1)S(1)}, u32[]{:S(2)}, u32[]{:S(2)}) collective-permute-start(bf16[192,512]{1,0:T(8,128)(2,1)S(1)} %get-tuple-element.20), channel_id=1, source_target_pairs={{0,64},{4,68},{8,72},{12,76},{16,80},{20,84},{24,88},{28,92},{32,9... | collective-permute-start | bytes 589832 | tf_op jit(solution)/shard_map/ppermute | solution.py:314
  30.6 9.8 %collective-permute-start.11 = (bf16[192,512]{1,0:T(8,128)(2,1)S(1)}, bf16[192,512]{1,0:T(8,128)(2,1)S(1)}, u32[]{:S(2)}, u32[]{:S(2)}) collective-permute-start(bf16[192,512]{1,0:T(8,128)(2,1)S(1)} %get-tuple-element.21), channel_id=1, source_target_pairs={{0,128},{4,132},{8,136},{12,140},{16,144},{20,148},{24,152},{28,15... | collective-permute-start | bytes 589832 | tf_op jit(solution)/shard_map/ppermute | solution.py:314
  33.1 7.4 %collective-permute-start.12 = (bf16[192,512]{1,0:T(8,128)(2,1)S(1)}, bf16[192,512]{1,0:T(8,128)(2,1)S(1)}, u32[]{:S(2)}, u32[]{:S(2)}) collective-permute-start(bf16[192,512]{1,0:T(8,128)(2,1)S(1)} %get-tuple-element.22), channel_id=1, source_target_pairs={{0,192},{4,196},{8,200},{12,204},{16,208},{20,212},{24,216},{28,22... | collective-permute-start | bytes 589832 | tf_op jit(solution)/shard_map/ppermute | solution.py:314
  34.2 4.7 %collective-permute-start.1 = (bf16[176,512]{1,0:T(8,128)(2,1)S(1)}, bf16[176,512]{1,0:T(8,128)(2,1)S(1)}, u32[]{:S(2)}, u32[]{:S(2)}) collective-permute-start(bf16[176,512]{1,0:T(8,128)(2,1)S(1)} %collective-permute-done.refs_2_), channel_id=1, source_target_pairs={{0,56},{4,60},{8,0},{12,4},{16,8},{20,12},{24,16},{28,20},{32,24},... | collective-permute-start | bytes 540680 | tf_op jit(solution)/shard_map/ppermute | solution.py:314
  34.2 6.0 %collective-permute-start.4 = (bf16[176,512]{1,0:T(8,128)(2,1)S(1)}, bf16[176,512]{1,0:T(8,128)(2,1)S(1)}, u32[]{:S(2)}, u32[]{:S(2)}) collective-permute-start(bf16[176,512]{1,0:T(8,128)(2,1)S(1)} %collective-permute-done.3.refs_3_), channel_id=1, source_target_pairs={{0,8},{4,12},{8,16},{12,20},{16,24},{20,28},{24,32},{28,36},{32,40... | collective-permute-start | bytes 540680 | tf_op jit(solution)/shard_map/ppermute | solution.py:314
  39.0 6.8 %collective-permute-start.5 = (bf16[176,512]{1,0:T(8,128)(2,1)S(1)}, bf16[176,512]{1,0:T(8,128)(2,1)S(1)}, u32[]{:S(2)}, u32[]{:S(2)}) collective-permute-start(bf16[176,512]{1,0:T(8,128)(2,1)S(1)} %collective-permute-done.1.refs_0_), channel_id=1, source_target_pairs={{0,56},{4,60},{8,0},{12,4},{16,8},{20,12},{24,16},{28,20},{32,24},... | collective-permute-start | bytes 540680 | tf_op jit(solution)/shard_map/ppermute | solution.py:314
  40.2 5.6 %collective-permute-start.6 = (bf16[176,512]{1,0:T(8,128)(2,1)S(1)}, bf16[176,512]{1,0:T(8,128)(2,1)S(1)}, u32[]{:S(2)}, u32[]{:S(2)}) collective-permute-start(bf16[176,512]{1,0:T(8,128)(2,1)S(1)} %collective-permute-done.4.refs_1_), channel_id=1, source_target_pairs={{0,8},{4,12},{8,16},{12,20},{16,24},{20,28},{24,32},{28,36},{32,40... | collective-permute-start | bytes 540680 | tf_op jit(solution)/shard_map/ppermute | solution.py:314
  40.5 8.9 %collective-permute-start.13 = (bf16[384,512]{1,0:T(8,128)(2,1)S(1)}, bf16[384,512]{1,0:T(8,128)(2,1)S(1)}, u32[]{:S(2)}, u32[]{:S(2)}) collective-permute-start(bf16[384,512]{1,0:T(8,128)(2,1)S(1)} %crossing.2), channel_id=1, source_target_pairs={{0,4},{4,0},{8,12},{12,8},{16,20},{20,16},{24,28},{28,24},{32,36},... | collective-permute-start | bytes 1179656 | tf_op jit(solution)/shard_map/ppermute | solution.py:314
  46.4 10.9 %collective-permute-start.7 = (bf16[192,512]{1,0:T(8,128)(2,1)S(1)}, bf16[192,512]{1,0:T(8,128)(2,1)S(1)}, u32[]{:S(2)}, u32[]{:S(2)}) collective-permute-start(bf16[192,512]{1,0:T(8,128)(2,1)S(1)} %get-tuple-element.16), channel_id=1, source_target_pairs={{0,64},{4,68},{8,72},{12,76},{16,80},{20,84},{24,88},{28,92},{32,9... | collective-permute-start | bytes 589832 | tf_op jit(solution)/shard_map/ppermute | solution.py:314
  46.8 10.5 %collective-permute-start.8 = (bf16[192,512]{1,0:T(8,128)(2,1)S(1)}, bf16[192,512]{1,0:T(8,128)(2,1)S(1)}, u32[]{:S(2)}, u32[]{:S(2)}) collective-permute-start(bf16[192,512]{1,0:T(8,128)(2,1)S(1)} %get-tuple-element.17), channel_id=1, source_target_pairs={{0,128},{4,132},{8,136},{12,140},{16,144},{20,148},{24,152},{28,15... | collective-permute-start | bytes 589832 | tf_op jit(solution)/shard_map/ppermute | solution.py:314
  47.6 9.7 %collective-permute-start.9 = (bf16[192,512]{1,0:T(8,128)(2,1)S(1)}, bf16[192,512]{1,0:T(8,128)(2,1)S(1)}, u32[]{:S(2)}, u32[]{:S(2)}) collective-permute-start(bf16[192,512]{1,0:T(8,128)(2,1)S(1)} %get-tuple-element.18), channel_id=1, source_target_pairs={{0,192},{4,196},{8,200},{12,204},{16,208},{20,212},{24,216},{28,22... | collective-permute-start | bytes 589832 | tf_op jit(solution)/shard_map/ppermute | solution.py:314
  57.3 7.2 %copy-start.7 = (f32[512]{0:T(512)S(1)}, f32[512]{0:T(512)}, u32[]{:S(2)}) copy-start(f32[512]{0:T(512)} %param.23) | copy-start | bytes 6148
  57.4 7.1 %collective-permute-start.14 = (bf16[384,512]{1,0:T(8,128)(2,1)S(1)}, bf16[384,512]{1,0:T(8,128)(2,1)S(1)}, u32[]{:S(2)}, u32[]{:S(2)}) collective-permute-start(bf16[384,512]{1,0:T(8,128)(2,1)S(1)} %crossing.3), channel_id=1, source_target_pairs={{0,4},{4,0},{8,12},{12,8},{16,20},{20,16},{24,28},{28,24},{32,36},... | collective-permute-start | bytes 1179656 | tf_op jit(solution)/shard_map/ppermute | solution.py:314
  64.5 20.5 %copy-start = (bf16[160,512]{1,0:T(8,128)(2,1)S(1)}, bf16[160,512]{1,0:T(8,128)(2,1)}, u32[]{:S(2)}) copy-start(bf16[160,512]{1,0:T(8,128)(2,1)} %nodes_ref.3) | copy-start | bytes 491524
  64.5 20.5 %copy-start.1 = (bf16[1024,512]{1,0:T(8,128)(2,1)S(1)}, bf16[1024,512]{1,0:T(8,128)(2,1)}, u32[]{:S(2)}) copy-start(bf16[1024,512]{1,0:T(8,128)(2,1)} %w1_ref.1) | copy-start | bytes 3145732
  64.5 20.5 %copy-start.3 = (bf16[512,512]{1,0:T(8,128)(2,1)S(1)}, bf16[512,512]{1,0:T(8,128)(2,1)}, u32[]{:S(2)}) copy-start(bf16[512,512]{1,0:T(8,128)(2,1)} %w2_ref.1) | copy-start | bytes 1572868
  64.5 20.5 %copy-start.5 = (f32[512]{0:T(512)S(1)}, f32[512]{0:T(512)}, u32[]{:S(2)}) copy-start(f32[512]{0:T(512)} %param.25) | copy-start | bytes 6148
  64.5 20.5 %copy-start.6 = (f32[512]{0:T(512)S(1)}, f32[512]{0:T(512)}, u32[]{:S(2)}) copy-start(f32[512]{0:T(512)} %param.27) | copy-start | bytes 6148
  71.0 9.4 %collective-permute-start.15 = (bf16[160,512]{1,0:T(8,128)(2,1)S(1)}, bf16[160,512]{1,0:T(8,128)(2,1)S(1)}, u32[]{:S(2)}, u32[]{:S(2)}) collective-permute-start(bf16[160,512]{1,0:T(8,128)(2,1)S(1)} %get-tuple-element.25), channel_id=1, source_target_pairs={{0,3},{1,0},{2,1},{3,2},{4,7},{5,4},{6,5},{7,6},{8,11},{9,8},{10,9... | collective-permute-start | bytes 491528 | tf_op jit(solution)/shard_map/ppermute | solution.py:391
  73.8 6.6 %collective-permute-start.16 = (bf16[160,512]{1,0:T(8,128)(2,1)S(1)}, bf16[160,512]{1,0:T(8,128)(2,1)S(1)}, u32[]{:S(2)}, u32[]{:S(2)}) collective-permute-start(bf16[160,512]{1,0:T(8,128)(2,1)S(1)} %get-tuple-element.26), channel_id=1, source_target_pairs={{0,2},{1,3},{2,0},{3,1},{4,6},{5,7},{6,4},{7,5},{8,10},{9,11},{10,... | collective-permute-start | bytes 491528 | tf_op jit(solution)/shard_map/ppermute | solution.py:391
  74.2 10.8 %collective-permute-start.17 = (bf16[160,512]{1,0:T(8,128)(2,1)S(1)}, bf16[160,512]{1,0:T(8,128)(2,1)S(1)}, u32[]{:S(2)}, u32[]{:S(2)}) collective-permute-start(bf16[160,512]{1,0:T(8,128)(2,1)S(1)} %get-tuple-element.27), channel_id=1, source_target_pairs={{0,1},{1,2},{2,3},{3,0},{4,5},{5,6},{6,7},{7,4},{8,9},{9,10},{10,1... | collective-permute-start | bytes 491528 | tf_op jit(solution)/shard_map/ppermute | solution.py:391
Sparse Core Ops, SparseCore 0:
  10.4 30.0 all-gather.1

commit v6 on v5

--- a/solution.py
+++ b/solution.py
@@ -14,6 +14,7 @@
 VMEM = pl.BlockSpec(memory_space=pltpu.VMEM)
 SMEM = pl.BlockSpec(memory_space=pltpu.SMEM)
 HBM = pl.BlockSpec(memory_space=pltpu.HBM)
+ANY = pl.BlockSpec(memory_space=pl.ANY)
 X, Z, C = 4, 8, 2
 TAIL = 16
 COST = 1 << 20
@@ -87,13 +88,22 @@
     )(me, lists, nodes)
 
 
-def select_kernel(pairs, cap, *refs):
-    blocks, outs = refs[: 2 * len(pairs)], refs[2 * len(pairs) :]
+def select_kernel(pairs, cap, extra, *refs):
+    count = 2 * len(pairs)
+    blocks, outs = list(refs[:count]), refs[count + extra : count + extra + X]
+    own = pairs[0][0] == 0
+    if own:
+        held, sem = refs[count + extra + X :]
+        fetch = pltpu.make_async_copy(blocks[0], held, sem)
+        fetch.start()
+        blocks[0] = held
     rows = blocks[0].shape[0] - TAIL
     lanes = X * C * 2 * cap
-    for at, pair in enumerate(pairs):
+    for at in reversed(range(len(pairs))):
         total = None
-        for side, dz in enumerate(pair):
+        for side, dz in reversed(list(enumerate(pairs[at]))):
+            if dz == 0:
+                fetch.wait()
             block = blocks[2 * at + side]
             wanted = block[rows:].astype(f32)[dz : dz + 1, :lanes].astype(i32)
             part = dot_first(hot_columns(wanted, rows), block[:rows])
@@ -107,18 +117,22 @@
                 outs[k][put : put + size] = total[first : first + size]
 
 
-def select(pairs, cap, blocks):
+def select(pairs, cap, blocks, *earlier):
     latent = blocks[0].shape[1]
     shape = jax.ShapeDtypeStruct((C * len(pairs) * 2 * cap, latent), bf16)
-    rows = blocks[0].shape[0]
-    return pl.pallas_call(
-        lambda *refs: select_kernel(pairs, cap, *refs),
-        in_specs=[VMEM] * len(blocks),
+    own = pairs[0][0] == 0
+    blocks = list(blocks)
+    if own:
+        blocks[0] = in_hbm(blocks[0])
+    return pl.pallas_call(
+        lambda *refs: select_kernel(pairs, cap, len(earlier), *refs),
+        in_specs=[HBM if own else VMEM] + [VMEM] * (len(blocks) - 1) + [ANY] * len(earlier),
         out_shape=[shape] * X,
+        scratch_shapes=[pltpu.VMEM(blocks[0].shape, bf16), pltpu.SemaphoreType.DMA] if own else [],
         compiler_params=pltpu.CompilerParams(vmem_limit_bytes=LIMIT),
         cost_estimate=pl.CostEstimate(flops=COST, bytes_accessed=0, transcendentals=0),
         name="select",
-    )(*blocks)
+    )(*blocks, *earlier)
 
 
 def cross_kernel(*refs):
@@ -147,31 +161,28 @@
     table_ref[put : put + X * size] = group[X][...]
 
 
-def before_kernel(*refs):
+def before_kernel(extra, *refs):
     recv_ref, send_ref, b1_ref = refs[:3]
-    group = refs[3 : 4 + X]
-    patch_hbm, edges_hbm, w1_hbm, out_hbm = refs[4 + X : 8 + X]
-    patch_ref, table_ref, edges_ref, w1_ref, out_ref, sems = refs[8 + X :]
-    fetch = pltpu.make_async_copy(patch_hbm, patch_ref, sems.at[2 + TILES])
-    fetch.start()
+    parts = refs[3:7]
+    edges_hbm, w1_hbm = refs[7:9]
+    out_hbm, table_ref, edges_ref, w1_ref, out_ref, sems = refs[9 + extra :]
     loads = [
-        pltpu.make_async_copy(edges_hbm, edges_ref, sems.at[0]),
-        pltpu.make_async_copy(w1_hbm, w1_ref, sems.at[1]),
+        pltpu.make_async_copy(w1_hbm, w1_ref, sems.at[0]),
+        pltpu.make_async_copy(edges_hbm, edges_ref, sems.at[1]),
     ]
     for load in loads:
         load.start()
     count, latent = edges_ref.shape
-    nodes = patch_ref.shape[0]
+    size = parts[0].shape[0]
+    nodes = table_ref.shape[0]
     tile = count // TILES
-    fill(table_ref, nodes, group)
-    fetch.wait()
-    table_ref[:nodes] = patch_ref[...].astype(bf16)
+    for k, part in enumerate(parts):
+        table_ref[k * size : (k + 1) * size] = part[...]
     stores = []
     for at in range(TILES):
         rows = slice(at * tile, (at + 1) * tile)
-        own = dot_first(hot_columns(recv_ref[:, rows], nodes), table_ref[:nodes]).astype(bf16)
-        hot = hot_columns(send_ref[:, rows], table_ref.shape[0])
-        near = dot_first(hot, table_ref[...]).astype(bf16)
+        own = dot_first(hot_columns(recv_ref[:, rows], nodes), table_ref[...]).astype(bf16)
+        near = dot_first(hot_columns(send_ref[:, rows], nodes), table_ref[...]).astype(bf16)
         if at == 0:
             for load in loads:
                 load.wait()
@@ -186,34 +197,33 @@
         store.wait()
 
 
-def edge_before(patch_rows, recv, send, b1, group, edges, w1):
+def edge_before(recv, send, b1, parts, edges, w1, *earlier):
     count, latent = edges.shape
-    table = patch_rows.shape[0] + sum(part.shape[0] for part in group[:X]) // C + group[X].shape[0]
-    return pl.pallas_call(
-        before_kernel,
-        in_specs=[VMEM] * (4 + X) + [HBM] * 3,
+    nodes = sum(part.shape[0] for part in parts)
+    return pl.pallas_call(
+        lambda *refs: before_kernel(len(earlier), *refs),
+        in_specs=[VMEM] * 7 + [HBM] * 2 + [ANY] * len(earlier),
         out_specs=HBM,
         out_shape=pltpu.HBM((count, latent), f32),
         scratch_shapes=[
-            pltpu.VMEM(patch_rows.shape, f32),
-            pltpu.VMEM((table, latent), bf16),
+            pltpu.VMEM((nodes, latent), bf16),
             pltpu.VMEM((count, latent), bf16),
             pltpu.VMEM(w1.shape, bf16),
             pltpu.VMEM((count, latent), f32),
-            pltpu.SemaphoreType.DMA((3 + TILES,)),
+            pltpu.SemaphoreType.DMA((2 + TILES,)),
         ],
         compiler_params=pltpu.CompilerParams(vmem_limit_bytes=32 << 20),
         cost_estimate=pl.CostEstimate(flops=COST, bytes_accessed=0, transcendentals=0),
         name="edge_before",
-    )(recv, send, b1, *group, in_hbm(patch_rows), in_hbm(edges), in_hbm(w1))
+    )(recv, send, b1, *parts, in_hbm(edges), in_hbm(w1), *earlier)
 
 
 def after_kernel(first_row, *refs):
     live_ref, send_ref, recv_ref, gain_ref = refs[:4]
-    group = refs[4 : 5 + X]
-    before_hbm, w1_hbm, w2_hbm, edges_hbm, out_hbm = refs[5 + X : 10 + X]
-    sums_refs = refs[10 + X : 14 + X]
-    table_ref, before_ref, w1_ref, w2_ref, edges_ref, far_ref, load_sems, store_sems = refs[14 + X :]
+    groups, refs = refs[4 : 6 + 2 * X], refs[6 + 2 * X :]
+    before_hbm, w1_hbm, w2_hbm, edges_hbm, out_hbm = refs[:5]
+    sums_refs = refs[5:9]
+    table_ref, before_ref, w1_ref, w2_ref, edges_ref, far_ref, load_sems, store_sems = refs[9:]
     count, latent = edges_ref.shape
     tile = count // TILES
     loads = [
@@ -224,7 +234,8 @@
     ]
     for load in loads:
         load.start()
-    fill(table_ref, 0, group)
+    fill(table_ref, 0, groups[: X + 1])
+    fill(table_ref, table_ref.shape[0] // 2, groups[X + 1 :])
     stores = []
     live = live_ref[0]
     hot = hot_columns(send_ref[...], table_ref.shape[0], first_row)
@@ -256,10 +267,10 @@
 
 def edge_after(first_row, live, send, recv, gain, group, before, w1, w2, edges, rows):
     count, latent = edges.shape
-    table = sum(part.shape[0] for part in group[:X]) // C + group[X].shape[0]
+    table = 2 * X * group[0].shape[0]
     return pl.pallas_call(
         lambda *refs: after_kernel(first_row, *refs),
-        in_specs=[SMEM] + [VMEM] * (4 + X) + [HBM] * 4,
+        in_specs=[SMEM] + [VMEM] * (5 + 2 * X) + [HBM] * 4,
         out_specs=[HBM] + [VMEM] * 4,
         out_shape=[jax.ShapeDtypeStruct((count, latent), bf16)]
         + [jax.ShapeDtypeStruct((rows, latent), f32 if k == 0 else bf16) for k in range(4)],
@@ -338,7 +349,9 @@
     feat = lax.axis_size("feat")
 
     block = pack(me.reshape(1), send_rows[0, 0].T, nodes)
-    patch_rows = lax.all_gather(nodes.astype(f32), "feat", axis=0, tiled=True)
+    parts = [nodes]
+    for k in range(1, feat):
+        parts.append(lax.ppermute(nodes, "feat", [(i, (i + k) % feat) for i in range(feat)]))
     up = lambda a: moved(a, lambda x, z, c: (x, z + 1, c))
     down = lambda a: moved(a, lambda x, z, c: (x, z - 1, c))
     held = {0: block}
@@ -350,7 +363,8 @@
 
     groups = []
     for pairs in BATCHES:
-        picked = select(pairs, cap, [held[dz] for pair in pairs for dz in pair])
+        earlier = parts[1:] if pairs is BATCHES[0] else []
+        picked = select(pairs, cap, [held[dz] for pair in pairs for dz in pair], *earlier)
         group = [picked[0]]
         for k in range(1, X):
             group.append(moved(picked[k], lambda x, z, c: (x + k, z, c)))
@@ -376,15 +390,16 @@
                 here = base + (s * X + k) * size + at * 2 * cap + side * cap
                 place = jnp.where(dz == value, here, place)
         base += X * C * len(pairs) * 2 * cap
-    send = jnp.where(sender_slot < patch, sender_slot, patch + place + entry).reshape(1, -1)
-    first_row = patch + len(BATCHES[0]) * 2 * cap * X * C
+    send = jnp.where(sender_slot < patch, near_row(sender_slot), patch + place + entry)
+    send = send.reshape(1, -1)
+    recv = near_row(receivers).reshape(1, -1)
     before = edge_before(
-        patch_rows, receivers.reshape(1, -1), send, edge_b1.reshape(1, -1), groups[0], edges, edge_w1
+        recv, send, edge_b1.reshape(1, -1), parts, edges, edge_w1, groups[1][0]
     )
     groups[1].append(swap(crossing(groups[1], before)))
     edges_out, *sums = edge_after(
-        first_row, live_edges, send, near_row(receivers).reshape(1, -1), edge_gain.reshape(1, -1),
-        groups[1], before, edge_w1, edge_w2, edges, rows,
+        patch, live_edges, send, recv, edge_gain.reshape(1, -1), groups[0] + groups[1], before,
+        edge_w1, edge_w2, edges, rows,
     )
     parts = [sums[0]]
     for k in range(1, feat):

time: 93.5 us -> 82.3 us (0.88)
  between operations: 14.9 us -> 1.47 us
  waiting for transfers between devices: 24.6 us -> 29.6 us
  other arithmetic: 1.74 us -> 0.06 us
    ppermute x0 -> x3, waiting for transfers between devices: none -> 9 us  [local(): lax.ppermute(nodes, 'feat', [(i, (i + k) % feat) for i in range(feat)])]
    ppermute x15, waiting for transfers between devices: 14.5 us -> 10.5 us  [moved(): return lax.ppermute(value, 'patch', pairs_of(move))]
    ppermute x0 -> x3, starting transfers between devices: none -> 3.78 us  [local(): lax.ppermute(nodes, 'feat', [(i, (i + k) % feat) for i in range(feat)])]
    ppermute x3, starting transfers between devices: 3.85 us -> 1.55 us  [local(): lax.ppermute(sums[k], 'feat', [(i, (i - k) % feat) for i in range(feat)])]
    ppermute x15, starting transfers between devices: 28.2 us -> 26.1 us  [moved(): return lax.ppermute(value, 'patch', pairs_of(move))]
    convert_element_type x1 -> x0, other arithmetic: 1.68 us -> none  [local(): patch_rows = lax.all_gather(nodes.astype(f32), 'feat', axis=0, tiled=True)]
    pallas_call x1, Pallas kernels: 6.5 us -> 7.49 us  [edge_after(): pl.pallas_call(lambda *refs: after_kernel(first_row, *refs), in_specs=[SM...]
  transfers between devices with their start and end apart: 19 -> 21, of which waited for: 7 -> 10; matrix products, arithmetic and copies ran while one was open for 0% -> 0% of each run, Pallas kernels for 12% -> 11%
where the time goes in v6:
time: 82.3 us; the launch traced here: 82.2 us
  starting transfers between devices  31.4 us (38%)
  waiting for transfers between devices  29.6 us (36%)
  Pallas kernels  19.6 us (24%)
  between operations  1.47 us (2%)
    ppermute x15, starting transfers between devices, moved(): return lax.ppermute(value, 'patch', pairs_of(move))  26.1 us
    ppermute x15, waiting for transfers between devices, moved(): return lax.ppermute(value, 'patch', pairs_of(move))  10.5 us
    ppermute x3, waiting for transfers between devices, local(): lax.ppermute(sums[k], 'feat', [(i, (i - k) % feat) for i in range(feat)])  10 us
    ppermute x3, waiting for transfers between devices, local(): lax.ppermute(nodes, 'feat', [(i, (i + k) % feat) for i in range(feat)])  9 us
    pallas_call x1, Pallas kernels, edge_after(): pl.pallas_call(lambda *refs: after_kernel(first_row, *refs), in_specs=[SM...  7.49 us
    pallas_call x1, Pallas kernels, edge_before(): pl.pallas_call(lambda *refs: before_kernel(len(earlier), *refs), in_specs...  6.73 us
    ppermute x3, starting transfers between devices, local(): lax.ppermute(nodes, 'feat', [(i, (i + k) % feat) for i in range(feat)])  3.78 us
    pallas_call x2, Pallas kernels, select(): pl.pallas_call(lambda *refs: select_kernel(pairs, cap, len(earlier), *ref...  1.94 us
  transfers between devices with their start and end apart: 21, of which 10 were waited for; matrix products, arithmetic and copies ran while one was open for 0% of the time, Pallas kernels for 11%

profile of v6, /device:TPU:1, one launch (start us, length us, event | category | flops | bytes accessed | tf_op | source)
XLA Modules:
  0.0 82.2 jit_solution(11420056871441294355)
XLA Ops:
  0.6 0.0 copy-start.7
  0.6 0.0 copy-start.8
  0.7 1.9 %pack.1.refs_0_ = bf16[176,512]{1,0:T(8,128)(2,1)} custom-call(s32[1]{0:T(128)} %bitcast.1.where_ref, s32[24,64]{1,0:T(8,128)} %bitcast.12, bf16[160,512]{1,0:T(8,128)(2,1)} %nodes_ref.3), custom_call_target="tpu_custom_call" | custom-call | tf_op jit(solution)/shard_map/pack/pallas_call | solution.py:83
  2.6 0.0 copy-start
  2.6 0.0 copy-start.3
  2.6 2.5 %collective-permute-start = (bf16[176,512]{1,0:T(8,128)(2,1)}, bf16[176,512]{1,0:T(8,128)(2,1)S(1)}, u32[]{:S(2)}, u32[]{:S(2)}) collective-permute-start(bf16[176,512]{1,0:T(8,128)(2,1)} %pack.1.refs_0_), channel_id=1, source_target_pairs={{0,8},{4,12},{8,16},{12,20},{16,24},{20,28},{24,32},{28,36},{32,40... | collective-permute-start | bytes 540680 | tf_op jit(solution)/shard_map/ppermute | solution.py:325
  5.1 4.0 %collective-permute-start.1 = (bf16[176,512]{1,0:T(8,128)(2,1)}, bf16[176,512]{1,0:T(8,128)(2,1)S(1)}, u32[]{:S(2)}, u32[]{:S(2)}) collective-permute-start(bf16[176,512]{1,0:T(8,128)(2,1)} %pack.1.refs_0_), channel_id=1, source_target_pairs={{0,56},{4,60},{8,0},{12,4},{16,8},{20,12},{24,16},{28,20},{32,24},... | collective-permute-start | bytes 540680 | tf_op jit(solution)/shard_map/ppermute | solution.py:325
  9.1 4.4 %collective-permute-done.refs_1_ = bf16[176,512]{1,0:T(8,128)(2,1)S(1)} collective-permute-done((bf16[176,512]{1,0:T(8,128)(2,1)}, bf16[176,512]{1,0:T(8,128)(2,1)S(1)}, u32[]{:S(2)}, u32[]{:S(2)}) %collective-permute-start) | collective-permute-done | bytes 180256 | tf_op jit(solution)/shard_map/ppermute | solution.py:325
  13.5 0.0 collective-permute-start.2
  13.5 0.0 collective-permute-done.1.refs_2_
  13.5 2.7 %collective-permute-start.10 = (bf16[176,512]{1,0:T(8,128)(2,1)S(1)}, bf16[176,512]{1,0:T(8,128)(2,1)S(1)}, u32[]{:S(2)}, u32[]{:S(2)}) collective-permute-start(bf16[176,512]{1,0:T(8,128)(2,1)S(1)} %collective-permute-done.1.refs_2_), channel_id=1, source_target_pairs={{0,56},{4,60},{8,0},{12,4},{16,8},{20,12},{24,16},{28,20},{32,24},... | collective-permute-start | bytes 540680 | tf_op jit(solution)/shard_map/ppermute | solution.py:325
  16.2 3.3 %collective-permute-done.2.refs_3_ = bf16[176,512]{1,0:T(8,128)(2,1)S(1)} collective-permute-done((bf16[176,512]{1,0:T(8,128)(2,1)S(1)}, bf16[176,512]{1,0:T(8,128)(2,1)S(1)}, u32[]{:S(2)}, u32[]{:S(2)}) %collective-permute-start.2) | collective-permute-done | bytes 180256 | tf_op jit(solution)/shard_map/ppermute | solution.py:325
  19.5 0.0 collective-permute-start.11
  19.5 2.7 %collective-permute-start.5 = (bf16[160,512]{1,0:T(8,128)(2,1)}, bf16[160,512]{1,0:T(8,128)(2,1)S(1)}, u32[]{:S(2)}, u32[]{:S(2)}) collective-permute-start(bf16[160,512]{1,0:T(8,128)(2,1)} %nodes_ref.3), channel_id=1, source_target_pairs={{0,3},{1,0},{2,1},{3,2},{4,7},{5,4},{6,5},{7,6},{8,11},{9,8},{10,9... | collective-permute-start | bytes 491528 | tf_op jit(solution)/shard_map/ppermute | solution.py:354
  22.2 0.3 collective-permute-start.4
  22.6 0.7 collective-permute-start.3
  23.3 2.7 %collective-permute-done.5.refs_6_ = bf16[160,512]{1,0:T(8,128)(2,1)S(1)} collective-permute-done((bf16[160,512]{1,0:T(8,128)(2,1)}, bf16[160,512]{1,0:T(8,128)(2,1)S(1)}, u32[]{:S(2)}, u32[]{:S(2)}) %collective-permute-start.5) | collective-permute-done | bytes 163872 | tf_op jit(solution)/shard_map/ppermute | solution.py:354
  26.0 2.3 %collective-permute-done.4.refs_5_ = bf16[160,512]{1,0:T(8,128)(2,1)S(1)} collective-permute-done((bf16[160,512]{1,0:T(8,128)(2,1)}, bf16[160,512]{1,0:T(8,128)(2,1)S(1)}, u32[]{:S(2)}, u32[]{:S(2)}) %collective-permute-start.4) | collective-permute-done | bytes 163872 | tf_op jit(solution)/shard_map/ppermute | solution.py:354
  28.2 4.1 %collective-permute-done.3.refs_4_ = bf16[160,512]{1,0:T(8,128)(2,1)S(1)} collective-permute-done((bf16[160,512]{1,0:T(8,128)(2,1)}, bf16[160,512]{1,0:T(8,128)(2,1)S(1)}, u32[]{:S(2)}, u32[]{:S(2)}) %collective-permute-start.3) | collective-permute-done | bytes 163872 | tf_op jit(solution)/shard_map/ppermute | solution.py:354
  32.3 1.3 %select.24 = (bf16[192,512]{1,0:T(8,128)(2,1)S(1)}, bf16[192,512]{1,0:T(8,128)(2,1)S(1)}, bf16[192,512]{1,0:T(8,128)(2,1)S(1)}, bf16[192,512]{1,0:T(8,128)(2,1)S(1)}) custom-call(bf16[176,512]{1,0:T(8,128)(2,1)} %pack.1.refs_0_, bf16[176,512]{1,0:T(8,128)(2,1)S(1)} %collective-permute-done.refs_1_, bf16[176,512]{1,0:T(8,128)(2,1)S(1)} %collective-permute-done.1.refs_2_, ...), custom_call_target="tpu_custom_call" | custom-call | flops 1048576 | tf_op jit(solution)/shard_map/select/pallas_call | solution.py:127
  33.6 1.3 %collective-permute-start.6 = (bf16[192,512]{1,0:T(8,128)(2,1)S(1)}, bf16[192,512]{1,0:T(8,128)(2,1)S(1)}, u32[]{:S(2)}, u32[]{:S(2)}) collective-permute-start(bf16[192,512]{1,0:T(8,128)(2,1)S(1)} %get-tuple-element.16), channel_id=1, source_target_pairs={{0,64},{4,68},{8,72},{12,76},{16,80},{20,84},{24,88},{28,92},{32,9... | collective-permute-start | bytes 589832 | tf_op jit(solution)/shard_map/ppermute | solution.py:325
  34.9 0.0 collective-permute-done.10.refs_0_
  34.9 0.9 %collective-permute-start.12 = (bf16[176,512]{1,0:T(8,128)(2,1)S(1)}, bf16[176,512]{1,0:T(8,128)(2,1)S(1)}, u32[]{:S(2)}, u32[]{:S(2)}) collective-permute-start(bf16[176,512]{1,0:T(8,128)(2,1)S(1)} %collective-permute-done.10.refs_0_), channel_id=1, source_target_pairs={{0,56},{4,60},{8,0},{12,4},{16,8},{20,12},{24,16},{28,20},{32,24},... | collective-permute-start | bytes 540680 | tf_op jit(solution)/shard_map/ppermute | solution.py:325
  35.9 0.0 collective-permute-done.11.refs_1_
  35.9 0.5 collective-permute-start.13
  36.4 2.5 %collective-permute-start.7 = (bf16[192,512]{1,0:T(8,128)(2,1)S(1)}, bf16[192,512]{1,0:T(8,128)(2,1)S(1)}, u32[]{:S(2)}, u32[]{:S(2)}) collective-permute-start(bf16[192,512]{1,0:T(8,128)(2,1)S(1)} %get-tuple-element.17), channel_id=1, source_target_pairs={{0,128},{4,132},{8,136},{12,140},{16,144},{20,148},{24,152},{28,15... | collective-permute-start | bytes 589832 | tf_op jit(solution)/shard_map/ppermute | solution.py:325
  38.8 1.2 %collective-permute-start.8 = (bf16[192,512]{1,0:T(8,128)(2,1)S(1)}, bf16[192,512]{1,0:T(8,128)(2,1)S(1)}, u32[]{:S(2)}, u32[]{:S(2)}) collective-permute-start(bf16[192,512]{1,0:T(8,128)(2,1)S(1)} %get-tuple-element.18), channel_id=1, source_target_pairs={{0,192},{4,196},{8,200},{12,204},{16,208},{20,212},{24,216},{28,22... | collective-permute-start | bytes 589832 | tf_op jit(solution)/shard_map/ppermute | solution.py:325
  40.0 0.0 collective-permute-done.12.refs_2_
  40.0 1.7 %collective-permute-done.13.refs_3_ = bf16[176,512]{1,0:T(8,128)(2,1)S(1)} collective-permute-done((bf16[176,512]{1,0:T(8,128)(2,1)S(1)}, bf16[176,512]{1,0:T(8,128)(2,1)S(1)}, u32[]{:S(2)}, u32[]{:S(2)}) %collective-permute-start.13) | collective-permute-done | bytes 180256 | tf_op jit(solution)/shard_map/ppermute | solution.py:325
  41.7 0.6 select.25
  42.3 1.0 %collective-permute-start.14 = (bf16[192,512]{1,0:T(8,128)(2,1)S(1)}, bf16[192,512]{1,0:T(8,128)(2,1)S(1)}, u32[]{:S(2)}, u32[]{:S(2)}) collective-permute-start(bf16[192,512]{1,0:T(8,128)(2,1)S(1)} %get-tuple-element.20), channel_id=1, source_target_pairs={{0,64},{4,68},{8,72},{12,76},{16,80},{20,84},{24,88},{28,92},{32,9... | collective-permute-start | bytes 589832 | tf_op jit(solution)/shard_map/ppermute | solution.py:325
  43.3 1.4 %collective-permute-start.15 = (bf16[192,512]{1,0:T(8,128)(2,1)S(1)}, bf16[192,512]{1,0:T(8,128)(2,1)S(1)}, u32[]{:S(2)}, u32[]{:S(2)}) collective-permute-start(bf16[192,512]{1,0:T(8,128)(2,1)S(1)} %get-tuple-element.21), channel_id=1, source_target_pairs={{0,128},{4,132},{8,136},{12,140},{16,144},{20,148},{24,152},{28,15... | collective-permute-start | bytes 589832 | tf_op jit(solution)/shard_map/ppermute | solution.py:325
  44.8 0.0 collective-permute-done.6.refs_1_.refs_5_
  44.8 1.9 %collective-permute-start.16 = (bf16[192,512]{1,0:T(8,128)(2,1)S(1)}, bf16[192,512]{1,0:T(8,128)(2,1)S(1)}, u32[]{:S(2)}, u32[]{:S(2)}) collective-permute-start(bf16[192,512]{1,0:T(8,128)(2,1)S(1)} %get-tuple-element.22), channel_id=1, source_target_pairs={{0,192},{4,196},{8,200},{12,204},{16,208},{20,212},{24,216},{28,22... | collective-permute-start | bytes 589832 | tf_op jit(solution)/shard_map/ppermute | solution.py:325
  46.6 0.0 copy-done.7
  46.6 0.0 copy-done.8
  46.6 0.1 fusion.4
  46.7 0.0 collective-permute-done.7.refs_2_.refs_6_
  46.7 0.0 collective-permute-done.8.refs_3_.refs_7_
  46.8 6.2 %collective-permute-start.9 = (bf16[384,512]{1,0:T(8,128)(2,1)S(1)}, bf16[384,512]{1,0:T(8,128)(2,1)S(1)}, u32[]{:S(2)}, u32[]{:S(2)}) collective-permute-start(bf16[384,512]{1,0:T(8,128)(2,1)S(1)} %crossing.2), channel_id=1, source_target_pairs={{0,4},{4,0},{8,12},{12,8},{16,20},{20,16},{24,28},{28,24},{32,36},... | collective-permute-start | bytes 1179656 | tf_op jit(solution)/shard_map/ppermute | solution.py:325
  53.0 0.0 copy-done
  53.0 0.0 copy-done.3
  53.0 6.7 %edge_before.1.refs_4_.refs_14_ = f32[1280,512]{1,0:T(8,128)} custom-call(s32[1,1280]{1,0:T(1,128)S(1)} %reshape.26.refs_0_.refs_2_, s32[1,1280]{1,0:T(1,128)S(1)} %reshape.25.refs_1_, f32[1,512]{1,0:T(1,128)S(1)} %bitcast.8, bf16[160,512]{1,0:T(8,128)(2,1)S(1)} %copy-done, bf16[160,512]{1,0:T(8,128)(2,1)S(1)} %collective-permute-done.3.refs_4_, ...), custom_call_target="tpu_custom_call" | custom-call | flops 1048576 | tf_op jit(solution)/shard_map/edge_before/pallas_call | solution.py:203
  59.7 0.0 copy-start.4
  59.7 0.0 collective-permute-done.14.refs_1_.refs_10_
  59.7 0.0 collective-permute-done.15.refs_2_.refs_11_
  59.7 0.0 collective-permute-done.16.refs_3_.refs_12_
  59.8 0.1 collective-permute-start.17
  60.6 0.0 collective-permute-done.9.refs_8_
  60.6 1.0 %collective-permute-done.17.refs_13_ = bf16[384,512]{1,0:T(8,128)(2,1)S(1)} collective-permute-done((bf16[384,512]{1,0:T(8,128)(2,1)S(1)}, bf16[384,512]{1,0:T(8,128)(2,1)S(1)}, u32[]{:S(2)}, u32[]{:S(2)}) %collective-permute-start.17) | collective-permute-done | bytes 393248 | tf_op jit(solution)/shard_map/ppermute | solution.py:325
  61.6 0.0 copy-done.4
  61.6 0.0 copy-start.6
  61.6 7.5 %edge_after.1 = (bf16[1280,512]{1,0:T(8,128)(2,1)}, f32[160,512]{1,0:T(8,128)S(1)}, bf16[160,512]{1,0:T(8,128)(2,1)S(1)}, bf16[160,512]{1,0:T(8,128)(2,1)S(1)}, bf16[160,512]{1,0:T(8,128)(2,1)S(1)}) custom-call(s32[1]{0:T(128)S(6)} %copy.16.refs_0_, s32[1,1280]{1,0:T(1,128)S(1)} %reshape.25.refs_1_, s32[1,1280]{1,0:T(1,128)S(1)} %reshape.26.refs_0_.refs_2_, ...), custom_call_target="tpu_custom_call" | custom-call | tf_op jit(solution)/shard_map/edge_after/pallas_call | solution.py:271
  69.1 0.4 collective-permute-start.18
  69.6 0.3 collective-permute-start.19
  69.8 0.8 %collective-permute-start.20 = (bf16[160,512]{1,0:T(8,128)(2,1)S(1)}, bf16[160,512]{1,0:T(8,128)(2,1)S(1)}, u32[]{:S(2)}, u32[]{:S(2)}) collective-permute-start(bf16[160,512]{1,0:T(8,128)(2,1)S(1)} %get-tuple-element.27), channel_id=1, source_target_pairs={{0,1},{1,2},{2,3},{3,0},{4,5},{5,6},{6,7},{7,4},{8,9},{9,10},{10,1... | collective-permute-start | bytes 491528 | tf_op jit(solution)/shard_map/ppermute | solution.py:406
  70.7 4.2 %collective-permute-done.18.p1_ref = bf16[160,512]{1,0:T(8,128)(2,1)S(1)} collective-permute-done((bf16[160,512]{1,0:T(8,128)(2,1)S(1)}, bf16[160,512]{1,0:T(8,128)(2,1)S(1)}, u32[]{:S(2)}, u32[]{:S(2)}) %collective-permute-start.18) | collective-permute-done | bytes 163872 | tf_op jit(solution)/shard_map/ppermute | solution.py:406
  74.9 1.6 %collective-permute-done.19.p2_ref = bf16[160,512]{1,0:T(8,128)(2,1)S(1)} collective-permute-done((bf16[160,512]{1,0:T(8,128)(2,1)S(1)}, bf16[160,512]{1,0:T(8,128)(2,1)S(1)}, u32[]{:S(2)}, u32[]{:S(2)}) %collective-permute-start.19) | collective-permute-done | bytes 163872 | tf_op jit(solution)/shard_map/ppermute | solution.py:406
  76.4 4.3 %collective-permute-done.20.p3_ref = bf16[160,512]{1,0:T(8,128)(2,1)S(1)} collective-permute-done((bf16[160,512]{1,0:T(8,128)(2,1)S(1)}, bf16[160,512]{1,0:T(8,128)(2,1)S(1)}, u32[]{:S(2)}, u32[]{:S(2)}) %collective-permute-start.20) | collective-permute-done | bytes 163872 | tf_op jit(solution)/shard_map/ppermute | solution.py:406
  80.7 0.0 copy-done.1
  80.7 0.0 copy-done.2
  80.7 0.0 copy-done.5
  80.7 0.0 copy-done.6
  80.7 1.5 %node_update.1 = bf16[160,512]{1,0:T(8,128)(2,1)} custom-call(bf16[160,512]{1,0:T(8,128)(2,1)S(1)} %copy-done, f32[160,512]{1,0:T(8,128)S(1)} %get-tuple-element.24.p0_ref, bf16[160,512]{1,0:T(8,128)(2,1)S(1)} %collective-permute-done.18.p1_ref, bf16[160,512]{1,0:T(8,128)(2,1)S(1)} %collective-permute-done.19.p2_ref, ...), custom_call_target="tpu_custom_call" | custom-call | tf_op jit(solution)/shard_map/node_update/pallas_call | solution.py:305
  (7 shorter events, 0.1 us)
Async XLA Ops:
  0.6 46.0 %copy-start.7 = (s32[1280]{0:T(1024)S(1)}, s32[1280]{0:T(1024)}, u32[]{:S(2)}) copy-start(s32[1280]{0:T(1024)} %param.17) | copy-start | bytes 15364
  0.6 46.0 %copy-start.8 = (s32[1280]{0:T(1024)S(1)}, s32[1280]{0:T(1024)}, u32[]{:S(2)}) copy-start(s32[1280]{0:T(1024)} %param.16) | copy-start | bytes 15364
  2.6 50.4 %copy-start = (bf16[160,512]{1,0:T(8,128)(2,1)S(1)}, bf16[160,512]{1,0:T(8,128)(2,1)}, u32[]{:S(2)}) copy-start(bf16[160,512]{1,0:T(8,128)(2,1)} %nodes_ref.3) | copy-start | bytes 491524
  2.6 50.4 %copy-start.3 = (f32[512]{0:T(512)S(1)}, f32[512]{0:T(512)}, u32[]{:S(2)}) copy-start(f32[512]{0:T(512)} %param.21) | copy-start | bytes 6148
  2.6 10.9 %collective-permute-start = (bf16[176,512]{1,0:T(8,128)(2,1)}, bf16[176,512]{1,0:T(8,128)(2,1)S(1)}, u32[]{:S(2)}, u32[]{:S(2)}) collective-permute-start(bf16[176,512]{1,0:T(8,128)(2,1)} %pack.1.refs_0_), channel_id=1, source_target_pairs={{0,8},{4,12},{8,16},{12,20},{16,24},{20,28},{24,32},{28,36},{32,40... | collective-permute-start | bytes 540680 | tf_op jit(solution)/shard_map/ppermute | solution.py:325
  5.1 8.4 %collective-permute-start.1 = (bf16[176,512]{1,0:T(8,128)(2,1)}, bf16[176,512]{1,0:T(8,128)(2,1)S(1)}, u32[]{:S(2)}, u32[]{:S(2)}) collective-permute-start(bf16[176,512]{1,0:T(8,128)(2,1)} %pack.1.refs_0_), channel_id=1, source_target_pairs={{0,56},{4,60},{8,0},{12,4},{16,8},{20,12},{24,16},{28,20},{32,24},... | collective-permute-start | bytes 540680 | tf_op jit(solution)/shard_map/ppermute | solution.py:325
  13.5 6.0 %collective-permute-start.2 = (bf16[176,512]{1,0:T(8,128)(2,1)S(1)}, bf16[176,512]{1,0:T(8,128)(2,1)S(1)}, u32[]{:S(2)}, u32[]{:S(2)}) collective-permute-start(bf16[176,512]{1,0:T(8,128)(2,1)S(1)} %collective-permute-done.refs_1_), channel_id=1, source_target_pairs={{0,8},{4,12},{8,16},{12,20},{16,24},{20,28},{24,32},{28,36},{32,40... | collective-permute-start | bytes 540680 | tf_op jit(solution)/shard_map/ppermute | solution.py:325
  13.5 21.4 %collective-permute-start.10 = (bf16[176,512]{1,0:T(8,128)(2,1)S(1)}, bf16[176,512]{1,0:T(8,128)(2,1)S(1)}, u32[]{:S(2)}, u32[]{:S(2)}) collective-permute-start(bf16[176,512]{1,0:T(8,128)(2,1)S(1)} %collective-permute-done.1.refs_2_), channel_id=1, source_target_pairs={{0,56},{4,60},{8,0},{12,4},{16,8},{20,12},{24,16},{28,20},{32,24},... | collective-permute-start | bytes 540680 | tf_op jit(solution)/shard_map/ppermute | solution.py:325
  19.5 16.4 %collective-permute-start.11 = (bf16[176,512]{1,0:T(8,128)(2,1)S(1)}, bf16[176,512]{1,0:T(8,128)(2,1)S(1)}, u32[]{:S(2)}, u32[]{:S(2)}) collective-permute-start(bf16[176,512]{1,0:T(8,128)(2,1)S(1)} %collective-permute-done.2.refs_3_), channel_id=1, source_target_pairs={{0,8},{4,12},{8,16},{12,20},{16,24},{20,28},{24,32},{28,36},{32,40... | collective-permute-start | bytes 540680 | tf_op jit(solution)/shard_map/ppermute | solution.py:325
  19.5 6.5 %collective-permute-start.5 = (bf16[160,512]{1,0:T(8,128)(2,1)}, bf16[160,512]{1,0:T(8,128)(2,1)S(1)}, u32[]{:S(2)}, u32[]{:S(2)}) collective-permute-start(bf16[160,512]{1,0:T(8,128)(2,1)} %nodes_ref.3), channel_id=1, source_target_pairs={{0,3},{1,0},{2,1},{3,2},{4,7},{5,4},{6,5},{7,6},{8,11},{9,8},{10,9... | collective-permute-start | bytes 491528 | tf_op jit(solution)/shard_map/ppermute | solution.py:354
  22.2 6.0 %collective-permute-start.4 = (bf16[160,512]{1,0:T(8,128)(2,1)}, bf16[160,512]{1,0:T(8,128)(2,1)S(1)}, u32[]{:S(2)}, u32[]{:S(2)}) collective-permute-start(bf16[160,512]{1,0:T(8,128)(2,1)} %nodes_ref.3), channel_id=1, source_target_pairs={{0,2},{1,3},{2,0},{3,1},{4,6},{5,7},{6,4},{7,5},{8,10},{9,11},{10,... | collective-permute-start | bytes 491528 | tf_op jit(solution)/shard_map/ppermute | solution.py:354
  22.6 9.7 %collective-permute-start.3 = (bf16[160,512]{1,0:T(8,128)(2,1)}, bf16[160,512]{1,0:T(8,128)(2,1)S(1)}, u32[]{:S(2)}, u32[]{:S(2)}) collective-permute-start(bf16[160,512]{1,0:T(8,128)(2,1)} %nodes_ref.3), channel_id=1, source_target_pairs={{0,1},{1,2},{2,3},{3,0},{4,5},{5,6},{6,7},{7,4},{8,9},{9,10},{10,1... | collective-permute-start | bytes 491528 | tf_op jit(solution)/shard_map/ppermute | solution.py:354
  33.6 11.1 %collective-permute-start.6 = (bf16[192,512]{1,0:T(8,128)(2,1)S(1)}, bf16[192,512]{1,0:T(8,128)(2,1)S(1)}, u32[]{:S(2)}, u32[]{:S(2)}) collective-permute-start(bf16[192,512]{1,0:T(8,128)(2,1)S(1)} %get-tuple-element.16), channel_id=1, source_target_pairs={{0,64},{4,68},{8,72},{12,76},{16,80},{20,84},{24,88},{28,92},{32,9... | collective-permute-start | bytes 589832 | tf_op jit(solution)/shard_map/ppermute | solution.py:325
  34.9 5.1 %collective-permute-start.12 = (bf16[176,512]{1,0:T(8,128)(2,1)S(1)}, bf16[176,512]{1,0:T(8,128)(2,1)S(1)}, u32[]{:S(2)}, u32[]{:S(2)}) collective-permute-start(bf16[176,512]{1,0:T(8,128)(2,1)S(1)} %collective-permute-done.10.refs_0_), channel_id=1, source_target_pairs={{0,56},{4,60},{8,0},{12,4},{16,8},{20,12},{24,16},{28,20},{32,24},... | collective-permute-start | bytes 540680 | tf_op jit(solution)/shard_map/ppermute | solution.py:325
  35.9 5.9 %collective-permute-start.13 = (bf16[176,512]{1,0:T(8,128)(2,1)S(1)}, bf16[176,512]{1,0:T(8,128)(2,1)S(1)}, u32[]{:S(2)}, u32[]{:S(2)}) collective-permute-start(bf16[176,512]{1,0:T(8,128)(2,1)S(1)} %collective-permute-done.11.refs_1_), channel_id=1, source_target_pairs={{0,8},{4,12},{8,16},{12,20},{16,24},{20,28},{24,32},{28,36},{32,40... | collective-permute-start | bytes 540680 | tf_op jit(solution)/shard_map/ppermute | solution.py:325
  36.4 10.3 %collective-permute-start.7 = (bf16[192,512]{1,0:T(8,128)(2,1)S(1)}, bf16[192,512]{1,0:T(8,128)(2,1)S(1)}, u32[]{:S(2)}, u32[]{:S(2)}) collective-permute-start(bf16[192,512]{1,0:T(8,128)(2,1)S(1)} %get-tuple-element.17), channel_id=1, source_target_pairs={{0,128},{4,132},{8,136},{12,140},{16,144},{20,148},{24,152},{28,15... | collective-permute-start | bytes 589832 | tf_op jit(solution)/shard_map/ppermute | solution.py:325
  38.8 7.9 %collective-permute-start.8 = (bf16[192,512]{1,0:T(8,128)(2,1)S(1)}, bf16[192,512]{1,0:T(8,128)(2,1)S(1)}, u32[]{:S(2)}, u32[]{:S(2)}) collective-permute-start(bf16[192,512]{1,0:T(8,128)(2,1)S(1)} %get-tuple-element.18), channel_id=1, source_target_pairs={{0,192},{4,196},{8,200},{12,204},{16,208},{20,212},{24,216},{28,22... | collective-permute-start | bytes 589832 | tf_op jit(solution)/shard_map/ppermute | solution.py:325
  42.3 17.4 %collective-permute-start.14 = (bf16[192,512]{1,0:T(8,128)(2,1)S(1)}, bf16[192,512]{1,0:T(8,128)(2,1)S(1)}, u32[]{:S(2)}, u32[]{:S(2)}) collective-permute-start(bf16[192,512]{1,0:T(8,128)(2,1)S(1)} %get-tuple-element.20), channel_id=1, source_target_pairs={{0,64},{4,68},{8,72},{12,76},{16,80},{20,84},{24,88},{28,92},{32,9... | collective-permute-start | bytes 589832 | tf_op jit(solution)/shard_map/ppermute | solution.py:325
  43.3 16.4 %collective-permute-start.15 = (bf16[192,512]{1,0:T(8,128)(2,1)S(1)}, bf16[192,512]{1,0:T(8,128)(2,1)S(1)}, u32[]{:S(2)}, u32[]{:S(2)}) collective-permute-start(bf16[192,512]{1,0:T(8,128)(2,1)S(1)} %get-tuple-element.21), channel_id=1, source_target_pairs={{0,128},{4,132},{8,136},{12,140},{16,144},{20,148},{24,152},{28,15... | collective-permute-start | bytes 589832 | tf_op jit(solution)/shard_map/ppermute | solution.py:325
  44.8 15.0 %collective-permute-start.16 = (bf16[192,512]{1,0:T(8,128)(2,1)S(1)}, bf16[192,512]{1,0:T(8,128)(2,1)S(1)}, u32[]{:S(2)}, u32[]{:S(2)}) collective-permute-start(bf16[192,512]{1,0:T(8,128)(2,1)S(1)} %get-tuple-element.22), channel_id=1, source_target_pairs={{0,192},{4,196},{8,200},{12,204},{16,208},{20,212},{24,216},{28,22... | collective-permute-start | bytes 589832 | tf_op jit(solution)/shard_map/ppermute | solution.py:325
  46.8 13.8 %collective-permute-start.9 = (bf16[384,512]{1,0:T(8,128)(2,1)S(1)}, bf16[384,512]{1,0:T(8,128)(2,1)S(1)}, u32[]{:S(2)}, u32[]{:S(2)}) collective-permute-start(bf16[384,512]{1,0:T(8,128)(2,1)S(1)} %crossing.2), channel_id=1, source_target_pairs={{0,4},{4,0},{8,12},{12,8},{16,20},{20,16},{24,28},{28,24},{32,36},... | collective-permute-start | bytes 1179656 | tf_op jit(solution)/shard_map/ppermute | solution.py:325
  59.7 1.9 %copy-start.4 = (f32[512]{0:T(512)S(1)}, f32[512]{0:T(512)}, u32[]{:S(2)}) copy-start(f32[512]{0:T(512)} %param.23) | copy-start | bytes 6148
  59.8 1.8 %collective-permute-start.17 = (bf16[384,512]{1,0:T(8,128)(2,1)S(1)}, bf16[384,512]{1,0:T(8,128)(2,1)S(1)}, u32[]{:S(2)}, u32[]{:S(2)}) collective-permute-start(bf16[384,512]{1,0:T(8,128)(2,1)S(1)} %crossing.3), channel_id=1, source_target_pairs={{0,4},{4,0},{8,12},{12,8},{16,20},{20,16},{24,28},{28,24},{32,36},... | collective-permute-start | bytes 1179656 | tf_op jit(solution)/shard_map/ppermute | solution.py:325
  61.6 19.1 %copy-start.1 = (bf16[1024,512]{1,0:T(8,128)(2,1)S(1)}, bf16[1024,512]{1,0:T(8,128)(2,1)}, u32[]{:S(2)}) copy-start(bf16[1024,512]{1,0:T(8,128)(2,1)} %w1_ref.1) | copy-start | bytes 3145732
  61.6 19.1 %copy-start.2 = (bf16[512,512]{1,0:T(8,128)(2,1)S(1)}, bf16[512,512]{1,0:T(8,128)(2,1)}, u32[]{:S(2)}) copy-start(bf16[512,512]{1,0:T(8,128)(2,1)} %w2_ref.1) | copy-start | bytes 1572868
  61.6 19.1 %copy-start.5 = (f32[512]{0:T(512)S(1)}, f32[512]{0:T(512)}, u32[]{:S(2)}) copy-start(f32[512]{0:T(512)} %param.25) | copy-start | bytes 6148
  61.6 19.1 %copy-start.6 = (f32[512]{0:T(512)S(1)}, f32[512]{0:T(512)}, u32[]{:S(2)}) copy-start(f32[512]{0:T(512)} %param.27) | copy-start | bytes 6148
  69.1 5.7 %collective-permute-start.18 = (bf16[160,512]{1,0:T(8,128)(2,1)S(1)}, bf16[160,512]{1,0:T(8,128)(2,1)S(1)}, u32[]{:S(2)}, u32[]{:S(2)}) collective-permute-start(bf16[160,512]{1,0:T(8,128)(2,1)S(1)} %get-tuple-element.25), channel_id=1, source_target_pairs={{0,3},{1,0},{2,1},{3,2},{4,7},{5,4},{6,5},{7,6},{8,11},{9,8},{10,9... | collective-permute-start | bytes 491528 | tf_op jit(solution)/shard_map/ppermute | solution.py:406
  69.6 6.9 %collective-permute-start.19 = (bf16[160,512]{1,0:T(8,128)(2,1)S(1)}, bf16[160,512]{1,0:T(8,128)(2,1)S(1)}, u32[]{:S(2)}, u32[]{:S(2)}) collective-permute-start(bf16[160,512]{1,0:T(8,128)(2,1)S(1)} %get-tuple-element.26), channel_id=1, source_target_pairs={{0,2},{1,3},{2,0},{3,1},{4,6},{5,7},{6,4},{7,5},{8,10},{9,11},{10,... | collective-permute-start | bytes 491528 | tf_op jit(solution)/shard_map/ppermute | solution.py:406
  69.8 10.9 %collective-permute-start.20 = (bf16[160,512]{1,0:T(8,128)(2,1)S(1)}, bf16[160,512]{1,0:T(8,128)(2,1)S(1)}, u32[]{:S(2)}, u32[]{:S(2)}) collective-permute-start(bf16[160,512]{1,0:T(8,128)(2,1)S(1)} %get-tuple-element.27), channel_id=1, source_target_pairs={{0,1},{1,2},{2,3},{3,0},{4,5},{5,6},{6,7},{7,4},{8,9},{9,10},{10,1... | collective-permute-start | bytes 491528 | tf_op jit(solution)/shard_map/ppermute | solution.py:406

commit v7 on v6

--- a/solution.py
+++ b/solution.py
@@ -10,6 +10,7 @@
 bf16 = jnp.bfloat16
 i32 = jnp.int32
 TILES = 2
+GATHERS = 1
 LIMIT = 16 << 20
 VMEM = pl.BlockSpec(memory_space=pltpu.VMEM)
 SMEM = pl.BlockSpec(memory_space=pltpu.SMEM)
@@ -47,6 +48,11 @@
 def hot_columns(row, count, first=0):
     ids = lax.broadcasted_iota(i32, (count, row.shape[1]), 0) + first
     return as_bf16(row == ids)
+
+
+def hot_rows(column, count, first=0):
+    ids = lax.broadcasted_iota(i32, (column.shape[0], count), 1) + first
+    return as_bf16(column == ids)
 
 
 def in_hbm(value):
@@ -133,6 +139,23 @@
         cost_estimate=pl.CostEstimate(flops=COST, bytes_accessed=0, transcendentals=0),
         name="select",
     )(*blocks, *earlier)
+
+
+def gate_kernel(*refs):
+    pass
+
+
+def gate(value, *earlier):
+    return pl.pallas_call(
+        gate_kernel,
+        in_specs=[ANY] * (1 + len(earlier)),
+        out_specs=ANY,
+        out_shape=jax.ShapeDtypeStruct(value.shape, value.dtype),
+        input_output_aliases={0: 0},
+        compiler_params=pltpu.CompilerParams(vmem_limit_bytes=1 << 20),
+        cost_estimate=pl.CostEstimate(flops=0, bytes_accessed=0, transcendentals=0),
+        name="gate",
+    )(value, *earlier)
 
 
 def cross_kernel(*refs):
@@ -238,8 +261,11 @@
     fill(table_ref, table_ref.shape[0] // 2, groups[X + 1 :])
     stores = []
     live = live_ref[0]
-    hot = hot_columns(send_ref[...], table_ref.shape[0], first_row)
-    far_ref[...] = dot_first(hot, table_ref[...]).astype(bf16)
+    size = count // GATHERS
+    for at in range(GATHERS):
+        rows = slice(at * size, (at + 1) * size)
+        hot = hot_rows(send_ref[rows], table_ref.shape[0], first_row)
+        far_ref[rows] = dot(hot, table_ref[...]).astype(bf16)
     for load in loads:
         load.wait()
     for at in range(TILES):
@@ -358,19 +384,19 @@
     forth = back = block
     for hop in range(1, 4):
         forth, back = up(forth), down(back)
+        if hop == 2:
+            forth = gate(forth, *parts[1:])
         held[hop], held[Z - hop] = forth, back
     held[4] = up(forth)
 
     groups = []
     for pairs in BATCHES:
-        earlier = parts[1:] if pairs is BATCHES[0] else []
-        picked = select(pairs, cap, [held[dz] for pair in pairs for dz in pair], *earlier)
+        picked = select(pairs, cap, [held[dz] for pair in pairs for dz in pair])
         group = [picked[0]]
         for k in range(1, X):
             group.append(moved(picked[k], lambda x, z, c: (x + k, z, c)))
         groups.append(group)
     swap = lambda a: moved(a, lambda x, z, c: (x, z, c + 1))
-    groups[0].append(swap(crossing(groups[0])))
 
     def near_row(row):
         return ((mine - row // rows) & (feat - 1)) * rows + row % rows
@@ -391,14 +417,13 @@
                 place = jnp.where(dz == value, here, place)
         base += X * C * len(pairs) * 2 * cap
     send = jnp.where(sender_slot < patch, near_row(sender_slot), patch + place + entry)
-    send = send.reshape(1, -1)
     recv = near_row(receivers).reshape(1, -1)
     before = edge_before(
-        recv, send, edge_b1.reshape(1, -1), parts, edges, edge_w1, groups[1][0]
+        recv, send.reshape(1, -1), edge_b1.reshape(1, -1), parts, edges, edge_w1, groups[1][0]
     )
-    groups[1].append(swap(crossing(groups[1], before)))
+    groups = [group + [swap(crossing(group, before))] for group in groups]
     edges_out, *sums = edge_after(
-        patch, live_edges, send, recv, edge_gain.reshape(1, -1), groups[0] + groups[1], before,
+        patch, live_edges, send.reshape(-1, 1), recv, edge_gain.reshape(1, -1), groups[0] + groups[1], before,
         edge_w1, edge_w2, edges, rows,
     )
     parts = [sums[0]]

time: 82.3 us -> 76.9 us (0.934)
  waiting for transfers between devices: 29.6 us -> 25.2 us
  Pallas kernels: 19.6 us -> 18.7 us
    ppermute x15, waiting for transfers between devices: 10.5 us -> 8.24 us  [moved(): return lax.ppermute(value, 'patch', pairs_of(move))]
    ppermute x3, waiting for transfers between devices: 9 us -> 7.24 us  [local(): lax.ppermute(nodes, 'feat', [(i, (i + k) % feat) for i in range(feat)])]
    pallas_call x1, Pallas kernels: 7.49 us -> 6.45 us  [edge_after(): pl.pallas_call(lambda *refs: after_kernel(first_row, *refs), in_specs=[SM...]
  transfers between devices with their start and end apart: 21 -> 21, of which waited for: 10 -> 11; matrix products, arithmetic and copies ran while one was open for 0% -> 0% of each run, Pallas kernels for 11% -> 11%
where the time goes in v7:
time: 76.9 us; the launch traced here: 76.7 us
  starting transfers between devices  30.9 us (40%)
  waiting for transfers between devices  25.2 us (33%)
  Pallas kernels  18.7 us (24%)
  between operations  1.5 us (2%)
    ppermute x15, starting transfers between devices, moved(): return lax.ppermute(value, 'patch', pairs_of(move))  25.6 us
    ppermute x3, waiting for transfers between devices, local(): lax.ppermute(sums[k], 'feat', [(i, (i - k) % feat) for i in range(feat)])  9.77 us
    ppermute x15, waiting for transfers between devices, moved(): return lax.ppermute(value, 'patch', pairs_of(move))  8.24 us
    ppermute x3, waiting for transfers between devices, local(): lax.ppermute(nodes, 'feat', [(i, (i + k) % feat) for i in range(feat)])  7.24 us
    pallas_call x1, Pallas kernels, edge_before(): pl.pallas_call(lambda *refs: before_kernel(len(earlier), *refs), in_specs...  6.74 us
    pallas_call x1, Pallas kernels, edge_after(): pl.pallas_call(lambda *refs: after_kernel(first_row, *refs), in_specs=[SM...  6.45 us
    ppermute x3, starting transfers between devices, local(): lax.ppermute(nodes, 'feat', [(i, (i + k) % feat) for i in range(feat)])  3.78 us
    pallas_call x1, Pallas kernels, pack(): pl.pallas_call(pack_kernel, in_specs=[SMEM, VMEM, VMEM], out_shape=jax.Sh...  2 us
  transfers between devices with their start and end apart: 21, of which 11 were waited for; matrix products, arithmetic and copies ran while one was open for 0% of the time, Pallas kernels for 11%

profile of v7, /device:TPU:1, one launch (start us, length us, event | category | flops | bytes accessed | tf_op | source)
XLA Modules:
  0.0 76.7 jit_solution(6934531742303347708)
XLA Ops:
  0.6 0.0 copy-start
  0.6 0.0 copy-start.7
  0.7 0.0 copy-start.8
  0.7 0.0 copy-start.3
  0.7 2.0 %pack.1.refs_0_ = bf16[176,512]{1,0:T(8,128)(2,1)} custom-call(s32[1]{0:T(128)} %bitcast.1.where_ref, s32[24,64]{1,0:T(8,128)} %bitcast.12, bf16[160,512]{1,0:T(8,128)(2,1)} %nodes_ref.3), custom_call_target="tpu_custom_call" | custom-call | tf_op jit(solution)/shard_map/pack/pallas_call | solution.py:89
  2.7 2.5 %collective-permute-start = (bf16[176,512]{1,0:T(8,128)(2,1)}, bf16[176,512]{1,0:T(8,128)(2,1)S(1)}, u32[]{:S(2)}, u32[]{:S(2)}) collective-permute-start(bf16[176,512]{1,0:T(8,128)(2,1)} %pack.1.refs_0_), channel_id=1, source_target_pairs={{0,8},{4,12},{8,16},{12,20},{16,24},{20,28},{24,32},{28,36},{32,40... | collective-permute-start | bytes 540680 | tf_op jit(solution)/shard_map/ppermute | solution.py:351
  5.1 3.9 %collective-permute-start.1 = (bf16[176,512]{1,0:T(8,128)(2,1)}, bf16[176,512]{1,0:T(8,128)(2,1)S(1)}, u32[]{:S(2)}, u32[]{:S(2)}) collective-permute-start(bf16[176,512]{1,0:T(8,128)(2,1)} %pack.1.refs_0_), channel_id=1, source_target_pairs={{0,56},{4,60},{8,0},{12,4},{16,8},{20,12},{24,16},{28,20},{32,24},... | collective-permute-start | bytes 540680 | tf_op jit(solution)/shard_map/ppermute | solution.py:351
  9.1 4.5 %collective-permute-done.refs_1_ = bf16[176,512]{1,0:T(8,128)(2,1)S(1)} collective-permute-done((bf16[176,512]{1,0:T(8,128)(2,1)}, bf16[176,512]{1,0:T(8,128)(2,1)S(1)}, u32[]{:S(2)}, u32[]{:S(2)}) %collective-permute-start) | collective-permute-done | bytes 180256 | tf_op jit(solution)/shard_map/ppermute | solution.py:351
  13.6 0.0 collective-permute-start.2
  13.6 2.7 %collective-permute-start.5 = (bf16[160,512]{1,0:T(8,128)(2,1)}, bf16[160,512]{1,0:T(8,128)(2,1)S(1)}, u32[]{:S(2)}, u32[]{:S(2)}) collective-permute-start(bf16[160,512]{1,0:T(8,128)(2,1)} %nodes_ref.3), channel_id=1, source_target_pairs={{0,3},{1,0},{2,1},{3,2},{4,7},{5,4},{6,5},{7,6},{8,11},{9,8},{10,9... | collective-permute-start | bytes 491528 | tf_op jit(solution)/shard_map/ppermute | solution.py:380
  16.3 0.3 collective-permute-start.4
  16.7 0.7 collective-permute-start.3
  17.3 0.0 collective-permute-done.1.refs_2_
  17.4 2.7 %collective-permute-start.9 = (bf16[176,512]{1,0:T(8,128)(2,1)S(1)}, bf16[176,512]{1,0:T(8,128)(2,1)S(1)}, u32[]{:S(2)}, u32[]{:S(2)}) collective-permute-start(bf16[176,512]{1,0:T(8,128)(2,1)S(1)} %collective-permute-done.1.refs_2_), channel_id=1, source_target_pairs={{0,56},{4,60},{8,0},{12,4},{16,8},{20,12},{24,16},{28,20},{32,24},... | collective-permute-start | bytes 540680 | tf_op jit(solution)/shard_map/ppermute | solution.py:351
  20.0 0.4 collective-permute-done.5.refs_3_.refs_6_
  20.4 1.9 %collective-permute-done.4.refs_2_.refs_5_ = bf16[160,512]{1,0:T(8,128)(2,1)S(1)} collective-permute-done((bf16[160,512]{1,0:T(8,128)(2,1)}, bf16[160,512]{1,0:T(8,128)(2,1)S(1)}, u32[]{:S(2)}, u32[]{:S(2)}) %collective-permute-start.4) | collective-permute-done | bytes 163872 | tf_op jit(solution)/shard_map/ppermute | solution.py:380
  22.3 5.0 %collective-permute-done.3.refs_1_.refs_4_ = bf16[160,512]{1,0:T(8,128)(2,1)S(1)} collective-permute-done((bf16[160,512]{1,0:T(8,128)(2,1)}, bf16[160,512]{1,0:T(8,128)(2,1)S(1)}, u32[]{:S(2)}, u32[]{:S(2)}) %collective-permute-start.3) | collective-permute-done | bytes 163872 | tf_op jit(solution)/shard_map/ppermute | solution.py:380
  27.3 0.0 collective-permute-done.2.refs_0_
  27.3 0.0 collective-permute-start.10
  27.3 1.3 %select.24 = (bf16[192,512]{1,0:T(8,128)(2,1)S(1)}, bf16[192,512]{1,0:T(8,128)(2,1)S(1)}, bf16[192,512]{1,0:T(8,128)(2,1)S(1)}, bf16[192,512]{1,0:T(8,128)(2,1)S(1)}) custom-call(bf16[176,512]{1,0:T(8,128)(2,1)} %pack.1.refs_0_, bf16[176,512]{1,0:T(8,128)(2,1)S(1)} %collective-permute-done.refs_1_, bf16[176,512]{1,0:T(8,128)(2,1)S(1)} %collective-permute-done.1.refs_2_, ...), custom_call_target="tpu_custom_call" | custom-call | flops 1048576 | tf_op jit(solution)/shard_map/select/pallas_call | solution.py:133
  28.6 1.3 %collective-permute-start.6 = (bf16[192,512]{1,0:T(8,128)(2,1)S(1)}, bf16[192,512]{1,0:T(8,128)(2,1)S(1)}, u32[]{:S(2)}, u32[]{:S(2)}) collective-permute-start(bf16[192,512]{1,0:T(8,128)(2,1)S(1)} %get-tuple-element.16), channel_id=1, source_target_pairs={{0,64},{4,68},{8,72},{12,76},{16,80},{20,84},{24,88},{28,92},{32,9... | collective-permute-start | bytes 589832 | tf_op jit(solution)/shard_map/ppermute | solution.py:351
  29.9 0.0 collective-permute-done.9.refs_0_
  29.9 2.7 %collective-permute-start.11 = (bf16[176,512]{1,0:T(8,128)(2,1)S(1)}, bf16[176,512]{1,0:T(8,128)(2,1)S(1)}, u32[]{:S(2)}, u32[]{:S(2)}) collective-permute-start(bf16[176,512]{1,0:T(8,128)(2,1)S(1)} %collective-permute-done.9.refs_0_), channel_id=1, source_target_pairs={{0,56},{4,60},{8,0},{12,4},{16,8},{20,12},{24,16},{28,20},{32,24},... | collective-permute-start | bytes 540680 | tf_op jit(solution)/shard_map/ppermute | solution.py:351
  32.6 1.1 %collective-permute-done.10.refs_1_ = bf16[176,512]{1,0:T(8,128)(2,1)S(1)} collective-permute-done((bf16[176,512]{1,0:T(8,128)(2,1)S(1)}, bf16[176,512]{1,0:T(8,128)(2,1)S(1)}, u32[]{:S(2)}, u32[]{:S(2)}) %collective-permute-start.10) | collective-permute-done | bytes 180256 | tf_op jit(solution)/shard_map/ppermute | solution.py:351
  33.7 0.0 collective-permute-start.12
  33.7 0.0 copy-done.7
  33.7 2.8 %collective-permute-start.7 = (bf16[192,512]{1,0:T(8,128)(2,1)S(1)}, bf16[192,512]{1,0:T(8,128)(2,1)S(1)}, u32[]{:S(2)}, u32[]{:S(2)}) collective-permute-start(bf16[192,512]{1,0:T(8,128)(2,1)S(1)} %get-tuple-element.17), channel_id=1, source_target_pairs={{0,128},{4,132},{8,136},{12,140},{16,144},{20,148},{24,152},{28,15... | collective-permute-start | bytes 589832 | tf_op jit(solution)/shard_map/ppermute | solution.py:351
  36.6 0.9 %collective-permute-start.8 = (bf16[192,512]{1,0:T(8,128)(2,1)S(1)}, bf16[192,512]{1,0:T(8,128)(2,1)S(1)}, u32[]{:S(2)}, u32[]{:S(2)}) collective-permute-start(bf16[192,512]{1,0:T(8,128)(2,1)S(1)} %get-tuple-element.18), channel_id=1, source_target_pairs={{0,192},{4,196},{8,200},{12,204},{16,208},{20,212},{24,216},{28,22... | collective-permute-start | bytes 589832 | tf_op jit(solution)/shard_map/ppermute | solution.py:351
  37.4 0.0 collective-permute-done.11.refs_2_
  37.4 1.8 %collective-permute-done.12.refs_3_ = bf16[176,512]{1,0:T(8,128)(2,1)S(1)} collective-permute-done((bf16[176,512]{1,0:T(8,128)(2,1)S(1)}, bf16[176,512]{1,0:T(8,128)(2,1)S(1)}, u32[]{:S(2)}, u32[]{:S(2)}) %collective-permute-start.12) | collective-permute-done | bytes 180256 | tf_op jit(solution)/shard_map/ppermute | solution.py:351
  39.2 0.6 select.25
  39.8 1.3 %collective-permute-start.14 = (bf16[192,512]{1,0:T(8,128)(2,1)S(1)}, bf16[192,512]{1,0:T(8,128)(2,1)S(1)}, u32[]{:S(2)}, u32[]{:S(2)}) collective-permute-start(bf16[192,512]{1,0:T(8,128)(2,1)S(1)} %get-tuple-element.20), channel_id=1, source_target_pairs={{0,64},{4,68},{8,72},{12,76},{16,80},{20,84},{24,88},{28,92},{32,9... | collective-permute-start | bytes 589832 | tf_op jit(solution)/shard_map/ppermute | solution.py:351
  41.1 2.5 %collective-permute-start.15 = (bf16[192,512]{1,0:T(8,128)(2,1)S(1)}, bf16[192,512]{1,0:T(8,128)(2,1)S(1)}, u32[]{:S(2)}, u32[]{:S(2)}) collective-permute-start(bf16[192,512]{1,0:T(8,128)(2,1)S(1)} %get-tuple-element.21), channel_id=1, source_target_pairs={{0,128},{4,132},{8,136},{12,140},{16,144},{20,148},{24,152},{28,15... | collective-permute-start | bytes 589832 | tf_op jit(solution)/shard_map/ppermute | solution.py:351
  43.6 0.0 collective-permute-done.6.refs_1_.refs_5_
  43.6 1.2 %collective-permute-start.16 = (bf16[192,512]{1,0:T(8,128)(2,1)S(1)}, bf16[192,512]{1,0:T(8,128)(2,1)S(1)}, u32[]{:S(2)}, u32[]{:S(2)}) collective-permute-start(bf16[192,512]{1,0:T(8,128)(2,1)S(1)} %get-tuple-element.22), channel_id=1, source_target_pairs={{0,192},{4,196},{8,200},{12,204},{16,208},{20,212},{24,216},{28,22... | collective-permute-start | bytes 589832 | tf_op jit(solution)/shard_map/ppermute | solution.py:351
  44.7 0.0 copy-done.8
  44.8 0.0 copy-done
  44.8 0.0 copy-done.3
  44.8 6.7 %edge_before.1.refs_4_.refs_14_ = f32[1280,512]{1,0:T(8,128)} custom-call(s32[1,1280]{1,0:T(1,128)S(1)} %reshape.29.refs_0_.refs_2_, s32[1,1280]{1,0:T(1,128)S(1)} %reshape.32.refs_1_, f32[1,512]{1,0:T(1,128)S(1)} %bitcast.8, bf16[160,512]{1,0:T(8,128)(2,1)S(1)} %copy-done, bf16[160,512]{1,0:T(8,128)(2,1)S(1)} %collective-permute-done.3.refs_1_.refs_4_, ...), custom_call_target="tpu_custom_call" | custom-call | flops 1048576 | tf_op jit(solution)/shard_map/edge_before/pallas_call | solution.py:226
  51.5 0.0 collective-permute-done.7.refs_2_.refs_6_
  51.6 0.0 collective-permute-done.8.refs_3_.refs_7_
  51.6 0.0 copy-start.4
  51.6 3.9 %collective-permute-start.13 = (bf16[384,512]{1,0:T(8,128)(2,1)S(1)}, bf16[384,512]{1,0:T(8,128)(2,1)S(1)}, u32[]{:S(2)}, u32[]{:S(2)}) collective-permute-start(bf16[384,512]{1,0:T(8,128)(2,1)S(1)} %crossing.2), channel_id=1, source_target_pairs={{0,4},{4,0},{8,12},{12,8},{16,20},{20,16},{24,28},{28,24},{32,36},... | collective-permute-start | bytes 1179656 | tf_op jit(solution)/shard_map/ppermute | solution.py:351
  55.5 0.0 collective-permute-done.14.refs_1_.refs_10_
  55.5 0.0 collective-permute-done.15.refs_2_.refs_11_
  55.5 0.0 collective-permute-done.16.refs_3_.refs_12_
  55.5 0.1 collective-permute-start.17
  55.6 0.2 reshape.36.refs_1_
  56.5 0.3 collective-permute-done.13.refs_8_
  56.8 0.6 collective-permute-done.17.refs_13_
  57.4 0.0 copy-done.4
  57.4 0.0 copy-start.6
  57.4 6.5 %edge_after.1 = (bf16[1280,512]{1,0:T(8,128)(2,1)}, f32[160,512]{1,0:T(8,128)S(1)}, bf16[160,512]{1,0:T(8,128)(2,1)S(1)}, bf16[160,512]{1,0:T(8,128)(2,1)S(1)}, bf16[160,512]{1,0:T(8,128)(2,1)S(1)}) custom-call(s32[1]{0:T(128)S(6)} %copy.19.refs_0_, s32[1280,1]{1,0:T(8,128)S(1)} %reshape.36.refs_1_, s32[1,1280]{1,0:T(1,128)S(1)} %reshape.29.refs_0_.refs_2_, ...), custom_call_target="tpu_custom_call" | custom-call | tf_op jit(solution)/shard_map/edge_after/pallas_call | solution.py:297
  63.9 0.1 collective-permute-start.18
  64.0 0.1 collective-permute-start.19
  64.1 1.4 %collective-permute-start.20 = (bf16[160,512]{1,0:T(8,128)(2,1)S(1)}, bf16[160,512]{1,0:T(8,128)(2,1)S(1)}, u32[]{:S(2)}, u32[]{:S(2)}) collective-permute-start(bf16[160,512]{1,0:T(8,128)(2,1)S(1)} %get-tuple-element.27), channel_id=1, source_target_pairs={{0,1},{1,2},{2,3},{3,0},{4,5},{5,6},{6,7},{7,4},{8,9},{9,10},{10,1... | collective-permute-start | bytes 491528 | tf_op jit(solution)/shard_map/ppermute | solution.py:431
  65.4 3.9 %collective-permute-done.18.p1_ref = bf16[160,512]{1,0:T(8,128)(2,1)S(1)} collective-permute-done((bf16[160,512]{1,0:T(8,128)(2,1)S(1)}, bf16[160,512]{1,0:T(8,128)(2,1)S(1)}, u32[]{:S(2)}, u32[]{:S(2)}) %collective-permute-start.18) | collective-permute-done | bytes 163872 | tf_op jit(solution)/shard_map/ppermute | solution.py:431
  69.4 1.6 %collective-permute-done.19.p2_ref = bf16[160,512]{1,0:T(8,128)(2,1)S(1)} collective-permute-done((bf16[160,512]{1,0:T(8,128)(2,1)S(1)}, bf16[160,512]{1,0:T(8,128)(2,1)S(1)}, u32[]{:S(2)}, u32[]{:S(2)}) %collective-permute-start.19) | collective-permute-done | bytes 163872 | tf_op jit(solution)/shard_map/ppermute | solution.py:431
  71.0 4.2 %collective-permute-done.20.p3_ref = bf16[160,512]{1,0:T(8,128)(2,1)S(1)} collective-permute-done((bf16[160,512]{1,0:T(8,128)(2,1)S(1)}, bf16[160,512]{1,0:T(8,128)(2,1)S(1)}, u32[]{:S(2)}, u32[]{:S(2)}) %collective-permute-start.20) | collective-permute-done | bytes 163872 | tf_op jit(solution)/shard_map/ppermute | solution.py:431
  75.2 0.0 copy-done.1
  75.2 0.0 copy-done.2
  75.2 0.0 copy-done.5
  75.2 0.0 copy-done.6
  75.2 1.5 %node_update.1 = bf16[160,512]{1,0:T(8,128)(2,1)} custom-call(bf16[160,512]{1,0:T(8,128)(2,1)S(1)} %copy-done, f32[160,512]{1,0:T(8,128)S(1)} %get-tuple-element.24.p0_ref, bf16[160,512]{1,0:T(8,128)(2,1)S(1)} %collective-permute-done.18.p1_ref, bf16[160,512]{1,0:T(8,128)(2,1)S(1)} %collective-permute-done.19.p2_ref, ...), custom_call_target="tpu_custom_call" | custom-call | tf_op jit(solution)/shard_map/node_update/pallas_call | solution.py:331
  (10 shorter events, 0.1 us)
Async XLA Ops:
  0.6 44.1 %copy-start = (bf16[160,512]{1,0:T(8,128)(2,1)S(1)}, bf16[160,512]{1,0:T(8,128)(2,1)}, u32[]{:S(2)}) copy-start(bf16[160,512]{1,0:T(8,128)(2,1)} %nodes_ref.3) | copy-start | bytes 491524
  0.6 33.0 %copy-start.7 = (s32[1280]{0:T(1024)S(1)}, s32[1280]{0:T(1024)}, u32[]{:S(2)}) copy-start(s32[1280]{0:T(1024)} %param.17) | copy-start | bytes 15364
  0.7 44.1 %copy-start.8 = (s32[1280]{0:T(1024)S(1)}, s32[1280]{0:T(1024)}, u32[]{:S(2)}) copy-start(s32[1280]{0:T(1024)} %param.16) | copy-start | bytes 15364
  0.7 44.1 %copy-start.3 = (f32[512]{0:T(512)S(1)}, f32[512]{0:T(512)}, u32[]{:S(2)}) copy-start(f32[512]{0:T(512)} %param.21) | copy-start | bytes 6148
  2.7 10.9 %collective-permute-start = (bf16[176,512]{1,0:T(8,128)(2,1)}, bf16[176,512]{1,0:T(8,128)(2,1)S(1)}, u32[]{:S(2)}, u32[]{:S(2)}) collective-permute-start(bf16[176,512]{1,0:T(8,128)(2,1)} %pack.1.refs_0_), channel_id=1, source_target_pairs={{0,8},{4,12},{8,16},{12,20},{16,24},{20,28},{24,32},{28,36},{32,40... | collective-permute-start | bytes 540680 | tf_op jit(solution)/shard_map/ppermute | solution.py:351
  5.1 12.2 %collective-permute-start.1 = (bf16[176,512]{1,0:T(8,128)(2,1)}, bf16[176,512]{1,0:T(8,128)(2,1)S(1)}, u32[]{:S(2)}, u32[]{:S(2)}) collective-permute-start(bf16[176,512]{1,0:T(8,128)(2,1)} %pack.1.refs_0_), channel_id=1, source_target_pairs={{0,56},{4,60},{8,0},{12,4},{16,8},{20,12},{24,16},{28,20},{32,24},... | collective-permute-start | bytes 540680 | tf_op jit(solution)/shard_map/ppermute | solution.py:351
  13.6 13.7 %collective-permute-start.2 = (bf16[176,512]{1,0:T(8,128)(2,1)S(1)}, bf16[176,512]{1,0:T(8,128)(2,1)S(1)}, u32[]{:S(2)}, u32[]{:S(2)}) collective-permute-start(bf16[176,512]{1,0:T(8,128)(2,1)S(1)} %collective-permute-done.refs_1_), channel_id=1, source_target_pairs={{0,8},{4,12},{8,16},{12,20},{16,24},{20,28},{24,32},{28,36},{32,40... | collective-permute-start | bytes 540680 | tf_op jit(solution)/shard_map/ppermute | solution.py:351
  13.6 6.9 %collective-permute-start.5 = (bf16[160,512]{1,0:T(8,128)(2,1)}, bf16[160,512]{1,0:T(8,128)(2,1)S(1)}, u32[]{:S(2)}, u32[]{:S(2)}) collective-permute-start(bf16[160,512]{1,0:T(8,128)(2,1)} %nodes_ref.3), channel_id=1, source_target_pairs={{0,3},{1,0},{2,1},{3,2},{4,7},{5,4},{6,5},{7,6},{8,11},{9,8},{10,9... | collective-permute-start | bytes 491528 | tf_op jit(solution)/shard_map/ppermute | solution.py:380
  16.3 6.0 %collective-permute-start.4 = (bf16[160,512]{1,0:T(8,128)(2,1)}, bf16[160,512]{1,0:T(8,128)(2,1)S(1)}, u32[]{:S(2)}, u32[]{:S(2)}) collective-permute-start(bf16[160,512]{1,0:T(8,128)(2,1)} %nodes_ref.3), channel_id=1, source_target_pairs={{0,2},{1,3},{2,0},{3,1},{4,6},{5,7},{6,4},{7,5},{8,10},{9,11},{10,... | collective-permute-start | bytes 491528 | tf_op jit(solution)/shard_map/ppermute | solution.py:380
  16.7 10.6 %collective-permute-start.3 = (bf16[160,512]{1,0:T(8,128)(2,1)}, bf16[160,512]{1,0:T(8,128)(2,1)S(1)}, u32[]{:S(2)}, u32[]{:S(2)}) collective-permute-start(bf16[160,512]{1,0:T(8,128)(2,1)} %nodes_ref.3), channel_id=1, source_target_pairs={{0,1},{1,2},{2,3},{3,0},{4,5},{5,6},{6,7},{7,4},{8,9},{9,10},{10,1... | collective-permute-start | bytes 491528 | tf_op jit(solution)/shard_map/ppermute | solution.py:380
  17.4 12.6 %collective-permute-start.9 = (bf16[176,512]{1,0:T(8,128)(2,1)S(1)}, bf16[176,512]{1,0:T(8,128)(2,1)S(1)}, u32[]{:S(2)}, u32[]{:S(2)}) collective-permute-start(bf16[176,512]{1,0:T(8,128)(2,1)S(1)} %collective-permute-done.1.refs_2_), channel_id=1, source_target_pairs={{0,56},{4,60},{8,0},{12,4},{16,8},{20,12},{24,16},{28,20},{32,24},... | collective-permute-start | bytes 540680 | tf_op jit(solution)/shard_map/ppermute | solution.py:351
  27.3 6.4 %collective-permute-start.10 = (bf16[176,512]{1,0:T(8,128)(2,1)S(1)}, bf16[176,512]{1,0:T(8,128)(2,1)S(1)}, u32[]{:S(2)}, u32[]{:S(2)}) collective-permute-start(bf16[176,512]{1,0:T(8,128)(2,1)S(1)} %gate.1.refs_3_), channel_id=1, source_target_pairs={{0,8},{4,12},{8,16},{12,20},{16,24},{20,28},{24,32},{28,36},{32,40... | collective-permute-start | bytes 540680 | tf_op jit(solution)/shard_map/ppermute | solution.py:351
  28.6 15.0 %collective-permute-start.6 = (bf16[192,512]{1,0:T(8,128)(2,1)S(1)}, bf16[192,512]{1,0:T(8,128)(2,1)S(1)}, u32[]{:S(2)}, u32[]{:S(2)}) collective-permute-start(bf16[192,512]{1,0:T(8,128)(2,1)S(1)} %get-tuple-element.16), channel_id=1, source_target_pairs={{0,64},{4,68},{8,72},{12,76},{16,80},{20,84},{24,88},{28,92},{32,9... | collective-permute-start | bytes 589832 | tf_op jit(solution)/shard_map/ppermute | solution.py:351
  29.9 7.5 %collective-permute-start.11 = (bf16[176,512]{1,0:T(8,128)(2,1)S(1)}, bf16[176,512]{1,0:T(8,128)(2,1)S(1)}, u32[]{:S(2)}, u32[]{:S(2)}) collective-permute-start(bf16[176,512]{1,0:T(8,128)(2,1)S(1)} %collective-permute-done.9.refs_0_), channel_id=1, source_target_pairs={{0,56},{4,60},{8,0},{12,4},{16,8},{20,12},{24,16},{28,20},{32,24},... | collective-permute-start | bytes 540680 | tf_op jit(solution)/shard_map/ppermute | solution.py:351
  33.7 5.6 %collective-permute-start.12 = (bf16[176,512]{1,0:T(8,128)(2,1)S(1)}, bf16[176,512]{1,0:T(8,128)(2,1)S(1)}, u32[]{:S(2)}, u32[]{:S(2)}) collective-permute-start(bf16[176,512]{1,0:T(8,128)(2,1)S(1)} %collective-permute-done.10.refs_1_), channel_id=1, source_target_pairs={{0,8},{4,12},{8,16},{12,20},{16,24},{20,28},{24,32},{28,36},{32,40... | collective-permute-start | bytes 540680 | tf_op jit(solution)/shard_map/ppermute | solution.py:351
  33.7 17.8 %collective-permute-start.7 = (bf16[192,512]{1,0:T(8,128)(2,1)S(1)}, bf16[192,512]{1,0:T(8,128)(2,1)S(1)}, u32[]{:S(2)}, u32[]{:S(2)}) collective-permute-start(bf16[192,512]{1,0:T(8,128)(2,1)S(1)} %get-tuple-element.17), channel_id=1, source_target_pairs={{0,128},{4,132},{8,136},{12,140},{16,144},{20,148},{24,152},{28,15... | collective-permute-start | bytes 589832 | tf_op jit(solution)/shard_map/ppermute | solution.py:351
  36.6 15.0 %collective-permute-start.8 = (bf16[192,512]{1,0:T(8,128)(2,1)S(1)}, bf16[192,512]{1,0:T(8,128)(2,1)S(1)}, u32[]{:S(2)}, u32[]{:S(2)}) collective-permute-start(bf16[192,512]{1,0:T(8,128)(2,1)S(1)} %get-tuple-element.18), channel_id=1, source_target_pairs={{0,192},{4,196},{8,200},{12,204},{16,208},{20,212},{24,216},{28,22... | collective-permute-start | bytes 589832 | tf_op jit(solution)/shard_map/ppermute | solution.py:351
  39.8 15.6 %collective-permute-start.14 = (bf16[192,512]{1,0:T(8,128)(2,1)S(1)}, bf16[192,512]{1,0:T(8,128)(2,1)S(1)}, u32[]{:S(2)}, u32[]{:S(2)}) collective-permute-start(bf16[192,512]{1,0:T(8,128)(2,1)S(1)} %get-tuple-element.20), channel_id=1, source_target_pairs={{0,64},{4,68},{8,72},{12,76},{16,80},{20,84},{24,88},{28,92},{32,9... | collective-permute-start | bytes 589832 | tf_op jit(solution)/shard_map/ppermute | solution.py:351
  41.1 14.3 %collective-permute-start.15 = (bf16[192,512]{1,0:T(8,128)(2,1)S(1)}, bf16[192,512]{1,0:T(8,128)(2,1)S(1)}, u32[]{:S(2)}, u32[]{:S(2)}) collective-permute-start(bf16[192,512]{1,0:T(8,128)(2,1)S(1)} %get-tuple-element.21), channel_id=1, source_target_pairs={{0,128},{4,132},{8,136},{12,140},{16,144},{20,148},{24,152},{28,15... | collective-permute-start | bytes 589832 | tf_op jit(solution)/shard_map/ppermute | solution.py:351
  43.6 11.9 %collective-permute-start.16 = (bf16[192,512]{1,0:T(8,128)(2,1)S(1)}, bf16[192,512]{1,0:T(8,128)(2,1)S(1)}, u32[]{:S(2)}, u32[]{:S(2)}) collective-permute-start(bf16[192,512]{1,0:T(8,128)(2,1)S(1)} %get-tuple-element.22), channel_id=1, source_target_pairs={{0,192},{4,196},{8,200},{12,204},{16,208},{20,212},{24,216},{28,22... | collective-permute-start | bytes 589832 | tf_op jit(solution)/shard_map/ppermute | solution.py:351
  51.6 5.8 %copy-start.4 = (f32[512]{0:T(512)S(1)}, f32[512]{0:T(512)}, u32[]{:S(2)}) copy-start(f32[512]{0:T(512)} %param.23) | copy-start | bytes 6148
  51.6 5.2 %collective-permute-start.13 = (bf16[384,512]{1,0:T(8,128)(2,1)S(1)}, bf16[384,512]{1,0:T(8,128)(2,1)S(1)}, u32[]{:S(2)}, u32[]{:S(2)}) collective-permute-start(bf16[384,512]{1,0:T(8,128)(2,1)S(1)} %crossing.2), channel_id=1, source_target_pairs={{0,4},{4,0},{8,12},{12,8},{16,20},{20,16},{24,28},{28,24},{32,36},... | collective-permute-start | bytes 1179656 | tf_op jit(solution)/shard_map/ppermute | solution.py:351
  55.5 1.9 %collective-permute-start.17 = (bf16[384,512]{1,0:T(8,128)(2,1)S(1)}, bf16[384,512]{1,0:T(8,128)(2,1)S(1)}, u32[]{:S(2)}, u32[]{:S(2)}) collective-permute-start(bf16[384,512]{1,0:T(8,128)(2,1)S(1)} %crossing.3), channel_id=1, source_target_pairs={{0,4},{4,0},{8,12},{12,8},{16,20},{20,16},{24,28},{28,24},{32,36},... | collective-permute-start | bytes 1179656 | tf_op jit(solution)/shard_map/ppermute | solution.py:351
  57.4 17.8 %copy-start.1 = (bf16[1024,512]{1,0:T(8,128)(2,1)S(1)}, bf16[1024,512]{1,0:T(8,128)(2,1)}, u32[]{:S(2)}) copy-start(bf16[1024,512]{1,0:T(8,128)(2,1)} %w1_ref.1) | copy-start | bytes 3145732
  57.4 17.8 %copy-start.2 = (bf16[512,512]{1,0:T(8,128)(2,1)S(1)}, bf16[512,512]{1,0:T(8,128)(2,1)}, u32[]{:S(2)}) copy-start(bf16[512,512]{1,0:T(8,128)(2,1)} %w2_ref.1) | copy-start | bytes 1572868
  57.4 17.8 %copy-start.5 = (f32[512]{0:T(512)S(1)}, f32[512]{0:T(512)}, u32[]{:S(2)}) copy-start(f32[512]{0:T(512)} %param.25) | copy-start | bytes 6148
  57.4 17.8 %copy-start.6 = (f32[512]{0:T(512)S(1)}, f32[512]{0:T(512)}, u32[]{:S(2)}) copy-start(f32[512]{0:T(512)} %param.27) | copy-start | bytes 6148
  63.9 5.5 %collective-permute-start.18 = (bf16[160,512]{1,0:T(8,128)(2,1)S(1)}, bf16[160,512]{1,0:T(8,128)(2,1)S(1)}, u32[]{:S(2)}, u32[]{:S(2)}) collective-permute-start(bf16[160,512]{1,0:T(8,128)(2,1)S(1)} %get-tuple-element.25), channel_id=1, source_target_pairs={{0,3},{1,0},{2,1},{3,2},{4,7},{5,4},{6,5},{7,6},{8,11},{9,8},{10,9... | collective-permute-start | bytes 491528 | tf_op jit(solution)/shard_map/ppermute | solution.py:431
  64.0 7.0 %collective-permute-start.19 = (bf16[160,512]{1,0:T(8,128)(2,1)S(1)}, bf16[160,512]{1,0:T(8,128)(2,1)S(1)}, u32[]{:S(2)}, u32[]{:S(2)}) collective-permute-start(bf16[160,512]{1,0:T(8,128)(2,1)S(1)} %get-tuple-element.26), channel_id=1, source_target_pairs={{0,2},{1,3},{2,0},{3,1},{4,6},{5,7},{6,4},{7,5},{8,10},{9,11},{10,... | collective-permute-start | bytes 491528 | tf_op jit(solution)/shard_map/ppermute | solution.py:431
  64.1 11.1 %collective-permute-start.20 = (bf16[160,512]{1,0:T(8,128)(2,1)S(1)}, bf16[160,512]{1,0:T(8,128)(2,1)S(1)}, u32[]{:S(2)}, u32[]{:S(2)}) collective-permute-start(bf16[160,512]{1,0:T(8,128)(2,1)S(1)} %get-tuple-element.27), channel_id=1, source_target_pairs={{0,1},{1,2},{2,3},{3,0},{4,5},{5,6},{6,7},{7,4},{8,9},{9,10},{10,1... | collective-permute-start | bytes 491528 | tf_op jit(solution)/shard_map/ppermute | solution.py:431

commit v8 on v7

--- a/solution.py
+++ b/solution.py
@@ -19,6 +19,7 @@
 X, Z, C = 4, 8, 2
 TAIL = 16
 COST = 1 << 20
+NEAR = (1, 3, 2)
 BATCHES = (((0, 1), (7, 2)), ((6, 3), (5, 4)))
 
 
@@ -160,28 +161,34 @@
 
 def cross_kernel(*refs):
     out_ref = refs[-1]
-    size = refs[0].shape[0] // C
-    for k in range(X):
-        out_ref[k * size : (k + 1) * size] = refs[k][size:]
+    put = 0
+    for ref in refs[: X * len(BATCHES)]:
+        size = ref.shape[0] // C
+        out_ref[put : put + size] = ref[size:]
+        put += size
 
 
 def crossing(parts, *earlier):
-    rows, latent = parts[0].shape
+    rows = sum(part.shape[0] for part in parts) // C
     return pl.pallas_call(
         cross_kernel,
-        in_specs=[VMEM] * X + [HBM] * len(earlier),
-        out_shape=jax.ShapeDtypeStruct((rows // C * X, latent), bf16),
+        in_specs=[VMEM] * len(parts) + [HBM] * len(earlier),
+        out_shape=jax.ShapeDtypeStruct((rows, parts[0].shape[1]), bf16),
         compiler_params=pltpu.CompilerParams(vmem_limit_bytes=LIMIT),
         name="crossing",
     )(*parts, *[in_hbm(part) for part in earlier])
 
 
-def fill(table_ref, put, group):
-    size = group[0].shape[0] // C
-    for k in range(X):
-        table_ref[put : put + size] = group[k][:size]
-        put += size
-    table_ref[put : put + X * size] = group[X][...]
+def fill(table_ref, parts, crossed):
+    put, taken = 0, 0
+    for at in range(len(BATCHES)):
+        group = parts[at * X : (at + 1) * X]
+        size = group[0].shape[0] // C
+        for part in group:
+            table_ref[put : put + size] = part[:size]
+            put += size
+        table_ref[put : put + X * size] = crossed[taken : taken + X * size]
+        put, taken = put + X * size, taken + X * size
 
 
 def before_kernel(extra, *refs):
@@ -243,7 +250,8 @@
 
 def after_kernel(first_row, *refs):
     live_ref, send_ref, recv_ref, gain_ref = refs[:4]
-    groups, refs = refs[4 : 6 + 2 * X], refs[6 + 2 * X :]
+    count = X * len(BATCHES)
+    parts, crossed, refs = refs[4 : 4 + count], refs[4 + count], refs[5 + count :]
     before_hbm, w1_hbm, w2_hbm, edges_hbm, out_hbm = refs[:5]
     sums_refs = refs[5:9]
     table_ref, before_ref, w1_ref, w2_ref, edges_ref, far_ref, load_sems, store_sems = refs[9:]
@@ -257,8 +265,7 @@
     ]
     for load in loads:
         load.start()
-    fill(table_ref, 0, groups[: X + 1])
-    fill(table_ref, table_ref.shape[0] // 2, groups[X + 1 :])
+    fill(table_ref, parts, crossed)
     stores = []
     live = live_ref[0]
     size = count // GATHERS
@@ -291,12 +298,12 @@
         store.wait()
 
 
-def edge_after(first_row, live, send, recv, gain, group, before, w1, w2, edges, rows):
+def edge_after(first_row, live, send, recv, gain, parts, before, w1, w2, edges, rows):
     count, latent = edges.shape
-    table = 2 * X * group[0].shape[0]
+    table = sum(part.shape[0] for part in parts[:-1]) // C + parts[-1].shape[0]
     return pl.pallas_call(
         lambda *refs: after_kernel(first_row, *refs),
-        in_specs=[SMEM] + [VMEM] * (5 + 2 * X) + [HBM] * 4,
+        in_specs=[SMEM] + [VMEM] * (3 + len(parts)) + [HBM] * 4,
         out_specs=[HBM] + [VMEM] * 4,
         out_shape=[jax.ShapeDtypeStruct((count, latent), bf16)]
         + [jax.ShapeDtypeStruct((rows, latent), f32 if k == 0 else bf16) for k in range(4)],
@@ -312,7 +319,7 @@
         ],
         compiler_params=pltpu.CompilerParams(vmem_limit_bytes=32 << 20),
         name="edge_after",
-    )(live, send, recv, gain, *group, *[in_hbm(part) for part in (before, w1, w2, edges)])
+    )(live, send, recv, gain, *parts, *[in_hbm(part) for part in (before, w1, w2, edges)])
 
 
 def node_kernel(nodes_ref, p0_ref, p1_ref, p2_ref, p3_ref, w1_ref, b1_ref, w2_ref, gain_ref, out_ref):
@@ -384,8 +391,7 @@
     forth = back = block
     for hop in range(1, 4):
         forth, back = up(forth), down(back)
-        if hop == 2:
-            forth = gate(forth, *parts[1:])
+        forth = gate(forth, parts[NEAR[hop - 1]])
         held[hop], held[Z - hop] = forth, back
     held[4] = up(forth)
 
@@ -421,9 +427,10 @@
     before = edge_before(
         recv, send.reshape(1, -1), edge_b1.reshape(1, -1), parts, edges, edge_w1, groups[1][0]
     )
-    groups = [group + [swap(crossing(group, before))] for group in groups]
+    arrived = groups[0] + groups[1]
+    arrived = arrived + [swap(crossing(arrived, before))]
     edges_out, *sums = edge_after(
-        patch, live_edges, send.reshape(-1, 1), recv, edge_gain.reshape(1, -1), groups[0] + groups[1], before,
+        patch, live_edges, send.reshape(-1, 1), recv, edge_gain.reshape(1, -1), arrived, before,
         edge_w1, edge_w2, edges, rows,
     )
     parts = [sums[0]]

time: 76.9 us -> 73.9 us (0.961)
  waiting for transfers between devices: 25.2 us -> 19 us
  starting transfers between devices: 30.9 us -> 34.3 us
    ppermute x3, waiting for transfers between devices: 7.24 us -> 0.98 us  [local(): lax.ppermute(nodes, 'feat', [(i, (i + k) % feat) for i in range(feat)])]
    ppermute x3, starting transfers between devices: 3.78 us -> 6.95 us  [local(): lax.ppermute(nodes, 'feat', [(i, (i + k) % feat) for i in range(feat)])]
    ppermute x3, starting transfers between devices: 1.53 us -> 2.43 us  [local(): lax.ppermute(sums[k], 'feat', [(i, (i - k) % feat) for i in range(feat)])]
    ppermute x15 -> x14, starting transfers between devices: 25.6 us -> 24.9 us  [moved(): return lax.ppermute(value, 'patch', pairs_of(move))]
    ppermute x15 -> x14, waiting for transfers between devices: 8.24 us -> 7.57 us  [moved(): return lax.ppermute(value, 'patch', pairs_of(move))]
  transfers between devices with their start and end apart: 21 -> 20, of which waited for: 11 -> 9; matrix products, arithmetic and copies ran while one was open for 0% -> 0% of each run, Pallas kernels for 11% -> 12%
where the time goes in v8:
time: 73.9 us; the launch traced here: 73.7 us
  starting transfers between devices  34.3 us (46%)
  waiting for transfers between devices  19 us (26%)
  Pallas kernels  18.6 us (25%)
  between operations  1.49 us (2%)
    ppermute x14, starting transfers between devices, moved(): return lax.ppermute(value, 'patch', pairs_of(move))  24.9 us
    ppermute x3, waiting for transfers between devices, local(): lax.ppermute(sums[k], 'feat', [(i, (i - k) % feat) for i in range(feat)])  10.5 us
    ppermute x14, waiting for transfers between devices, moved(): return lax.ppermute(value, 'patch', pairs_of(move))  7.57 us
    ppermute x3, starting transfers between devices, local(): lax.ppermute(nodes, 'feat', [(i, (i + k) % feat) for i in range(feat)])  6.95 us
    pallas_call x1, Pallas kernels, edge_before(): pl.pallas_call(lambda *refs: before_kernel(len(earlier), *refs), in_specs...  6.74 us
    pallas_call x1, Pallas kernels, edge_after(): pl.pallas_call(lambda *refs: after_kernel(first_row, *refs), in_specs=[SM...  6.45 us
    ppermute x3, starting transfers between devices, local(): lax.ppermute(sums[k], 'feat', [(i, (i - k) % feat) for i in range(feat)])  2.43 us
    pallas_call x2, Pallas kernels, select(): pl.pallas_call(lambda *refs: select_kernel(pairs, cap, len(earlier), *ref...  1.95 us
  transfers between devices with their start and end apart: 20, of which 9 were waited for; matrix products, arithmetic and copies ran while one was open for 0% of the time, Pallas kernels for 12%

profile of v8, /device:TPU:1, one launch (start us, length us, event | category | flops | bytes accessed | tf_op | source)
XLA Modules:
  0.0 73.7 jit_solution(12784853881539478305)
XLA Ops:
  0.6 1.9 %pack.1.refs_0_ = bf16[176,512]{1,0:T(8,128)(2,1)} custom-call(s32[1]{0:T(128)} %bitcast.1.where_ref, s32[24,64]{1,0:T(8,128)} %bitcast.12, bf16[160,512]{1,0:T(8,128)(2,1)} %nodes_ref.3), custom_call_target="tpu_custom_call" | custom-call | tf_op jit(solution)/shard_map/pack/pallas_call | solution.py:90
  2.6 0.0 copy-start.7
  2.6 0.0 copy-start.8
  2.6 0.0 copy-start
  2.6 0.0 copy-start.3
  2.6 2.5 %collective-permute-start = (bf16[176,512]{1,0:T(8,128)(2,1)}, bf16[176,512]{1,0:T(8,128)(2,1)S(1)}, u32[]{:S(2)}, u32[]{:S(2)}) collective-permute-start(bf16[176,512]{1,0:T(8,128)(2,1)} %pack.1.refs_0_), channel_id=1, source_target_pairs={{0,8},{4,12},{8,16},{12,20},{16,24},{20,28},{24,32},{28,36},{32,40... | collective-permute-start | bytes 540680 | tf_op jit(solution)/shard_map/ppermute | solution.py:358
  5.1 1.3 %collective-permute-start.1 = (bf16[160,512]{1,0:T(8,128)(2,1)}, bf16[160,512]{1,0:T(8,128)(2,1)S(1)}, u32[]{:S(2)}, u32[]{:S(2)}) collective-permute-start(bf16[160,512]{1,0:T(8,128)(2,1)} %nodes_ref.3), channel_id=1, source_target_pairs={{0,1},{1,2},{2,3},{3,0},{4,5},{5,6},{6,7},{7,4},{8,9},{9,10},{10,1... | collective-permute-start | bytes 491528 | tf_op jit(solution)/shard_map/ppermute | solution.py:387
  6.4 4.0 %collective-permute-start.2 = (bf16[176,512]{1,0:T(8,128)(2,1)}, bf16[176,512]{1,0:T(8,128)(2,1)S(1)}, u32[]{:S(2)}, u32[]{:S(2)}) collective-permute-start(bf16[176,512]{1,0:T(8,128)(2,1)} %pack.1.refs_0_), channel_id=1, source_target_pairs={{0,56},{4,60},{8,0},{12,4},{16,8},{20,12},{24,16},{28,20},{32,24},... | collective-permute-start | bytes 540680 | tf_op jit(solution)/shard_map/ppermute | solution.py:358
  10.4 1.0 %collective-permute-done.1.refs_1_.refs_4_ = bf16[160,512]{1,0:T(8,128)(2,1)S(1)} collective-permute-done((bf16[160,512]{1,0:T(8,128)(2,1)}, bf16[160,512]{1,0:T(8,128)(2,1)S(1)}, u32[]{:S(2)}, u32[]{:S(2)}) %collective-permute-start.1) | collective-permute-done | bytes 163872 | tf_op jit(solution)/shard_map/ppermute | solution.py:387
  11.4 2.1 %collective-permute-done.refs_0_ = bf16[176,512]{1,0:T(8,128)(2,1)S(1)} collective-permute-done((bf16[176,512]{1,0:T(8,128)(2,1)}, bf16[176,512]{1,0:T(8,128)(2,1)S(1)}, u32[]{:S(2)}, u32[]{:S(2)}) %collective-permute-start) | collective-permute-done | bytes 180256 | tf_op jit(solution)/shard_map/ppermute | solution.py:358
  13.5 0.0 collective-permute-start.3
  13.5 2.7 %collective-permute-start.4 = (bf16[160,512]{1,0:T(8,128)(2,1)}, bf16[160,512]{1,0:T(8,128)(2,1)S(1)}, u32[]{:S(2)}, u32[]{:S(2)}) collective-permute-start(bf16[160,512]{1,0:T(8,128)(2,1)} %nodes_ref.3), channel_id=1, source_target_pairs={{0,3},{1,0},{2,1},{3,2},{4,7},{5,4},{6,5},{7,6},{8,11},{9,8},{10,9... | collective-permute-start | bytes 491528 | tf_op jit(solution)/shard_map/ppermute | solution.py:387
  16.3 0.0 collective-permute-done.2.refs_2_
  16.3 2.7 %collective-permute-start.8 = (bf16[176,512]{1,0:T(8,128)(2,1)S(1)}, bf16[176,512]{1,0:T(8,128)(2,1)S(1)}, u32[]{:S(2)}, u32[]{:S(2)}) collective-permute-start(bf16[176,512]{1,0:T(8,128)(2,1)S(1)} %collective-permute-done.2.refs_2_), channel_id=1, source_target_pairs={{0,56},{4,60},{8,0},{12,4},{16,8},{20,12},{24,16},{28,20},{32,24},... | collective-permute-start | bytes 540680 | tf_op jit(solution)/shard_map/ppermute | solution.py:358
  19.0 0.0 collective-permute-done.4.refs_1_.refs_6_
  19.0 0.6 collective-permute-done.3.refs_0_
  19.6 0.0 collective-permute-start.9
  19.6 2.9 %collective-permute-start.10 = (bf16[160,512]{1,0:T(8,128)(2,1)}, bf16[160,512]{1,0:T(8,128)(2,1)S(1)}, u32[]{:S(2)}, u32[]{:S(2)}) collective-permute-start(bf16[160,512]{1,0:T(8,128)(2,1)} %nodes_ref.3), channel_id=1, source_target_pairs={{0,2},{1,3},{2,0},{3,1},{4,6},{5,7},{6,4},{7,5},{8,10},{9,11},{10,... | collective-permute-start | bytes 491528 | tf_op jit(solution)/shard_map/ppermute | solution.py:387
  22.5 1.3 %select.24 = (bf16[192,512]{1,0:T(8,128)(2,1)S(1)}, bf16[192,512]{1,0:T(8,128)(2,1)S(1)}, bf16[192,512]{1,0:T(8,128)(2,1)S(1)}, bf16[192,512]{1,0:T(8,128)(2,1)S(1)}) custom-call(bf16[176,512]{1,0:T(8,128)(2,1)} %pack.1.refs_0_, bf16[176,512]{1,0:T(8,128)(2,1)S(1)} %gate.3.refs_1_, bf16[176,512]{1,0:T(8,128)(2,1)S(1)} %collective-permute-done.2.refs_2_, ...), custom_call_target="tpu_custom_call" | custom-call | flops 1048576 | tf_op jit(solution)/shard_map/select/pallas_call | solution.py:134
  23.8 1.3 %collective-permute-start.5 = (bf16[192,512]{1,0:T(8,128)(2,1)S(1)}, bf16[192,512]{1,0:T(8,128)(2,1)S(1)}, u32[]{:S(2)}, u32[]{:S(2)}) collective-permute-start(bf16[192,512]{1,0:T(8,128)(2,1)S(1)} %get-tuple-element.16), channel_id=1, source_target_pairs={{0,64},{4,68},{8,72},{12,76},{16,80},{20,84},{24,88},{28,92},{32,9... | collective-permute-start | bytes 589832 | tf_op jit(solution)/shard_map/ppermute | solution.py:358
  25.1 0.0 collective-permute-done.8.refs_0_
  25.1 2.7 %collective-permute-start.11 = (bf16[176,512]{1,0:T(8,128)(2,1)S(1)}, bf16[176,512]{1,0:T(8,128)(2,1)S(1)}, u32[]{:S(2)}, u32[]{:S(2)}) collective-permute-start(bf16[176,512]{1,0:T(8,128)(2,1)S(1)} %collective-permute-done.8.refs_0_), channel_id=1, source_target_pairs={{0,56},{4,60},{8,0},{12,4},{16,8},{20,12},{24,16},{28,20},{32,24},... | collective-permute-start | bytes 540680 | tf_op jit(solution)/shard_map/ppermute | solution.py:358
  27.8 0.0 collective-permute-done.10.refs_1_.refs_5_
  27.8 0.0 collective-permute-done.9.refs_0_
  27.8 0.0 collective-permute-start.12
  27.9 2.7 %collective-permute-start.6 = (bf16[192,512]{1,0:T(8,128)(2,1)S(1)}, bf16[192,512]{1,0:T(8,128)(2,1)S(1)}, u32[]{:S(2)}, u32[]{:S(2)}) collective-permute-start(bf16[192,512]{1,0:T(8,128)(2,1)S(1)} %get-tuple-element.17), channel_id=1, source_target_pairs={{0,128},{4,132},{8,136},{12,140},{16,144},{20,148},{24,152},{28,15... | collective-permute-start | bytes 589832 | tf_op jit(solution)/shard_map/ppermute | solution.py:358
  30.6 1.0 %collective-permute-start.7 = (bf16[192,512]{1,0:T(8,128)(2,1)S(1)}, bf16[192,512]{1,0:T(8,128)(2,1)S(1)}, u32[]{:S(2)}, u32[]{:S(2)}) collective-permute-start(bf16[192,512]{1,0:T(8,128)(2,1)S(1)} %get-tuple-element.18), channel_id=1, source_target_pairs={{0,192},{4,196},{8,200},{12,204},{16,208},{20,212},{24,216},{28,22... | collective-permute-start | bytes 589832 | tf_op jit(solution)/shard_map/ppermute | solution.py:358
  31.5 0.0 collective-permute-done.11.refs_2_
  31.6 2.0 %collective-permute-done.12.refs_3_ = bf16[176,512]{1,0:T(8,128)(2,1)S(1)} collective-permute-done((bf16[176,512]{1,0:T(8,128)(2,1)S(1)}, bf16[176,512]{1,0:T(8,128)(2,1)S(1)}, u32[]{:S(2)}, u32[]{:S(2)}) %collective-permute-start.12) | collective-permute-done | bytes 180256 | tf_op jit(solution)/shard_map/ppermute | solution.py:358
  33.6 0.6 select.25
  34.2 1.1 %collective-permute-start.13 = (bf16[192,512]{1,0:T(8,128)(2,1)S(1)}, bf16[192,512]{1,0:T(8,128)(2,1)S(1)}, u32[]{:S(2)}, u32[]{:S(2)}) collective-permute-start(bf16[192,512]{1,0:T(8,128)(2,1)S(1)} %get-tuple-element.20), channel_id=1, source_target_pairs={{0,64},{4,68},{8,72},{12,76},{16,80},{20,84},{24,88},{28,92},{32,9... | collective-permute-start | bytes 589832 | tf_op jit(solution)/shard_map/ppermute | solution.py:358
  35.3 1.4 %collective-permute-start.14 = (bf16[192,512]{1,0:T(8,128)(2,1)S(1)}, bf16[192,512]{1,0:T(8,128)(2,1)S(1)}, u32[]{:S(2)}, u32[]{:S(2)}) collective-permute-start(bf16[192,512]{1,0:T(8,128)(2,1)S(1)} %get-tuple-element.21), channel_id=1, source_target_pairs={{0,128},{4,132},{8,136},{12,140},{16,144},{20,148},{24,152},{28,15... | collective-permute-start | bytes 589832 | tf_op jit(solution)/shard_map/ppermute | solution.py:358
  36.7 0.0 collective-permute-done.5.refs_1_.refs_5_
  36.7 1.9 %collective-permute-start.15 = (bf16[192,512]{1,0:T(8,128)(2,1)S(1)}, bf16[192,512]{1,0:T(8,128)(2,1)S(1)}, u32[]{:S(2)}, u32[]{:S(2)}) collective-permute-start(bf16[192,512]{1,0:T(8,128)(2,1)S(1)} %get-tuple-element.22), channel_id=1, source_target_pairs={{0,192},{4,196},{8,200},{12,204},{16,208},{20,212},{24,216},{28,22... | collective-permute-start | bytes 589832 | tf_op jit(solution)/shard_map/ppermute | solution.py:358
  38.6 0.0 copy-done.7
  38.6 0.0 copy-done.8
  38.6 0.1 fusion.4
  38.7 0.0 copy-done
  38.7 0.0 copy-done.3
  38.7 6.7 %edge_before.1.refs_8_.refs_13_ = f32[1280,512]{1,0:T(8,128)} custom-call(s32[1,1280]{1,0:T(1,128)S(1)} %reshape.29.refs_0_.refs_2_, s32[1,1280]{1,0:T(1,128)S(1)} %reshape.32.refs_1_, f32[1,512]{1,0:T(1,128)S(1)} %bitcast.8, bf16[160,512]{1,0:T(8,128)(2,1)S(1)} %copy-done, bf16[160,512]{1,0:T(8,128)(2,1)S(1)} %collective-permute-done.1.refs_1_.refs_4_, ...), custom_call_target="tpu_custom_call" | custom-call | flops 1048576 | tf_op jit(solution)/shard_map/edge_before/pallas_call | solution.py:233
  45.4 0.0 collective-permute-done.6.refs_2_.refs_6_
  45.4 0.0 collective-permute-done.7.refs_3_.refs_7_
  45.5 0.0 collective-permute-done.13.refs_5_.refs_9_
  45.5 0.0 collective-permute-done.14.refs_6_.refs_10_
  45.5 1.8 %collective-permute-done.15.refs_7_.refs_11_ = bf16[192,512]{1,0:T(8,128)(2,1)S(1)} collective-permute-done((bf16[192,512]{1,0:T(8,128)(2,1)S(1)}, bf16[192,512]{1,0:T(8,128)(2,1)S(1)}, u32[]{:S(2)}, u32[]{:S(2)}) %collective-permute-start.15) | collective-permute-done | bytes 196640 | tf_op jit(solution)/shard_map/ppermute | solution.py:358
  47.2 0.0 copy-start.4
  47.2 0.1 crossing.1
  47.3 3.6 %collective-permute-start.16 = (bf16[768,512]{1,0:T(8,128)(2,1)S(1)}, bf16[768,512]{1,0:T(8,128)(2,1)S(1)}, u32[]{:S(2)}, u32[]{:S(2)}) collective-permute-start(bf16[768,512]{1,0:T(8,128)(2,1)S(1)} %crossing.1), channel_id=1, source_target_pairs={{0,4},{4,0},{8,12},{12,8},{16,20},{20,16},{24,28},{28,24},{32,36},... | collective-permute-start | bytes 2359304 | tf_op jit(solution)/shard_map/ppermute | solution.py:358
  50.9 0.2 reshape.36.refs_1_
  51.8 1.0 %collective-permute-done.16.refs_12_ = bf16[768,512]{1,0:T(8,128)(2,1)S(1)} collective-permute-done((bf16[768,512]{1,0:T(8,128)(2,1)S(1)}, bf16[768,512]{1,0:T(8,128)(2,1)S(1)}, u32[]{:S(2)}, u32[]{:S(2)}) %collective-permute-start.16) | collective-permute-done | bytes 786464 | tf_op jit(solution)/shard_map/ppermute | solution.py:358
  52.8 0.0 copy-done.4
  52.8 0.0 copy-start.6
  52.9 6.5 %edge_after.1 = (bf16[1280,512]{1,0:T(8,128)(2,1)}, f32[160,512]{1,0:T(8,128)S(1)}, bf16[160,512]{1,0:T(8,128)(2,1)S(1)}, bf16[160,512]{1,0:T(8,128)(2,1)S(1)}, bf16[160,512]{1,0:T(8,128)(2,1)S(1)}) custom-call(s32[1]{0:T(128)S(6)} %copy.23.refs_0_, s32[1280,1]{1,0:T(8,128)S(1)} %reshape.36.refs_1_, s32[1,1280]{1,0:T(1,128)S(1)} %reshape.29.refs_0_.refs_2_, ...), custom_call_target="tpu_custom_call" | custom-call | tf_op jit(solution)/shard_map/edge_after/pallas_call | solution.py:304
  59.3 1.8 %collective-permute-start.17 = (bf16[160,512]{1,0:T(8,128)(2,1)S(1)}, bf16[160,512]{1,0:T(8,128)(2,1)S(1)}, u32[]{:S(2)}, u32[]{:S(2)}) collective-permute-start(bf16[160,512]{1,0:T(8,128)(2,1)S(1)} %get-tuple-element.25), channel_id=1, source_target_pairs={{0,3},{1,0},{2,1},{3,2},{4,7},{5,4},{6,5},{7,6},{8,11},{9,8},{10,9... | collective-permute-start | bytes 491528 | tf_op jit(solution)/shard_map/ppermute | solution.py:438
  61.1 0.5 collective-permute-start.18
  61.6 0.2 collective-permute-start.19
  61.7 3.1 %collective-permute-done.17.p1_ref = bf16[160,512]{1,0:T(8,128)(2,1)S(1)} collective-permute-done((bf16[160,512]{1,0:T(8,128)(2,1)S(1)}, bf16[160,512]{1,0:T(8,128)(2,1)S(1)}, u32[]{:S(2)}, u32[]{:S(2)}) %collective-permute-start.17) | collective-permute-done | bytes 163872 | tf_op jit(solution)/shard_map/ppermute | solution.py:438
  64.8 2.9 %collective-permute-done.18.p2_ref = bf16[160,512]{1,0:T(8,128)(2,1)S(1)} collective-permute-done((bf16[160,512]{1,0:T(8,128)(2,1)S(1)}, bf16[160,512]{1,0:T(8,128)(2,1)S(1)}, u32[]{:S(2)}, u32[]{:S(2)}) %collective-permute-start.18) | collective-permute-done | bytes 163872 | tf_op jit(solution)/shard_map/ppermute | solution.py:438
  67.7 4.5 %collective-permute-done.19.p3_ref = bf16[160,512]{1,0:T(8,128)(2,1)S(1)} collective-permute-done((bf16[160,512]{1,0:T(8,128)(2,1)S(1)}, bf16[160,512]{1,0:T(8,128)(2,1)S(1)}, u32[]{:S(2)}, u32[]{:S(2)}) %collective-permute-start.19) | collective-permute-done | bytes 163872 | tf_op jit(solution)/shard_map/ppermute | solution.py:438
  72.2 0.0 copy-done.1
  72.2 0.0 copy-done.2
  72.2 0.0 copy-done.5
  72.2 0.0 copy-done.6
  72.2 1.5 %node_update.1 = bf16[160,512]{1,0:T(8,128)(2,1)} custom-call(bf16[160,512]{1,0:T(8,128)(2,1)S(1)} %copy-done, f32[160,512]{1,0:T(8,128)S(1)} %get-tuple-element.24.p0_ref, bf16[160,512]{1,0:T(8,128)(2,1)S(1)} %collective-permute-done.17.p1_ref, bf16[160,512]{1,0:T(8,128)(2,1)S(1)} %collective-permute-done.18.p2_ref, ...), custom_call_target="tpu_custom_call" | custom-call | tf_op jit(solution)/shard_map/node_update/pallas_call | solution.py:338
  (8 shorter events, 0.0 us)
Async XLA Ops:
  2.6 36.0 %copy-start.7 = (s32[1280]{0:T(1024)S(1)}, s32[1280]{0:T(1024)}, u32[]{:S(2)}) copy-start(s32[1280]{0:T(1024)} %param.17) | copy-start | bytes 15364
  2.6 36.0 %copy-start.8 = (s32[1280]{0:T(1024)S(1)}, s32[1280]{0:T(1024)}, u32[]{:S(2)}) copy-start(s32[1280]{0:T(1024)} %param.16) | copy-start | bytes 15364
  2.6 36.1 %copy-start = (bf16[160,512]{1,0:T(8,128)(2,1)S(1)}, bf16[160,512]{1,0:T(8,128)(2,1)}, u32[]{:S(2)}) copy-start(bf16[160,512]{1,0:T(8,128)(2,1)} %nodes_ref.3) | copy-start | bytes 491524
  2.6 36.1 %copy-start.3 = (f32[512]{0:T(512)S(1)}, f32[512]{0:T(512)}, u32[]{:S(2)}) copy-start(f32[512]{0:T(512)} %param.21) | copy-start | bytes 6148
  2.6 11.0 %collective-permute-start = (bf16[176,512]{1,0:T(8,128)(2,1)}, bf16[176,512]{1,0:T(8,128)(2,1)S(1)}, u32[]{:S(2)}, u32[]{:S(2)}) collective-permute-start(bf16[176,512]{1,0:T(8,128)(2,1)} %pack.1.refs_0_), channel_id=1, source_target_pairs={{0,8},{4,12},{8,16},{12,20},{16,24},{20,28},{24,32},{28,36},{32,40... | collective-permute-start | bytes 540680 | tf_op jit(solution)/shard_map/ppermute | solution.py:358
  5.1 6.3 %collective-permute-start.1 = (bf16[160,512]{1,0:T(8,128)(2,1)}, bf16[160,512]{1,0:T(8,128)(2,1)S(1)}, u32[]{:S(2)}, u32[]{:S(2)}) collective-permute-start(bf16[160,512]{1,0:T(8,128)(2,1)} %nodes_ref.3), channel_id=1, source_target_pairs={{0,1},{1,2},{2,3},{3,0},{4,5},{5,6},{6,7},{7,4},{8,9},{9,10},{10,1... | collective-permute-start | bytes 491528 | tf_op jit(solution)/shard_map/ppermute | solution.py:387
  6.4 9.9 %collective-permute-start.2 = (bf16[176,512]{1,0:T(8,128)(2,1)}, bf16[176,512]{1,0:T(8,128)(2,1)S(1)}, u32[]{:S(2)}, u32[]{:S(2)}) collective-permute-start(bf16[176,512]{1,0:T(8,128)(2,1)} %pack.1.refs_0_), channel_id=1, source_target_pairs={{0,56},{4,60},{8,0},{12,4},{16,8},{20,12},{24,16},{28,20},{32,24},... | collective-permute-start | bytes 540680 | tf_op jit(solution)/shard_map/ppermute | solution.py:358
  13.5 6.0 %collective-permute-start.3 = (bf16[176,512]{1,0:T(8,128)(2,1)S(1)}, bf16[176,512]{1,0:T(8,128)(2,1)S(1)}, u32[]{:S(2)}, u32[]{:S(2)}) collective-permute-start(bf16[176,512]{1,0:T(8,128)(2,1)S(1)} %gate.3.refs_1_), channel_id=1, source_target_pairs={{0,8},{4,12},{8,16},{12,20},{16,24},{20,28},{24,32},{28,36},{32,40... | collective-permute-start | bytes 540680 | tf_op jit(solution)/shard_map/ppermute | solution.py:358
  13.5 5.4 %collective-permute-start.4 = (bf16[160,512]{1,0:T(8,128)(2,1)}, bf16[160,512]{1,0:T(8,128)(2,1)S(1)}, u32[]{:S(2)}, u32[]{:S(2)}) collective-permute-start(bf16[160,512]{1,0:T(8,128)(2,1)} %nodes_ref.3), channel_id=1, source_target_pairs={{0,3},{1,0},{2,1},{3,2},{4,7},{5,4},{6,5},{7,6},{8,11},{9,8},{10,9... | collective-permute-start | bytes 491528 | tf_op jit(solution)/shard_map/ppermute | solution.py:387
  16.3 8.8 %collective-permute-start.8 = (bf16[176,512]{1,0:T(8,128)(2,1)S(1)}, bf16[176,512]{1,0:T(8,128)(2,1)S(1)}, u32[]{:S(2)}, u32[]{:S(2)}) collective-permute-start(bf16[176,512]{1,0:T(8,128)(2,1)S(1)} %collective-permute-done.2.refs_2_), channel_id=1, source_target_pairs={{0,56},{4,60},{8,0},{12,4},{16,8},{20,12},{24,16},{28,20},{32,24},... | collective-permute-start | bytes 540680 | tf_op jit(solution)/shard_map/ppermute | solution.py:358
  19.6 8.2 %collective-permute-start.9 = (bf16[176,512]{1,0:T(8,128)(2,1)S(1)}, bf16[176,512]{1,0:T(8,128)(2,1)S(1)}, u32[]{:S(2)}, u32[]{:S(2)}) collective-permute-start(bf16[176,512]{1,0:T(8,128)(2,1)S(1)} %gate.4.refs_3_), channel_id=1, source_target_pairs={{0,8},{4,12},{8,16},{12,20},{16,24},{20,28},{24,32},{28,36},{32,40... | collective-permute-start | bytes 540680 | tf_op jit(solution)/shard_map/ppermute | solution.py:358
  19.6 8.2 %collective-permute-start.10 = (bf16[160,512]{1,0:T(8,128)(2,1)}, bf16[160,512]{1,0:T(8,128)(2,1)S(1)}, u32[]{:S(2)}, u32[]{:S(2)}) collective-permute-start(bf16[160,512]{1,0:T(8,128)(2,1)} %nodes_ref.3), channel_id=1, source_target_pairs={{0,2},{1,3},{2,0},{3,1},{4,6},{5,7},{6,4},{7,5},{8,10},{9,11},{10,... | collective-permute-start | bytes 491528 | tf_op jit(solution)/shard_map/ppermute | solution.py:387
  23.8 12.9 %collective-permute-start.5 = (bf16[192,512]{1,0:T(8,128)(2,1)S(1)}, bf16[192,512]{1,0:T(8,128)(2,1)S(1)}, u32[]{:S(2)}, u32[]{:S(2)}) collective-permute-start(bf16[192,512]{1,0:T(8,128)(2,1)S(1)} %get-tuple-element.16), channel_id=1, source_target_pairs={{0,64},{4,68},{8,72},{12,76},{16,80},{20,84},{24,88},{28,92},{32,9... | collective-permute-start | bytes 589832 | tf_op jit(solution)/shard_map/ppermute | solution.py:358
  25.1 6.4 %collective-permute-start.11 = (bf16[176,512]{1,0:T(8,128)(2,1)S(1)}, bf16[176,512]{1,0:T(8,128)(2,1)S(1)}, u32[]{:S(2)}, u32[]{:S(2)}) collective-permute-start(bf16[176,512]{1,0:T(8,128)(2,1)S(1)} %collective-permute-done.8.refs_0_), channel_id=1, source_target_pairs={{0,56},{4,60},{8,0},{12,4},{16,8},{20,12},{24,16},{28,20},{32,24},... | collective-permute-start | bytes 540680 | tf_op jit(solution)/shard_map/ppermute | solution.py:358
  27.8 5.8 %collective-permute-start.12 = (bf16[176,512]{1,0:T(8,128)(2,1)S(1)}, bf16[176,512]{1,0:T(8,128)(2,1)S(1)}, u32[]{:S(2)}, u32[]{:S(2)}) collective-permute-start(bf16[176,512]{1,0:T(8,128)(2,1)S(1)} %gate.5.refs_1_), channel_id=1, source_target_pairs={{0,8},{4,12},{8,16},{12,20},{16,24},{20,28},{24,32},{28,36},{32,40... | collective-permute-start | bytes 540680 | tf_op jit(solution)/shard_map/ppermute | solution.py:358
  27.9 17.6 %collective-permute-start.6 = (bf16[192,512]{1,0:T(8,128)(2,1)S(1)}, bf16[192,512]{1,0:T(8,128)(2,1)S(1)}, u32[]{:S(2)}, u32[]{:S(2)}) collective-permute-start(bf16[192,512]{1,0:T(8,128)(2,1)S(1)} %get-tuple-element.17), channel_id=1, source_target_pairs={{0,128},{4,132},{8,136},{12,140},{16,144},{20,148},{24,152},{28,15... | collective-permute-start | bytes 589832 | tf_op jit(solution)/shard_map/ppermute | solution.py:358
  30.6 14.9 %collective-permute-start.7 = (bf16[192,512]{1,0:T(8,128)(2,1)S(1)}, bf16[192,512]{1,0:T(8,128)(2,1)S(1)}, u32[]{:S(2)}, u32[]{:S(2)}) collective-permute-start(bf16[192,512]{1,0:T(8,128)(2,1)S(1)} %get-tuple-element.18), channel_id=1, source_target_pairs={{0,192},{4,196},{8,200},{12,204},{16,208},{20,212},{24,216},{28,22... | collective-permute-start | bytes 589832 | tf_op jit(solution)/shard_map/ppermute | solution.py:358
  34.2 11.3 %collective-permute-start.13 = (bf16[192,512]{1,0:T(8,128)(2,1)S(1)}, bf16[192,512]{1,0:T(8,128)(2,1)S(1)}, u32[]{:S(2)}, u32[]{:S(2)}) collective-permute-start(bf16[192,512]{1,0:T(8,128)(2,1)S(1)} %get-tuple-element.20), channel_id=1, source_target_pairs={{0,64},{4,68},{8,72},{12,76},{16,80},{20,84},{24,88},{28,92},{32,9... | collective-permute-start | bytes 589832 | tf_op jit(solution)/shard_map/ppermute | solution.py:358
  35.3 10.2 %collective-permute-start.14 = (bf16[192,512]{1,0:T(8,128)(2,1)S(1)}, bf16[192,512]{1,0:T(8,128)(2,1)S(1)}, u32[]{:S(2)}, u32[]{:S(2)}) collective-permute-start(bf16[192,512]{1,0:T(8,128)(2,1)S(1)} %get-tuple-element.21), channel_id=1, source_target_pairs={{0,128},{4,132},{8,136},{12,140},{16,144},{20,148},{24,152},{28,15... | collective-permute-start | bytes 589832 | tf_op jit(solution)/shard_map/ppermute | solution.py:358
  36.7 10.5 %collective-permute-start.15 = (bf16[192,512]{1,0:T(8,128)(2,1)S(1)}, bf16[192,512]{1,0:T(8,128)(2,1)S(1)}, u32[]{:S(2)}, u32[]{:S(2)}) collective-permute-start(bf16[192,512]{1,0:T(8,128)(2,1)S(1)} %get-tuple-element.22), channel_id=1, source_target_pairs={{0,192},{4,196},{8,200},{12,204},{16,208},{20,212},{24,216},{28,22... | collective-permute-start | bytes 589832 | tf_op jit(solution)/shard_map/ppermute | solution.py:358
  47.2 5.6 %copy-start.4 = (f32[512]{0:T(512)S(1)}, f32[512]{0:T(512)}, u32[]{:S(2)}) copy-start(f32[512]{0:T(512)} %param.23) | copy-start | bytes 6148
  47.3 5.5 %collective-permute-start.16 = (bf16[768,512]{1,0:T(8,128)(2,1)S(1)}, bf16[768,512]{1,0:T(8,128)(2,1)S(1)}, u32[]{:S(2)}, u32[]{:S(2)}) collective-permute-start(bf16[768,512]{1,0:T(8,128)(2,1)S(1)} %crossing.1), channel_id=1, source_target_pairs={{0,4},{4,0},{8,12},{12,8},{16,20},{20,16},{24,28},{28,24},{32,36},... | collective-permute-start | bytes 2359304 | tf_op jit(solution)/shard_map/ppermute | solution.py:358
  52.8 19.4 %copy-start.1 = (bf16[1024,512]{1,0:T(8,128)(2,1)S(1)}, bf16[1024,512]{1,0:T(8,128)(2,1)}, u32[]{:S(2)}) copy-start(bf16[1024,512]{1,0:T(8,128)(2,1)} %w1_ref.1) | copy-start | bytes 3145732
  52.8 19.4 %copy-start.2 = (bf16[512,512]{1,0:T(8,128)(2,1)S(1)}, bf16[512,512]{1,0:T(8,128)(2,1)}, u32[]{:S(2)}) copy-start(bf16[512,512]{1,0:T(8,128)(2,1)} %w2_ref.1) | copy-start | bytes 1572868
  52.8 19.4 %copy-start.5 = (f32[512]{0:T(512)S(1)}, f32[512]{0:T(512)}, u32[]{:S(2)}) copy-start(f32[512]{0:T(512)} %param.25) | copy-start | bytes 6148
  52.8 19.4 %copy-start.6 = (f32[512]{0:T(512)S(1)}, f32[512]{0:T(512)}, u32[]{:S(2)}) copy-start(f32[512]{0:T(512)} %param.27) | copy-start | bytes 6148
  59.3 5.5 %collective-permute-start.17 = (bf16[160,512]{1,0:T(8,128)(2,1)S(1)}, bf16[160,512]{1,0:T(8,128)(2,1)S(1)}, u32[]{:S(2)}, u32[]{:S(2)}) collective-permute-start(bf16[160,512]{1,0:T(8,128)(2,1)S(1)} %get-tuple-element.25), channel_id=1, source_target_pairs={{0,3},{1,0},{2,1},{3,2},{4,7},{5,4},{6,5},{7,6},{8,11},{9,8},{10,9... | collective-permute-start | bytes 491528 | tf_op jit(solution)/shard_map/ppermute | solution.py:438
  61.1 6.6 %collective-permute-start.18 = (bf16[160,512]{1,0:T(8,128)(2,1)S(1)}, bf16[160,512]{1,0:T(8,128)(2,1)S(1)}, u32[]{:S(2)}, u32[]{:S(2)}) collective-permute-start(bf16[160,512]{1,0:T(8,128)(2,1)S(1)} %get-tuple-element.26), channel_id=1, source_target_pairs={{0,2},{1,3},{2,0},{3,1},{4,6},{5,7},{6,4},{7,5},{8,10},{9,11},{10,... | collective-permute-start | bytes 491528 | tf_op jit(solution)/shard_map/ppermute | solution.py:438
  61.6 10.6 %collective-permute-start.19 = (bf16[160,512]{1,0:T(8,128)(2,1)S(1)}, bf16[160,512]{1,0:T(8,128)(2,1)S(1)}, u32[]{:S(2)}, u32[]{:S(2)}) collective-permute-start(bf16[160,512]{1,0:T(8,128)(2,1)S(1)} %get-tuple-element.27), channel_id=1, source_target_pairs={{0,1},{1,2},{2,3},{3,0},{4,5},{5,6},{6,7},{7,4},{8,9},{9,10},{10,1... | collective-permute-start | bytes 491528 | tf_op jit(solution)/shard_map/ppermute | solution.py:438

commit v9 on v8

--- a/solution.py
+++ b/solution.py
@@ -64,10 +64,11 @@
     return (dz >= 1) & (dz <= 4)
 
 
-def pack_kernel(where_ref, lists_ref, nodes_ref, out_ref):
-    rows, latent = nodes_ref.shape
+def pack_kernel(where_ref, lists_ref, nodes_hbm, out_hbm, tail_ref, sems):
+    rows, latent = nodes_hbm.shape
     cap, peers = lists_ref.shape
-    out_ref[:rows] = nodes_ref[...]
+    body = pltpu.make_async_copy(nodes_hbm, out_hbm.at[pl.ds(0, rows)], sems.at[0])
+    body.start()
     me = where_ref[0]
     x, z, c = me // (Z * C), me // C % Z, me % C
     lane = lax.broadcasted_iota(i32, (cap, latent), 1)
@@ -83,16 +84,22 @@
     row = lax.broadcasted_iota(i32, (TAIL, peers), 0)
     peer = lax.broadcasted_iota(i32, (TAIL, peers), 1)
     pick = as_bf16(row == ((peer // C % Z - z) & (Z - 1)))
-    out_ref[rows:] = (dot(pick, listed) - 1.0).astype(bf16)
+    tail_ref[...] = (dot(pick, listed) - 1.0).astype(bf16)
+    tail = pltpu.make_async_copy(tail_ref, out_hbm.at[pl.ds(rows, TAIL)], sems.at[1])
+    tail.start()
+    tail.wait()
+    body.wait()
 
 
 def pack(me, lists, nodes):
     return pl.pallas_call(
         pack_kernel,
-        in_specs=[SMEM, VMEM, VMEM],
-        out_shape=jax.ShapeDtypeStruct((nodes.shape[0] + TAIL, nodes.shape[1]), bf16),
+        in_specs=[SMEM, VMEM, HBM],
+        out_specs=HBM,
+        out_shape=pltpu.HBM((nodes.shape[0] + TAIL, nodes.shape[1]), bf16),
+        scratch_shapes=[pltpu.VMEM((TAIL, nodes.shape[1]), bf16), pltpu.SemaphoreType.DMA((2,))],
         name="pack",
-    )(me, lists, nodes)
+    )(me, lists, in_hbm(nodes))
 
 
 def select_kernel(pairs, cap, extra, *refs):
@@ -382,9 +389,11 @@
     feat = lax.axis_size("feat")
 
     block = pack(me.reshape(1), send_rows[0, 0].T, nodes)
-    parts = [nodes]
-    for k in range(1, feat):
-        parts.append(lax.ppermute(nodes, "feat", [(i, (i + k) % feat) for i in range(feat)]))
+    def around(value, k):
+        return lax.ppermute(value, "feat", [(i, (i + k) % feat) for i in range(feat)])
+
+    after_one = around(nodes, 1)
+    parts = [nodes, after_one, around(after_one, 1), around(nodes, feat - 1)]
     up = lambda a: moved(a, lambda x, z, c: (x, z + 1, c))
     down = lambda a: moved(a, lambda x, z, c: (x, z - 1, c))
     held = {0: block}

time: 73.9 us -> 78 us (1.055)
  Pallas kernels: 18.6 us -> 23.4 us
  waiting for transfers between devices: 19 us -> 17.1 us
  starting transfers between devices: 34.3 us -> 35.4 us
    pallas_call x1, Pallas kernels: 1.92 us -> 6.79 us  [pack(): pl.pallas_call(pack_kernel, in_specs=[SMEM, VMEM, HBM], out_specs=HBM, ou...]
    ppermute x14, starting transfers between devices: 24.9 us -> 27.4 us  [moved(): return lax.ppermute(value, 'patch', pairs_of(move))]
    ppermute x3, starting transfers between devices: 6.95 us -> 5.33 us  [around(): lax.ppermute(value, 'feat', [(i, (i + k) % feat) for i in range(feat)])]
    ppermute x14, waiting for transfers between devices: 7.57 us -> 6.06 us  [moved(): return lax.ppermute(value, 'patch', pairs_of(move))]
  transfers between devices with their start and end apart: 20 -> 20, of which waited for: 9 -> 9; matrix products, arithmetic and copies ran while one was open for 0% -> 0% of each run, Pallas kernels for 12% -> 11%
where the time goes in v9:
time: 78 us; the launch traced here: 77.7 us
  starting transfers between devices  35.4 us (45%)
  Pallas kernels  23.4 us (30%)
  waiting for transfers between devices  17.1 us (22%)
  between operations  1.49 us (2%)
    ppermute x14, starting transfers between devices, moved(): return lax.ppermute(value, 'patch', pairs_of(move))  27.4 us
    ppermute x3, waiting for transfers between devices, local(): lax.ppermute(sums[k], 'feat', [(i, (i - k) % feat) for i in range(feat)])  10.1 us
    pallas_call x1, Pallas kernels, pack(): pl.pallas_call(pack_kernel, in_specs=[SMEM, VMEM, HBM], out_specs=HBM, ou...  6.79 us
    pallas_call x1, Pallas kernels, edge_before(): pl.pallas_call(lambda *refs: before_kernel(len(earlier), *refs), in_specs...  6.74 us
    pallas_call x1, Pallas kernels, edge_after(): pl.pallas_call(lambda *refs: after_kernel(first_row, *refs), in_specs=[SM...  6.45 us
    ppermute x14, waiting for transfers between devices, moved(): return lax.ppermute(value, 'patch', pairs_of(move))  6.06 us
    ppermute x3, starting transfers between devices, around(): lax.ppermute(value, 'feat', [(i, (i + k) % feat) for i in range(feat)])  5.33 us
    ppermute x3, starting transfers between devices, local(): lax.ppermute(sums[k], 'feat', [(i, (i - k) % feat) for i in range(feat)])  2.66 us
  transfers between devices with their start and end apart: 20, of which 9 were waited for; matrix products, arithmetic and copies ran while one was open for 0% of the time, Pallas kernels for 11%

profile of v9, /device:TPU:1, one launch (start us, length us, event | category | flops | bytes accessed | tf_op | source)
XLA Modules:
  0.0 77.7 jit_solution(3361998631102695815)
XLA Ops:
  0.6 6.8 %pack.1.refs_0_ = bf16[176,512]{1,0:T(8,128)(2,1)} custom-call(s32[1]{0:T(128)} %bitcast.1.where_ref, s32[24,64]{1,0:T(8,128)} %bitcast.12, bf16[160,512]{1,0:T(8,128)(2,1)} %nodes_ref.1), custom_call_target="tpu_custom_call" | custom-call | tf_op jit(solution)/shard_map/pack/pallas_call | solution.py:95
  7.4 0.0 copy-start.7
  7.4 0.0 copy-start.8
  7.5 0.0 copy-start
  7.5 0.0 copy-start.3
  7.5 2.5 %collective-permute-start = (bf16[176,512]{1,0:T(8,128)(2,1)}, bf16[176,512]{1,0:T(8,128)(2,1)S(1)}, u32[]{:S(2)}, u32[]{:S(2)}) collective-permute-start(bf16[176,512]{1,0:T(8,128)(2,1)} %pack.1.refs_0_), channel_id=1, source_target_pairs={{0,8},{4,12},{8,16},{12,20},{16,24},{20,28},{24,32},{28,36},{32,40... | collective-permute-start | bytes 540680 | tf_op jit(solution)/shard_map/ppermute | solution.py:365
  10.0 1.3 %collective-permute-start.1 = (bf16[160,512]{1,0:T(8,128)(2,1)}, bf16[160,512]{1,0:T(8,128)(2,1)S(1)}, u32[]{:S(2)}, u32[]{:S(2)}) collective-permute-start(bf16[160,512]{1,0:T(8,128)(2,1)} %nodes_ref.1), channel_id=1, source_target_pairs={{0,1},{1,2},{2,3},{3,0},{4,5},{5,6},{6,7},{7,4},{8,9},{9,10},{10,1... | collective-permute-start | bytes 491528 | tf_op jit(solution)/shard_map/ppermute | solution.py:393
  11.3 4.0 %collective-permute-start.2 = (bf16[176,512]{1,0:T(8,128)(2,1)}, bf16[176,512]{1,0:T(8,128)(2,1)S(1)}, u32[]{:S(2)}, u32[]{:S(2)}) collective-permute-start(bf16[176,512]{1,0:T(8,128)(2,1)} %pack.1.refs_0_), channel_id=1, source_target_pairs={{0,56},{4,60},{8,0},{12,4},{16,8},{20,12},{24,16},{28,20},{32,24},... | collective-permute-start | bytes 540680 | tf_op jit(solution)/shard_map/ppermute | solution.py:365
  15.3 1.0 %collective-permute-done.1.refs_1_.refs_4_ = bf16[160,512]{1,0:T(8,128)(2,1)S(1)} collective-permute-done((bf16[160,512]{1,0:T(8,128)(2,1)}, bf16[160,512]{1,0:T(8,128)(2,1)S(1)}, u32[]{:S(2)}, u32[]{:S(2)}) %collective-permute-start.1) | collective-permute-done | bytes 163872 | tf_op jit(solution)/shard_map/ppermute | solution.py:393
  16.3 2.1 %collective-permute-done.refs_0_ = bf16[176,512]{1,0:T(8,128)(2,1)S(1)} collective-permute-done((bf16[176,512]{1,0:T(8,128)(2,1)}, bf16[176,512]{1,0:T(8,128)(2,1)S(1)}, u32[]{:S(2)}, u32[]{:S(2)}) %collective-permute-start) | collective-permute-done | bytes 180256 | tf_op jit(solution)/shard_map/ppermute | solution.py:365
  18.4 0.0 collective-permute-start.3
  18.5 2.7 %collective-permute-start.4 = (bf16[160,512]{1,0:T(8,128)(2,1)}, bf16[160,512]{1,0:T(8,128)(2,1)S(1)}, u32[]{:S(2)}, u32[]{:S(2)}) collective-permute-start(bf16[160,512]{1,0:T(8,128)(2,1)} %nodes_ref.1), channel_id=1, source_target_pairs={{0,3},{1,0},{2,1},{3,2},{4,7},{5,4},{6,5},{7,6},{8,11},{9,8},{10,9... | collective-permute-start | bytes 491528 | tf_op jit(solution)/shard_map/ppermute | solution.py:393
  21.2 0.0 collective-permute-done.2.refs_2_
  21.2 2.7 %collective-permute-start.8 = (bf16[176,512]{1,0:T(8,128)(2,1)S(1)}, bf16[176,512]{1,0:T(8,128)(2,1)S(1)}, u32[]{:S(2)}, u32[]{:S(2)}) collective-permute-start(bf16[176,512]{1,0:T(8,128)(2,1)S(1)} %collective-permute-done.2.refs_2_), channel_id=1, source_target_pairs={{0,56},{4,60},{8,0},{12,4},{16,8},{20,12},{24,16},{28,20},{32,24},... | collective-permute-start | bytes 540680 | tf_op jit(solution)/shard_map/ppermute | solution.py:365
  23.9 0.0 collective-permute-done.4.refs_1_.refs_6_
  23.9 0.6 collective-permute-done.3.refs_0_
  24.5 0.0 collective-permute-start.9
  24.5 1.3 %collective-permute-start.10 = (bf16[160,512]{1,0:T(8,128)(2,1)S(1)}, bf16[160,512]{1,0:T(8,128)(2,1)S(1)}, u32[]{:S(2)}, u32[]{:S(2)}) collective-permute-start(bf16[160,512]{1,0:T(8,128)(2,1)S(1)} %collective-permute-done.1.refs_1_.refs_4_), channel_id=1, source_target_pairs={{0,1},{1,2},{2,3},{3,0},{4,5},{5,6},{6,7},{7,4},{8,9},{9,10},{10,1... | collective-permute-start | bytes 491528 | tf_op jit(solution)/shard_map/ppermute | solution.py:393
  25.8 1.3 %select.24 = (bf16[192,512]{1,0:T(8,128)(2,1)S(1)}, bf16[192,512]{1,0:T(8,128)(2,1)S(1)}, bf16[192,512]{1,0:T(8,128)(2,1)S(1)}, bf16[192,512]{1,0:T(8,128)(2,1)S(1)}) custom-call(bf16[176,512]{1,0:T(8,128)(2,1)} %pack.1.refs_0_, bf16[176,512]{1,0:T(8,128)(2,1)S(1)} %gate.3.refs_1_, bf16[176,512]{1,0:T(8,128)(2,1)S(1)} %collective-permute-done.2.refs_2_, ...), custom_call_target="tpu_custom_call" | custom-call | flops 1048576 | tf_op jit(solution)/shard_map/select/pallas_call | solution.py:141
  27.1 1.3 %collective-permute-start.5 = (bf16[192,512]{1,0:T(8,128)(2,1)S(1)}, bf16[192,512]{1,0:T(8,128)(2,1)S(1)}, u32[]{:S(2)}, u32[]{:S(2)}) collective-permute-start(bf16[192,512]{1,0:T(8,128)(2,1)S(1)} %get-tuple-element.16), channel_id=1, source_target_pairs={{0,64},{4,68},{8,72},{12,76},{16,80},{20,84},{24,88},{28,92},{32,9... | collective-permute-start | bytes 589832 | tf_op jit(solution)/shard_map/ppermute | solution.py:365
  28.4 0.0 collective-permute-done.8.refs_0_
  28.4 2.7 %collective-permute-start.11 = (bf16[176,512]{1,0:T(8,128)(2,1)S(1)}, bf16[176,512]{1,0:T(8,128)(2,1)S(1)}, u32[]{:S(2)}, u32[]{:S(2)}) collective-permute-start(bf16[176,512]{1,0:T(8,128)(2,1)S(1)} %collective-permute-done.8.refs_0_), channel_id=1, source_target_pairs={{0,56},{4,60},{8,0},{12,4},{16,8},{20,12},{24,16},{28,20},{32,24},... | collective-permute-start | bytes 540680 | tf_op jit(solution)/shard_map/ppermute | solution.py:365
  31.1 0.0 collective-permute-done.10.refs_1_.refs_5_
  31.1 0.0 collective-permute-done.9.refs_0_
  31.1 1.1 %collective-permute-start.12 = (bf16[176,512]{1,0:T(8,128)(2,1)S(1)}, bf16[176,512]{1,0:T(8,128)(2,1)S(1)}, u32[]{:S(2)}, u32[]{:S(2)}) collective-permute-start(bf16[176,512]{1,0:T(8,128)(2,1)S(1)} %gate.5.refs_1_), channel_id=1, source_target_pairs={{0,8},{4,12},{8,16},{12,20},{16,24},{20,28},{24,32},{28,36},{32,40... | collective-permute-start | bytes 540680 | tf_op jit(solution)/shard_map/ppermute | solution.py:365
  32.2 2.7 %collective-permute-start.6 = (bf16[192,512]{1,0:T(8,128)(2,1)S(1)}, bf16[192,512]{1,0:T(8,128)(2,1)S(1)}, u32[]{:S(2)}, u32[]{:S(2)}) collective-permute-start(bf16[192,512]{1,0:T(8,128)(2,1)S(1)} %get-tuple-element.17), channel_id=1, source_target_pairs={{0,128},{4,132},{8,136},{12,140},{16,144},{20,148},{24,152},{28,15... | collective-permute-start | bytes 589832 | tf_op jit(solution)/shard_map/ppermute | solution.py:365
  35.0 0.9 %collective-permute-start.7 = (bf16[192,512]{1,0:T(8,128)(2,1)S(1)}, bf16[192,512]{1,0:T(8,128)(2,1)S(1)}, u32[]{:S(2)}, u32[]{:S(2)}) collective-permute-start(bf16[192,512]{1,0:T(8,128)(2,1)S(1)} %get-tuple-element.18), channel_id=1, source_target_pairs={{0,192},{4,196},{8,200},{12,204},{16,208},{20,212},{24,216},{28,22... | collective-permute-start | bytes 589832 | tf_op jit(solution)/shard_map/ppermute | solution.py:365
  35.8 0.0 collective-permute-done.11.refs_2_
  35.8 0.8 %collective-permute-done.12.refs_3_ = bf16[176,512]{1,0:T(8,128)(2,1)S(1)} collective-permute-done((bf16[176,512]{1,0:T(8,128)(2,1)S(1)}, bf16[176,512]{1,0:T(8,128)(2,1)S(1)}, u32[]{:S(2)}, u32[]{:S(2)}) %collective-permute-start.12) | collective-permute-done | bytes 180256 | tf_op jit(solution)/shard_map/ppermute | solution.py:365
  36.7 0.6 select.25
  37.3 1.3 %collective-permute-start.13 = (bf16[192,512]{1,0:T(8,128)(2,1)S(1)}, bf16[192,512]{1,0:T(8,128)(2,1)S(1)}, u32[]{:S(2)}, u32[]{:S(2)}) collective-permute-start(bf16[192,512]{1,0:T(8,128)(2,1)S(1)} %get-tuple-element.20), channel_id=1, source_target_pairs={{0,64},{4,68},{8,72},{12,76},{16,80},{20,84},{24,88},{28,92},{32,9... | collective-permute-start | bytes 589832 | tf_op jit(solution)/shard_map/ppermute | solution.py:365
  38.6 1.4 %collective-permute-start.14 = (bf16[192,512]{1,0:T(8,128)(2,1)S(1)}, bf16[192,512]{1,0:T(8,128)(2,1)S(1)}, u32[]{:S(2)}, u32[]{:S(2)}) collective-permute-start(bf16[192,512]{1,0:T(8,128)(2,1)S(1)} %get-tuple-element.21), channel_id=1, source_target_pairs={{0,128},{4,132},{8,136},{12,140},{16,144},{20,148},{24,152},{28,15... | collective-permute-start | bytes 589832 | tf_op jit(solution)/shard_map/ppermute | solution.py:365
  40.0 0.0 collective-permute-done.5.refs_1_.refs_5_
  40.0 1.9 %collective-permute-start.15 = (bf16[192,512]{1,0:T(8,128)(2,1)S(1)}, bf16[192,512]{1,0:T(8,128)(2,1)S(1)}, u32[]{:S(2)}, u32[]{:S(2)}) collective-permute-start(bf16[192,512]{1,0:T(8,128)(2,1)S(1)} %get-tuple-element.22), channel_id=1, source_target_pairs={{0,192},{4,196},{8,200},{12,204},{16,208},{20,212},{24,216},{28,22... | collective-permute-start | bytes 589832 | tf_op jit(solution)/shard_map/ppermute | solution.py:365
  41.9 0.0 copy-done.7
  41.9 0.0 copy-done.8
  41.9 0.1 fusion.4
  42.0 0.0 copy-done
  42.0 0.0 copy-done.3
  42.0 6.7 %edge_before.1.refs_8_.refs_13_ = f32[1280,512]{1,0:T(8,128)} custom-call(s32[1,1280]{1,0:T(1,128)S(1)} %reshape.29.refs_0_.refs_2_, s32[1,1280]{1,0:T(1,128)S(1)} %reshape.32.refs_1_, f32[1,512]{1,0:T(1,128)S(1)} %bitcast.8, bf16[160,512]{1,0:T(8,128)(2,1)S(1)} %copy-done, bf16[160,512]{1,0:T(8,128)(2,1)S(1)} %collective-permute-done.1.refs_1_.refs_4_, ...), custom_call_target="tpu_custom_call" | custom-call | flops 1048576 | tf_op jit(solution)/shard_map/edge_before/pallas_call | solution.py:240
  48.7 0.0 collective-permute-done.6.refs_2_.refs_6_
  48.7 0.0 collective-permute-done.7.refs_3_.refs_7_
  48.8 0.0 collective-permute-done.13.refs_5_.refs_9_
  48.8 0.0 collective-permute-done.14.refs_6_.refs_10_
  48.8 1.5 %collective-permute-done.15.refs_7_.refs_11_ = bf16[192,512]{1,0:T(8,128)(2,1)S(1)} collective-permute-done((bf16[192,512]{1,0:T(8,128)(2,1)S(1)}, bf16[192,512]{1,0:T(8,128)(2,1)S(1)}, u32[]{:S(2)}, u32[]{:S(2)}) %collective-permute-start.15) | collective-permute-done | bytes 196640 | tf_op jit(solution)/shard_map/ppermute | solution.py:365
  50.2 0.0 copy-start.4
  50.2 0.1 crossing.1
  50.3 4.8 %collective-permute-start.16 = (bf16[768,512]{1,0:T(8,128)(2,1)S(1)}, bf16[768,512]{1,0:T(8,128)(2,1)S(1)}, u32[]{:S(2)}, u32[]{:S(2)}) collective-permute-start(bf16[768,512]{1,0:T(8,128)(2,1)S(1)} %crossing.1), channel_id=1, source_target_pairs={{0,4},{4,0},{8,12},{12,8},{16,20},{20,16},{24,28},{28,24},{32,36},... | collective-permute-start | bytes 2359304 | tf_op jit(solution)/shard_map/ppermute | solution.py:365
  55.1 0.2 reshape.36.refs_1_
  56.0 1.0 %collective-permute-done.16.refs_12_ = bf16[768,512]{1,0:T(8,128)(2,1)S(1)} collective-permute-done((bf16[768,512]{1,0:T(8,128)(2,1)S(1)}, bf16[768,512]{1,0:T(8,128)(2,1)S(1)}, u32[]{:S(2)}, u32[]{:S(2)}) %collective-permute-start.16) | collective-permute-done | bytes 786464 | tf_op jit(solution)/shard_map/ppermute | solution.py:365
  57.0 0.0 copy-done.4
  57.0 0.0 copy-start.6
  57.0 6.5 %edge_after.1 = (bf16[1280,512]{1,0:T(8,128)(2,1)}, f32[160,512]{1,0:T(8,128)S(1)}, bf16[160,512]{1,0:T(8,128)(2,1)S(1)}, bf16[160,512]{1,0:T(8,128)(2,1)S(1)}, bf16[160,512]{1,0:T(8,128)(2,1)S(1)}) custom-call(s32[1]{0:T(128)S(6)} %copy.23.refs_0_, s32[1280,1]{1,0:T(8,128)S(1)} %reshape.36.refs_1_, s32[1,1280]{1,0:T(1,128)S(1)} %reshape.29.refs_0_.refs_2_, ...), custom_call_target="tpu_custom_call" | custom-call | tf_op jit(solution)/shard_map/edge_after/pallas_call | solution.py:311
  63.5 1.6 %collective-permute-start.17 = (bf16[160,512]{1,0:T(8,128)(2,1)S(1)}, bf16[160,512]{1,0:T(8,128)(2,1)S(1)}, u32[]{:S(2)}, u32[]{:S(2)}) collective-permute-start(bf16[160,512]{1,0:T(8,128)(2,1)S(1)} %get-tuple-element.25), channel_id=1, source_target_pairs={{0,3},{1,0},{2,1},{3,2},{4,7},{5,4},{6,5},{7,6},{8,11},{9,8},{10,9... | collective-permute-start | bytes 491528 | tf_op jit(solution)/shard_map/ppermute | solution.py:447
  65.1 0.6 collective-permute-start.18
  65.8 0.4 collective-permute-start.19
  66.2 2.8 %collective-permute-done.17.p1_ref = bf16[160,512]{1,0:T(8,128)(2,1)S(1)} collective-permute-done((bf16[160,512]{1,0:T(8,128)(2,1)S(1)}, bf16[160,512]{1,0:T(8,128)(2,1)S(1)}, u32[]{:S(2)}, u32[]{:S(2)}) %collective-permute-start.17) | collective-permute-done | bytes 163872 | tf_op jit(solution)/shard_map/ppermute | solution.py:447
  69.0 2.8 %collective-permute-done.18.p2_ref = bf16[160,512]{1,0:T(8,128)(2,1)S(1)} collective-permute-done((bf16[160,512]{1,0:T(8,128)(2,1)S(1)}, bf16[160,512]{1,0:T(8,128)(2,1)S(1)}, u32[]{:S(2)}, u32[]{:S(2)}) %collective-permute-start.18) | collective-permute-done | bytes 163872 | tf_op jit(solution)/shard_map/ppermute | solution.py:447
  71.8 4.5 %collective-permute-done.19.p3_ref = bf16[160,512]{1,0:T(8,128)(2,1)S(1)} collective-permute-done((bf16[160,512]{1,0:T(8,128)(2,1)S(1)}, bf16[160,512]{1,0:T(8,128)(2,1)S(1)}, u32[]{:S(2)}, u32[]{:S(2)}) %collective-permute-start.19) | collective-permute-done | bytes 163872 | tf_op jit(solution)/shard_map/ppermute | solution.py:447
  76.3 0.0 copy-done.1
  76.3 0.0 copy-done.2
  76.3 0.0 copy-done.5
  76.3 0.0 copy-done.6
  76.3 1.5 %node_update.1 = bf16[160,512]{1,0:T(8,128)(2,1)} custom-call(bf16[160,512]{1,0:T(8,128)(2,1)S(1)} %copy-done, f32[160,512]{1,0:T(8,128)S(1)} %get-tuple-element.24.p0_ref, bf16[160,512]{1,0:T(8,128)(2,1)S(1)} %collective-permute-done.17.p1_ref, bf16[160,512]{1,0:T(8,128)(2,1)S(1)} %collective-permute-done.18.p2_ref, ...), custom_call_target="tpu_custom_call" | custom-call | tf_op jit(solution)/shard_map/node_update/pallas_call | solution.py:345
  (8 shorter events, 0.0 us)
Async XLA Ops:
  7.4 34.4 %copy-start.7 = (s32[1280]{0:T(1024)S(1)}, s32[1280]{0:T(1024)}, u32[]{:S(2)}) copy-start(s32[1280]{0:T(1024)} %param.17) | copy-start | bytes 15364
  7.4 34.4 %copy-start.8 = (s32[1280]{0:T(1024)S(1)}, s32[1280]{0:T(1024)}, u32[]{:S(2)}) copy-start(s32[1280]{0:T(1024)} %param.16) | copy-start | bytes 15364
  7.5 34.5 %copy-start = (bf16[160,512]{1,0:T(8,128)(2,1)S(1)}, bf16[160,512]{1,0:T(8,128)(2,1)}, u32[]{:S(2)}) copy-start(bf16[160,512]{1,0:T(8,128)(2,1)} %nodes_ref.1) | copy-start | bytes 491524
  7.5 34.5 %copy-start.3 = (f32[512]{0:T(512)S(1)}, f32[512]{0:T(512)}, u32[]{:S(2)}) copy-start(f32[512]{0:T(512)} %param.21) | copy-start | bytes 6148
  7.5 11.0 %collective-permute-start = (bf16[176,512]{1,0:T(8,128)(2,1)}, bf16[176,512]{1,0:T(8,128)(2,1)S(1)}, u32[]{:S(2)}, u32[]{:S(2)}) collective-permute-start(bf16[176,512]{1,0:T(8,128)(2,1)} %pack.1.refs_0_), channel_id=1, source_target_pairs={{0,8},{4,12},{8,16},{12,20},{16,24},{20,28},{24,32},{28,36},{32,40... | collective-permute-start | bytes 540680 | tf_op jit(solution)/shard_map/ppermute | solution.py:365
  10.0 6.3 %collective-permute-start.1 = (bf16[160,512]{1,0:T(8,128)(2,1)}, bf16[160,512]{1,0:T(8,128)(2,1)S(1)}, u32[]{:S(2)}, u32[]{:S(2)}) collective-permute-start(bf16[160,512]{1,0:T(8,128)(2,1)} %nodes_ref.1), channel_id=1, source_target_pairs={{0,1},{1,2},{2,3},{3,0},{4,5},{5,6},{6,7},{7,4},{8,9},{9,10},{10,1... | collective-permute-start | bytes 491528 | tf_op jit(solution)/shard_map/ppermute | solution.py:393
  11.3 9.9 %collective-permute-start.2 = (bf16[176,512]{1,0:T(8,128)(2,1)}, bf16[176,512]{1,0:T(8,128)(2,1)S(1)}, u32[]{:S(2)}, u32[]{:S(2)}) collective-permute-start(bf16[176,512]{1,0:T(8,128)(2,1)} %pack.1.refs_0_), channel_id=1, source_target_pairs={{0,56},{4,60},{8,0},{12,4},{16,8},{20,12},{24,16},{28,20},{32,24},... | collective-permute-start | bytes 540680 | tf_op jit(solution)/shard_map/ppermute | solution.py:365
  18.4 6.0 %collective-permute-start.3 = (bf16[176,512]{1,0:T(8,128)(2,1)S(1)}, bf16[176,512]{1,0:T(8,128)(2,1)S(1)}, u32[]{:S(2)}, u32[]{:S(2)}) collective-permute-start(bf16[176,512]{1,0:T(8,128)(2,1)S(1)} %gate.3.refs_1_), channel_id=1, source_target_pairs={{0,8},{4,12},{8,16},{12,20},{16,24},{20,28},{24,32},{28,36},{32,40... | collective-permute-start | bytes 540680 | tf_op jit(solution)/shard_map/ppermute | solution.py:365
  18.5 5.4 %collective-permute-start.4 = (bf16[160,512]{1,0:T(8,128)(2,1)}, bf16[160,512]{1,0:T(8,128)(2,1)S(1)}, u32[]{:S(2)}, u32[]{:S(2)}) collective-permute-start(bf16[160,512]{1,0:T(8,128)(2,1)} %nodes_ref.1), channel_id=1, source_target_pairs={{0,3},{1,0},{2,1},{3,2},{4,7},{5,4},{6,5},{7,6},{8,11},{9,8},{10,9... | collective-permute-start | bytes 491528 | tf_op jit(solution)/shard_map/ppermute | solution.py:393
  21.2 7.2 %collective-permute-start.8 = (bf16[176,512]{1,0:T(8,128)(2,1)S(1)}, bf16[176,512]{1,0:T(8,128)(2,1)S(1)}, u32[]{:S(2)}, u32[]{:S(2)}) collective-permute-start(bf16[176,512]{1,0:T(8,128)(2,1)S(1)} %collective-permute-done.2.refs_2_), channel_id=1, source_target_pairs={{0,56},{4,60},{8,0},{12,4},{16,8},{20,12},{24,16},{28,20},{32,24},... | collective-permute-start | bytes 540680 | tf_op jit(solution)/shard_map/ppermute | solution.py:365
  24.5 6.6 %collective-permute-start.9 = (bf16[176,512]{1,0:T(8,128)(2,1)S(1)}, bf16[176,512]{1,0:T(8,128)(2,1)S(1)}, u32[]{:S(2)}, u32[]{:S(2)}) collective-permute-start(bf16[176,512]{1,0:T(8,128)(2,1)S(1)} %gate.4.refs_3_), channel_id=1, source_target_pairs={{0,8},{4,12},{8,16},{12,20},{16,24},{20,28},{24,32},{28,36},{32,40... | collective-permute-start | bytes 540680 | tf_op jit(solution)/shard_map/ppermute | solution.py:365
  24.5 6.6 %collective-permute-start.10 = (bf16[160,512]{1,0:T(8,128)(2,1)S(1)}, bf16[160,512]{1,0:T(8,128)(2,1)S(1)}, u32[]{:S(2)}, u32[]{:S(2)}) collective-permute-start(bf16[160,512]{1,0:T(8,128)(2,1)S(1)} %collective-permute-done.1.refs_1_.refs_4_), channel_id=1, source_target_pairs={{0,1},{1,2},{2,3},{3,0},{4,5},{5,6},{6,7},{7,4},{8,9},{9,10},{10,1... | collective-permute-start | bytes 491528 | tf_op jit(solution)/shard_map/ppermute | solution.py:393
  27.1 12.9 %collective-permute-start.5 = (bf16[192,512]{1,0:T(8,128)(2,1)S(1)}, bf16[192,512]{1,0:T(8,128)(2,1)S(1)}, u32[]{:S(2)}, u32[]{:S(2)}) collective-permute-start(bf16[192,512]{1,0:T(8,128)(2,1)S(1)} %get-tuple-element.16), channel_id=1, source_target_pairs={{0,64},{4,68},{8,72},{12,76},{16,80},{20,84},{24,88},{28,92},{32,9... | collective-permute-start | bytes 589832 | tf_op jit(solution)/shard_map/ppermute | solution.py:365
  28.4 7.4 %collective-permute-start.11 = (bf16[176,512]{1,0:T(8,128)(2,1)S(1)}, bf16[176,512]{1,0:T(8,128)(2,1)S(1)}, u32[]{:S(2)}, u32[]{:S(2)}) collective-permute-start(bf16[176,512]{1,0:T(8,128)(2,1)S(1)} %collective-permute-done.8.refs_0_), channel_id=1, source_target_pairs={{0,56},{4,60},{8,0},{12,4},{16,8},{20,12},{24,16},{28,20},{32,24},... | collective-permute-start | bytes 540680 | tf_op jit(solution)/shard_map/ppermute | solution.py:365
  31.1 5.6 %collective-permute-start.12 = (bf16[176,512]{1,0:T(8,128)(2,1)S(1)}, bf16[176,512]{1,0:T(8,128)(2,1)S(1)}, u32[]{:S(2)}, u32[]{:S(2)}) collective-permute-start(bf16[176,512]{1,0:T(8,128)(2,1)S(1)} %gate.5.refs_1_), channel_id=1, source_target_pairs={{0,8},{4,12},{8,16},{12,20},{16,24},{20,28},{24,32},{28,36},{32,40... | collective-permute-start | bytes 540680 | tf_op jit(solution)/shard_map/ppermute | solution.py:365
  32.2 16.5 %collective-permute-start.6 = (bf16[192,512]{1,0:T(8,128)(2,1)S(1)}, bf16[192,512]{1,0:T(8,128)(2,1)S(1)}, u32[]{:S(2)}, u32[]{:S(2)}) collective-permute-start(bf16[192,512]{1,0:T(8,128)(2,1)S(1)} %get-tuple-element.17), channel_id=1, source_target_pairs={{0,128},{4,132},{8,136},{12,140},{16,144},{20,148},{24,152},{28,15... | collective-permute-start | bytes 589832 | tf_op jit(solution)/shard_map/ppermute | solution.py:365
  35.0 13.8 %collective-permute-start.7 = (bf16[192,512]{1,0:T(8,128)(2,1)S(1)}, bf16[192,512]{1,0:T(8,128)(2,1)S(1)}, u32[]{:S(2)}, u32[]{:S(2)}) collective-permute-start(bf16[192,512]{1,0:T(8,128)(2,1)S(1)} %get-tuple-element.18), channel_id=1, source_target_pairs={{0,192},{4,196},{8,200},{12,204},{16,208},{20,212},{24,216},{28,22... | collective-permute-start | bytes 589832 | tf_op jit(solution)/shard_map/ppermute | solution.py:365
  37.3 11.5 %collective-permute-start.13 = (bf16[192,512]{1,0:T(8,128)(2,1)S(1)}, bf16[192,512]{1,0:T(8,128)(2,1)S(1)}, u32[]{:S(2)}, u32[]{:S(2)}) collective-permute-start(bf16[192,512]{1,0:T(8,128)(2,1)S(1)} %get-tuple-element.20), channel_id=1, source_target_pairs={{0,64},{4,68},{8,72},{12,76},{16,80},{20,84},{24,88},{28,92},{32,9... | collective-permute-start | bytes 589832 | tf_op jit(solution)/shard_map/ppermute | solution.py:365
  38.6 10.2 %collective-permute-start.14 = (bf16[192,512]{1,0:T(8,128)(2,1)S(1)}, bf16[192,512]{1,0:T(8,128)(2,1)S(1)}, u32[]{:S(2)}, u32[]{:S(2)}) collective-permute-start(bf16[192,512]{1,0:T(8,128)(2,1)S(1)} %get-tuple-element.21), channel_id=1, source_target_pairs={{0,128},{4,132},{8,136},{12,140},{16,144},{20,148},{24,152},{28,15... | collective-permute-start | bytes 589832 | tf_op jit(solution)/shard_map/ppermute | solution.py:365
  40.0 10.2 %collective-permute-start.15 = (bf16[192,512]{1,0:T(8,128)(2,1)S(1)}, bf16[192,512]{1,0:T(8,128)(2,1)S(1)}, u32[]{:S(2)}, u32[]{:S(2)}) collective-permute-start(bf16[192,512]{1,0:T(8,128)(2,1)S(1)} %get-tuple-element.22), channel_id=1, source_target_pairs={{0,192},{4,196},{8,200},{12,204},{16,208},{20,212},{24,216},{28,22... | collective-permute-start | bytes 589832 | tf_op jit(solution)/shard_map/ppermute | solution.py:365
  50.2 6.8 %copy-start.4 = (f32[512]{0:T(512)S(1)}, f32[512]{0:T(512)}, u32[]{:S(2)}) copy-start(f32[512]{0:T(512)} %param.23) | copy-start | bytes 6148
  50.3 6.7 %collective-permute-start.16 = (bf16[768,512]{1,0:T(8,128)(2,1)S(1)}, bf16[768,512]{1,0:T(8,128)(2,1)S(1)}, u32[]{:S(2)}, u32[]{:S(2)}) collective-permute-start(bf16[768,512]{1,0:T(8,128)(2,1)S(1)} %crossing.1), channel_id=1, source_target_pairs={{0,4},{4,0},{8,12},{12,8},{16,20},{20,16},{24,28},{28,24},{32,36},... | collective-permute-start | bytes 2359304 | tf_op jit(solution)/shard_map/ppermute | solution.py:365
  57.0 19.2 %copy-start.1 = (bf16[1024,512]{1,0:T(8,128)(2,1)S(1)}, bf16[1024,512]{1,0:T(8,128)(2,1)}, u32[]{:S(2)}) copy-start(bf16[1024,512]{1,0:T(8,128)(2,1)} %w1_ref.1) | copy-start | bytes 3145732
  57.0 19.2 %copy-start.2 = (bf16[512,512]{1,0:T(8,128)(2,1)S(1)}, bf16[512,512]{1,0:T(8,128)(2,1)}, u32[]{:S(2)}) copy-start(bf16[512,512]{1,0:T(8,128)(2,1)} %w2_ref.1) | copy-start | bytes 1572868
  57.0 19.2 %copy-start.5 = (f32[512]{0:T(512)S(1)}, f32[512]{0:T(512)}, u32[]{:S(2)}) copy-start(f32[512]{0:T(512)} %param.25) | copy-start | bytes 6148
  57.0 19.2 %copy-start.6 = (f32[512]{0:T(512)S(1)}, f32[512]{0:T(512)}, u32[]{:S(2)}) copy-start(f32[512]{0:T(512)} %param.27) | copy-start | bytes 6148
  63.5 5.5 %collective-permute-start.17 = (bf16[160,512]{1,0:T(8,128)(2,1)S(1)}, bf16[160,512]{1,0:T(8,128)(2,1)S(1)}, u32[]{:S(2)}, u32[]{:S(2)}) collective-permute-start(bf16[160,512]{1,0:T(8,128)(2,1)S(1)} %get-tuple-element.25), channel_id=1, source_target_pairs={{0,3},{1,0},{2,1},{3,2},{4,7},{5,4},{6,5},{7,6},{8,11},{9,8},{10,9... | collective-permute-start | bytes 491528 | tf_op jit(solution)/shard_map/ppermute | solution.py:447
  65.1 6.6 %collective-permute-start.18 = (bf16[160,512]{1,0:T(8,128)(2,1)S(1)}, bf16[160,512]{1,0:T(8,128)(2,1)S(1)}, u32[]{:S(2)}, u32[]{:S(2)}) collective-permute-start(bf16[160,512]{1,0:T(8,128)(2,1)S(1)} %get-tuple-element.26), channel_id=1, source_target_pairs={{0,2},{1,3},{2,0},{3,1},{4,6},{5,7},{6,4},{7,5},{8,10},{9,11},{10,... | collective-permute-start | bytes 491528 | tf_op jit(solution)/shard_map/ppermute | solution.py:447
  65.8 10.5 %collective-permute-start.19 = (bf16[160,512]{1,0:T(8,128)(2,1)S(1)}, bf16[160,512]{1,0:T(8,128)(2,1)S(1)}, u32[]{:S(2)}, u32[]{:S(2)}) collective-permute-start(bf16[160,512]{1,0:T(8,128)(2,1)S(1)} %get-tuple-element.27), channel_id=1, source_target_pairs={{0,1},{1,2},{2,3},{3,0},{4,5},{5,6},{6,7},{7,4},{8,9},{9,10},{10,1... | collective-permute-start | bytes 491528 | tf_op jit(solution)/shard_map/ppermute | solution.py:447

commit v10 on v9

--- a/solution.py
+++ b/solution.py
@@ -20,6 +20,7 @@
 TAIL = 16
 COST = 1 << 20
 NEAR = (1, 3, 2)
+FAR_FIRST = (2, 1, 3)
 BATCHES = (((0, 1), (7, 2)), ((6, 3), (5, 4)))
 
 
@@ -64,10 +65,10 @@
     return (dz >= 1) & (dz <= 4)
 
 
-def pack_kernel(where_ref, lists_ref, nodes_hbm, out_hbm, tail_ref, sems):
+def pack_kernel(where_ref, lists_ref, nodes_hbm, out_hbm, block_ref, sems):
     rows, latent = nodes_hbm.shape
     cap, peers = lists_ref.shape
-    body = pltpu.make_async_copy(nodes_hbm, out_hbm.at[pl.ds(0, rows)], sems.at[0])
+    body = pltpu.make_async_copy(nodes_hbm, block_ref.at[pl.ds(0, rows)], sems.at[0])
     body.start()
     me = where_ref[0]
     x, z, c = me // (Z * C), me // C % Z, me % C
@@ -84,11 +85,11 @@
     row = lax.broadcasted_iota(i32, (TAIL, peers), 0)
     peer = lax.broadcasted_iota(i32, (TAIL, peers), 1)
     pick = as_bf16(row == ((peer // C % Z - z) & (Z - 1)))
-    tail_ref[...] = (dot(pick, listed) - 1.0).astype(bf16)
-    tail = pltpu.make_async_copy(tail_ref, out_hbm.at[pl.ds(rows, TAIL)], sems.at[1])
-    tail.start()
-    tail.wait()
+    block_ref[rows:] = (dot(pick, listed) - 1.0).astype(bf16)
     body.wait()
+    store = pltpu.make_async_copy(block_ref, out_hbm, sems.at[1])
+    store.start()
+    store.wait()
 
 
 def pack(me, lists, nodes):
@@ -97,7 +98,10 @@
         in_specs=[SMEM, VMEM, HBM],
         out_specs=HBM,
         out_shape=pltpu.HBM((nodes.shape[0] + TAIL, nodes.shape[1]), bf16),
-        scratch_shapes=[pltpu.VMEM((TAIL, nodes.shape[1]), bf16), pltpu.SemaphoreType.DMA((2,))],
+        scratch_shapes=[
+            pltpu.VMEM((nodes.shape[0] + TAIL, nodes.shape[1]), bf16),
+            pltpu.SemaphoreType.DMA((2,)),
+        ],
         name="pack",
     )(me, lists, in_hbm(nodes))
 
@@ -169,7 +173,7 @@
 def cross_kernel(*refs):
     out_ref = refs[-1]
     put = 0
-    for ref in refs[: X * len(BATCHES)]:
+    for ref in refs[:X]:
         size = ref.shape[0] // C
         out_ref[put : put + size] = ref[size:]
         put += size
@@ -186,16 +190,15 @@
     )(*parts, *[in_hbm(part) for part in earlier])
 
 
-def fill(table_ref, parts, crossed):
-    put, taken = 0, 0
-    for at in range(len(BATCHES)):
-        group = parts[at * X : (at + 1) * X]
-        size = group[0].shape[0] // C
-        for part in group:
+def fill(table_ref, groups):
+    put = 0
+    for at in range(0, len(groups), X + 1):
+        size = groups[at].shape[0] // C
+        for part in groups[at : at + X]:
             table_ref[put : put + size] = part[:size]
             put += size
-        table_ref[put : put + X * size] = crossed[taken : taken + X * size]
-        put, taken = put + X * size, taken + X * size
+        table_ref[put : put + X * size] = groups[at + X][...]
+        put += X * size
 
 
 def before_kernel(extra, *refs):
@@ -257,8 +260,8 @@
 
 def after_kernel(first_row, *refs):
     live_ref, send_ref, recv_ref, gain_ref = refs[:4]
-    count = X * len(BATCHES)
-    parts, crossed, refs = refs[4 : 4 + count], refs[4 + count], refs[5 + count :]
+    count = (X + 1) * len(BATCHES)
+    groups, refs = refs[4 : 4 + count], refs[4 + count :]
     before_hbm, w1_hbm, w2_hbm, edges_hbm, out_hbm = refs[:5]
     sums_refs = refs[5:9]
     table_ref, before_ref, w1_ref, w2_ref, edges_ref, far_ref, load_sems, store_sems = refs[9:]
@@ -272,7 +275,7 @@
     ]
     for load in loads:
         load.start()
-    fill(table_ref, parts, crossed)
+    fill(table_ref, groups)
     stores = []
     live = live_ref[0]
     size = count // GATHERS
@@ -305,9 +308,9 @@
         store.wait()
 
 
-def edge_after(first_row, live, send, recv, gain, parts, before, w1, w2, edges, rows):
+def edge_after(cap, first_row, live, send, recv, gain, parts, before, w1, w2, edges, rows):
     count, latent = edges.shape
-    table = sum(part.shape[0] for part in parts[:-1]) // C + parts[-1].shape[0]
+    table = X * Z * C * cap
     return pl.pallas_call(
         lambda *refs: after_kernel(first_row, *refs),
         in_specs=[SMEM] + [VMEM] * (3 + len(parts)) + [HBM] * 4,
@@ -407,10 +410,10 @@
     groups = []
     for pairs in BATCHES:
         picked = select(pairs, cap, [held[dz] for pair in pairs for dz in pair])
-        group = [picked[0]]
-        for k in range(1, X):
-            group.append(moved(picked[k], lambda x, z, c: (x + k, z, c)))
-        groups.append(group)
+        arrived = {0: picked[0]}
+        for k in FAR_FIRST:
+            arrived[k] = moved(picked[k], lambda x, z, c: (x + k, z, c))
+        groups.append([arrived[k] for k in range(X)])
     swap = lambda a: moved(a, lambda x, z, c: (x, z, c + 1))
 
     def near_row(row):
@@ -436,15 +439,16 @@
     before = edge_before(
         recv, send.reshape(1, -1), edge_b1.reshape(1, -1), parts, edges, edge_w1, groups[1][0]
     )
-    arrived = groups[0] + groups[1]
-    arrived = arrived + [swap(crossing(arrived, before))]
+    early = groups[0] + [swap(crossing(groups[0], before))]
+    late = groups[1] + [swap(crossing(groups[1], before))]
     edges_out, *sums = edge_after(
-        patch, live_edges, send.reshape(-1, 1), recv, edge_gain.reshape(1, -1), arrived, before,
+        cap, patch, live_edges, send.reshape(-1, 1), recv, edge_gain.reshape(1, -1), early + late, before,
         edge_w1, edge_w2, edges, rows,
     )
-    parts = [sums[0]]
-    for k in range(1, feat):
-        parts.append(lax.ppermute(sums[k], "feat", [(i, (i - k) % feat) for i in range(feat)]))
+    arrived = {0: sums[0]}
+    for k in FAR_FIRST:
+        arrived[k] = around(sums[k], feat - k)
+    parts = [arrived[k] for k in range(feat)]
     nodes_out = node_update(
         nodes, parts, node_w1, node_b1.reshape(1, -1), node_w2, node_gain.reshape(1, -1)
     )

time: 78 us -> 73 us (0.936)
  Pallas kernels: 23.4 us -> 19 us
  waiting for transfers between devices: 17.1 us -> 14.7 us
  starting transfers between devices: 35.4 us -> 37.3 us
    ppermute x3 -> x0, waiting for transfers between devices: 10.1 us -> none  [local(): lax.ppermute(sums[k], 'feat', [(i, (i - k) % feat) for i in range(feat)])]
    ppermute x3 -> x6, waiting for transfers between devices: 0.98 us -> 10.6 us  [around(): lax.ppermute(value, 'feat', [(i, (i + k) % feat) for i in range(feat)])]
    pallas_call x1, Pallas kernels: 6.79 us -> 2.32 us  [pack(): pl.pallas_call(pack_kernel, in_specs=[SMEM, VMEM, HBM], out_specs=HBM, ou...]
    ppermute x3 -> x6, starting transfers between devices: 5.33 us -> 8.52 us  [around(): lax.ppermute(value, 'feat', [(i, (i + k) % feat) for i in range(feat)])]
    ppermute x3 -> x0, starting transfers between devices: 2.66 us -> none  [local(): lax.ppermute(sums[k], 'feat', [(i, (i - k) % feat) for i in range(feat)])]
    ppermute x14 -> x15, waiting for transfers between devices: 6.06 us -> 4.04 us  [moved(): return lax.ppermute(value, 'patch', pairs_of(move))]
    ppermute x14 -> x15, starting transfers between devices: 27.4 us -> 28.8 us  [moved(): return lax.ppermute(value, 'patch', pairs_of(move))]
  transfers between devices with their start and end apart: 20 -> 21, of which waited for: 9 -> 8; matrix products, arithmetic and copies ran while one was open for 0% -> 0% of each run, Pallas kernels for 11% -> 12%
where the time goes in v10:
time: 73 us; the launch traced here: 72.8 us
  starting transfers between devices  37.3 us (51%)
  Pallas kernels  19 us (26%)
  waiting for transfers between devices  14.7 us (20%)
  between operations  1.5 us (2%)
    ppermute x15, starting transfers between devices, moved(): return lax.ppermute(value, 'patch', pairs_of(move))  28.8 us
    ppermute x6, waiting for transfers between devices, around(): lax.ppermute(value, 'feat', [(i, (i + k) % feat) for i in range(feat)])  10.6 us
    ppermute x6, starting transfers between devices, around(): lax.ppermute(value, 'feat', [(i, (i + k) % feat) for i in range(feat)])  8.52 us
    pallas_call x1, Pallas kernels, edge_before(): pl.pallas_call(lambda *refs: before_kernel(len(earlier), *refs), in_specs...  6.74 us
    pallas_call x1, Pallas kernels, edge_after(): pl.pallas_call(lambda *refs: after_kernel(first_row, *refs), in_specs=[SM...  6.45 us
    ppermute x15, waiting for transfers between devices, moved(): return lax.ppermute(value, 'patch', pairs_of(move))  4.04 us
    pallas_call x1, Pallas kernels, pack(): pl.pallas_call(pack_kernel, in_specs=[SMEM, VMEM, HBM], out_specs=HBM, ou...  2.32 us
    pallas_call x2, Pallas kernels, select(): pl.pallas_call(lambda *refs: select_kernel(pairs, cap, len(earlier), *ref...  1.95 us
  transfers between devices with their start and end apart: 21, of which 8 were waited for; matrix products, arithmetic and copies ran while one was open for 0% of the time, Pallas kernels for 12%

profile of v10, /device:TPU:1, one launch (start us, length us, event | category | flops | bytes accessed | tf_op | source)
XLA Modules:
  0.0 72.8 jit_solution(1521929667142281520)
XLA Ops:
  0.6 2.3 %pack.1.refs_0_ = bf16[176,512]{1,0:T(8,128)(2,1)} custom-call(s32[1]{0:T(128)} %bitcast.1.where_ref, s32[24,64]{1,0:T(8,128)} %bitcast.12, bf16[160,512]{1,0:T(8,128)(2,1)} %nodes_ref.1), custom_call_target="tpu_custom_call" | custom-call | tf_op jit(solution)/shard_map/pack/pallas_call | solution.py:96
  3.0 0.0 copy-start.7
  3.0 0.0 copy-start.8
  3.0 0.0 copy-start
  3.0 0.0 copy-start.3
  3.0 2.5 %collective-permute-start = (bf16[176,512]{1,0:T(8,128)(2,1)}, bf16[176,512]{1,0:T(8,128)(2,1)S(1)}, u32[]{:S(2)}, u32[]{:S(2)}) collective-permute-start(bf16[176,512]{1,0:T(8,128)(2,1)} %pack.1.refs_0_), channel_id=1, source_target_pairs={{0,8},{4,12},{8,16},{12,20},{16,24},{20,28},{24,32},{28,36},{32,40... | collective-permute-start | bytes 540680 | tf_op jit(solution)/shard_map/ppermute | solution.py:368
  5.6 1.3 %collective-permute-start.1 = (bf16[160,512]{1,0:T(8,128)(2,1)}, bf16[160,512]{1,0:T(8,128)(2,1)S(1)}, u32[]{:S(2)}, u32[]{:S(2)}) collective-permute-start(bf16[160,512]{1,0:T(8,128)(2,1)} %nodes_ref.1), channel_id=1, source_target_pairs={{0,1},{1,2},{2,3},{3,0},{4,5},{5,6},{6,7},{7,4},{8,9},{9,10},{10,1... | collective-permute-start | bytes 491528 | tf_op jit(solution)/shard_map/ppermute | solution.py:396
  6.9 4.0 %collective-permute-start.2 = (bf16[176,512]{1,0:T(8,128)(2,1)}, bf16[176,512]{1,0:T(8,128)(2,1)S(1)}, u32[]{:S(2)}, u32[]{:S(2)}) collective-permute-start(bf16[176,512]{1,0:T(8,128)(2,1)} %pack.1.refs_0_), channel_id=1, source_target_pairs={{0,56},{4,60},{8,0},{12,4},{16,8},{20,12},{24,16},{28,20},{32,24},... | collective-permute-start | bytes 540680 | tf_op jit(solution)/shard_map/ppermute | solution.py:368
  10.9 1.0 %collective-permute-done.1.refs_1_.refs_4_ = bf16[160,512]{1,0:T(8,128)(2,1)S(1)} collective-permute-done((bf16[160,512]{1,0:T(8,128)(2,1)}, bf16[160,512]{1,0:T(8,128)(2,1)S(1)}, u32[]{:S(2)}, u32[]{:S(2)}) %collective-permute-start.1) | collective-permute-done | bytes 163872 | tf_op jit(solution)/shard_map/ppermute | solution.py:396
  11.9 2.1 %collective-permute-done.refs_0_ = bf16[176,512]{1,0:T(8,128)(2,1)S(1)} collective-permute-done((bf16[176,512]{1,0:T(8,128)(2,1)}, bf16[176,512]{1,0:T(8,128)(2,1)S(1)}, u32[]{:S(2)}, u32[]{:S(2)}) %collective-permute-start) | collective-permute-done | bytes 180256 | tf_op jit(solution)/shard_map/ppermute | solution.py:368
  14.0 0.0 collective-permute-start.3
  14.0 2.7 %collective-permute-start.4 = (bf16[160,512]{1,0:T(8,128)(2,1)}, bf16[160,512]{1,0:T(8,128)(2,1)S(1)}, u32[]{:S(2)}, u32[]{:S(2)}) collective-permute-start(bf16[160,512]{1,0:T(8,128)(2,1)} %nodes_ref.1), channel_id=1, source_target_pairs={{0,3},{1,0},{2,1},{3,2},{4,7},{5,4},{6,5},{7,6},{8,11},{9,8},{10,9... | collective-permute-start | bytes 491528 | tf_op jit(solution)/shard_map/ppermute | solution.py:396
  16.7 0.0 collective-permute-done.2.refs_2_
  16.7 2.7 %collective-permute-start.9 = (bf16[176,512]{1,0:T(8,128)(2,1)S(1)}, bf16[176,512]{1,0:T(8,128)(2,1)S(1)}, u32[]{:S(2)}, u32[]{:S(2)}) collective-permute-start(bf16[176,512]{1,0:T(8,128)(2,1)S(1)} %collective-permute-done.2.refs_2_), channel_id=1, source_target_pairs={{0,56},{4,60},{8,0},{12,4},{16,8},{20,12},{24,16},{28,20},{32,24},... | collective-permute-start | bytes 540680 | tf_op jit(solution)/shard_map/ppermute | solution.py:368
  19.4 0.0 collective-permute-done.4.refs_1_.refs_6_
  19.4 0.6 collective-permute-done.3.refs_0_
  20.0 0.0 collective-permute-start.10
  20.0 1.3 %collective-permute-start.8 = (bf16[160,512]{1,0:T(8,128)(2,1)S(1)}, bf16[160,512]{1,0:T(8,128)(2,1)S(1)}, u32[]{:S(2)}, u32[]{:S(2)}) collective-permute-start(bf16[160,512]{1,0:T(8,128)(2,1)S(1)} %collective-permute-done.1.refs_1_.refs_4_), channel_id=1, source_target_pairs={{0,1},{1,2},{2,3},{3,0},{4,5},{5,6},{6,7},{7,4},{8,9},{9,10},{10,1... | collective-permute-start | bytes 491528 | tf_op jit(solution)/shard_map/ppermute | solution.py:396
  21.3 1.3 %select.24 = (bf16[192,512]{1,0:T(8,128)(2,1)S(1)}, bf16[192,512]{1,0:T(8,128)(2,1)S(1)}, bf16[192,512]{1,0:T(8,128)(2,1)S(1)}, bf16[192,512]{1,0:T(8,128)(2,1)S(1)}) custom-call(bf16[176,512]{1,0:T(8,128)(2,1)} %pack.1.refs_0_, bf16[176,512]{1,0:T(8,128)(2,1)S(1)} %gate.3.refs_1_, bf16[176,512]{1,0:T(8,128)(2,1)S(1)} %collective-permute-done.2.refs_2_, ...), custom_call_target="tpu_custom_call" | custom-call | flops 1048576 | tf_op jit(solution)/shard_map/select/pallas_call | solution.py:145
  22.7 1.3 %collective-permute-start.5 = (bf16[192,512]{1,0:T(8,128)(2,1)S(1)}, bf16[192,512]{1,0:T(8,128)(2,1)S(1)}, u32[]{:S(2)}, u32[]{:S(2)}) collective-permute-start(bf16[192,512]{1,0:T(8,128)(2,1)S(1)} %get-tuple-element.16), channel_id=1, source_target_pairs={{0,64},{4,68},{8,72},{12,76},{16,80},{20,84},{24,88},{28,92},{32,9... | collective-permute-start | bytes 589832 | tf_op jit(solution)/shard_map/ppermute | solution.py:368
  23.9 0.0 collective-permute-done.9.refs_0_
  23.9 2.7 %collective-permute-start.11 = (bf16[176,512]{1,0:T(8,128)(2,1)S(1)}, bf16[176,512]{1,0:T(8,128)(2,1)S(1)}, u32[]{:S(2)}, u32[]{:S(2)}) collective-permute-start(bf16[176,512]{1,0:T(8,128)(2,1)S(1)} %collective-permute-done.9.refs_0_), channel_id=1, source_target_pairs={{0,56},{4,60},{8,0},{12,4},{16,8},{20,12},{24,16},{28,20},{32,24},... | collective-permute-start | bytes 540680 | tf_op jit(solution)/shard_map/ppermute | solution.py:368
  26.6 0.0 collective-permute-done.8.refs_1_.refs_5_
  26.6 0.0 collective-permute-done.10.refs_0_
  26.6 1.1 %collective-permute-start.12 = (bf16[176,512]{1,0:T(8,128)(2,1)S(1)}, bf16[176,512]{1,0:T(8,128)(2,1)S(1)}, u32[]{:S(2)}, u32[]{:S(2)}) collective-permute-start(bf16[176,512]{1,0:T(8,128)(2,1)S(1)} %gate.5.refs_1_), channel_id=1, source_target_pairs={{0,8},{4,12},{8,16},{12,20},{16,24},{20,28},{24,32},{28,36},{32,40... | collective-permute-start | bytes 540680 | tf_op jit(solution)/shard_map/ppermute | solution.py:368
  27.7 2.7 %collective-permute-start.6 = (bf16[192,512]{1,0:T(8,128)(2,1)S(1)}, bf16[192,512]{1,0:T(8,128)(2,1)S(1)}, u32[]{:S(2)}, u32[]{:S(2)}) collective-permute-start(bf16[192,512]{1,0:T(8,128)(2,1)S(1)} %get-tuple-element.17), channel_id=1, source_target_pairs={{0,128},{4,132},{8,136},{12,140},{16,144},{20,148},{24,152},{28,15... | collective-permute-start | bytes 589832 | tf_op jit(solution)/shard_map/ppermute | solution.py:368
  30.5 0.9 %collective-permute-start.7 = (bf16[192,512]{1,0:T(8,128)(2,1)S(1)}, bf16[192,512]{1,0:T(8,128)(2,1)S(1)}, u32[]{:S(2)}, u32[]{:S(2)}) collective-permute-start(bf16[192,512]{1,0:T(8,128)(2,1)S(1)} %get-tuple-element.18), channel_id=1, source_target_pairs={{0,192},{4,196},{8,200},{12,204},{16,208},{20,212},{24,216},{28,22... | collective-permute-start | bytes 589832 | tf_op jit(solution)/shard_map/ppermute | solution.py:368
  31.4 0.0 collective-permute-done.11.refs_2_
  31.4 0.8 %collective-permute-done.12.refs_3_ = bf16[176,512]{1,0:T(8,128)(2,1)S(1)} collective-permute-done((bf16[176,512]{1,0:T(8,128)(2,1)S(1)}, bf16[176,512]{1,0:T(8,128)(2,1)S(1)}, u32[]{:S(2)}, u32[]{:S(2)}) %collective-permute-start.12) | collective-permute-done | bytes 180256 | tf_op jit(solution)/shard_map/ppermute | solution.py:368
  32.2 0.6 select.25
  32.8 1.3 %collective-permute-start.14 = (bf16[192,512]{1,0:T(8,128)(2,1)S(1)}, bf16[192,512]{1,0:T(8,128)(2,1)S(1)}, u32[]{:S(2)}, u32[]{:S(2)}) collective-permute-start(bf16[192,512]{1,0:T(8,128)(2,1)S(1)} %get-tuple-element.20), channel_id=1, source_target_pairs={{0,64},{4,68},{8,72},{12,76},{16,80},{20,84},{24,88},{28,92},{32,9... | collective-permute-start | bytes 589832 | tf_op jit(solution)/shard_map/ppermute | solution.py:368
  34.1 1.4 %collective-permute-start.15 = (bf16[192,512]{1,0:T(8,128)(2,1)S(1)}, bf16[192,512]{1,0:T(8,128)(2,1)S(1)}, u32[]{:S(2)}, u32[]{:S(2)}) collective-permute-start(bf16[192,512]{1,0:T(8,128)(2,1)S(1)} %get-tuple-element.21), channel_id=1, source_target_pairs={{0,128},{4,132},{8,136},{12,140},{16,144},{20,148},{24,152},{28,15... | collective-permute-start | bytes 589832 | tf_op jit(solution)/shard_map/ppermute | solution.py:368
  35.5 0.0 collective-permute-done.5.refs_1_.refs_5_
  35.5 1.9 %collective-permute-start.16 = (bf16[192,512]{1,0:T(8,128)(2,1)S(1)}, bf16[192,512]{1,0:T(8,128)(2,1)S(1)}, u32[]{:S(2)}, u32[]{:S(2)}) collective-permute-start(bf16[192,512]{1,0:T(8,128)(2,1)S(1)} %get-tuple-element.22), channel_id=1, source_target_pairs={{0,192},{4,196},{8,200},{12,204},{16,208},{20,212},{24,216},{28,22... | collective-permute-start | bytes 589832 | tf_op jit(solution)/shard_map/ppermute | solution.py:368
  37.4 0.0 copy-done.7
  37.4 0.0 copy-done.8
  37.4 0.1 fusion.4
  37.5 0.0 copy-done
  37.5 0.0 copy-done.3
  37.5 6.7 %edge_before.1.refs_4_.refs_14_ = f32[1280,512]{1,0:T(8,128)} custom-call(s32[1,1280]{1,0:T(1,128)S(1)} %reshape.29.refs_0_.refs_2_, s32[1,1280]{1,0:T(1,128)S(1)} %reshape.32.refs_1_, f32[1,512]{1,0:T(1,128)S(1)} %bitcast.8, bf16[160,512]{1,0:T(8,128)(2,1)S(1)} %copy-done, bf16[160,512]{1,0:T(8,128)(2,1)S(1)} %collective-permute-done.1.refs_1_.refs_4_, ...), custom_call_target="tpu_custom_call" | custom-call | flops 1048576 | tf_op jit(solution)/shard_map/edge_before/pallas_call | solution.py:243
  44.3 0.0 collective-permute-done.6.refs_2_.refs_6_
  44.3 0.0 collective-permute-done.7.refs_3_.refs_7_
  44.3 0.0 copy-start.4
  44.3 5.3 %collective-permute-start.13 = (bf16[384,512]{1,0:T(8,128)(2,1)S(1)}, bf16[384,512]{1,0:T(8,128)(2,1)S(1)}, u32[]{:S(2)}, u32[]{:S(2)}) collective-permute-start(bf16[384,512]{1,0:T(8,128)(2,1)S(1)} %crossing.2), channel_id=1, source_target_pairs={{0,4},{4,0},{8,12},{12,8},{16,20},{20,16},{24,28},{28,24},{32,36},... | collective-permute-start | bytes 1179656 | tf_op jit(solution)/shard_map/ppermute | solution.py:368
  49.7 0.0 collective-permute-done.14.refs_1_.refs_10_
  49.7 0.0 collective-permute-done.15.refs_2_.refs_11_
  49.7 0.0 collective-permute-done.16.refs_3_.refs_12_
  49.7 0.9 %collective-permute-start.17 = (bf16[384,512]{1,0:T(8,128)(2,1)S(1)}, bf16[384,512]{1,0:T(8,128)(2,1)S(1)}, u32[]{:S(2)}, u32[]{:S(2)}) collective-permute-start(bf16[384,512]{1,0:T(8,128)(2,1)S(1)} %crossing.3), channel_id=1, source_target_pairs={{0,4},{4,0},{8,12},{12,8},{16,20},{20,16},{24,28},{28,24},{32,36},... | collective-permute-start | bytes 1179656 | tf_op jit(solution)/shard_map/ppermute | solution.py:368
  50.6 0.2 reshape.36.refs_1_
  51.5 0.0 collective-permute-done.13.refs_8_
  51.5 0.5 collective-permute-done.17.refs_13_
  52.0 0.0 copy-done.4
  52.0 0.0 copy-start.6
  52.0 6.5 %edge_after.1 = (bf16[1280,512]{1,0:T(8,128)(2,1)}, f32[160,512]{1,0:T(8,128)S(1)}, bf16[160,512]{1,0:T(8,128)(2,1)S(1)}, bf16[160,512]{1,0:T(8,128)(2,1)S(1)}, bf16[160,512]{1,0:T(8,128)(2,1)S(1)}) custom-call(s32[1]{0:T(128)S(6)} %copy.23.refs_0_, s32[1280,1]{1,0:T(8,128)S(1)} %reshape.36.refs_1_, s32[1,1280]{1,0:T(1,128)S(1)} %reshape.29.refs_0_.refs_2_, ...), custom_call_target="tpu_custom_call" | custom-call | tf_op jit(solution)/shard_map/edge_after/pallas_call | solution.py:314
  58.4 1.7 %collective-permute-start.18 = (bf16[160,512]{1,0:T(8,128)(2,1)S(1)}, bf16[160,512]{1,0:T(8,128)(2,1)S(1)}, u32[]{:S(2)}, u32[]{:S(2)}) collective-permute-start(bf16[160,512]{1,0:T(8,128)(2,1)S(1)} %get-tuple-element.25), channel_id=1, source_target_pairs={{0,3},{1,0},{2,1},{3,2},{4,7},{5,4},{6,5},{7,6},{8,11},{9,8},{10,9... | collective-permute-start | bytes 491528 | tf_op jit(solution)/shard_map/ppermute | solution.py:396
  60.2 1.1 %collective-permute-start.19 = (bf16[160,512]{1,0:T(8,128)(2,1)S(1)}, bf16[160,512]{1,0:T(8,128)(2,1)S(1)}, u32[]{:S(2)}, u32[]{:S(2)}) collective-permute-start(bf16[160,512]{1,0:T(8,128)(2,1)S(1)} %get-tuple-element.26), channel_id=1, source_target_pairs={{0,2},{1,3},{2,0},{3,1},{4,6},{5,7},{6,4},{7,5},{8,10},{9,11},{10,... | collective-permute-start | bytes 491528 | tf_op jit(solution)/shard_map/ppermute | solution.py:396
  61.2 0.4 collective-permute-start.20
  61.6 2.3 %collective-permute-done.18.p1_ref = bf16[160,512]{1,0:T(8,128)(2,1)S(1)} collective-permute-done((bf16[160,512]{1,0:T(8,128)(2,1)S(1)}, bf16[160,512]{1,0:T(8,128)(2,1)S(1)}, u32[]{:S(2)}, u32[]{:S(2)}) %collective-permute-start.18) | collective-permute-done | bytes 163872 | tf_op jit(solution)/shard_map/ppermute | solution.py:396
  63.9 2.8 %collective-permute-done.19.p2_ref = bf16[160,512]{1,0:T(8,128)(2,1)S(1)} collective-permute-done((bf16[160,512]{1,0:T(8,128)(2,1)S(1)}, bf16[160,512]{1,0:T(8,128)(2,1)S(1)}, u32[]{:S(2)}, u32[]{:S(2)}) %collective-permute-start.19) | collective-permute-done | bytes 163872 | tf_op jit(solution)/shard_map/ppermute | solution.py:396
  66.8 4.5 %collective-permute-done.20.p3_ref = bf16[160,512]{1,0:T(8,128)(2,1)S(1)} collective-permute-done((bf16[160,512]{1,0:T(8,128)(2,1)S(1)}, bf16[160,512]{1,0:T(8,128)(2,1)S(1)}, u32[]{:S(2)}, u32[]{:S(2)}) %collective-permute-start.20) | collective-permute-done | bytes 163872 | tf_op jit(solution)/shard_map/ppermute | solution.py:396
  71.3 0.0 copy-done.1
  71.3 0.0 copy-done.2
  71.3 0.0 copy-done.5
  71.3 1.5 %node_update.1 = bf16[160,512]{1,0:T(8,128)(2,1)} custom-call(bf16[160,512]{1,0:T(8,128)(2,1)S(1)} %copy-done, f32[160,512]{1,0:T(8,128)S(1)} %get-tuple-element.24.p0_ref, bf16[160,512]{1,0:T(8,128)(2,1)S(1)} %collective-permute-done.18.p1_ref, bf16[160,512]{1,0:T(8,128)(2,1)S(1)} %collective-permute-done.19.p2_ref, ...), custom_call_target="tpu_custom_call" | custom-call | tf_op jit(solution)/shard_map/node_update/pallas_call | solution.py:348
  (11 shorter events, 0.1 us)
Async XLA Ops:
  3.0 34.4 %copy-start.7 = (s32[1280]{0:T(1024)S(1)}, s32[1280]{0:T(1024)}, u32[]{:S(2)}) copy-start(s32[1280]{0:T(1024)} %param.17) | copy-start | bytes 15364
  3.0 34.4 %copy-start.8 = (s32[1280]{0:T(1024)S(1)}, s32[1280]{0:T(1024)}, u32[]{:S(2)}) copy-start(s32[1280]{0:T(1024)} %param.16) | copy-start | bytes 15364
  3.0 34.5 %copy-start = (bf16[160,512]{1,0:T(8,128)(2,1)S(1)}, bf16[160,512]{1,0:T(8,128)(2,1)}, u32[]{:S(2)}) copy-start(bf16[160,512]{1,0:T(8,128)(2,1)} %nodes_ref.1) | copy-start | bytes 491524
  3.0 34.5 %copy-start.3 = (f32[512]{0:T(512)S(1)}, f32[512]{0:T(512)}, u32[]{:S(2)}) copy-start(f32[512]{0:T(512)} %param.21) | copy-start | bytes 6148
  3.0 11.0 %collective-permute-start = (bf16[176,512]{1,0:T(8,128)(2,1)}, bf16[176,512]{1,0:T(8,128)(2,1)S(1)}, u32[]{:S(2)}, u32[]{:S(2)}) collective-permute-start(bf16[176,512]{1,0:T(8,128)(2,1)} %pack.1.refs_0_), channel_id=1, source_target_pairs={{0,8},{4,12},{8,16},{12,20},{16,24},{20,28},{24,32},{28,36},{32,40... | collective-permute-start | bytes 540680 | tf_op jit(solution)/shard_map/ppermute | solution.py:368
  5.6 6.3 %collective-permute-start.1 = (bf16[160,512]{1,0:T(8,128)(2,1)}, bf16[160,512]{1,0:T(8,128)(2,1)S(1)}, u32[]{:S(2)}, u32[]{:S(2)}) collective-permute-start(bf16[160,512]{1,0:T(8,128)(2,1)} %nodes_ref.1), channel_id=1, source_target_pairs={{0,1},{1,2},{2,3},{3,0},{4,5},{5,6},{6,7},{7,4},{8,9},{9,10},{10,1... | collective-permute-start | bytes 491528 | tf_op jit(solution)/shard_map/ppermute | solution.py:396
  6.9 9.9 %collective-permute-start.2 = (bf16[176,512]{1,0:T(8,128)(2,1)}, bf16[176,512]{1,0:T(8,128)(2,1)S(1)}, u32[]{:S(2)}, u32[]{:S(2)}) collective-permute-start(bf16[176,512]{1,0:T(8,128)(2,1)} %pack.1.refs_0_), channel_id=1, source_target_pairs={{0,56},{4,60},{8,0},{12,4},{16,8},{20,12},{24,16},{28,20},{32,24},... | collective-permute-start | bytes 540680 | tf_op jit(solution)/shard_map/ppermute | solution.py:368
  14.0 6.0 %collective-permute-start.3 = (bf16[176,512]{1,0:T(8,128)(2,1)S(1)}, bf16[176,512]{1,0:T(8,128)(2,1)S(1)}, u32[]{:S(2)}, u32[]{:S(2)}) collective-permute-start(bf16[176,512]{1,0:T(8,128)(2,1)S(1)} %gate.3.refs_1_), channel_id=1, source_target_pairs={{0,8},{4,12},{8,16},{12,20},{16,24},{20,28},{24,32},{28,36},{32,40... | collective-permute-start | bytes 540680 | tf_op jit(solution)/shard_map/ppermute | solution.py:368
  14.0 5.4 %collective-permute-start.4 = (bf16[160,512]{1,0:T(8,128)(2,1)}, bf16[160,512]{1,0:T(8,128)(2,1)S(1)}, u32[]{:S(2)}, u32[]{:S(2)}) collective-permute-start(bf16[160,512]{1,0:T(8,128)(2,1)} %nodes_ref.1), channel_id=1, source_target_pairs={{0,3},{1,0},{2,1},{3,2},{4,7},{5,4},{6,5},{7,6},{8,11},{9,8},{10,9... | collective-permute-start | bytes 491528 | tf_op jit(solution)/shard_map/ppermute | solution.py:396
  16.7 7.2 %collective-permute-start.9 = (bf16[176,512]{1,0:T(8,128)(2,1)S(1)}, bf16[176,512]{1,0:T(8,128)(2,1)S(1)}, u32[]{:S(2)}, u32[]{:S(2)}) collective-permute-start(bf16[176,512]{1,0:T(8,128)(2,1)S(1)} %collective-permute-done.2.refs_2_), channel_id=1, source_target_pairs={{0,56},{4,60},{8,0},{12,4},{16,8},{20,12},{24,16},{28,20},{32,24},... | collective-permute-start | bytes 540680 | tf_op jit(solution)/shard_map/ppermute | solution.py:368
  20.0 6.6 %collective-permute-start.10 = (bf16[176,512]{1,0:T(8,128)(2,1)S(1)}, bf16[176,512]{1,0:T(8,128)(2,1)S(1)}, u32[]{:S(2)}, u32[]{:S(2)}) collective-permute-start(bf16[176,512]{1,0:T(8,128)(2,1)S(1)} %gate.4.refs_3_), channel_id=1, source_target_pairs={{0,8},{4,12},{8,16},{12,20},{16,24},{20,28},{24,32},{28,36},{32,40... | collective-permute-start | bytes 540680 | tf_op jit(solution)/shard_map/ppermute | solution.py:368
  20.0 6.6 %collective-permute-start.8 = (bf16[160,512]{1,0:T(8,128)(2,1)S(1)}, bf16[160,512]{1,0:T(8,128)(2,1)S(1)}, u32[]{:S(2)}, u32[]{:S(2)}) collective-permute-start(bf16[160,512]{1,0:T(8,128)(2,1)S(1)} %collective-permute-done.1.refs_1_.refs_4_), channel_id=1, source_target_pairs={{0,1},{1,2},{2,3},{3,0},{4,5},{5,6},{6,7},{7,4},{8,9},{9,10},{10,1... | collective-permute-start | bytes 491528 | tf_op jit(solution)/shard_map/ppermute | solution.py:396
  22.7 12.9 %collective-permute-start.5 = (bf16[192,512]{1,0:T(8,128)(2,1)S(1)}, bf16[192,512]{1,0:T(8,128)(2,1)S(1)}, u32[]{:S(2)}, u32[]{:S(2)}) collective-permute-start(bf16[192,512]{1,0:T(8,128)(2,1)S(1)} %get-tuple-element.16), channel_id=1, source_target_pairs={{0,64},{4,68},{8,72},{12,76},{16,80},{20,84},{24,88},{28,92},{32,9... | collective-permute-start | bytes 589832 | tf_op jit(solution)/shard_map/ppermute | solution.py:368
  23.9 7.4 %collective-permute-start.11 = (bf16[176,512]{1,0:T(8,128)(2,1)S(1)}, bf16[176,512]{1,0:T(8,128)(2,1)S(1)}, u32[]{:S(2)}, u32[]{:S(2)}) collective-permute-start(bf16[176,512]{1,0:T(8,128)(2,1)S(1)} %collective-permute-done.9.refs_0_), channel_id=1, source_target_pairs={{0,56},{4,60},{8,0},{12,4},{16,8},{20,12},{24,16},{28,20},{32,24},... | collective-permute-start | bytes 540680 | tf_op jit(solution)/shard_map/ppermute | solution.py:368
  26.6 5.6 %collective-permute-start.12 = (bf16[176,512]{1,0:T(8,128)(2,1)S(1)}, bf16[176,512]{1,0:T(8,128)(2,1)S(1)}, u32[]{:S(2)}, u32[]{:S(2)}) collective-permute-start(bf16[176,512]{1,0:T(8,128)(2,1)S(1)} %gate.5.refs_1_), channel_id=1, source_target_pairs={{0,8},{4,12},{8,16},{12,20},{16,24},{20,28},{24,32},{28,36},{32,40... | collective-permute-start | bytes 540680 | tf_op jit(solution)/shard_map/ppermute | solution.py:368
  27.7 16.5 %collective-permute-start.6 = (bf16[192,512]{1,0:T(8,128)(2,1)S(1)}, bf16[192,512]{1,0:T(8,128)(2,1)S(1)}, u32[]{:S(2)}, u32[]{:S(2)}) collective-permute-start(bf16[192,512]{1,0:T(8,128)(2,1)S(1)} %get-tuple-element.17), channel_id=1, source_target_pairs={{0,128},{4,132},{8,136},{12,140},{16,144},{20,148},{24,152},{28,15... | collective-permute-start | bytes 589832 | tf_op jit(solution)/shard_map/ppermute | solution.py:368
  30.5 13.8 %collective-permute-start.7 = (bf16[192,512]{1,0:T(8,128)(2,1)S(1)}, bf16[192,512]{1,0:T(8,128)(2,1)S(1)}, u32[]{:S(2)}, u32[]{:S(2)}) collective-permute-start(bf16[192,512]{1,0:T(8,128)(2,1)S(1)} %get-tuple-element.18), channel_id=1, source_target_pairs={{0,192},{4,196},{8,200},{12,204},{16,208},{20,212},{24,216},{28,22... | collective-permute-start | bytes 589832 | tf_op jit(solution)/shard_map/ppermute | solution.py:368
  32.8 16.9 %collective-permute-start.14 = (bf16[192,512]{1,0:T(8,128)(2,1)S(1)}, bf16[192,512]{1,0:T(8,128)(2,1)S(1)}, u32[]{:S(2)}, u32[]{:S(2)}) collective-permute-start(bf16[192,512]{1,0:T(8,128)(2,1)S(1)} %get-tuple-element.20), channel_id=1, source_target_pairs={{0,64},{4,68},{8,72},{12,76},{16,80},{20,84},{24,88},{28,92},{32,9... | collective-permute-start | bytes 589832 | tf_op jit(solution)/shard_map/ppermute | solution.py:368
  34.1 15.6 %collective-permute-start.15 = (bf16[192,512]{1,0:T(8,128)(2,1)S(1)}, bf16[192,512]{1,0:T(8,128)(2,1)S(1)}, u32[]{:S(2)}, u32[]{:S(2)}) collective-permute-start(bf16[192,512]{1,0:T(8,128)(2,1)S(1)} %get-tuple-element.21), channel_id=1, source_target_pairs={{0,128},{4,132},{8,136},{12,140},{16,144},{20,148},{24,152},{28,15... | collective-permute-start | bytes 589832 | tf_op jit(solution)/shard_map/ppermute | solution.py:368
  35.5 14.2 %collective-permute-start.16 = (bf16[192,512]{1,0:T(8,128)(2,1)S(1)}, bf16[192,512]{1,0:T(8,128)(2,1)S(1)}, u32[]{:S(2)}, u32[]{:S(2)}) collective-permute-start(bf16[192,512]{1,0:T(8,128)(2,1)S(1)} %get-tuple-element.22), channel_id=1, source_target_pairs={{0,192},{4,196},{8,200},{12,204},{16,208},{20,212},{24,216},{28,22... | collective-permute-start | bytes 589832 | tf_op jit(solution)/shard_map/ppermute | solution.py:368
  44.3 7.7 %copy-start.4 = (f32[512]{0:T(512)S(1)}, f32[512]{0:T(512)}, u32[]{:S(2)}) copy-start(f32[512]{0:T(512)} %param.23) | copy-start | bytes 6148
  44.3 7.2 %collective-permute-start.13 = (bf16[384,512]{1,0:T(8,128)(2,1)S(1)}, bf16[384,512]{1,0:T(8,128)(2,1)S(1)}, u32[]{:S(2)}, u32[]{:S(2)}) collective-permute-start(bf16[384,512]{1,0:T(8,128)(2,1)S(1)} %crossing.2), channel_id=1, source_target_pairs={{0,4},{4,0},{8,12},{12,8},{16,20},{20,16},{24,28},{28,24},{32,36},... | collective-permute-start | bytes 1179656 | tf_op jit(solution)/shard_map/ppermute | solution.py:368
  49.7 2.2 %collective-permute-start.17 = (bf16[384,512]{1,0:T(8,128)(2,1)S(1)}, bf16[384,512]{1,0:T(8,128)(2,1)S(1)}, u32[]{:S(2)}, u32[]{:S(2)}) collective-permute-start(bf16[384,512]{1,0:T(8,128)(2,1)S(1)} %crossing.3), channel_id=1, source_target_pairs={{0,4},{4,0},{8,12},{12,8},{16,20},{20,16},{24,28},{28,24},{32,36},... | collective-permute-start | bytes 1179656 | tf_op jit(solution)/shard_map/ppermute | solution.py:368
  52.0 19.3 %copy-start.1 = (bf16[1024,512]{1,0:T(8,128)(2,1)S(1)}, bf16[1024,512]{1,0:T(8,128)(2,1)}, u32[]{:S(2)}) copy-start(bf16[1024,512]{1,0:T(8,128)(2,1)} %w1_ref.1) | copy-start | bytes 3145732
  52.0 19.3 %copy-start.2 = (bf16[512,512]{1,0:T(8,128)(2,1)S(1)}, bf16[512,512]{1,0:T(8,128)(2,1)}, u32[]{:S(2)}) copy-start(bf16[512,512]{1,0:T(8,128)(2,1)} %w2_ref.1) | copy-start | bytes 1572868
  52.0 19.3 %copy-start.5 = (f32[512]{0:T(512)S(1)}, f32[512]{0:T(512)}, u32[]{:S(2)}) copy-start(f32[512]{0:T(512)} %param.25) | copy-start | bytes 6148
  52.0 19.3 %copy-start.6 = (f32[512]{0:T(512)S(1)}, f32[512]{0:T(512)}, u32[]{:S(2)}) copy-start(f32[512]{0:T(512)} %param.27) | copy-start | bytes 6148
  58.4 5.5 %collective-permute-start.18 = (bf16[160,512]{1,0:T(8,128)(2,1)S(1)}, bf16[160,512]{1,0:T(8,128)(2,1)S(1)}, u32[]{:S(2)}, u32[]{:S(2)}) collective-permute-start(bf16[160,512]{1,0:T(8,128)(2,1)S(1)} %get-tuple-element.25), channel_id=1, source_target_pairs={{0,3},{1,0},{2,1},{3,2},{4,7},{5,4},{6,5},{7,6},{8,11},{9,8},{10,9... | collective-permute-start | bytes 491528 | tf_op jit(solution)/shard_map/ppermute | solution.py:396
  60.2 6.6 %collective-permute-start.19 = (bf16[160,512]{1,0:T(8,128)(2,1)S(1)}, bf16[160,512]{1,0:T(8,128)(2,1)S(1)}, u32[]{:S(2)}, u32[]{:S(2)}) collective-permute-start(bf16[160,512]{1,0:T(8,128)(2,1)S(1)} %get-tuple-element.26), channel_id=1, source_target_pairs={{0,2},{1,3},{2,0},{3,1},{4,6},{5,7},{6,4},{7,5},{8,10},{9,11},{10,... | collective-permute-start | bytes 491528 | tf_op jit(solution)/shard_map/ppermute | solution.py:396
  61.2 10.0 %collective-permute-start.20 = (bf16[160,512]{1,0:T(8,128)(2,1)S(1)}, bf16[160,512]{1,0:T(8,128)(2,1)S(1)}, u32[]{:S(2)}, u32[]{:S(2)}) collective-permute-start(bf16[160,512]{1,0:T(8,128)(2,1)S(1)} %get-tuple-element.27), channel_id=1, source_target_pairs={{0,1},{1,2},{2,3},{3,0},{4,5},{5,6},{6,7},{7,4},{8,9},{9,10},{10,1... | collective-permute-start | bytes 491528 | tf_op jit(solution)/shard_map/ppermute | solution.py:396

commit v11 on v10

--- a/solution.py
+++ b/solution.py
@@ -19,8 +19,7 @@
 X, Z, C = 4, 8, 2
 TAIL = 16
 COST = 1 << 20
-NEAR = (1, 3, 2)
-FAR_FIRST = (2, 1, 3)
+NEAR = (1, 3)
 BATCHES = (((0, 1), (7, 2)), ((6, 3), (5, 4)))
 
 
@@ -65,11 +64,10 @@
     return (dz >= 1) & (dz <= 4)
 
 
-def pack_kernel(where_ref, lists_ref, nodes_hbm, out_hbm, block_ref, sems):
-    rows, latent = nodes_hbm.shape
+def pack_kernel(where_ref, lists_ref, nodes_ref, out_ref):
+    rows, latent = nodes_ref.shape
     cap, peers = lists_ref.shape
-    body = pltpu.make_async_copy(nodes_hbm, block_ref.at[pl.ds(0, rows)], sems.at[0])
-    body.start()
+    out_ref[:rows] = nodes_ref[...]
     me = where_ref[0]
     x, z, c = me // (Z * C), me // C % Z, me % C
     lane = lax.broadcasted_iota(i32, (cap, latent), 1)
@@ -85,25 +83,16 @@
     row = lax.broadcasted_iota(i32, (TAIL, peers), 0)
     peer = lax.broadcasted_iota(i32, (TAIL, peers), 1)
     pick = as_bf16(row == ((peer // C % Z - z) & (Z - 1)))
-    block_ref[rows:] = (dot(pick, listed) - 1.0).astype(bf16)
-    body.wait()
-    store = pltpu.make_async_copy(block_ref, out_hbm, sems.at[1])
-    store.start()
-    store.wait()
+    out_ref[rows:] = (dot(pick, listed) - 1.0).astype(bf16)
 
 
 def pack(me, lists, nodes):
     return pl.pallas_call(
         pack_kernel,
-        in_specs=[SMEM, VMEM, HBM],
-        out_specs=HBM,
-        out_shape=pltpu.HBM((nodes.shape[0] + TAIL, nodes.shape[1]), bf16),
-        scratch_shapes=[
-            pltpu.VMEM((nodes.shape[0] + TAIL, nodes.shape[1]), bf16),
-            pltpu.SemaphoreType.DMA((2,)),
-        ],
+        in_specs=[SMEM, VMEM, VMEM],
+        out_shape=jax.ShapeDtypeStruct((nodes.shape[0] + TAIL, nodes.shape[1]), bf16),
         name="pack",
-    )(me, lists, in_hbm(nodes))
+    )(me, lists, nodes)
 
 
 def select_kernel(pairs, cap, extra, *refs):
@@ -183,11 +172,11 @@
     rows = sum(part.shape[0] for part in parts) // C
     return pl.pallas_call(
         cross_kernel,
-        in_specs=[VMEM] * len(parts) + [HBM] * len(earlier),
+        in_specs=[VMEM] * len(parts) + [ANY] * len(earlier),
         out_shape=jax.ShapeDtypeStruct((rows, parts[0].shape[1]), bf16),
         compiler_params=pltpu.CompilerParams(vmem_limit_bytes=LIMIT),
         name="crossing",
-    )(*parts, *[in_hbm(part) for part in earlier])
+    )(*parts, *earlier)
 
 
 def fill(table_ref, groups):
@@ -403,15 +392,17 @@
     forth = back = block
     for hop in range(1, 4):
         forth, back = up(forth), down(back)
-        forth = gate(forth, parts[NEAR[hop - 1]])
+        if hop < 3:
+            forth = gate(forth, parts[NEAR[hop - 1]])
         held[hop], held[Z - hop] = forth, back
     held[4] = up(forth)
 
     groups = []
     for pairs in BATCHES:
-        picked = select(pairs, cap, [held[dz] for pair in pairs for dz in pair])
+        earlier = [parts[2]] if pairs is BATCHES[1] else []
+        picked = select(pairs, cap, [held[dz] for pair in pairs for dz in pair], *earlier)
         arrived = {0: picked[0]}
-        for k in FAR_FIRST:
+        for k in range(1, X):
             arrived[k] = moved(picked[k], lambda x, z, c: (x + k, z, c))
         groups.append([arrived[k] for k in range(X)])
     swap = lambda a: moved(a, lambda x, z, c: (x, z, c + 1))
@@ -436,17 +427,18 @@
         base += X * C * len(pairs) * 2 * cap
     send = jnp.where(sender_slot < patch, near_row(sender_slot), patch + place + entry)
     recv = near_row(receivers).reshape(1, -1)
+    crossed = crossing(groups[0], groups[1][0])
     before = edge_before(
-        recv, send.reshape(1, -1), edge_b1.reshape(1, -1), parts, edges, edge_w1, groups[1][0]
+        recv, send.reshape(1, -1), edge_b1.reshape(1, -1), parts, edges, edge_w1, crossed
     )
-    early = groups[0] + [swap(crossing(groups[0], before))]
-    late = groups[1] + [swap(crossing(groups[1], before))]
+    early = groups[0] + [swap(crossed)]
+    late = groups[1] + [swap(crossing(groups[1], in_hbm(before)))]
     edges_out, *sums = edge_after(
         cap, patch, live_edges, send.reshape(-1, 1), recv, edge_gain.reshape(1, -1), early + late, before,
         edge_w1, edge_w2, edges, rows,
     )
     arrived = {0: sums[0]}
-    for k in FAR_FIRST:
+    for k in range(1, feat):
         arrived[k] = around(sums[k], feat - k)
     parts = [arrived[k] for k in range(feat)]
     nodes_out = node_update(

time: 73 us -> 74.2 us (1.016)
  waiting for transfers between devices: 14.7 us -> 16.6 us
  starting transfers between devices: 37.3 us -> 36.2 us
    ppermute x15, starting transfers between devices: 28.8 us -> 26.4 us  [moved(): return lax.ppermute(value, 'patch', pairs_of(move))]
    ppermute x15, waiting for transfers between devices: 4.04 us -> 5.63 us  [moved(): return lax.ppermute(value, 'patch', pairs_of(move))]
    ppermute x6, starting transfers between devices: 8.52 us -> 9.85 us  [around(): lax.ppermute(value, 'feat', [(i, (i + k) % feat) for i in range(feat)])]
  transfers between devices with their start and end apart: 21 -> 21, of which waited for: 8 -> 7; matrix products, arithmetic and copies ran while one was open for 0% -> 0% of each run, Pallas kernels for 12% -> 12%
where the time goes in v11:
time: 74.2 us; the launch traced here: 73.3 us
  starting transfers between devices  36.2 us (49%)
  Pallas kernels  18.6 us (25%)
  waiting for transfers between devices  16.6 us (22%)
  between operations  1.54 us (2%)
    ppermute x15, starting transfers between devices, moved(): return lax.ppermute(value, 'patch', pairs_of(move))  26.4 us
    ppermute x6, waiting for transfers between devices, around(): lax.ppermute(value, 'feat', [(i, (i + k) % feat) for i in range(feat)])  11 us
    ppermute x6, starting transfers between devices, around(): lax.ppermute(value, 'feat', [(i, (i + k) % feat) for i in range(feat)])  9.85 us
    pallas_call x1, Pallas kernels, edge_before(): pl.pallas_call(lambda *refs: before_kernel(len(earlier), *refs), in_specs...  6.74 us
    pallas_call x1, Pallas kernels, edge_after(): pl.pallas_call(lambda *refs: after_kernel(first_row, *refs), in_specs=[SM...  6.46 us
    ppermute x15, waiting for transfers between devices, moved(): return lax.ppermute(value, 'patch', pairs_of(move))  5.63 us
    pallas_call x2, Pallas kernels, select(): pl.pallas_call(lambda *refs: select_kernel(pairs, cap, len(earlier), *ref...  1.94 us
    pallas_call x1, Pallas kernels, pack(): pl.pallas_call(pack_kernel, in_specs=[SMEM, VMEM, VMEM], out_shape=jax.Sh...  1.93 us
  transfers between devices with their start and end apart: 21, of which 7 were waited for; matrix products, arithmetic and copies ran while one was open for 0% of the time, Pallas kernels for 12%

profile of v11, /device:TPU:1, one launch (start us, length us, event | category | flops | bytes accessed | tf_op | source)
XLA Modules:
  0.0 73.3 jit_solution(13471736245926359416)
XLA Ops:
  0.6 0.0 copy-start.7
  0.6 0.0 copy-start.8
  0.7 1.9 %pack.1.refs_0_ = bf16[176,512]{1,0:T(8,128)(2,1)} custom-call(s32[1]{0:T(128)} %bitcast.1.where_ref, s32[24,64]{1,0:T(8,128)} %bitcast.12, bf16[160,512]{1,0:T(8,128)(2,1)} %nodes_ref.3), custom_call_target="tpu_custom_call" | custom-call | tf_op jit(solution)/shard_map/pack/pallas_call | solution.py:90
  2.6 2.5 %collective-permute-start = (bf16[176,512]{1,0:T(8,128)(2,1)}, bf16[176,512]{1,0:T(8,128)(2,1)S(1)}, u32[]{:S(2)}, u32[]{:S(2)}) collective-permute-start(bf16[176,512]{1,0:T(8,128)(2,1)} %pack.1.refs_0_), channel_id=1, source_target_pairs={{0,8},{4,12},{8,16},{12,20},{16,24},{20,28},{24,32},{28,36},{32,40... | collective-permute-start | bytes 540680 | tf_op jit(solution)/shard_map/ppermute | solution.py:357
  5.0 1.3 %collective-permute-start.1 = (bf16[160,512]{1,0:T(8,128)(2,1)}, bf16[160,512]{1,0:T(8,128)(2,1)S(1)}, u32[]{:S(2)}, u32[]{:S(2)}) collective-permute-start(bf16[160,512]{1,0:T(8,128)(2,1)} %nodes_ref.3), channel_id=1, source_target_pairs={{0,1},{1,2},{2,3},{3,0},{4,5},{5,6},{6,7},{7,4},{8,9},{9,10},{10,1... | collective-permute-start | bytes 491528 | tf_op jit(solution)/shard_map/ppermute | solution.py:385
  6.3 3.9 %collective-permute-start.2 = (bf16[176,512]{1,0:T(8,128)(2,1)}, bf16[176,512]{1,0:T(8,128)(2,1)S(1)}, u32[]{:S(2)}, u32[]{:S(2)}) collective-permute-start(bf16[176,512]{1,0:T(8,128)(2,1)} %pack.1.refs_0_), channel_id=1, source_target_pairs={{0,56},{4,60},{8,0},{12,4},{16,8},{20,12},{24,16},{28,20},{32,24},... | collective-permute-start | bytes 540680 | tf_op jit(solution)/shard_map/ppermute | solution.py:357
  10.3 1.1 %collective-permute-done.1.refs_1_.refs_4_ = bf16[160,512]{1,0:T(8,128)(2,1)S(1)} collective-permute-done((bf16[160,512]{1,0:T(8,128)(2,1)}, bf16[160,512]{1,0:T(8,128)(2,1)S(1)}, u32[]{:S(2)}, u32[]{:S(2)}) %collective-permute-start.1) | collective-permute-done | bytes 163872 | tf_op jit(solution)/shard_map/ppermute | solution.py:385
  11.3 2.1 %collective-permute-done.refs_0_ = bf16[176,512]{1,0:T(8,128)(2,1)S(1)} collective-permute-done((bf16[176,512]{1,0:T(8,128)(2,1)}, bf16[176,512]{1,0:T(8,128)(2,1)S(1)}, u32[]{:S(2)}, u32[]{:S(2)}) %collective-permute-start) | collective-permute-done | bytes 180256 | tf_op jit(solution)/shard_map/ppermute | solution.py:357
  13.5 0.0 collective-permute-start.3
  13.5 2.7 %collective-permute-start.4 = (bf16[160,512]{1,0:T(8,128)(2,1)}, bf16[160,512]{1,0:T(8,128)(2,1)S(1)}, u32[]{:S(2)}, u32[]{:S(2)}) collective-permute-start(bf16[160,512]{1,0:T(8,128)(2,1)} %nodes_ref.3), channel_id=1, source_target_pairs={{0,3},{1,0},{2,1},{3,2},{4,7},{5,4},{6,5},{7,6},{8,11},{9,8},{10,9... | collective-permute-start | bytes 491528 | tf_op jit(solution)/shard_map/ppermute | solution.py:385
  16.2 0.0 collective-permute-done.2.refs_2_
  16.2 2.7 %collective-permute-start.8 = (bf16[176,512]{1,0:T(8,128)(2,1)S(1)}, bf16[176,512]{1,0:T(8,128)(2,1)S(1)}, u32[]{:S(2)}, u32[]{:S(2)}) collective-permute-start(bf16[176,512]{1,0:T(8,128)(2,1)S(1)} %collective-permute-done.2.refs_2_), channel_id=1, source_target_pairs={{0,56},{4,60},{8,0},{12,4},{16,8},{20,12},{24,16},{28,20},{32,24},... | collective-permute-start | bytes 540680 | tf_op jit(solution)/shard_map/ppermute | solution.py:357
  18.9 0.0 collective-permute-done.4.refs_1_.refs_6_
  18.9 0.6 collective-permute-done.3.refs_0_
  19.5 0.0 copy-start
  19.5 0.0 collective-permute-start.9
  19.6 1.4 %collective-permute-start.12 = (bf16[160,512]{1,0:T(8,128)(2,1)S(1)}, bf16[160,512]{1,0:T(8,128)(2,1)S(1)}, u32[]{:S(2)}, u32[]{:S(2)}) collective-permute-start(bf16[160,512]{1,0:T(8,128)(2,1)S(1)} %collective-permute-done.1.refs_1_.refs_4_), channel_id=1, source_target_pairs={{0,1},{1,2},{2,3},{3,0},{4,5},{5,6},{6,7},{7,4},{8,9},{9,10},{10,1... | collective-permute-start | bytes 491528 | tf_op jit(solution)/shard_map/ppermute | solution.py:385
  20.9 1.3 %select.24 = (bf16[192,512]{1,0:T(8,128)(2,1)S(1)}, bf16[192,512]{1,0:T(8,128)(2,1)S(1)}, bf16[192,512]{1,0:T(8,128)(2,1)S(1)}, bf16[192,512]{1,0:T(8,128)(2,1)S(1)}) custom-call(bf16[176,512]{1,0:T(8,128)(2,1)} %pack.1.refs_0_, bf16[176,512]{1,0:T(8,128)(2,1)S(1)} %gate.2.refs_1_, bf16[176,512]{1,0:T(8,128)(2,1)S(1)} %collective-permute-done.2.refs_2_, ...), custom_call_target="tpu_custom_call" | custom-call | flops 1048576 | tf_op jit(solution)/shard_map/select/pallas_call | solution.py:134
  22.3 1.3 %collective-permute-start.5 = (bf16[192,512]{1,0:T(8,128)(2,1)S(1)}, bf16[192,512]{1,0:T(8,128)(2,1)S(1)}, u32[]{:S(2)}, u32[]{:S(2)}) collective-permute-start(bf16[192,512]{1,0:T(8,128)(2,1)S(1)} %get-tuple-element.16), channel_id=1, source_target_pairs={{0,64},{4,68},{8,72},{12,76},{16,80},{20,84},{24,88},{28,92},{32,9... | collective-permute-start | bytes 589832 | tf_op jit(solution)/shard_map/ppermute | solution.py:357
  23.6 0.0 collective-permute-done.8.refs_0_
  23.6 2.6 %collective-permute-start.10 = (bf16[176,512]{1,0:T(8,128)(2,1)S(1)}, bf16[176,512]{1,0:T(8,128)(2,1)S(1)}, u32[]{:S(2)}, u32[]{:S(2)}) collective-permute-start(bf16[176,512]{1,0:T(8,128)(2,1)S(1)} %collective-permute-done.8.refs_0_), channel_id=1, source_target_pairs={{0,56},{4,60},{8,0},{12,4},{16,8},{20,12},{24,16},{28,20},{32,24},... | collective-permute-start | bytes 540680 | tf_op jit(solution)/shard_map/ppermute | solution.py:357
  26.1 0.0 collective-permute-done.9.refs_1_
  26.1 0.0 collective-permute-start.11
  26.1 0.0 copy-done.7
  26.1 0.1 fusion.4
  26.2 2.5 %collective-permute-start.6 = (bf16[192,512]{1,0:T(8,128)(2,1)S(1)}, bf16[192,512]{1,0:T(8,128)(2,1)S(1)}, u32[]{:S(2)}, u32[]{:S(2)}) collective-permute-start(bf16[192,512]{1,0:T(8,128)(2,1)S(1)} %get-tuple-element.17), channel_id=1, source_target_pairs={{0,128},{4,132},{8,136},{12,140},{16,144},{20,148},{24,152},{28,15... | collective-permute-start | bytes 589832 | tf_op jit(solution)/shard_map/ppermute | solution.py:357
  28.7 0.0 collective-permute-done.12.refs_4_.refs_5_
  28.7 1.2 %collective-permute-start.7 = (bf16[192,512]{1,0:T(8,128)(2,1)S(1)}, bf16[192,512]{1,0:T(8,128)(2,1)S(1)}, u32[]{:S(2)}, u32[]{:S(2)}) collective-permute-start(bf16[192,512]{1,0:T(8,128)(2,1)S(1)} %get-tuple-element.18), channel_id=1, source_target_pairs={{0,192},{4,196},{8,200},{12,204},{16,208},{20,212},{24,216},{28,22... | collective-permute-start | bytes 589832 | tf_op jit(solution)/shard_map/ppermute | solution.py:357
  29.9 0.0 collective-permute-done.10.refs_2_
  29.9 2.1 %collective-permute-done.11.refs_3_ = bf16[176,512]{1,0:T(8,128)(2,1)S(1)} collective-permute-done((bf16[176,512]{1,0:T(8,128)(2,1)S(1)}, bf16[176,512]{1,0:T(8,128)(2,1)S(1)}, u32[]{:S(2)}, u32[]{:S(2)}) %collective-permute-start.11) | collective-permute-done | bytes 180256 | tf_op jit(solution)/shard_map/ppermute | solution.py:357
  32.0 0.6 select.25
  32.6 1.0 %collective-permute-start.14 = (bf16[192,512]{1,0:T(8,128)(2,1)S(1)}, bf16[192,512]{1,0:T(8,128)(2,1)S(1)}, u32[]{:S(2)}, u32[]{:S(2)}) collective-permute-start(bf16[192,512]{1,0:T(8,128)(2,1)S(1)} %get-tuple-element.20), channel_id=1, source_target_pairs={{0,64},{4,68},{8,72},{12,76},{16,80},{20,84},{24,88},{28,92},{32,9... | collective-permute-start | bytes 589832 | tf_op jit(solution)/shard_map/ppermute | solution.py:357
  33.6 1.5 %collective-permute-start.15 = (bf16[192,512]{1,0:T(8,128)(2,1)S(1)}, bf16[192,512]{1,0:T(8,128)(2,1)S(1)}, u32[]{:S(2)}, u32[]{:S(2)}) collective-permute-start(bf16[192,512]{1,0:T(8,128)(2,1)S(1)} %get-tuple-element.21), channel_id=1, source_target_pairs={{0,128},{4,132},{8,136},{12,140},{16,144},{20,148},{24,152},{28,15... | collective-permute-start | bytes 589832 | tf_op jit(solution)/shard_map/ppermute | solution.py:357
  35.1 0.0 collective-permute-done.5.refs_1_.refs_5_
  35.1 1.8 %collective-permute-start.16 = (bf16[192,512]{1,0:T(8,128)(2,1)S(1)}, bf16[192,512]{1,0:T(8,128)(2,1)S(1)}, u32[]{:S(2)}, u32[]{:S(2)}) collective-permute-start(bf16[192,512]{1,0:T(8,128)(2,1)S(1)} %get-tuple-element.22), channel_id=1, source_target_pairs={{0,192},{4,196},{8,200},{12,204},{16,208},{20,212},{24,216},{28,22... | collective-permute-start | bytes 589832 | tf_op jit(solution)/shard_map/ppermute | solution.py:357
  36.9 0.0 copy-done.8
  36.9 0.0 collective-permute-done.6.refs_2_.refs_6_
  36.9 0.0 collective-permute-done.7.refs_3_.refs_7_
  37.0 5.3 %collective-permute-start.13 = (bf16[384,512]{1,0:T(8,128)(2,1)S(1)}, bf16[384,512]{1,0:T(8,128)(2,1)S(1)}, u32[]{:S(2)}, u32[]{:S(2)}) collective-permute-start(bf16[384,512]{1,0:T(8,128)(2,1)S(1)} %crossing.2.refs_9_), channel_id=1, source_target_pairs={{0,4},{4,0},{8,12},{12,8},{16,20},{20,16},{24,28},{28,24},{32,36},... | collective-permute-start | bytes 1179656 | tf_op jit(solution)/shard_map/ppermute | solution.py:357
  42.3 0.0 copy-done
  42.3 0.0 copy-done.3
  42.3 6.7 %edge_before.1.refs_4_.refs_14_ = f32[1280,512]{1,0:T(8,128)} custom-call(s32[1,1280]{1,0:T(1,128)S(1)} %reshape.29.refs_0_.refs_2_, s32[1,1280]{1,0:T(1,128)S(1)} %reshape.32.refs_1_, f32[1,512]{1,0:T(1,128)S(1)} %bitcast.8, bf16[160,512]{1,0:T(8,128)(2,1)S(1)} %copy-done, bf16[160,512]{1,0:T(8,128)(2,1)S(1)} %collective-permute-done.1.refs_1_.refs_4_, ...), custom_call_target="tpu_custom_call" | custom-call | flops 1048576 | tf_op jit(solution)/shard_map/edge_before/pallas_call | solution.py:232
  49.1 0.0 copy-start.4
  49.1 0.0 collective-permute-done.14.refs_1_.refs_10_
  49.1 0.0 collective-permute-done.15.refs_2_.refs_11_
  49.1 0.0 collective-permute-done.16.refs_3_.refs_12_
  49.2 0.1 collective-permute-start.17
  49.3 0.2 reshape.36.refs_1_
  50.2 0.0 collective-permute-done.13.refs_8_
  50.2 0.8 %collective-permute-done.17.refs_13_ = bf16[384,512]{1,0:T(8,128)(2,1)S(1)} collective-permute-done((bf16[384,512]{1,0:T(8,128)(2,1)S(1)}, bf16[384,512]{1,0:T(8,128)(2,1)S(1)}, u32[]{:S(2)}, u32[]{:S(2)}) %collective-permute-start.17) | collective-permute-done | bytes 393248 | tf_op jit(solution)/shard_map/ppermute | solution.py:357
  51.0 0.0 copy-done.4
  51.0 0.0 copy-start.6
  51.0 6.5 %edge_after.1 = (bf16[1280,512]{1,0:T(8,128)(2,1)}, f32[160,512]{1,0:T(8,128)S(1)}, bf16[160,512]{1,0:T(8,128)(2,1)S(1)}, bf16[160,512]{1,0:T(8,128)(2,1)S(1)}, bf16[160,512]{1,0:T(8,128)(2,1)S(1)}) custom-call(s32[1]{0:T(128)S(6)} %copy.21.refs_0_, s32[1280,1]{1,0:T(8,128)S(1)} %reshape.36.refs_1_, s32[1,1280]{1,0:T(1,128)S(1)} %reshape.29.refs_0_.refs_2_, ...), custom_call_target="tpu_custom_call" | custom-call | tf_op jit(solution)/shard_map/edge_after/pallas_call | solution.py:303
  57.5 3.8 %collective-permute-start.18 = (bf16[160,512]{1,0:T(8,128)(2,1)S(1)}, bf16[160,512]{1,0:T(8,128)(2,1)S(1)}, u32[]{:S(2)}, u32[]{:S(2)}) collective-permute-start(bf16[160,512]{1,0:T(8,128)(2,1)S(1)} %get-tuple-element.25), channel_id=1, source_target_pairs={{0,3},{1,0},{2,1},{3,2},{4,7},{5,4},{6,5},{7,6},{8,11},{9,8},{10,9... | collective-permute-start | bytes 491528 | tf_op jit(solution)/shard_map/ppermute | solution.py:385
  61.2 0.0 collective-permute-start.19
  61.2 0.7 collective-permute-start.20
  61.9 6.4 %collective-permute-done.18.p1_ref = bf16[160,512]{1,0:T(8,128)(2,1)S(1)} collective-permute-done((bf16[160,512]{1,0:T(8,128)(2,1)S(1)}, bf16[160,512]{1,0:T(8,128)(2,1)S(1)}, u32[]{:S(2)}, u32[]{:S(2)}) %collective-permute-start.18) | collective-permute-done | bytes 163872 | tf_op jit(solution)/shard_map/ppermute | solution.py:385
  68.3 0.0 collective-permute-done.19.p2_ref
  68.3 3.5 %collective-permute-done.20.p3_ref = bf16[160,512]{1,0:T(8,128)(2,1)S(1)} collective-permute-done((bf16[160,512]{1,0:T(8,128)(2,1)S(1)}, bf16[160,512]{1,0:T(8,128)(2,1)S(1)}, u32[]{:S(2)}, u32[]{:S(2)}) %collective-permute-start.20) | collective-permute-done | bytes 163872 | tf_op jit(solution)/shard_map/ppermute | solution.py:385
  71.8 0.0 copy-done.1
  71.8 0.0 copy-done.2
  71.8 0.0 copy-done.5
  71.8 0.0 copy-done.6
  71.8 1.5 %node_update.1 = bf16[160,512]{1,0:T(8,128)(2,1)} custom-call(bf16[160,512]{1,0:T(8,128)(2,1)S(1)} %copy-done, f32[160,512]{1,0:T(8,128)S(1)} %get-tuple-element.24.p0_ref, bf16[160,512]{1,0:T(8,128)(2,1)S(1)} %collective-permute-done.18.p1_ref, bf16[160,512]{1,0:T(8,128)(2,1)S(1)} %collective-permute-done.19.p2_ref, ...), custom_call_target="tpu_custom_call" | custom-call | tf_op jit(solution)/shard_map/node_update/pallas_call | solution.py:337
  (11 shorter events, 0.1 us)
Async XLA Ops:
  0.6 25.5 %copy-start.7 = (s32[1280]{0:T(1024)S(1)}, s32[1280]{0:T(1024)}, u32[]{:S(2)}) copy-start(s32[1280]{0:T(1024)} %param.17) | copy-start | bytes 15364
  0.6 36.3 %copy-start.8 = (s32[1280]{0:T(1024)S(1)}, s32[1280]{0:T(1024)}, u32[]{:S(2)}) copy-start(s32[1280]{0:T(1024)} %param.16) | copy-start | bytes 15364
  2.6 10.9 %collective-permute-start = (bf16[176,512]{1,0:T(8,128)(2,1)}, bf16[176,512]{1,0:T(8,128)(2,1)S(1)}, u32[]{:S(2)}, u32[]{:S(2)}) collective-permute-start(bf16[176,512]{1,0:T(8,128)(2,1)} %pack.1.refs_0_), channel_id=1, source_target_pairs={{0,8},{4,12},{8,16},{12,20},{16,24},{20,28},{24,32},{28,36},{32,40... | collective-permute-start | bytes 540680 | tf_op jit(solution)/shard_map/ppermute | solution.py:357
  5.0 6.3 %collective-permute-start.1 = (bf16[160,512]{1,0:T(8,128)(2,1)}, bf16[160,512]{1,0:T(8,128)(2,1)S(1)}, u32[]{:S(2)}, u32[]{:S(2)}) collective-permute-start(bf16[160,512]{1,0:T(8,128)(2,1)} %nodes_ref.3), channel_id=1, source_target_pairs={{0,1},{1,2},{2,3},{3,0},{4,5},{5,6},{6,7},{7,4},{8,9},{9,10},{10,1... | collective-permute-start | bytes 491528 | tf_op jit(solution)/shard_map/ppermute | solution.py:385
  6.3 9.9 %collective-permute-start.2 = (bf16[176,512]{1,0:T(8,128)(2,1)}, bf16[176,512]{1,0:T(8,128)(2,1)S(1)}, u32[]{:S(2)}, u32[]{:S(2)}) collective-permute-start(bf16[176,512]{1,0:T(8,128)(2,1)} %pack.1.refs_0_), channel_id=1, source_target_pairs={{0,56},{4,60},{8,0},{12,4},{16,8},{20,12},{24,16},{28,20},{32,24},... | collective-permute-start | bytes 540680 | tf_op jit(solution)/shard_map/ppermute | solution.py:357
  13.5 6.0 %collective-permute-start.3 = (bf16[176,512]{1,0:T(8,128)(2,1)S(1)}, bf16[176,512]{1,0:T(8,128)(2,1)S(1)}, u32[]{:S(2)}, u32[]{:S(2)}) collective-permute-start(bf16[176,512]{1,0:T(8,128)(2,1)S(1)} %gate.2.refs_1_), channel_id=1, source_target_pairs={{0,8},{4,12},{8,16},{12,20},{16,24},{20,28},{24,32},{28,36},{32,40... | collective-permute-start | bytes 540680 | tf_op jit(solution)/shard_map/ppermute | solution.py:357
  13.5 5.4 %collective-permute-start.4 = (bf16[160,512]{1,0:T(8,128)(2,1)}, bf16[160,512]{1,0:T(8,128)(2,1)S(1)}, u32[]{:S(2)}, u32[]{:S(2)}) collective-permute-start(bf16[160,512]{1,0:T(8,128)(2,1)} %nodes_ref.3), channel_id=1, source_target_pairs={{0,3},{1,0},{2,1},{3,2},{4,7},{5,4},{6,5},{7,6},{8,11},{9,8},{10,9... | collective-permute-start | bytes 491528 | tf_op jit(solution)/shard_map/ppermute | solution.py:385
  16.2 7.3 %collective-permute-start.8 = (bf16[176,512]{1,0:T(8,128)(2,1)S(1)}, bf16[176,512]{1,0:T(8,128)(2,1)S(1)}, u32[]{:S(2)}, u32[]{:S(2)}) collective-permute-start(bf16[176,512]{1,0:T(8,128)(2,1)S(1)} %collective-permute-done.2.refs_2_), channel_id=1, source_target_pairs={{0,56},{4,60},{8,0},{12,4},{16,8},{20,12},{24,16},{28,20},{32,24},... | collective-permute-start | bytes 540680 | tf_op jit(solution)/shard_map/ppermute | solution.py:357
  19.5 22.8 %copy-start = (bf16[160,512]{1,0:T(8,128)(2,1)S(1)}, bf16[160,512]{1,0:T(8,128)(2,1)}, u32[]{:S(2)}) copy-start(bf16[160,512]{1,0:T(8,128)(2,1)} %nodes_ref.3) | copy-start | bytes 491524
  19.5 22.8 %copy-start.3 = (f32[512]{0:T(512)S(1)}, f32[512]{0:T(512)}, u32[]{:S(2)}) copy-start(f32[512]{0:T(512)} %param.21) | copy-start | bytes 6148
  19.5 6.6 %collective-permute-start.9 = (bf16[176,512]{1,0:T(8,128)(2,1)S(1)}, bf16[176,512]{1,0:T(8,128)(2,1)S(1)}, u32[]{:S(2)}, u32[]{:S(2)}) collective-permute-start(bf16[176,512]{1,0:T(8,128)(2,1)S(1)} %gate.3.refs_3_), channel_id=1, source_target_pairs={{0,8},{4,12},{8,16},{12,20},{16,24},{20,28},{24,32},{28,36},{32,40... | collective-permute-start | bytes 540680 | tf_op jit(solution)/shard_map/ppermute | solution.py:357
  19.6 9.2 %collective-permute-start.12 = (bf16[160,512]{1,0:T(8,128)(2,1)S(1)}, bf16[160,512]{1,0:T(8,128)(2,1)S(1)}, u32[]{:S(2)}, u32[]{:S(2)}) collective-permute-start(bf16[160,512]{1,0:T(8,128)(2,1)S(1)} %collective-permute-done.1.refs_1_.refs_4_), channel_id=1, source_target_pairs={{0,1},{1,2},{2,3},{3,0},{4,5},{5,6},{6,7},{7,4},{8,9},{9,10},{10,1... | collective-permute-start | bytes 491528 | tf_op jit(solution)/shard_map/ppermute | solution.py:385
  22.3 12.8 %collective-permute-start.5 = (bf16[192,512]{1,0:T(8,128)(2,1)S(1)}, bf16[192,512]{1,0:T(8,128)(2,1)S(1)}, u32[]{:S(2)}, u32[]{:S(2)}) collective-permute-start(bf16[192,512]{1,0:T(8,128)(2,1)S(1)} %get-tuple-element.16), channel_id=1, source_target_pairs={{0,64},{4,68},{8,72},{12,76},{16,80},{20,84},{24,88},{28,92},{32,9... | collective-permute-start | bytes 589832 | tf_op jit(solution)/shard_map/ppermute | solution.py:357
  23.6 6.3 %collective-permute-start.10 = (bf16[176,512]{1,0:T(8,128)(2,1)S(1)}, bf16[176,512]{1,0:T(8,128)(2,1)S(1)}, u32[]{:S(2)}, u32[]{:S(2)}) collective-permute-start(bf16[176,512]{1,0:T(8,128)(2,1)S(1)} %collective-permute-done.8.refs_0_), channel_id=1, source_target_pairs={{0,56},{4,60},{8,0},{12,4},{16,8},{20,12},{24,16},{28,20},{32,24},... | collective-permute-start | bytes 540680 | tf_op jit(solution)/shard_map/ppermute | solution.py:357
  26.1 5.9 %collective-permute-start.11 = (bf16[176,512]{1,0:T(8,128)(2,1)S(1)}, bf16[176,512]{1,0:T(8,128)(2,1)S(1)}, u32[]{:S(2)}, u32[]{:S(2)}) collective-permute-start(bf16[176,512]{1,0:T(8,128)(2,1)S(1)} %collective-permute-done.9.refs_1_), channel_id=1, source_target_pairs={{0,8},{4,12},{8,16},{12,20},{16,24},{20,28},{24,32},{28,36},{32,40... | collective-permute-start | bytes 540680 | tf_op jit(solution)/shard_map/ppermute | solution.py:357
  26.2 10.7 %collective-permute-start.6 = (bf16[192,512]{1,0:T(8,128)(2,1)S(1)}, bf16[192,512]{1,0:T(8,128)(2,1)S(1)}, u32[]{:S(2)}, u32[]{:S(2)}) collective-permute-start(bf16[192,512]{1,0:T(8,128)(2,1)S(1)} %get-tuple-element.17), channel_id=1, source_target_pairs={{0,128},{4,132},{8,136},{12,140},{16,144},{20,148},{24,152},{28,15... | collective-permute-start | bytes 589832 | tf_op jit(solution)/shard_map/ppermute | solution.py:357
  28.7 8.2 %collective-permute-start.7 = (bf16[192,512]{1,0:T(8,128)(2,1)S(1)}, bf16[192,512]{1,0:T(8,128)(2,1)S(1)}, u32[]{:S(2)}, u32[]{:S(2)}) collective-permute-start(bf16[192,512]{1,0:T(8,128)(2,1)S(1)} %get-tuple-element.18), channel_id=1, source_target_pairs={{0,192},{4,196},{8,200},{12,204},{16,208},{20,212},{24,216},{28,22... | collective-permute-start | bytes 589832 | tf_op jit(solution)/shard_map/ppermute | solution.py:357
  32.6 16.5 %collective-permute-start.14 = (bf16[192,512]{1,0:T(8,128)(2,1)S(1)}, bf16[192,512]{1,0:T(8,128)(2,1)S(1)}, u32[]{:S(2)}, u32[]{:S(2)}) collective-permute-start(bf16[192,512]{1,0:T(8,128)(2,1)S(1)} %get-tuple-element.20), channel_id=1, source_target_pairs={{0,64},{4,68},{8,72},{12,76},{16,80},{20,84},{24,88},{28,92},{32,9... | collective-permute-start | bytes 589832 | tf_op jit(solution)/shard_map/ppermute | solution.py:357
  33.6 15.5 %collective-permute-start.15 = (bf16[192,512]{1,0:T(8,128)(2,1)S(1)}, bf16[192,512]{1,0:T(8,128)(2,1)S(1)}, u32[]{:S(2)}, u32[]{:S(2)}) collective-permute-start(bf16[192,512]{1,0:T(8,128)(2,1)S(1)} %get-tuple-element.21), channel_id=1, source_target_pairs={{0,128},{4,132},{8,136},{12,140},{16,144},{20,148},{24,152},{28,15... | collective-permute-start | bytes 589832 | tf_op jit(solution)/shard_map/ppermute | solution.py:357
  35.1 14.0 %collective-permute-start.16 = (bf16[192,512]{1,0:T(8,128)(2,1)S(1)}, bf16[192,512]{1,0:T(8,128)(2,1)S(1)}, u32[]{:S(2)}, u32[]{:S(2)}) collective-permute-start(bf16[192,512]{1,0:T(8,128)(2,1)S(1)} %get-tuple-element.22), channel_id=1, source_target_pairs={{0,192},{4,196},{8,200},{12,204},{16,208},{20,212},{24,216},{28,22... | collective-permute-start | bytes 589832 | tf_op jit(solution)/shard_map/ppermute | solution.py:357
  37.0 13.2 %collective-permute-start.13 = (bf16[384,512]{1,0:T(8,128)(2,1)S(1)}, bf16[384,512]{1,0:T(8,128)(2,1)S(1)}, u32[]{:S(2)}, u32[]{:S(2)}) collective-permute-start(bf16[384,512]{1,0:T(8,128)(2,1)S(1)} %crossing.2.refs_9_), channel_id=1, source_target_pairs={{0,4},{4,0},{8,12},{12,8},{16,20},{20,16},{24,28},{28,24},{32,36},... | collective-permute-start | bytes 1179656 | tf_op jit(solution)/shard_map/ppermute | solution.py:357
  49.1 1.9 %copy-start.4 = (f32[512]{0:T(512)S(1)}, f32[512]{0:T(512)}, u32[]{:S(2)}) copy-start(f32[512]{0:T(512)} %param.23) | copy-start | bytes 6148
  49.2 1.8 %collective-permute-start.17 = (bf16[384,512]{1,0:T(8,128)(2,1)S(1)}, bf16[384,512]{1,0:T(8,128)(2,1)S(1)}, u32[]{:S(2)}, u32[]{:S(2)}) collective-permute-start(bf16[384,512]{1,0:T(8,128)(2,1)S(1)} %crossing.3), channel_id=1, source_target_pairs={{0,4},{4,0},{8,12},{12,8},{16,20},{20,16},{24,28},{28,24},{32,36},... | collective-permute-start | bytes 1179656 | tf_op jit(solution)/shard_map/ppermute | solution.py:357
  51.0 20.8 %copy-start.1 = (bf16[1024,512]{1,0:T(8,128)(2,1)S(1)}, bf16[1024,512]{1,0:T(8,128)(2,1)}, u32[]{:S(2)}) copy-start(bf16[1024,512]{1,0:T(8,128)(2,1)} %w1_ref.1) | copy-start | bytes 3145732
  51.0 20.8 %copy-start.2 = (bf16[512,512]{1,0:T(8,128)(2,1)S(1)}, bf16[512,512]{1,0:T(8,128)(2,1)}, u32[]{:S(2)}) copy-start(bf16[512,512]{1,0:T(8,128)(2,1)} %w2_ref.1) | copy-start | bytes 1572868
  51.0 20.8 %copy-start.5 = (f32[512]{0:T(512)S(1)}, f32[512]{0:T(512)}, u32[]{:S(2)}) copy-start(f32[512]{0:T(512)} %param.25) | copy-start | bytes 6148
  51.0 20.8 %copy-start.6 = (f32[512]{0:T(512)S(1)}, f32[512]{0:T(512)}, u32[]{:S(2)}) copy-start(f32[512]{0:T(512)} %param.27) | copy-start | bytes 6148
  57.5 10.8 %collective-permute-start.18 = (bf16[160,512]{1,0:T(8,128)(2,1)S(1)}, bf16[160,512]{1,0:T(8,128)(2,1)S(1)}, u32[]{:S(2)}, u32[]{:S(2)}) collective-permute-start(bf16[160,512]{1,0:T(8,128)(2,1)S(1)} %get-tuple-element.25), channel_id=1, source_target_pairs={{0,3},{1,0},{2,1},{3,2},{4,7},{5,4},{6,5},{7,6},{8,11},{9,8},{10,9... | collective-permute-start | bytes 491528 | tf_op jit(solution)/shard_map/ppermute | solution.py:385
  61.2 7.1 %collective-permute-start.19 = (bf16[160,512]{1,0:T(8,128)(2,1)S(1)}, bf16[160,512]{1,0:T(8,128)(2,1)S(1)}, u32[]{:S(2)}, u32[]{:S(2)}) collective-permute-start(bf16[160,512]{1,0:T(8,128)(2,1)S(1)} %get-tuple-element.26), channel_id=1, source_target_pairs={{0,2},{1,3},{2,0},{3,1},{4,6},{5,7},{6,4},{7,5},{8,10},{9,11},{10,... | collective-permute-start | bytes 491528 | tf_op jit(solution)/shard_map/ppermute | solution.py:385
  61.2 10.6 %collective-permute-start.20 = (bf16[160,512]{1,0:T(8,128)(2,1)S(1)}, bf16[160,512]{1,0:T(8,128)(2,1)S(1)}, u32[]{:S(2)}, u32[]{:S(2)}) collective-permute-start(bf16[160,512]{1,0:T(8,128)(2,1)S(1)} %get-tuple-element.27), channel_id=1, source_target_pairs={{0,1},{1,2},{2,3},{3,0},{4,5},{5,6},{6,7},{7,4},{8,9},{9,10},{10,1... | collective-permute-start | bytes 491528 | tf_op jit(solution)/shard_map/ppermute | solution.py:385

commit v12 on v11

--- a/solution.py
+++ b/solution.py
@@ -10,6 +10,7 @@
 bf16 = jnp.bfloat16
 i32 = jnp.int32
 TILES = 2
+BEFORE_TILES = 2
 GATHERS = 1
 LIMIT = 16 << 20
 VMEM = pl.BlockSpec(memory_space=pltpu.VMEM)
@@ -172,7 +173,7 @@
     rows = sum(part.shape[0] for part in parts) // C
     return pl.pallas_call(
         cross_kernel,
-        in_specs=[VMEM] * len(parts) + [ANY] * len(earlier),
+        in_specs=[VMEM] * len(parts) + [HBM] * len(earlier),
         out_shape=jax.ShapeDtypeStruct((rows, parts[0].shape[1]), bf16),
         compiler_params=pltpu.CompilerParams(vmem_limit_bytes=LIMIT),
         name="crossing",
@@ -195,32 +196,34 @@
     parts = refs[3:7]
     edges_hbm, w1_hbm = refs[7:9]
     out_hbm, table_ref, edges_ref, w1_ref, out_ref, sems = refs[9 + extra :]
-    loads = [
-        pltpu.make_async_copy(w1_hbm, w1_ref, sems.at[0]),
-        pltpu.make_async_copy(edges_hbm, edges_ref, sems.at[1]),
-    ]
-    for load in loads:
-        load.start()
     count, latent = edges_ref.shape
     size = parts[0].shape[0]
     nodes = table_ref.shape[0]
-    tile = count // TILES
+    tile = count // BEFORE_TILES
+    loads = [pltpu.make_async_copy(w1_hbm, w1_ref, sems.at[0])]
+    for at in range(BEFORE_TILES):
+        part = pl.ds(at * tile, tile)
+        loads.append(
+            pltpu.make_async_copy(edges_hbm.at[part], edges_ref.at[part], sems.at[1 + at])
+        )
+    for load in loads:
+        load.start()
     for k, part in enumerate(parts):
         table_ref[k * size : (k + 1) * size] = part[...]
     stores = []
-    for at in range(TILES):
+    for at in range(BEFORE_TILES):
         rows = slice(at * tile, (at + 1) * tile)
         own = dot_first(hot_columns(recv_ref[:, rows], nodes), table_ref[...]).astype(bf16)
         near = dot_first(hot_columns(send_ref[:, rows], nodes), table_ref[...]).astype(bf16)
         if at == 0:
-            for load in loads:
-                load.wait()
+            loads[0].wait()
+        loads[1 + at].wait()
         total = dot(edges_ref[rows], w1_ref[:latent])
         total = total + dot(near, w1_ref[latent : 2 * latent])
         total = total + dot(own, w1_ref[2 * latent :])
         out_ref[rows] = total + b1_ref[...]
         part = pl.ds(at * tile, tile)
-        stores.append(pltpu.make_async_copy(out_ref.at[part], out_hbm.at[part], sems.at[2 + at]))
+        stores.append(pltpu.make_async_copy(out_ref.at[part], out_hbm.at[part], sems.at[1 + BEFORE_TILES + at]))
         stores[-1].start()
     for store in stores:
         store.wait()
@@ -239,7 +242,7 @@
             pltpu.VMEM((count, latent), bf16),
             pltpu.VMEM(w1.shape, bf16),
             pltpu.VMEM((count, latent), f32),
-            pltpu.SemaphoreType.DMA((2 + TILES,)),
+            pltpu.SemaphoreType.DMA((1 + 2 * BEFORE_TILES,)),
         ],
         compiler_params=pltpu.CompilerParams(vmem_limit_bytes=32 << 20),
         cost_estimate=pl.CostEstimate(flops=COST, bytes_accessed=0, transcendentals=0),
@@ -427,11 +430,10 @@
         base += X * C * len(pairs) * 2 * cap
     send = jnp.where(sender_slot < patch, near_row(sender_slot), patch + place + entry)
     recv = near_row(receivers).reshape(1, -1)
-    crossed = crossing(groups[0], groups[1][0])
     before = edge_before(
-        recv, send.reshape(1, -1), edge_b1.reshape(1, -1), parts, edges, edge_w1, crossed
+        recv, send.reshape(1, -1), edge_b1.reshape(1, -1), parts, edges, edge_w1, groups[1][0]
     )
-    early = groups[0] + [swap(crossed)]
+    early = groups[0] + [swap(crossing(groups[0], in_hbm(before)))]
     late = groups[1] + [swap(crossing(groups[1], in_hbm(before)))]
     edges_out, *sums = edge_after(
         cap, patch, live_edges, send.reshape(-1, 1), recv, edge_gain.reshape(1, -1), early + late, before,

time: 74.2 us -> 72.4 us (0.976)
    ppermute x6, starting transfers between devices: 9.85 us -> 8.89 us  [around(): lax.ppermute(value, 'feat', [(i, (i + k) % feat) for i in range(feat)])]
  transfers between devices with their start and end apart: 21 -> 21, of which waited for: 7 -> 9; matrix products, arithmetic and copies ran while one was open for 0% -> 0% of each run, Pallas kernels for 12% -> 12%
where the time goes in v12:
time: 72.4 us; the launch traced here: 72.2 us
  starting transfers between devices  35.5 us (49%)
  Pallas kernels  18.6 us (26%)
  waiting for transfers between devices  16.3 us (23%)
  between operations  1.49 us (2%)
    ppermute x15, starting transfers between devices, moved(): return lax.ppermute(value, 'patch', pairs_of(move))  26.6 us
    ppermute x6, waiting for transfers between devices, around(): lax.ppermute(value, 'feat', [(i, (i + k) % feat) for i in range(feat)])  10.7 us
    ppermute x6, starting transfers between devices, around(): lax.ppermute(value, 'feat', [(i, (i + k) % feat) for i in range(feat)])  8.89 us
    pallas_call x1, Pallas kernels, edge_before(): pl.pallas_call(lambda *refs: before_kernel(len(earlier), *refs), in_specs...  6.68 us
    pallas_call x1, Pallas kernels, edge_after(): pl.pallas_call(lambda *refs: after_kernel(first_row, *refs), in_specs=[SM...  6.46 us
    ppermute x15, waiting for transfers between devices, moved(): return lax.ppermute(value, 'patch', pairs_of(move))  5.58 us
    pallas_call x1, Pallas kernels, pack(): pl.pallas_call(pack_kernel, in_specs=[SMEM, VMEM, VMEM], out_shape=jax.Sh...  1.96 us
    pallas_call x2, Pallas kernels, select(): pl.pallas_call(lambda *refs: select_kernel(pairs, cap, len(earlier), *ref...  1.94 us
  transfers between devices with their start and end apart: 21, of which 9 were waited for; matrix products, arithmetic and copies ran while one was open for 0% of the time, Pallas kernels for 12%

profile of v12, /device:TPU:1, one launch (start us, length us, event | category | flops | bytes accessed | tf_op | source)
XLA Modules:
  0.0 72.2 jit_solution(13119850364187621896)
XLA Ops:
  0.6 0.0 copy-start.7
  0.6 0.0 copy-start.8
  0.7 0.0 copy-start
  0.7 0.0 copy-start.3
  0.7 2.0 %pack.1.refs_0_ = bf16[176,512]{1,0:T(8,128)(2,1)} custom-call(s32[1]{0:T(128)} %bitcast.1.where_ref, s32[24,64]{1,0:T(8,128)} %bitcast.12, bf16[160,512]{1,0:T(8,128)(2,1)} %nodes_ref.3), custom_call_target="tpu_custom_call" | custom-call | tf_op jit(solution)/shard_map/pack/pallas_call | solution.py:91
  2.6 2.5 %collective-permute-start = (bf16[176,512]{1,0:T(8,128)(2,1)}, bf16[176,512]{1,0:T(8,128)(2,1)S(1)}, u32[]{:S(2)}, u32[]{:S(2)}) collective-permute-start(bf16[176,512]{1,0:T(8,128)(2,1)} %pack.1.refs_0_), channel_id=1, source_target_pairs={{0,8},{4,12},{8,16},{12,20},{16,24},{20,28},{24,32},{28,36},{32,40... | collective-permute-start | bytes 540680 | tf_op jit(solution)/shard_map/ppermute | solution.py:360
  5.1 1.3 %collective-permute-start.1 = (bf16[160,512]{1,0:T(8,128)(2,1)}, bf16[160,512]{1,0:T(8,128)(2,1)S(1)}, u32[]{:S(2)}, u32[]{:S(2)}) collective-permute-start(bf16[160,512]{1,0:T(8,128)(2,1)} %nodes_ref.3), channel_id=1, source_target_pairs={{0,1},{1,2},{2,3},{3,0},{4,5},{5,6},{6,7},{7,4},{8,9},{9,10},{10,1... | collective-permute-start | bytes 491528 | tf_op jit(solution)/shard_map/ppermute | solution.py:388
  6.4 3.9 %collective-permute-start.2 = (bf16[176,512]{1,0:T(8,128)(2,1)}, bf16[176,512]{1,0:T(8,128)(2,1)S(1)}, u32[]{:S(2)}, u32[]{:S(2)}) collective-permute-start(bf16[176,512]{1,0:T(8,128)(2,1)} %pack.1.refs_0_), channel_id=1, source_target_pairs={{0,56},{4,60},{8,0},{12,4},{16,8},{20,12},{24,16},{28,20},{32,24},... | collective-permute-start | bytes 540680 | tf_op jit(solution)/shard_map/ppermute | solution.py:360
  10.3 1.1 %collective-permute-done.1.refs_1_.refs_4_ = bf16[160,512]{1,0:T(8,128)(2,1)S(1)} collective-permute-done((bf16[160,512]{1,0:T(8,128)(2,1)}, bf16[160,512]{1,0:T(8,128)(2,1)S(1)}, u32[]{:S(2)}, u32[]{:S(2)}) %collective-permute-start.1) | collective-permute-done | bytes 163872 | tf_op jit(solution)/shard_map/ppermute | solution.py:388
  11.4 2.1 %collective-permute-done.refs_0_ = bf16[176,512]{1,0:T(8,128)(2,1)S(1)} collective-permute-done((bf16[176,512]{1,0:T(8,128)(2,1)}, bf16[176,512]{1,0:T(8,128)(2,1)S(1)}, u32[]{:S(2)}, u32[]{:S(2)}) %collective-permute-start) | collective-permute-done | bytes 180256 | tf_op jit(solution)/shard_map/ppermute | solution.py:360
  13.5 0.0 collective-permute-start.3
  13.5 2.7 %collective-permute-start.4 = (bf16[160,512]{1,0:T(8,128)(2,1)}, bf16[160,512]{1,0:T(8,128)(2,1)S(1)}, u32[]{:S(2)}, u32[]{:S(2)}) collective-permute-start(bf16[160,512]{1,0:T(8,128)(2,1)} %nodes_ref.3), channel_id=1, source_target_pairs={{0,3},{1,0},{2,1},{3,2},{4,7},{5,4},{6,5},{7,6},{8,11},{9,8},{10,9... | collective-permute-start | bytes 491528 | tf_op jit(solution)/shard_map/ppermute | solution.py:388
  16.3 0.0 collective-permute-done.2.refs_2_
  16.3 2.7 %collective-permute-start.9 = (bf16[176,512]{1,0:T(8,128)(2,1)S(1)}, bf16[176,512]{1,0:T(8,128)(2,1)S(1)}, u32[]{:S(2)}, u32[]{:S(2)}) collective-permute-start(bf16[176,512]{1,0:T(8,128)(2,1)S(1)} %collective-permute-done.2.refs_2_), channel_id=1, source_target_pairs={{0,56},{4,60},{8,0},{12,4},{16,8},{20,12},{24,16},{28,20},{32,24},... | collective-permute-start | bytes 540680 | tf_op jit(solution)/shard_map/ppermute | solution.py:360
  18.9 0.0 collective-permute-done.4.refs_1_.refs_6_
  18.9 0.6 collective-permute-done.3.refs_0_
  19.6 0.0 collective-permute-start.10
  19.6 1.3 %collective-permute-start.8 = (bf16[160,512]{1,0:T(8,128)(2,1)S(1)}, bf16[160,512]{1,0:T(8,128)(2,1)S(1)}, u32[]{:S(2)}, u32[]{:S(2)}) collective-permute-start(bf16[160,512]{1,0:T(8,128)(2,1)S(1)} %collective-permute-done.1.refs_1_.refs_4_), channel_id=1, source_target_pairs={{0,1},{1,2},{2,3},{3,0},{4,5},{5,6},{6,7},{7,4},{8,9},{9,10},{10,1... | collective-permute-start | bytes 491528 | tf_op jit(solution)/shard_map/ppermute | solution.py:388
  20.9 1.3 %select.24 = (bf16[192,512]{1,0:T(8,128)(2,1)S(1)}, bf16[192,512]{1,0:T(8,128)(2,1)S(1)}, bf16[192,512]{1,0:T(8,128)(2,1)S(1)}, bf16[192,512]{1,0:T(8,128)(2,1)S(1)}) custom-call(bf16[176,512]{1,0:T(8,128)(2,1)} %pack.1.refs_0_, bf16[176,512]{1,0:T(8,128)(2,1)S(1)} %gate.2.refs_1_, bf16[176,512]{1,0:T(8,128)(2,1)S(1)} %collective-permute-done.2.refs_2_, ...), custom_call_target="tpu_custom_call" | custom-call | flops 1048576 | tf_op jit(solution)/shard_map/select/pallas_call | solution.py:135
  22.2 1.3 %collective-permute-start.5 = (bf16[192,512]{1,0:T(8,128)(2,1)S(1)}, bf16[192,512]{1,0:T(8,128)(2,1)S(1)}, u32[]{:S(2)}, u32[]{:S(2)}) collective-permute-start(bf16[192,512]{1,0:T(8,128)(2,1)S(1)} %get-tuple-element.16), channel_id=1, source_target_pairs={{0,64},{4,68},{8,72},{12,76},{16,80},{20,84},{24,88},{28,92},{32,9... | collective-permute-start | bytes 589832 | tf_op jit(solution)/shard_map/ppermute | solution.py:360
  23.5 0.0 collective-permute-done.9.refs_0_
  23.5 2.7 %collective-permute-start.11 = (bf16[176,512]{1,0:T(8,128)(2,1)S(1)}, bf16[176,512]{1,0:T(8,128)(2,1)S(1)}, u32[]{:S(2)}, u32[]{:S(2)}) collective-permute-start(bf16[176,512]{1,0:T(8,128)(2,1)S(1)} %collective-permute-done.9.refs_0_), channel_id=1, source_target_pairs={{0,56},{4,60},{8,0},{12,4},{16,8},{20,12},{24,16},{28,20},{32,24},... | collective-permute-start | bytes 540680 | tf_op jit(solution)/shard_map/ppermute | solution.py:360
  26.2 0.0 collective-permute-done.10.refs_1_
  26.2 0.0 collective-permute-start.12
  26.2 0.0 copy-done.7
  26.2 0.1 fusion.4
  26.3 2.5 %collective-permute-start.6 = (bf16[192,512]{1,0:T(8,128)(2,1)S(1)}, bf16[192,512]{1,0:T(8,128)(2,1)S(1)}, u32[]{:S(2)}, u32[]{:S(2)}) collective-permute-start(bf16[192,512]{1,0:T(8,128)(2,1)S(1)} %get-tuple-element.17), channel_id=1, source_target_pairs={{0,128},{4,132},{8,136},{12,140},{16,144},{20,148},{24,152},{28,15... | collective-permute-start | bytes 589832 | tf_op jit(solution)/shard_map/ppermute | solution.py:360
  28.8 0.0 collective-permute-done.8.refs_4_.refs_5_
  28.8 1.2 %collective-permute-start.7 = (bf16[192,512]{1,0:T(8,128)(2,1)S(1)}, bf16[192,512]{1,0:T(8,128)(2,1)S(1)}, u32[]{:S(2)}, u32[]{:S(2)}) collective-permute-start(bf16[192,512]{1,0:T(8,128)(2,1)S(1)} %get-tuple-element.18), channel_id=1, source_target_pairs={{0,192},{4,196},{8,200},{12,204},{16,208},{20,212},{24,216},{28,22... | collective-permute-start | bytes 589832 | tf_op jit(solution)/shard_map/ppermute | solution.py:360
  29.9 0.0 collective-permute-done.11.refs_2_
  29.9 2.0 %collective-permute-done.12.refs_3_ = bf16[176,512]{1,0:T(8,128)(2,1)S(1)} collective-permute-done((bf16[176,512]{1,0:T(8,128)(2,1)S(1)}, bf16[176,512]{1,0:T(8,128)(2,1)S(1)}, u32[]{:S(2)}, u32[]{:S(2)}) %collective-permute-start.12) | collective-permute-done | bytes 180256 | tf_op jit(solution)/shard_map/ppermute | solution.py:360
  31.9 0.6 select.25
  32.5 1.1 %collective-permute-start.14 = (bf16[192,512]{1,0:T(8,128)(2,1)S(1)}, bf16[192,512]{1,0:T(8,128)(2,1)S(1)}, u32[]{:S(2)}, u32[]{:S(2)}) collective-permute-start(bf16[192,512]{1,0:T(8,128)(2,1)S(1)} %get-tuple-element.20), channel_id=1, source_target_pairs={{0,64},{4,68},{8,72},{12,76},{16,80},{20,84},{24,88},{28,92},{32,9... | collective-permute-start | bytes 589832 | tf_op jit(solution)/shard_map/ppermute | solution.py:360
  33.6 1.5 %collective-permute-start.15 = (bf16[192,512]{1,0:T(8,128)(2,1)S(1)}, bf16[192,512]{1,0:T(8,128)(2,1)S(1)}, u32[]{:S(2)}, u32[]{:S(2)}) collective-permute-start(bf16[192,512]{1,0:T(8,128)(2,1)S(1)} %get-tuple-element.21), channel_id=1, source_target_pairs={{0,128},{4,132},{8,136},{12,140},{16,144},{20,148},{24,152},{28,15... | collective-permute-start | bytes 589832 | tf_op jit(solution)/shard_map/ppermute | solution.py:360
  35.1 0.0 collective-permute-done.5.refs_1_.refs_5_
  35.2 1.8 %collective-permute-start.16 = (bf16[192,512]{1,0:T(8,128)(2,1)S(1)}, bf16[192,512]{1,0:T(8,128)(2,1)S(1)}, u32[]{:S(2)}, u32[]{:S(2)}) collective-permute-start(bf16[192,512]{1,0:T(8,128)(2,1)S(1)} %get-tuple-element.22), channel_id=1, source_target_pairs={{0,192},{4,196},{8,200},{12,204},{16,208},{20,212},{24,216},{28,22... | collective-permute-start | bytes 589832 | tf_op jit(solution)/shard_map/ppermute | solution.py:360
  36.9 0.0 copy-done.8
  37.0 0.0 copy-done
  37.0 0.0 copy-done.3
  37.0 6.7 %edge_before.1.refs_4_.refs_14_ = f32[1280,512]{1,0:T(8,128)} custom-call(s32[1,1280]{1,0:T(1,128)S(1)} %reshape.29.refs_0_.refs_2_, s32[1,1280]{1,0:T(1,128)S(1)} %reshape.32.refs_1_, f32[1,512]{1,0:T(1,128)S(1)} %bitcast.8, bf16[160,512]{1,0:T(8,128)(2,1)S(1)} %copy-done, bf16[160,512]{1,0:T(8,128)(2,1)S(1)} %collective-permute-done.1.refs_1_.refs_4_, ...), custom_call_target="tpu_custom_call" | custom-call | flops 1048576 | tf_op jit(solution)/shard_map/edge_before/pallas_call | solution.py:235
  43.7 0.0 collective-permute-done.6.refs_2_.refs_6_
  43.7 0.0 collective-permute-done.7.refs_3_.refs_7_
  43.7 0.0 copy-start.4
  43.8 5.3 %collective-permute-start.13 = (bf16[384,512]{1,0:T(8,128)(2,1)S(1)}, bf16[384,512]{1,0:T(8,128)(2,1)S(1)}, u32[]{:S(2)}, u32[]{:S(2)}) collective-permute-start(bf16[384,512]{1,0:T(8,128)(2,1)S(1)} %crossing.2), channel_id=1, source_target_pairs={{0,4},{4,0},{8,12},{12,8},{16,20},{20,16},{24,28},{28,24},{32,36},... | collective-permute-start | bytes 1179656 | tf_op jit(solution)/shard_map/ppermute | solution.py:360
  49.1 0.0 collective-permute-done.14.refs_1_.refs_10_
  49.1 0.0 collective-permute-done.15.refs_2_.refs_11_
  49.1 0.0 collective-permute-done.16.refs_3_.refs_12_
  49.2 0.1 collective-permute-start.17
  49.3 0.2 reshape.36.refs_1_
  50.2 0.3 collective-permute-done.13.refs_8_
  50.5 0.6 collective-permute-done.17.refs_13_
  51.0 0.0 copy-done.4
  51.0 0.0 copy-start.6
  51.0 6.5 %edge_after.1 = (bf16[1280,512]{1,0:T(8,128)(2,1)}, f32[160,512]{1,0:T(8,128)S(1)}, bf16[160,512]{1,0:T(8,128)(2,1)S(1)}, bf16[160,512]{1,0:T(8,128)(2,1)S(1)}, bf16[160,512]{1,0:T(8,128)(2,1)S(1)}) custom-call(s32[1]{0:T(128)S(6)} %copy.21.refs_0_, s32[1280,1]{1,0:T(8,128)S(1)} %reshape.36.refs_1_, s32[1,1280]{1,0:T(1,128)S(1)} %reshape.29.refs_0_.refs_2_, ...), custom_call_target="tpu_custom_call" | custom-call | tf_op jit(solution)/shard_map/edge_after/pallas_call | solution.py:306
  57.5 2.1 %collective-permute-start.18 = (bf16[160,512]{1,0:T(8,128)(2,1)S(1)}, bf16[160,512]{1,0:T(8,128)(2,1)S(1)}, u32[]{:S(2)}, u32[]{:S(2)}) collective-permute-start(bf16[160,512]{1,0:T(8,128)(2,1)S(1)} %get-tuple-element.25), channel_id=1, source_target_pairs={{0,3},{1,0},{2,1},{3,2},{4,7},{5,4},{6,5},{7,6},{8,11},{9,8},{10,9... | collective-permute-start | bytes 491528 | tf_op jit(solution)/shard_map/ppermute | solution.py:388
  59.6 1.1 %collective-permute-start.19 = (bf16[160,512]{1,0:T(8,128)(2,1)S(1)}, bf16[160,512]{1,0:T(8,128)(2,1)S(1)}, u32[]{:S(2)}, u32[]{:S(2)}) collective-permute-start(bf16[160,512]{1,0:T(8,128)(2,1)S(1)} %get-tuple-element.26), channel_id=1, source_target_pairs={{0,2},{1,3},{2,0},{3,1},{4,6},{5,7},{6,4},{7,5},{8,10},{9,11},{10,... | collective-permute-start | bytes 491528 | tf_op jit(solution)/shard_map/ppermute | solution.py:388
  60.7 0.4 collective-permute-start.20
  61.1 2.1 %collective-permute-done.18.p1_ref = bf16[160,512]{1,0:T(8,128)(2,1)S(1)} collective-permute-done((bf16[160,512]{1,0:T(8,128)(2,1)S(1)}, bf16[160,512]{1,0:T(8,128)(2,1)S(1)}, u32[]{:S(2)}, u32[]{:S(2)}) %collective-permute-start.18) | collective-permute-done | bytes 163872 | tf_op jit(solution)/shard_map/ppermute | solution.py:388
  63.1 3.1 %collective-permute-done.19.p2_ref = bf16[160,512]{1,0:T(8,128)(2,1)S(1)} collective-permute-done((bf16[160,512]{1,0:T(8,128)(2,1)S(1)}, bf16[160,512]{1,0:T(8,128)(2,1)S(1)}, u32[]{:S(2)}, u32[]{:S(2)}) %collective-permute-start.19) | collective-permute-done | bytes 163872 | tf_op jit(solution)/shard_map/ppermute | solution.py:388
  66.2 4.5 %collective-permute-done.20.p3_ref = bf16[160,512]{1,0:T(8,128)(2,1)S(1)} collective-permute-done((bf16[160,512]{1,0:T(8,128)(2,1)S(1)}, bf16[160,512]{1,0:T(8,128)(2,1)S(1)}, u32[]{:S(2)}, u32[]{:S(2)}) %collective-permute-start.20) | collective-permute-done | bytes 163872 | tf_op jit(solution)/shard_map/ppermute | solution.py:388
  70.7 0.0 copy-done.1
  70.7 0.0 copy-done.2
  70.7 0.0 copy-done.5
  70.7 1.5 %node_update.1 = bf16[160,512]{1,0:T(8,128)(2,1)} custom-call(bf16[160,512]{1,0:T(8,128)(2,1)S(1)} %copy-done, f32[160,512]{1,0:T(8,128)S(1)} %get-tuple-element.24.p0_ref, bf16[160,512]{1,0:T(8,128)(2,1)S(1)} %collective-permute-done.18.p1_ref, bf16[160,512]{1,0:T(8,128)(2,1)S(1)} %collective-permute-done.19.p2_ref, ...), custom_call_target="tpu_custom_call" | custom-call | tf_op jit(solution)/shard_map/node_update/pallas_call | solution.py:340
  (11 shorter events, 0.1 us)
Async XLA Ops:
  0.6 25.5 %copy-start.7 = (s32[1280]{0:T(1024)S(1)}, s32[1280]{0:T(1024)}, u32[]{:S(2)}) copy-start(s32[1280]{0:T(1024)} %param.17) | copy-start | bytes 15364
  0.6 36.3 %copy-start.8 = (s32[1280]{0:T(1024)S(1)}, s32[1280]{0:T(1024)}, u32[]{:S(2)}) copy-start(s32[1280]{0:T(1024)} %param.16) | copy-start | bytes 15364
  0.7 36.3 %copy-start = (bf16[160,512]{1,0:T(8,128)(2,1)S(1)}, bf16[160,512]{1,0:T(8,128)(2,1)}, u32[]{:S(2)}) copy-start(bf16[160,512]{1,0:T(8,128)(2,1)} %nodes_ref.3) | copy-start | bytes 491524
  0.7 36.3 %copy-start.3 = (f32[512]{0:T(512)S(1)}, f32[512]{0:T(512)}, u32[]{:S(2)}) copy-start(f32[512]{0:T(512)} %param.21) | copy-start | bytes 6148
  2.6 10.9 %collective-permute-start = (bf16[176,512]{1,0:T(8,128)(2,1)}, bf16[176,512]{1,0:T(8,128)(2,1)S(1)}, u32[]{:S(2)}, u32[]{:S(2)}) collective-permute-start(bf16[176,512]{1,0:T(8,128)(2,1)} %pack.1.refs_0_), channel_id=1, source_target_pairs={{0,8},{4,12},{8,16},{12,20},{16,24},{20,28},{24,32},{28,36},{32,40... | collective-permute-start | bytes 540680 | tf_op jit(solution)/shard_map/ppermute | solution.py:360
  5.1 6.3 %collective-permute-start.1 = (bf16[160,512]{1,0:T(8,128)(2,1)}, bf16[160,512]{1,0:T(8,128)(2,1)S(1)}, u32[]{:S(2)}, u32[]{:S(2)}) collective-permute-start(bf16[160,512]{1,0:T(8,128)(2,1)} %nodes_ref.3), channel_id=1, source_target_pairs={{0,1},{1,2},{2,3},{3,0},{4,5},{5,6},{6,7},{7,4},{8,9},{9,10},{10,1... | collective-permute-start | bytes 491528 | tf_op jit(solution)/shard_map/ppermute | solution.py:388
  6.4 9.9 %collective-permute-start.2 = (bf16[176,512]{1,0:T(8,128)(2,1)}, bf16[176,512]{1,0:T(8,128)(2,1)S(1)}, u32[]{:S(2)}, u32[]{:S(2)}) collective-permute-start(bf16[176,512]{1,0:T(8,128)(2,1)} %pack.1.refs_0_), channel_id=1, source_target_pairs={{0,56},{4,60},{8,0},{12,4},{16,8},{20,12},{24,16},{28,20},{32,24},... | collective-permute-start | bytes 540680 | tf_op jit(solution)/shard_map/ppermute | solution.py:360
  13.5 6.0 %collective-permute-start.3 = (bf16[176,512]{1,0:T(8,128)(2,1)S(1)}, bf16[176,512]{1,0:T(8,128)(2,1)S(1)}, u32[]{:S(2)}, u32[]{:S(2)}) collective-permute-start(bf16[176,512]{1,0:T(8,128)(2,1)S(1)} %gate.2.refs_1_), channel_id=1, source_target_pairs={{0,8},{4,12},{8,16},{12,20},{16,24},{20,28},{24,32},{28,36},{32,40... | collective-permute-start | bytes 540680 | tf_op jit(solution)/shard_map/ppermute | solution.py:360
  13.5 5.4 %collective-permute-start.4 = (bf16[160,512]{1,0:T(8,128)(2,1)}, bf16[160,512]{1,0:T(8,128)(2,1)S(1)}, u32[]{:S(2)}, u32[]{:S(2)}) collective-permute-start(bf16[160,512]{1,0:T(8,128)(2,1)} %nodes_ref.3), channel_id=1, source_target_pairs={{0,3},{1,0},{2,1},{3,2},{4,7},{5,4},{6,5},{7,6},{8,11},{9,8},{10,9... | collective-permute-start | bytes 491528 | tf_op jit(solution)/shard_map/ppermute | solution.py:388
  16.3 7.2 %collective-permute-start.9 = (bf16[176,512]{1,0:T(8,128)(2,1)S(1)}, bf16[176,512]{1,0:T(8,128)(2,1)S(1)}, u32[]{:S(2)}, u32[]{:S(2)}) collective-permute-start(bf16[176,512]{1,0:T(8,128)(2,1)S(1)} %collective-permute-done.2.refs_2_), channel_id=1, source_target_pairs={{0,56},{4,60},{8,0},{12,4},{16,8},{20,12},{24,16},{28,20},{32,24},... | collective-permute-start | bytes 540680 | tf_op jit(solution)/shard_map/ppermute | solution.py:360
  19.6 6.6 %collective-permute-start.10 = (bf16[176,512]{1,0:T(8,128)(2,1)S(1)}, bf16[176,512]{1,0:T(8,128)(2,1)S(1)}, u32[]{:S(2)}, u32[]{:S(2)}) collective-permute-start(bf16[176,512]{1,0:T(8,128)(2,1)S(1)} %gate.3.refs_3_), channel_id=1, source_target_pairs={{0,8},{4,12},{8,16},{12,20},{16,24},{20,28},{24,32},{28,36},{32,40... | collective-permute-start | bytes 540680 | tf_op jit(solution)/shard_map/ppermute | solution.py:360
  19.6 9.2 %collective-permute-start.8 = (bf16[160,512]{1,0:T(8,128)(2,1)S(1)}, bf16[160,512]{1,0:T(8,128)(2,1)S(1)}, u32[]{:S(2)}, u32[]{:S(2)}) collective-permute-start(bf16[160,512]{1,0:T(8,128)(2,1)S(1)} %collective-permute-done.1.refs_1_.refs_4_), channel_id=1, source_target_pairs={{0,1},{1,2},{2,3},{3,0},{4,5},{5,6},{6,7},{7,4},{8,9},{9,10},{10,1... | collective-permute-start | bytes 491528 | tf_op jit(solution)/shard_map/ppermute | solution.py:388
  22.2 13.0 %collective-permute-start.5 = (bf16[192,512]{1,0:T(8,128)(2,1)S(1)}, bf16[192,512]{1,0:T(8,128)(2,1)S(1)}, u32[]{:S(2)}, u32[]{:S(2)}) collective-permute-start(bf16[192,512]{1,0:T(8,128)(2,1)S(1)} %get-tuple-element.16), channel_id=1, source_target_pairs={{0,64},{4,68},{8,72},{12,76},{16,80},{20,84},{24,88},{28,92},{32,9... | collective-permute-start | bytes 589832 | tf_op jit(solution)/shard_map/ppermute | solution.py:360
  23.5 6.5 %collective-permute-start.11 = (bf16[176,512]{1,0:T(8,128)(2,1)S(1)}, bf16[176,512]{1,0:T(8,128)(2,1)S(1)}, u32[]{:S(2)}, u32[]{:S(2)}) collective-permute-start(bf16[176,512]{1,0:T(8,128)(2,1)S(1)} %collective-permute-done.9.refs_0_), channel_id=1, source_target_pairs={{0,56},{4,60},{8,0},{12,4},{16,8},{20,12},{24,16},{28,20},{32,24},... | collective-permute-start | bytes 540680 | tf_op jit(solution)/shard_map/ppermute | solution.py:360
  26.2 5.7 %collective-permute-start.12 = (bf16[176,512]{1,0:T(8,128)(2,1)S(1)}, bf16[176,512]{1,0:T(8,128)(2,1)S(1)}, u32[]{:S(2)}, u32[]{:S(2)}) collective-permute-start(bf16[176,512]{1,0:T(8,128)(2,1)S(1)} %collective-permute-done.10.refs_1_), channel_id=1, source_target_pairs={{0,8},{4,12},{8,16},{12,20},{16,24},{20,28},{24,32},{28,36},{32,40... | collective-permute-start | bytes 540680 | tf_op jit(solution)/shard_map/ppermute | solution.py:360
  26.3 17.4 %collective-permute-start.6 = (bf16[192,512]{1,0:T(8,128)(2,1)S(1)}, bf16[192,512]{1,0:T(8,128)(2,1)S(1)}, u32[]{:S(2)}, u32[]{:S(2)}) collective-permute-start(bf16[192,512]{1,0:T(8,128)(2,1)S(1)} %get-tuple-element.17), channel_id=1, source_target_pairs={{0,128},{4,132},{8,136},{12,140},{16,144},{20,148},{24,152},{28,15... | collective-permute-start | bytes 589832 | tf_op jit(solution)/shard_map/ppermute | solution.py:360
  28.8 14.9 %collective-permute-start.7 = (bf16[192,512]{1,0:T(8,128)(2,1)S(1)}, bf16[192,512]{1,0:T(8,128)(2,1)S(1)}, u32[]{:S(2)}, u32[]{:S(2)}) collective-permute-start(bf16[192,512]{1,0:T(8,128)(2,1)S(1)} %get-tuple-element.18), channel_id=1, source_target_pairs={{0,192},{4,196},{8,200},{12,204},{16,208},{20,212},{24,216},{28,22... | collective-permute-start | bytes 589832 | tf_op jit(solution)/shard_map/ppermute | solution.py:360
  32.5 16.6 %collective-permute-start.14 = (bf16[192,512]{1,0:T(8,128)(2,1)S(1)}, bf16[192,512]{1,0:T(8,128)(2,1)S(1)}, u32[]{:S(2)}, u32[]{:S(2)}) collective-permute-start(bf16[192,512]{1,0:T(8,128)(2,1)S(1)} %get-tuple-element.20), channel_id=1, source_target_pairs={{0,64},{4,68},{8,72},{12,76},{16,80},{20,84},{24,88},{28,92},{32,9... | collective-permute-start | bytes 589832 | tf_op jit(solution)/shard_map/ppermute | solution.py:360
  33.6 15.5 %collective-permute-start.15 = (bf16[192,512]{1,0:T(8,128)(2,1)S(1)}, bf16[192,512]{1,0:T(8,128)(2,1)S(1)}, u32[]{:S(2)}, u32[]{:S(2)}) collective-permute-start(bf16[192,512]{1,0:T(8,128)(2,1)S(1)} %get-tuple-element.21), channel_id=1, source_target_pairs={{0,128},{4,132},{8,136},{12,140},{16,144},{20,148},{24,152},{28,15... | collective-permute-start | bytes 589832 | tf_op jit(solution)/shard_map/ppermute | solution.py:360
  35.2 14.0 %collective-permute-start.16 = (bf16[192,512]{1,0:T(8,128)(2,1)S(1)}, bf16[192,512]{1,0:T(8,128)(2,1)S(1)}, u32[]{:S(2)}, u32[]{:S(2)}) collective-permute-start(bf16[192,512]{1,0:T(8,128)(2,1)S(1)} %get-tuple-element.22), channel_id=1, source_target_pairs={{0,192},{4,196},{8,200},{12,204},{16,208},{20,212},{24,216},{28,22... | collective-permute-start | bytes 589832 | tf_op jit(solution)/shard_map/ppermute | solution.py:360
  43.7 7.3 %copy-start.4 = (f32[512]{0:T(512)S(1)}, f32[512]{0:T(512)}, u32[]{:S(2)}) copy-start(f32[512]{0:T(512)} %param.23) | copy-start | bytes 6148
  43.8 6.7 %collective-permute-start.13 = (bf16[384,512]{1,0:T(8,128)(2,1)S(1)}, bf16[384,512]{1,0:T(8,128)(2,1)S(1)}, u32[]{:S(2)}, u32[]{:S(2)}) collective-permute-start(bf16[384,512]{1,0:T(8,128)(2,1)S(1)} %crossing.2), channel_id=1, source_target_pairs={{0,4},{4,0},{8,12},{12,8},{16,20},{20,16},{24,28},{28,24},{32,36},... | collective-permute-start | bytes 1179656 | tf_op jit(solution)/shard_map/ppermute | solution.py:360
  49.2 1.9 %collective-permute-start.17 = (bf16[384,512]{1,0:T(8,128)(2,1)S(1)}, bf16[384,512]{1,0:T(8,128)(2,1)S(1)}, u32[]{:S(2)}, u32[]{:S(2)}) collective-permute-start(bf16[384,512]{1,0:T(8,128)(2,1)S(1)} %crossing.3), channel_id=1, source_target_pairs={{0,4},{4,0},{8,12},{12,8},{16,20},{20,16},{24,28},{28,24},{32,36},... | collective-permute-start | bytes 1179656 | tf_op jit(solution)/shard_map/ppermute | solution.py:360
  51.0 19.7 %copy-start.1 = (bf16[1024,512]{1,0:T(8,128)(2,1)S(1)}, bf16[1024,512]{1,0:T(8,128)(2,1)}, u32[]{:S(2)}) copy-start(bf16[1024,512]{1,0:T(8,128)(2,1)} %w1_ref.1) | copy-start | bytes 3145732
  51.0 19.7 %copy-start.2 = (bf16[512,512]{1,0:T(8,128)(2,1)S(1)}, bf16[512,512]{1,0:T(8,128)(2,1)}, u32[]{:S(2)}) copy-start(bf16[512,512]{1,0:T(8,128)(2,1)} %w2_ref.1) | copy-start | bytes 1572868
  51.0 19.7 %copy-start.5 = (f32[512]{0:T(512)S(1)}, f32[512]{0:T(512)}, u32[]{:S(2)}) copy-start(f32[512]{0:T(512)} %param.25) | copy-start | bytes 6148
  51.0 19.7 %copy-start.6 = (f32[512]{0:T(512)S(1)}, f32[512]{0:T(512)}, u32[]{:S(2)}) copy-start(f32[512]{0:T(512)} %param.27) | copy-start | bytes 6148
  57.5 5.6 %collective-permute-start.18 = (bf16[160,512]{1,0:T(8,128)(2,1)S(1)}, bf16[160,512]{1,0:T(8,128)(2,1)S(1)}, u32[]{:S(2)}, u32[]{:S(2)}) collective-permute-start(bf16[160,512]{1,0:T(8,128)(2,1)S(1)} %get-tuple-element.25), channel_id=1, source_target_pairs={{0,3},{1,0},{2,1},{3,2},{4,7},{5,4},{6,5},{7,6},{8,11},{9,8},{10,9... | collective-permute-start | bytes 491528 | tf_op jit(solution)/shard_map/ppermute | solution.py:388
  59.6 6.6 %collective-permute-start.19 = (bf16[160,512]{1,0:T(8,128)(2,1)S(1)}, bf16[160,512]{1,0:T(8,128)(2,1)S(1)}, u32[]{:S(2)}, u32[]{:S(2)}) collective-permute-start(bf16[160,512]{1,0:T(8,128)(2,1)S(1)} %get-tuple-element.26), channel_id=1, source_target_pairs={{0,2},{1,3},{2,0},{3,1},{4,6},{5,7},{6,4},{7,5},{8,10},{9,11},{10,... | collective-permute-start | bytes 491528 | tf_op jit(solution)/shard_map/ppermute | solution.py:388
  60.7 10.1 %collective-permute-start.20 = (bf16[160,512]{1,0:T(8,128)(2,1)S(1)}, bf16[160,512]{1,0:T(8,128)(2,1)S(1)}, u32[]{:S(2)}, u32[]{:S(2)}) collective-permute-start(bf16[160,512]{1,0:T(8,128)(2,1)S(1)} %get-tuple-element.27), channel_id=1, source_target_pairs={{0,1},{1,2},{2,3},{3,0},{4,5},{5,6},{6,7},{7,4},{8,9},{9,10},{10,1... | collective-permute-start | bytes 491528 | tf_op jit(solution)/shard_map/ppermute | solution.py:388

commit v13 on v12

--- a/solution.py
+++ b/solution.py
@@ -65,10 +65,14 @@
     return (dz >= 1) & (dz <= 4)
 
 
-def pack_kernel(where_ref, lists_ref, nodes_ref, out_ref):
-    rows, latent = nodes_ref.shape
+def pack_kernel(where_ref, lists_hbm, nodes_hbm, out_ref, lists_ref, sems):
+    rows, latent = nodes_hbm.shape
     cap, peers = lists_ref.shape
-    out_ref[:rows] = nodes_ref[...]
+    body = pltpu.make_async_copy(nodes_hbm, out_ref.at[pl.ds(0, rows)], sems.at[0])
+    body.start()
+    load = pltpu.make_async_copy(lists_hbm, lists_ref, sems.at[1])
+    load.start()
+    load.wait()
     me = where_ref[0]
     x, z, c = me // (Z * C), me // C % Z, me % C
     lane = lax.broadcasted_iota(i32, (cap, latent), 1)
@@ -85,33 +89,29 @@
     peer = lax.broadcasted_iota(i32, (TAIL, peers), 1)
     pick = as_bf16(row == ((peer // C % Z - z) & (Z - 1)))
     out_ref[rows:] = (dot(pick, listed) - 1.0).astype(bf16)
+    body.wait()
 
 
 def pack(me, lists, nodes):
     return pl.pallas_call(
         pack_kernel,
-        in_specs=[SMEM, VMEM, VMEM],
+        in_specs=[SMEM, HBM, HBM],
+        out_specs=VMEM,
         out_shape=jax.ShapeDtypeStruct((nodes.shape[0] + TAIL, nodes.shape[1]), bf16),
+        scratch_shapes=[pltpu.VMEM(lists.shape, i32), pltpu.SemaphoreType.DMA((2,))],
+        compiler_params=pltpu.CompilerParams(vmem_limit_bytes=4 << 20),
         name="pack",
-    )(me, lists, nodes)
+    )(me, in_hbm(lists), in_hbm(nodes))
 
 
 def select_kernel(pairs, cap, extra, *refs):
     count = 2 * len(pairs)
     blocks, outs = list(refs[:count]), refs[count + extra : count + extra + X]
-    own = pairs[0][0] == 0
-    if own:
-        held, sem = refs[count + extra + X :]
-        fetch = pltpu.make_async_copy(blocks[0], held, sem)
-        fetch.start()
-        blocks[0] = held
     rows = blocks[0].shape[0] - TAIL
     lanes = X * C * 2 * cap
-    for at in reversed(range(len(pairs))):
+    for at in range(len(pairs)):
         total = None
-        for side, dz in reversed(list(enumerate(pairs[at]))):
-            if dz == 0:
-                fetch.wait()
+        for side, dz in enumerate(pairs[at]):
             block = blocks[2 * at + side]
             wanted = block[rows:].astype(f32)[dz : dz + 1, :lanes].astype(i32)
             part = dot_first(hot_columns(wanted, rows), block[:rows])
@@ -128,15 +128,10 @@
 def select(pairs, cap, blocks, *earlier):
     latent = blocks[0].shape[1]
     shape = jax.ShapeDtypeStruct((C * len(pairs) * 2 * cap, latent), bf16)
-    own = pairs[0][0] == 0
-    blocks = list(blocks)
-    if own:
-        blocks[0] = in_hbm(blocks[0])
     return pl.pallas_call(
         lambda *refs: select_kernel(pairs, cap, len(earlier), *refs),
-        in_specs=[HBM if own else VMEM] + [VMEM] * (len(blocks) - 1) + [ANY] * len(earlier),
+        in_specs=[VMEM] * len(blocks) + [ANY] * len(earlier),
         out_shape=[shape] * X,
-        scratch_shapes=[pltpu.VMEM(blocks[0].shape, bf16), pltpu.SemaphoreType.DMA] if own else [],
         compiler_params=pltpu.CompilerParams(vmem_limit_bytes=LIMIT),
         cost_estimate=pl.CostEstimate(flops=COST, bytes_accessed=0, transcendentals=0),
         name="select",

time: 72.4 us -> 71.5 us (0.988)
  Pallas kernels: 18.6 us -> 17 us
    pallas_call x1, Pallas kernels: 1.96 us -> 1.16 us  [pack(): pl.pallas_call(pack_kernel, in_specs=[SMEM, HBM, HBM], out_specs=VMEM, ou...]
    pallas_call x2, Pallas kernels: 1.94 us -> 1.21 us  [select(): pl.pallas_call(lambda *refs: select_kernel(pairs, cap, len(earlier), *ref...]
  transfers between devices with their start and end apart: 21 -> 21, of which waited for: 9 -> 9; matrix products, arithmetic and copies ran while one was open for 0% -> 0% of each run, Pallas kernels for 12% -> 11%
where the time goes in v13:
time: 71.5 us; the launch traced here: 71.3 us
  starting transfers between devices  36 us (50%)
  Pallas kernels  17 us (24%)
  waiting for transfers between devices  16.4 us (23%)
  between operations  1.5 us (2%)
    ppermute x15, starting transfers between devices, moved(): return lax.ppermute(value, 'patch', pairs_of(move))  26.8 us
    ppermute x6, waiting for transfers between devices, around(): lax.ppermute(value, 'feat', [(i, (i + k) % feat) for i in range(feat)])  11.1 us
    ppermute x6, starting transfers between devices, around(): lax.ppermute(value, 'feat', [(i, (i + k) % feat) for i in range(feat)])  9.18 us
    pallas_call x1, Pallas kernels, edge_before(): pl.pallas_call(lambda *refs: before_kernel(len(earlier), *refs), in_specs...  6.68 us
    pallas_call x1, Pallas kernels, edge_after(): pl.pallas_call(lambda *refs: after_kernel(first_row, *refs), in_specs=[SM...  6.46 us
    ppermute x15, waiting for transfers between devices, moved(): return lax.ppermute(value, 'patch', pairs_of(move))  5.37 us
    pallas_call x1, Pallas kernels, node_update(): pl.pallas_call(node_kernel, in_specs=[VMEM] * 9, out_shape=jax.ShapeDtype...  1.47 us
  transfers between devices with their start and end apart: 21, of which 9 were waited for; matrix products, arithmetic and copies ran while one was open for 0% of the time, Pallas kernels for 11%

profile of v13, /device:TPU:1, one launch (start us, length us, event | category | flops | bytes accessed | tf_op | source)
XLA Modules:
  0.0 71.3 jit_solution(10646432903451944994)
XLA Ops:
  0.6 0.0 copy-start.7
  0.6 0.0 copy-start.8
  0.7 0.0 copy-start
  0.7 0.0 copy-start.3
  0.7 1.2 %pack.1.refs_0_ = bf16[176,512]{1,0:T(8,128)(2,1)S(1)} custom-call(s32[1]{0:T(128)} %bitcast.1.where_ref, s32[24,64]{1,0:T(8,128)} %bitcast.12, bf16[160,512]{1,0:T(8,128)(2,1)} %nodes_ref.1), custom_call_target="tpu_custom_call" | custom-call | tf_op jit(solution)/shard_map/pack/pallas_call | solution.py:96
  1.8 2.5 %collective-permute-start = (bf16[176,512]{1,0:T(8,128)(2,1)S(1)}, bf16[176,512]{1,0:T(8,128)(2,1)S(1)}, u32[]{:S(2)}, u32[]{:S(2)}) collective-permute-start(bf16[176,512]{1,0:T(8,128)(2,1)S(1)} %pack.1.refs_0_), channel_id=1, source_target_pairs={{0,8},{4,12},{8,16},{12,20},{16,24},{20,28},{24,32},{28,36},{32,40... | collective-permute-start | bytes 540680 | tf_op jit(solution)/shard_map/ppermute | solution.py:355
  4.4 1.3 %collective-permute-start.1 = (bf16[160,512]{1,0:T(8,128)(2,1)}, bf16[160,512]{1,0:T(8,128)(2,1)S(1)}, u32[]{:S(2)}, u32[]{:S(2)}) collective-permute-start(bf16[160,512]{1,0:T(8,128)(2,1)} %nodes_ref.1), channel_id=1, source_target_pairs={{0,1},{1,2},{2,3},{3,0},{4,5},{5,6},{6,7},{7,4},{8,9},{9,10},{10,1... | collective-permute-start | bytes 491528 | tf_op jit(solution)/shard_map/ppermute | solution.py:383
  5.7 4.0 %collective-permute-start.2 = (bf16[176,512]{1,0:T(8,128)(2,1)S(1)}, bf16[176,512]{1,0:T(8,128)(2,1)S(1)}, u32[]{:S(2)}, u32[]{:S(2)}) collective-permute-start(bf16[176,512]{1,0:T(8,128)(2,1)S(1)} %pack.1.refs_0_), channel_id=1, source_target_pairs={{0,56},{4,60},{8,0},{12,4},{16,8},{20,12},{24,16},{28,20},{32,24},... | collective-permute-start | bytes 540680 | tf_op jit(solution)/shard_map/ppermute | solution.py:355
  9.7 1.0 %collective-permute-done.1.refs_1_.refs_4_ = bf16[160,512]{1,0:T(8,128)(2,1)S(1)} collective-permute-done((bf16[160,512]{1,0:T(8,128)(2,1)}, bf16[160,512]{1,0:T(8,128)(2,1)S(1)}, u32[]{:S(2)}, u32[]{:S(2)}) %collective-permute-start.1) | collective-permute-done | bytes 163872 | tf_op jit(solution)/shard_map/ppermute | solution.py:383
  10.7 1.9 %collective-permute-done.refs_0_ = bf16[176,512]{1,0:T(8,128)(2,1)S(1)} collective-permute-done((bf16[176,512]{1,0:T(8,128)(2,1)S(1)}, bf16[176,512]{1,0:T(8,128)(2,1)S(1)}, u32[]{:S(2)}, u32[]{:S(2)}) %collective-permute-start) | collective-permute-done | bytes 180256 | tf_op jit(solution)/shard_map/ppermute | solution.py:355
  12.6 0.0 collective-permute-start.3
  12.6 2.7 %collective-permute-start.4 = (bf16[160,512]{1,0:T(8,128)(2,1)}, bf16[160,512]{1,0:T(8,128)(2,1)S(1)}, u32[]{:S(2)}, u32[]{:S(2)}) collective-permute-start(bf16[160,512]{1,0:T(8,128)(2,1)} %nodes_ref.1), channel_id=1, source_target_pairs={{0,3},{1,0},{2,1},{3,2},{4,7},{5,4},{6,5},{7,6},{8,11},{9,8},{10,9... | collective-permute-start | bytes 491528 | tf_op jit(solution)/shard_map/ppermute | solution.py:383
  15.3 0.0 collective-permute-done.2.refs_2_
  15.3 2.7 %collective-permute-start.9 = (bf16[176,512]{1,0:T(8,128)(2,1)S(1)}, bf16[176,512]{1,0:T(8,128)(2,1)S(1)}, u32[]{:S(2)}, u32[]{:S(2)}) collective-permute-start(bf16[176,512]{1,0:T(8,128)(2,1)S(1)} %collective-permute-done.2.refs_2_), channel_id=1, source_target_pairs={{0,56},{4,60},{8,0},{12,4},{16,8},{20,12},{24,16},{28,20},{32,24},... | collective-permute-start | bytes 540680 | tf_op jit(solution)/shard_map/ppermute | solution.py:355
  18.0 0.0 collective-permute-done.4.refs_1_.refs_6_
  18.0 0.6 collective-permute-done.3.refs_0_
  18.6 0.0 collective-permute-start.10
  18.6 1.3 %collective-permute-start.8 = (bf16[160,512]{1,0:T(8,128)(2,1)S(1)}, bf16[160,512]{1,0:T(8,128)(2,1)S(1)}, u32[]{:S(2)}, u32[]{:S(2)}) collective-permute-start(bf16[160,512]{1,0:T(8,128)(2,1)S(1)} %collective-permute-done.1.refs_1_.refs_4_), channel_id=1, source_target_pairs={{0,1},{1,2},{2,3},{3,0},{4,5},{5,6},{6,7},{7,4},{8,9},{9,10},{10,1... | collective-permute-start | bytes 491528 | tf_op jit(solution)/shard_map/ppermute | solution.py:383
  19.9 0.6 select.24
  20.5 1.3 %collective-permute-start.5 = (bf16[192,512]{1,0:T(8,128)(2,1)S(1)}, bf16[192,512]{1,0:T(8,128)(2,1)S(1)}, u32[]{:S(2)}, u32[]{:S(2)}) collective-permute-start(bf16[192,512]{1,0:T(8,128)(2,1)S(1)} %get-tuple-element.16), channel_id=1, source_target_pairs={{0,64},{4,68},{8,72},{12,76},{16,80},{20,84},{24,88},{28,92},{32,9... | collective-permute-start | bytes 589832 | tf_op jit(solution)/shard_map/ppermute | solution.py:355
  21.8 0.0 collective-permute-done.9.refs_0_
  21.8 2.7 %collective-permute-start.11 = (bf16[176,512]{1,0:T(8,128)(2,1)S(1)}, bf16[176,512]{1,0:T(8,128)(2,1)S(1)}, u32[]{:S(2)}, u32[]{:S(2)}) collective-permute-start(bf16[176,512]{1,0:T(8,128)(2,1)S(1)} %collective-permute-done.9.refs_0_), channel_id=1, source_target_pairs={{0,56},{4,60},{8,0},{12,4},{16,8},{20,12},{24,16},{28,20},{32,24},... | collective-permute-start | bytes 540680 | tf_op jit(solution)/shard_map/ppermute | solution.py:355
  24.5 0.0 collective-permute-done.10.refs_1_
  24.5 0.0 collective-permute-start.12
  24.5 0.0 copy-done.7
  24.5 0.1 fusion.4
  24.6 2.5 %collective-permute-start.6 = (bf16[192,512]{1,0:T(8,128)(2,1)S(1)}, bf16[192,512]{1,0:T(8,128)(2,1)S(1)}, u32[]{:S(2)}, u32[]{:S(2)}) collective-permute-start(bf16[192,512]{1,0:T(8,128)(2,1)S(1)} %get-tuple-element.17), channel_id=1, source_target_pairs={{0,128},{4,132},{8,136},{12,140},{16,144},{20,148},{24,152},{28,15... | collective-permute-start | bytes 589832 | tf_op jit(solution)/shard_map/ppermute | solution.py:355
  27.1 0.0 collective-permute-done.8.refs_4_.refs_5_
  27.1 1.2 %collective-permute-start.7 = (bf16[192,512]{1,0:T(8,128)(2,1)S(1)}, bf16[192,512]{1,0:T(8,128)(2,1)S(1)}, u32[]{:S(2)}, u32[]{:S(2)}) collective-permute-start(bf16[192,512]{1,0:T(8,128)(2,1)S(1)} %get-tuple-element.18), channel_id=1, source_target_pairs={{0,192},{4,196},{8,200},{12,204},{16,208},{20,212},{24,216},{28,22... | collective-permute-start | bytes 589832 | tf_op jit(solution)/shard_map/ppermute | solution.py:355
  28.3 0.0 collective-permute-done.11.refs_2_
  28.3 2.0 %collective-permute-done.12.refs_3_ = bf16[176,512]{1,0:T(8,128)(2,1)S(1)} collective-permute-done((bf16[176,512]{1,0:T(8,128)(2,1)S(1)}, bf16[176,512]{1,0:T(8,128)(2,1)S(1)}, u32[]{:S(2)}, u32[]{:S(2)}) %collective-permute-start.12) | collective-permute-done | bytes 180256 | tf_op jit(solution)/shard_map/ppermute | solution.py:355
  30.3 0.6 select.25
  30.9 1.1 %collective-permute-start.14 = (bf16[192,512]{1,0:T(8,128)(2,1)S(1)}, bf16[192,512]{1,0:T(8,128)(2,1)S(1)}, u32[]{:S(2)}, u32[]{:S(2)}) collective-permute-start(bf16[192,512]{1,0:T(8,128)(2,1)S(1)} %get-tuple-element.20), channel_id=1, source_target_pairs={{0,64},{4,68},{8,72},{12,76},{16,80},{20,84},{24,88},{28,92},{32,9... | collective-permute-start | bytes 589832 | tf_op jit(solution)/shard_map/ppermute | solution.py:355
  32.0 2.1 %collective-permute-start.15 = (bf16[192,512]{1,0:T(8,128)(2,1)S(1)}, bf16[192,512]{1,0:T(8,128)(2,1)S(1)}, u32[]{:S(2)}, u32[]{:S(2)}) collective-permute-start(bf16[192,512]{1,0:T(8,128)(2,1)S(1)} %get-tuple-element.21), channel_id=1, source_target_pairs={{0,128},{4,132},{8,136},{12,140},{16,144},{20,148},{24,152},{28,15... | collective-permute-start | bytes 589832 | tf_op jit(solution)/shard_map/ppermute | solution.py:355
  34.1 0.0 collective-permute-done.5.refs_1_.refs_5_
  34.1 1.2 %collective-permute-start.16 = (bf16[192,512]{1,0:T(8,128)(2,1)S(1)}, bf16[192,512]{1,0:T(8,128)(2,1)S(1)}, u32[]{:S(2)}, u32[]{:S(2)}) collective-permute-start(bf16[192,512]{1,0:T(8,128)(2,1)S(1)} %get-tuple-element.22), channel_id=1, source_target_pairs={{0,192},{4,196},{8,200},{12,204},{16,208},{20,212},{24,216},{28,22... | collective-permute-start | bytes 589832 | tf_op jit(solution)/shard_map/ppermute | solution.py:355
  35.3 0.0 copy-done.8
  35.3 0.0 copy-done
  35.3 0.0 copy-done.3
  35.3 6.7 %edge_before.1.refs_4_.refs_14_ = f32[1280,512]{1,0:T(8,128)} custom-call(s32[1,1280]{1,0:T(1,128)S(1)} %reshape.29.refs_0_.refs_2_, s32[1,1280]{1,0:T(1,128)S(1)} %reshape.32.refs_1_, f32[1,512]{1,0:T(1,128)S(1)} %bitcast.8, bf16[160,512]{1,0:T(8,128)(2,1)S(1)} %copy-done, bf16[160,512]{1,0:T(8,128)(2,1)S(1)} %collective-permute-done.1.refs_1_.refs_4_, ...), custom_call_target="tpu_custom_call" | custom-call | flops 1048576 | tf_op jit(solution)/shard_map/edge_before/pallas_call | solution.py:230
  42.0 0.0 collective-permute-done.6.refs_2_.refs_6_
  42.0 0.0 collective-permute-done.7.refs_3_.refs_7_
  42.1 0.0 copy-start.4
  42.1 5.3 %collective-permute-start.13 = (bf16[384,512]{1,0:T(8,128)(2,1)S(1)}, bf16[384,512]{1,0:T(8,128)(2,1)S(1)}, u32[]{:S(2)}, u32[]{:S(2)}) collective-permute-start(bf16[384,512]{1,0:T(8,128)(2,1)S(1)} %crossing.2), channel_id=1, source_target_pairs={{0,4},{4,0},{8,12},{12,8},{16,20},{20,16},{24,28},{28,24},{32,36},... | collective-permute-start | bytes 1179656 | tf_op jit(solution)/shard_map/ppermute | solution.py:355
  47.4 0.0 collective-permute-done.14.refs_1_.refs_10_
  47.5 0.0 collective-permute-done.15.refs_2_.refs_11_
  47.5 0.0 collective-permute-done.16.refs_3_.refs_12_
  47.5 0.1 collective-permute-start.17
  47.6 0.2 reshape.36.refs_1_
  48.5 0.3 collective-permute-done.13.refs_8_
  48.8 0.6 collective-permute-done.17.refs_13_
  49.4 0.0 copy-done.4
  49.4 0.0 copy-start.6
  49.4 6.5 %edge_after.1 = (bf16[1280,512]{1,0:T(8,128)(2,1)}, f32[160,512]{1,0:T(8,128)S(1)}, bf16[160,512]{1,0:T(8,128)(2,1)S(1)}, bf16[160,512]{1,0:T(8,128)(2,1)S(1)}, bf16[160,512]{1,0:T(8,128)(2,1)S(1)}) custom-call(s32[1]{0:T(128)S(6)} %copy.21.refs_0_, s32[1280,1]{1,0:T(8,128)S(1)} %reshape.36.refs_1_, s32[1,1280]{1,0:T(1,128)S(1)} %reshape.29.refs_0_.refs_2_, ...), custom_call_target="tpu_custom_call" | custom-call | tf_op jit(solution)/shard_map/edge_after/pallas_call | solution.py:301
  55.9 2.8 %collective-permute-start.18 = (bf16[160,512]{1,0:T(8,128)(2,1)S(1)}, bf16[160,512]{1,0:T(8,128)(2,1)S(1)}, u32[]{:S(2)}, u32[]{:S(2)}) collective-permute-start(bf16[160,512]{1,0:T(8,128)(2,1)S(1)} %get-tuple-element.25), channel_id=1, source_target_pairs={{0,3},{1,0},{2,1},{3,2},{4,7},{5,4},{6,5},{7,6},{8,11},{9,8},{10,9... | collective-permute-start | bytes 491528 | tf_op jit(solution)/shard_map/ppermute | solution.py:383
  58.7 0.4 collective-permute-start.19
  59.0 0.7 collective-permute-start.20
  59.7 5.5 %collective-permute-done.18.p1_ref = bf16[160,512]{1,0:T(8,128)(2,1)S(1)} collective-permute-done((bf16[160,512]{1,0:T(8,128)(2,1)S(1)}, bf16[160,512]{1,0:T(8,128)(2,1)S(1)}, u32[]{:S(2)}, u32[]{:S(2)}) %collective-permute-start.18) | collective-permute-done | bytes 163872 | tf_op jit(solution)/shard_map/ppermute | solution.py:383
  65.3 0.1 collective-permute-done.19.p2_ref
  65.3 4.5 %collective-permute-done.20.p3_ref = bf16[160,512]{1,0:T(8,128)(2,1)S(1)} collective-permute-done((bf16[160,512]{1,0:T(8,128)(2,1)S(1)}, bf16[160,512]{1,0:T(8,128)(2,1)S(1)}, u32[]{:S(2)}, u32[]{:S(2)}) %collective-permute-start.20) | collective-permute-done | bytes 163872 | tf_op jit(solution)/shard_map/ppermute | solution.py:383
  69.8 0.0 copy-done.1
  69.8 0.0 copy-done.2
  69.8 0.0 copy-done.6
  69.8 1.5 %node_update.1 = bf16[160,512]{1,0:T(8,128)(2,1)} custom-call(bf16[160,512]{1,0:T(8,128)(2,1)S(1)} %copy-done, f32[160,512]{1,0:T(8,128)S(1)} %get-tuple-element.24.p0_ref, bf16[160,512]{1,0:T(8,128)(2,1)S(1)} %collective-permute-done.18.p1_ref, bf16[160,512]{1,0:T(8,128)(2,1)S(1)} %collective-permute-done.19.p2_ref, ...), custom_call_target="tpu_custom_call" | custom-call | tf_op jit(solution)/shard_map/node_update/pallas_call | solution.py:335
  (11 shorter events, 0.1 us)
Async XLA Ops:
  0.6 23.9 %copy-start.7 = (s32[1280]{0:T(1024)S(1)}, s32[1280]{0:T(1024)}, u32[]{:S(2)}) copy-start(s32[1280]{0:T(1024)} %param.17) | copy-start | bytes 15364
  0.6 34.6 %copy-start.8 = (s32[1280]{0:T(1024)S(1)}, s32[1280]{0:T(1024)}, u32[]{:S(2)}) copy-start(s32[1280]{0:T(1024)} %param.16) | copy-start | bytes 15364
  0.7 34.7 %copy-start = (bf16[160,512]{1,0:T(8,128)(2,1)S(1)}, bf16[160,512]{1,0:T(8,128)(2,1)}, u32[]{:S(2)}) copy-start(bf16[160,512]{1,0:T(8,128)(2,1)} %nodes_ref.1) | copy-start | bytes 491524
  0.7 34.7 %copy-start.3 = (f32[512]{0:T(512)S(1)}, f32[512]{0:T(512)}, u32[]{:S(2)}) copy-start(f32[512]{0:T(512)} %param.21) | copy-start | bytes 6148
  1.8 10.8 %collective-permute-start = (bf16[176,512]{1,0:T(8,128)(2,1)S(1)}, bf16[176,512]{1,0:T(8,128)(2,1)S(1)}, u32[]{:S(2)}, u32[]{:S(2)}) collective-permute-start(bf16[176,512]{1,0:T(8,128)(2,1)S(1)} %pack.1.refs_0_), channel_id=1, source_target_pairs={{0,8},{4,12},{8,16},{12,20},{16,24},{20,28},{24,32},{28,36},{32,40... | collective-permute-start | bytes 540680 | tf_op jit(solution)/shard_map/ppermute | solution.py:355
  4.4 6.3 %collective-permute-start.1 = (bf16[160,512]{1,0:T(8,128)(2,1)}, bf16[160,512]{1,0:T(8,128)(2,1)S(1)}, u32[]{:S(2)}, u32[]{:S(2)}) collective-permute-start(bf16[160,512]{1,0:T(8,128)(2,1)} %nodes_ref.1), channel_id=1, source_target_pairs={{0,1},{1,2},{2,3},{3,0},{4,5},{5,6},{6,7},{7,4},{8,9},{9,10},{10,1... | collective-permute-start | bytes 491528 | tf_op jit(solution)/shard_map/ppermute | solution.py:383
  5.7 9.7 %collective-permute-start.2 = (bf16[176,512]{1,0:T(8,128)(2,1)S(1)}, bf16[176,512]{1,0:T(8,128)(2,1)S(1)}, u32[]{:S(2)}, u32[]{:S(2)}) collective-permute-start(bf16[176,512]{1,0:T(8,128)(2,1)S(1)} %pack.1.refs_0_), channel_id=1, source_target_pairs={{0,56},{4,60},{8,0},{12,4},{16,8},{20,12},{24,16},{28,20},{32,24},... | collective-permute-start | bytes 540680 | tf_op jit(solution)/shard_map/ppermute | solution.py:355
  12.6 6.0 %collective-permute-start.3 = (bf16[176,512]{1,0:T(8,128)(2,1)S(1)}, bf16[176,512]{1,0:T(8,128)(2,1)S(1)}, u32[]{:S(2)}, u32[]{:S(2)}) collective-permute-start(bf16[176,512]{1,0:T(8,128)(2,1)S(1)} %gate.2.refs_1_), channel_id=1, source_target_pairs={{0,8},{4,12},{8,16},{12,20},{16,24},{20,28},{24,32},{28,36},{32,40... | collective-permute-start | bytes 540680 | tf_op jit(solution)/shard_map/ppermute | solution.py:355
  12.6 5.4 %collective-permute-start.4 = (bf16[160,512]{1,0:T(8,128)(2,1)}, bf16[160,512]{1,0:T(8,128)(2,1)S(1)}, u32[]{:S(2)}, u32[]{:S(2)}) collective-permute-start(bf16[160,512]{1,0:T(8,128)(2,1)} %nodes_ref.1), channel_id=1, source_target_pairs={{0,3},{1,0},{2,1},{3,2},{4,7},{5,4},{6,5},{7,6},{8,11},{9,8},{10,9... | collective-permute-start | bytes 491528 | tf_op jit(solution)/shard_map/ppermute | solution.py:383
  15.3 6.5 %collective-permute-start.9 = (bf16[176,512]{1,0:T(8,128)(2,1)S(1)}, bf16[176,512]{1,0:T(8,128)(2,1)S(1)}, u32[]{:S(2)}, u32[]{:S(2)}) collective-permute-start(bf16[176,512]{1,0:T(8,128)(2,1)S(1)} %collective-permute-done.2.refs_2_), channel_id=1, source_target_pairs={{0,56},{4,60},{8,0},{12,4},{16,8},{20,12},{24,16},{28,20},{32,24},... | collective-permute-start | bytes 540680 | tf_op jit(solution)/shard_map/ppermute | solution.py:355
  18.6 5.9 %collective-permute-start.10 = (bf16[176,512]{1,0:T(8,128)(2,1)S(1)}, bf16[176,512]{1,0:T(8,128)(2,1)S(1)}, u32[]{:S(2)}, u32[]{:S(2)}) collective-permute-start(bf16[176,512]{1,0:T(8,128)(2,1)S(1)} %gate.3.refs_3_), channel_id=1, source_target_pairs={{0,8},{4,12},{8,16},{12,20},{16,24},{20,28},{24,32},{28,36},{32,40... | collective-permute-start | bytes 540680 | tf_op jit(solution)/shard_map/ppermute | solution.py:355
  18.6 8.5 %collective-permute-start.8 = (bf16[160,512]{1,0:T(8,128)(2,1)S(1)}, bf16[160,512]{1,0:T(8,128)(2,1)S(1)}, u32[]{:S(2)}, u32[]{:S(2)}) collective-permute-start(bf16[160,512]{1,0:T(8,128)(2,1)S(1)} %collective-permute-done.1.refs_1_.refs_4_), channel_id=1, source_target_pairs={{0,1},{1,2},{2,3},{3,0},{4,5},{5,6},{6,7},{7,4},{8,9},{9,10},{10,1... | collective-permute-start | bytes 491528 | tf_op jit(solution)/shard_map/ppermute | solution.py:383
  20.5 13.6 %collective-permute-start.5 = (bf16[192,512]{1,0:T(8,128)(2,1)S(1)}, bf16[192,512]{1,0:T(8,128)(2,1)S(1)}, u32[]{:S(2)}, u32[]{:S(2)}) collective-permute-start(bf16[192,512]{1,0:T(8,128)(2,1)S(1)} %get-tuple-element.16), channel_id=1, source_target_pairs={{0,64},{4,68},{8,72},{12,76},{16,80},{20,84},{24,88},{28,92},{32,9... | collective-permute-start | bytes 589832 | tf_op jit(solution)/shard_map/ppermute | solution.py:355
  21.8 6.5 %collective-permute-start.11 = (bf16[176,512]{1,0:T(8,128)(2,1)S(1)}, bf16[176,512]{1,0:T(8,128)(2,1)S(1)}, u32[]{:S(2)}, u32[]{:S(2)}) collective-permute-start(bf16[176,512]{1,0:T(8,128)(2,1)S(1)} %collective-permute-done.9.refs_0_), channel_id=1, source_target_pairs={{0,56},{4,60},{8,0},{12,4},{16,8},{20,12},{24,16},{28,20},{32,24},... | collective-permute-start | bytes 540680 | tf_op jit(solution)/shard_map/ppermute | solution.py:355
  24.5 5.7 %collective-permute-start.12 = (bf16[176,512]{1,0:T(8,128)(2,1)S(1)}, bf16[176,512]{1,0:T(8,128)(2,1)S(1)}, u32[]{:S(2)}, u32[]{:S(2)}) collective-permute-start(bf16[176,512]{1,0:T(8,128)(2,1)S(1)} %collective-permute-done.10.refs_1_), channel_id=1, source_target_pairs={{0,8},{4,12},{8,16},{12,20},{16,24},{20,28},{24,32},{28,36},{32,40... | collective-permute-start | bytes 540680 | tf_op jit(solution)/shard_map/ppermute | solution.py:355
  24.6 17.4 %collective-permute-start.6 = (bf16[192,512]{1,0:T(8,128)(2,1)S(1)}, bf16[192,512]{1,0:T(8,128)(2,1)S(1)}, u32[]{:S(2)}, u32[]{:S(2)}) collective-permute-start(bf16[192,512]{1,0:T(8,128)(2,1)S(1)} %get-tuple-element.17), channel_id=1, source_target_pairs={{0,128},{4,132},{8,136},{12,140},{16,144},{20,148},{24,152},{28,15... | collective-permute-start | bytes 589832 | tf_op jit(solution)/shard_map/ppermute | solution.py:355
  27.1 14.9 %collective-permute-start.7 = (bf16[192,512]{1,0:T(8,128)(2,1)S(1)}, bf16[192,512]{1,0:T(8,128)(2,1)S(1)}, u32[]{:S(2)}, u32[]{:S(2)}) collective-permute-start(bf16[192,512]{1,0:T(8,128)(2,1)S(1)} %get-tuple-element.18), channel_id=1, source_target_pairs={{0,192},{4,196},{8,200},{12,204},{16,208},{20,212},{24,216},{28,22... | collective-permute-start | bytes 589832 | tf_op jit(solution)/shard_map/ppermute | solution.py:355
  30.9 16.6 %collective-permute-start.14 = (bf16[192,512]{1,0:T(8,128)(2,1)S(1)}, bf16[192,512]{1,0:T(8,128)(2,1)S(1)}, u32[]{:S(2)}, u32[]{:S(2)}) collective-permute-start(bf16[192,512]{1,0:T(8,128)(2,1)S(1)} %get-tuple-element.20), channel_id=1, source_target_pairs={{0,64},{4,68},{8,72},{12,76},{16,80},{20,84},{24,88},{28,92},{32,9... | collective-permute-start | bytes 589832 | tf_op jit(solution)/shard_map/ppermute | solution.py:355
  32.0 15.5 %collective-permute-start.15 = (bf16[192,512]{1,0:T(8,128)(2,1)S(1)}, bf16[192,512]{1,0:T(8,128)(2,1)S(1)}, u32[]{:S(2)}, u32[]{:S(2)}) collective-permute-start(bf16[192,512]{1,0:T(8,128)(2,1)S(1)} %get-tuple-element.21), channel_id=1, source_target_pairs={{0,128},{4,132},{8,136},{12,140},{16,144},{20,148},{24,152},{28,15... | collective-permute-start | bytes 589832 | tf_op jit(solution)/shard_map/ppermute | solution.py:355
  34.1 13.4 %collective-permute-start.16 = (bf16[192,512]{1,0:T(8,128)(2,1)S(1)}, bf16[192,512]{1,0:T(8,128)(2,1)S(1)}, u32[]{:S(2)}, u32[]{:S(2)}) collective-permute-start(bf16[192,512]{1,0:T(8,128)(2,1)S(1)} %get-tuple-element.22), channel_id=1, source_target_pairs={{0,192},{4,196},{8,200},{12,204},{16,208},{20,212},{24,216},{28,22... | collective-permute-start | bytes 589832 | tf_op jit(solution)/shard_map/ppermute | solution.py:355
  42.1 7.3 %copy-start.4 = (f32[512]{0:T(512)S(1)}, f32[512]{0:T(512)}, u32[]{:S(2)}) copy-start(f32[512]{0:T(512)} %param.23) | copy-start | bytes 6148
  42.1 6.7 %collective-permute-start.13 = (bf16[384,512]{1,0:T(8,128)(2,1)S(1)}, bf16[384,512]{1,0:T(8,128)(2,1)S(1)}, u32[]{:S(2)}, u32[]{:S(2)}) collective-permute-start(bf16[384,512]{1,0:T(8,128)(2,1)S(1)} %crossing.2), channel_id=1, source_target_pairs={{0,4},{4,0},{8,12},{12,8},{16,20},{20,16},{24,28},{28,24},{32,36},... | collective-permute-start | bytes 1179656 | tf_op jit(solution)/shard_map/ppermute | solution.py:355
  47.5 1.9 %collective-permute-start.17 = (bf16[384,512]{1,0:T(8,128)(2,1)S(1)}, bf16[384,512]{1,0:T(8,128)(2,1)S(1)}, u32[]{:S(2)}, u32[]{:S(2)}) collective-permute-start(bf16[384,512]{1,0:T(8,128)(2,1)S(1)} %crossing.3), channel_id=1, source_target_pairs={{0,4},{4,0},{8,12},{12,8},{16,20},{20,16},{24,28},{28,24},{32,36},... | collective-permute-start | bytes 1179656 | tf_op jit(solution)/shard_map/ppermute | solution.py:355
  49.4 20.4 %copy-start.1 = (bf16[1024,512]{1,0:T(8,128)(2,1)S(1)}, bf16[1024,512]{1,0:T(8,128)(2,1)}, u32[]{:S(2)}) copy-start(bf16[1024,512]{1,0:T(8,128)(2,1)} %w1_ref.1) | copy-start | bytes 3145732
  49.4 20.4 %copy-start.2 = (bf16[512,512]{1,0:T(8,128)(2,1)S(1)}, bf16[512,512]{1,0:T(8,128)(2,1)}, u32[]{:S(2)}) copy-start(bf16[512,512]{1,0:T(8,128)(2,1)} %w2_ref.1) | copy-start | bytes 1572868
  49.4 20.4 %copy-start.5 = (f32[512]{0:T(512)S(1)}, f32[512]{0:T(512)}, u32[]{:S(2)}) copy-start(f32[512]{0:T(512)} %param.25) | copy-start | bytes 6148
  49.4 20.4 %copy-start.6 = (f32[512]{0:T(512)S(1)}, f32[512]{0:T(512)}, u32[]{:S(2)}) copy-start(f32[512]{0:T(512)} %param.27) | copy-start | bytes 6148
  55.9 9.4 %collective-permute-start.18 = (bf16[160,512]{1,0:T(8,128)(2,1)S(1)}, bf16[160,512]{1,0:T(8,128)(2,1)S(1)}, u32[]{:S(2)}, u32[]{:S(2)}) collective-permute-start(bf16[160,512]{1,0:T(8,128)(2,1)S(1)} %get-tuple-element.25), channel_id=1, source_target_pairs={{0,3},{1,0},{2,1},{3,2},{4,7},{5,4},{6,5},{7,6},{8,11},{9,8},{10,9... | collective-permute-start | bytes 491528 | tf_op jit(solution)/shard_map/ppermute | solution.py:383
  58.7 6.6 %collective-permute-start.19 = (bf16[160,512]{1,0:T(8,128)(2,1)S(1)}, bf16[160,512]{1,0:T(8,128)(2,1)S(1)}, u32[]{:S(2)}, u32[]{:S(2)}) collective-permute-start(bf16[160,512]{1,0:T(8,128)(2,1)S(1)} %get-tuple-element.26), channel_id=1, source_target_pairs={{0,2},{1,3},{2,0},{3,1},{4,6},{5,7},{6,4},{7,5},{8,10},{9,11},{10,... | collective-permute-start | bytes 491528 | tf_op jit(solution)/shard_map/ppermute | solution.py:383
  59.0 10.8 %collective-permute-start.20 = (bf16[160,512]{1,0:T(8,128)(2,1)S(1)}, bf16[160,512]{1,0:T(8,128)(2,1)S(1)}, u32[]{:S(2)}, u32[]{:S(2)}) collective-permute-start(bf16[160,512]{1,0:T(8,128)(2,1)S(1)} %get-tuple-element.27), channel_id=1, source_target_pairs={{0,1},{1,2},{2,3},{3,0},{4,5},{5,6},{6,7},{7,4},{8,9},{9,10},{10,1... | collective-permute-start | bytes 491528 | tf_op jit(solution)/shard_map/ppermute | solution.py:383

commit v14 on v13

--- a/solution.py
+++ b/solution.py
@@ -390,8 +390,10 @@
     forth = back = block
     for hop in range(1, 4):
         forth, back = up(forth), down(back)
-        if hop < 3:
-            forth = gate(forth, parts[NEAR[hop - 1]])
+        if hop == 1:
+            forth = gate(forth, parts[NEAR[0]])
+        if hop == 2:
+            back = gate(back, parts[NEAR[1]])
         held[hop], held[Z - hop] = forth, back
     held[4] = up(forth)
 

time: 71.5 us -> 74.2 us (1.038)
  waiting for transfers between devices: 16.4 us -> 19.3 us
    ppermute x6, waiting for transfers between devices: 11.1 us -> 13.9 us  [around(): lax.ppermute(value, 'feat', [(i, (i + k) % feat) for i in range(feat)])]
    ppermute x6, starting transfers between devices: 9.18 us -> 7.93 us  [around(): lax.ppermute(value, 'feat', [(i, (i + k) % feat) for i in range(feat)])]
    ppermute x15, starting transfers between devices: 26.8 us -> 27.9 us  [moved(): return lax.ppermute(value, 'patch', pairs_of(move))]
  transfers between devices with their start and end apart: 21 -> 21, of which waited for: 9 -> 10; matrix products, arithmetic and copies ran while one was open for 0% -> 0% of each run, Pallas kernels for 11% -> 11%
where the time goes in v14:
time: 74.2 us; the launch traced here: 74 us
  starting transfers between devices  35.8 us (48%)
  waiting for transfers between devices  19.3 us (26%)
  Pallas kernels  17 us (23%)
  between operations  1.5 us (2%)
    ppermute x15, starting transfers between devices, moved(): return lax.ppermute(value, 'patch', pairs_of(move))  27.9 us
    ppermute x6, waiting for transfers between devices, around(): lax.ppermute(value, 'feat', [(i, (i + k) % feat) for i in range(feat)])  13.9 us
    ppermute x6, starting transfers between devices, around(): lax.ppermute(value, 'feat', [(i, (i + k) % feat) for i in range(feat)])  7.93 us
    pallas_call x1, Pallas kernels, edge_before(): pl.pallas_call(lambda *refs: before_kernel(len(earlier), *refs), in_specs...  6.68 us
    pallas_call x1, Pallas kernels, edge_after(): pl.pallas_call(lambda *refs: after_kernel(first_row, *refs), in_specs=[SM...  6.46 us
    ppermute x15, waiting for transfers between devices, moved(): return lax.ppermute(value, 'patch', pairs_of(move))  5.4 us
  transfers between devices with their start and end apart: 21, of which 10 were waited for; matrix products, arithmetic and copies ran while one was open for 0% of the time, Pallas kernels for 11%

profile of v14, /device:TPU:1, one launch (start us, length us, event | category | flops | bytes accessed | tf_op | source)
XLA Modules:
  0.0 74.0 jit_solution(4903602818483495680)
XLA Ops:
  0.6 0.0 copy-start.7
  0.6 0.0 copy-start.8
  0.7 0.0 copy-start
  0.7 0.0 copy-start.3
  0.7 1.2 %pack.1.refs_0_ = bf16[176,512]{1,0:T(8,128)(2,1)S(1)} custom-call(s32[1]{0:T(128)} %bitcast.1.where_ref, s32[24,64]{1,0:T(8,128)} %bitcast.12, bf16[160,512]{1,0:T(8,128)(2,1)} %nodes_ref.1), custom_call_target="tpu_custom_call" | custom-call | tf_op jit(solution)/shard_map/pack/pallas_call | solution.py:96
  1.8 2.5 %collective-permute-start = (bf16[176,512]{1,0:T(8,128)(2,1)S(1)}, bf16[176,512]{1,0:T(8,128)(2,1)S(1)}, u32[]{:S(2)}, u32[]{:S(2)}) collective-permute-start(bf16[176,512]{1,0:T(8,128)(2,1)S(1)} %pack.1.refs_0_), channel_id=1, source_target_pairs={{0,8},{4,12},{8,16},{12,20},{16,24},{20,28},{24,32},{28,36},{32,40... | collective-permute-start | bytes 540680 | tf_op jit(solution)/shard_map/ppermute | solution.py:355
  4.4 1.3 %collective-permute-start.1 = (bf16[160,512]{1,0:T(8,128)(2,1)}, bf16[160,512]{1,0:T(8,128)(2,1)S(1)}, u32[]{:S(2)}, u32[]{:S(2)}) collective-permute-start(bf16[160,512]{1,0:T(8,128)(2,1)} %nodes_ref.1), channel_id=1, source_target_pairs={{0,1},{1,2},{2,3},{3,0},{4,5},{5,6},{6,7},{7,4},{8,9},{9,10},{10,1... | collective-permute-start | bytes 491528 | tf_op jit(solution)/shard_map/ppermute | solution.py:383
  5.7 4.0 %collective-permute-start.2 = (bf16[176,512]{1,0:T(8,128)(2,1)S(1)}, bf16[176,512]{1,0:T(8,128)(2,1)S(1)}, u32[]{:S(2)}, u32[]{:S(2)}) collective-permute-start(bf16[176,512]{1,0:T(8,128)(2,1)S(1)} %pack.1.refs_0_), channel_id=1, source_target_pairs={{0,56},{4,60},{8,0},{12,4},{16,8},{20,12},{24,16},{28,20},{32,24},... | collective-permute-start | bytes 540680 | tf_op jit(solution)/shard_map/ppermute | solution.py:355
  9.7 1.0 %collective-permute-done.1.refs_1_.refs_4_ = bf16[160,512]{1,0:T(8,128)(2,1)S(1)} collective-permute-done((bf16[160,512]{1,0:T(8,128)(2,1)}, bf16[160,512]{1,0:T(8,128)(2,1)S(1)}, u32[]{:S(2)}, u32[]{:S(2)}) %collective-permute-start.1) | collective-permute-done | bytes 163872 | tf_op jit(solution)/shard_map/ppermute | solution.py:383
  10.7 1.9 %collective-permute-done.refs_0_ = bf16[176,512]{1,0:T(8,128)(2,1)S(1)} collective-permute-done((bf16[176,512]{1,0:T(8,128)(2,1)S(1)}, bf16[176,512]{1,0:T(8,128)(2,1)S(1)}, u32[]{:S(2)}, u32[]{:S(2)}) %collective-permute-start) | collective-permute-done | bytes 180256 | tf_op jit(solution)/shard_map/ppermute | solution.py:355
  12.6 0.0 collective-permute-start.3
  12.6 0.0 collective-permute-done.2.refs_2_
  12.6 3.4 %collective-permute-start.9 = (bf16[176,512]{1,0:T(8,128)(2,1)S(1)}, bf16[176,512]{1,0:T(8,128)(2,1)S(1)}, u32[]{:S(2)}, u32[]{:S(2)}) collective-permute-start(bf16[176,512]{1,0:T(8,128)(2,1)S(1)} %collective-permute-done.2.refs_2_), channel_id=1, source_target_pairs={{0,56},{4,60},{8,0},{12,4},{16,8},{20,12},{24,16},{28,20},{32,24},... | collective-permute-start | bytes 540680 | tf_op jit(solution)/shard_map/ppermute | solution.py:355
  16.0 2.6 %collective-permute-done.3.refs_3_ = bf16[176,512]{1,0:T(8,128)(2,1)S(1)} collective-permute-done((bf16[176,512]{1,0:T(8,128)(2,1)S(1)}, bf16[176,512]{1,0:T(8,128)(2,1)S(1)}, u32[]{:S(2)}, u32[]{:S(2)}) %collective-permute-start.3) | collective-permute-done | bytes 180256 | tf_op jit(solution)/shard_map/ppermute | solution.py:355
  18.6 0.0 collective-permute-start.10
  18.6 2.7 %collective-permute-start.8 = (bf16[160,512]{1,0:T(8,128)(2,1)}, bf16[160,512]{1,0:T(8,128)(2,1)S(1)}, u32[]{:S(2)}, u32[]{:S(2)}) collective-permute-start(bf16[160,512]{1,0:T(8,128)(2,1)} %nodes_ref.1), channel_id=1, source_target_pairs={{0,3},{1,0},{2,1},{3,2},{4,7},{5,4},{6,5},{7,6},{8,11},{9,8},{10,9... | collective-permute-start | bytes 491528 | tf_op jit(solution)/shard_map/ppermute | solution.py:383
  21.4 0.6 select.24
  22.0 1.3 %collective-permute-start.4 = (bf16[192,512]{1,0:T(8,128)(2,1)S(1)}, bf16[192,512]{1,0:T(8,128)(2,1)S(1)}, u32[]{:S(2)}, u32[]{:S(2)}) collective-permute-start(bf16[192,512]{1,0:T(8,128)(2,1)S(1)} %get-tuple-element.16), channel_id=1, source_target_pairs={{0,64},{4,68},{8,72},{12,76},{16,80},{20,84},{24,88},{28,92},{32,9... | collective-permute-start | bytes 589832 | tf_op jit(solution)/shard_map/ppermute | solution.py:355
  23.3 0.7 collective-permute-done.8.refs_1_.refs_6_
  23.9 0.0 collective-permute-done.9.refs_0_
  24.0 2.7 %collective-permute-start.11 = (bf16[176,512]{1,0:T(8,128)(2,1)S(1)}, bf16[176,512]{1,0:T(8,128)(2,1)S(1)}, u32[]{:S(2)}, u32[]{:S(2)}) collective-permute-start(bf16[176,512]{1,0:T(8,128)(2,1)S(1)} %gate.3.refs_0_), channel_id=1, source_target_pairs={{0,56},{4,60},{8,0},{12,4},{16,8},{20,12},{24,16},{28,20},{32,24},... | collective-permute-start | bytes 540680 | tf_op jit(solution)/shard_map/ppermute | solution.py:355
  26.6 0.0 collective-permute-done.10.refs_1_
  26.6 0.0 collective-permute-start.12
  26.6 0.6 collective-permute-start.7
  27.2 2.7 %collective-permute-start.5 = (bf16[192,512]{1,0:T(8,128)(2,1)S(1)}, bf16[192,512]{1,0:T(8,128)(2,1)S(1)}, u32[]{:S(2)}, u32[]{:S(2)}) collective-permute-start(bf16[192,512]{1,0:T(8,128)(2,1)S(1)} %get-tuple-element.17), channel_id=1, source_target_pairs={{0,128},{4,132},{8,136},{12,140},{16,144},{20,148},{24,152},{28,15... | collective-permute-start | bytes 589832 | tf_op jit(solution)/shard_map/ppermute | solution.py:355
  29.9 2.4 %collective-permute-done.7.refs_4_.refs_5_ = bf16[160,512]{1,0:T(8,128)(2,1)S(1)} collective-permute-done((bf16[160,512]{1,0:T(8,128)(2,1)S(1)}, bf16[160,512]{1,0:T(8,128)(2,1)S(1)}, u32[]{:S(2)}, u32[]{:S(2)}) %collective-permute-start.7) | collective-permute-done | bytes 163872 | tf_op jit(solution)/shard_map/ppermute | solution.py:383
  32.4 2.5 %collective-permute-start.6 = (bf16[192,512]{1,0:T(8,128)(2,1)S(1)}, bf16[192,512]{1,0:T(8,128)(2,1)S(1)}, u32[]{:S(2)}, u32[]{:S(2)}) collective-permute-start(bf16[192,512]{1,0:T(8,128)(2,1)S(1)} %get-tuple-element.18), channel_id=1, source_target_pairs={{0,192},{4,196},{8,200},{12,204},{16,208},{20,212},{24,216},{28,22... | collective-permute-start | bytes 589832 | tf_op jit(solution)/shard_map/ppermute | solution.py:355
  34.8 0.0 collective-permute-done.11.refs_2_
  34.8 0.0 collective-permute-done.12.refs_3_
  34.8 0.6 select.25
  35.5 0.1 collective-permute-start.14
  35.5 1.7 %collective-permute-start.15 = (bf16[192,512]{1,0:T(8,128)(2,1)S(1)}, bf16[192,512]{1,0:T(8,128)(2,1)S(1)}, u32[]{:S(2)}, u32[]{:S(2)}) collective-permute-start(bf16[192,512]{1,0:T(8,128)(2,1)S(1)} %get-tuple-element.21), channel_id=1, source_target_pairs={{0,128},{4,132},{8,136},{12,140},{16,144},{20,148},{24,152},{28,15... | collective-permute-start | bytes 589832 | tf_op jit(solution)/shard_map/ppermute | solution.py:355
  37.3 0.0 collective-permute-done.4.refs_1_.refs_5_
  37.3 0.9 %collective-permute-start.16 = (bf16[192,512]{1,0:T(8,128)(2,1)S(1)}, bf16[192,512]{1,0:T(8,128)(2,1)S(1)}, u32[]{:S(2)}, u32[]{:S(2)}) collective-permute-start(bf16[192,512]{1,0:T(8,128)(2,1)S(1)} %get-tuple-element.22), channel_id=1, source_target_pairs={{0,192},{4,196},{8,200},{12,204},{16,208},{20,212},{24,216},{28,22... | collective-permute-start | bytes 589832 | tf_op jit(solution)/shard_map/ppermute | solution.py:355
  38.2 0.0 copy-done.7
  38.2 0.0 copy-done.8
  38.2 0.1 fusion.4
  38.3 0.0 copy-done
  38.3 0.0 copy-done.3
  38.3 6.7 %edge_before.1.refs_4_.refs_14_ = f32[1280,512]{1,0:T(8,128)} custom-call(s32[1,1280]{1,0:T(1,128)S(1)} %reshape.29.refs_0_.refs_2_, s32[1,1280]{1,0:T(1,128)S(1)} %reshape.32.refs_1_, f32[1,512]{1,0:T(1,128)S(1)} %bitcast.8, bf16[160,512]{1,0:T(8,128)(2,1)S(1)} %copy-done, bf16[160,512]{1,0:T(8,128)(2,1)S(1)} %collective-permute-done.1.refs_1_.refs_4_, ...), custom_call_target="tpu_custom_call" | custom-call | flops 1048576 | tf_op jit(solution)/shard_map/edge_before/pallas_call | solution.py:230
  45.0 0.0 collective-permute-done.5.refs_2_.refs_6_
  45.0 0.0 collective-permute-done.6.refs_3_.refs_7_
  45.1 0.0 copy-start.4
  45.1 5.8 %collective-permute-start.13 = (bf16[384,512]{1,0:T(8,128)(2,1)S(1)}, bf16[384,512]{1,0:T(8,128)(2,1)S(1)}, u32[]{:S(2)}, u32[]{:S(2)}) collective-permute-start(bf16[384,512]{1,0:T(8,128)(2,1)S(1)} %crossing.2), channel_id=1, source_target_pairs={{0,4},{4,0},{8,12},{12,8},{16,20},{20,16},{24,28},{28,24},{32,36},... | collective-permute-start | bytes 1179656 | tf_op jit(solution)/shard_map/ppermute | solution.py:355
  50.9 0.0 collective-permute-done.14.refs_1_.refs_10_
  50.9 0.0 collective-permute-done.15.refs_2_.refs_11_
  50.9 0.0 collective-permute-done.16.refs_3_.refs_12_
  51.0 0.1 collective-permute-start.17
  51.1 0.2 reshape.36.refs_1_
  52.0 0.3 collective-permute-done.13.refs_8_
  52.3 0.6 collective-permute-done.17.refs_13_
  52.9 0.0 copy-done.4
  52.9 0.0 copy-start.6
  52.9 6.5 %edge_after.1 = (bf16[1280,512]{1,0:T(8,128)(2,1)}, f32[160,512]{1,0:T(8,128)S(1)}, bf16[160,512]{1,0:T(8,128)(2,1)S(1)}, bf16[160,512]{1,0:T(8,128)(2,1)S(1)}, bf16[160,512]{1,0:T(8,128)(2,1)S(1)}) custom-call(s32[1]{0:T(128)S(6)} %copy.21.refs_0_, s32[1280,1]{1,0:T(8,128)S(1)} %reshape.36.refs_1_, s32[1,1280]{1,0:T(1,128)S(1)} %reshape.29.refs_0_.refs_2_, ...), custom_call_target="tpu_custom_call" | custom-call | tf_op jit(solution)/shard_map/edge_after/pallas_call | solution.py:301
  59.3 2.7 %collective-permute-start.18 = (bf16[160,512]{1,0:T(8,128)(2,1)S(1)}, bf16[160,512]{1,0:T(8,128)(2,1)S(1)}, u32[]{:S(2)}, u32[]{:S(2)}) collective-permute-start(bf16[160,512]{1,0:T(8,128)(2,1)S(1)} %get-tuple-element.25), channel_id=1, source_target_pairs={{0,3},{1,0},{2,1},{3,2},{4,7},{5,4},{6,5},{7,6},{8,11},{9,8},{10,9... | collective-permute-start | bytes 491528 | tf_op jit(solution)/shard_map/ppermute | solution.py:383
  62.0 0.0 collective-permute-start.19
  62.0 0.7 collective-permute-start.20
  62.7 5.9 %collective-permute-done.18.p1_ref = bf16[160,512]{1,0:T(8,128)(2,1)S(1)} collective-permute-done((bf16[160,512]{1,0:T(8,128)(2,1)S(1)}, bf16[160,512]{1,0:T(8,128)(2,1)S(1)}, u32[]{:S(2)}, u32[]{:S(2)}) %collective-permute-start.18) | collective-permute-done | bytes 163872 | tf_op jit(solution)/shard_map/ppermute | solution.py:383
  68.6 0.1 collective-permute-done.19.p2_ref
  68.7 3.9 %collective-permute-done.20.p3_ref = bf16[160,512]{1,0:T(8,128)(2,1)S(1)} collective-permute-done((bf16[160,512]{1,0:T(8,128)(2,1)S(1)}, bf16[160,512]{1,0:T(8,128)(2,1)S(1)}, u32[]{:S(2)}, u32[]{:S(2)}) %collective-permute-start.20) | collective-permute-done | bytes 163872 | tf_op jit(solution)/shard_map/ppermute | solution.py:383
  72.5 0.0 copy-done.1
  72.5 0.0 copy-done.5
  72.5 0.0 copy-done.6
  72.6 1.5 %node_update.1 = bf16[160,512]{1,0:T(8,128)(2,1)} custom-call(bf16[160,512]{1,0:T(8,128)(2,1)S(1)} %copy-done, f32[160,512]{1,0:T(8,128)S(1)} %get-tuple-element.24.p0_ref, bf16[160,512]{1,0:T(8,128)(2,1)S(1)} %collective-permute-done.18.p1_ref, bf16[160,512]{1,0:T(8,128)(2,1)S(1)} %collective-permute-done.19.p2_ref, ...), custom_call_target="tpu_custom_call" | custom-call | tf_op jit(solution)/shard_map/node_update/pallas_call | solution.py:335
  (10 shorter events, 0.1 us)
Async XLA Ops:
  0.6 37.6 %copy-start.7 = (s32[1280]{0:T(1024)S(1)}, s32[1280]{0:T(1024)}, u32[]{:S(2)}) copy-start(s32[1280]{0:T(1024)} %param.17) | copy-start | bytes 15364
  0.6 37.6 %copy-start.8 = (s32[1280]{0:T(1024)S(1)}, s32[1280]{0:T(1024)}, u32[]{:S(2)}) copy-start(s32[1280]{0:T(1024)} %param.16) | copy-start | bytes 15364
  0.7 37.7 %copy-start = (bf16[160,512]{1,0:T(8,128)(2,1)S(1)}, bf16[160,512]{1,0:T(8,128)(2,1)}, u32[]{:S(2)}) copy-start(bf16[160,512]{1,0:T(8,128)(2,1)} %nodes_ref.1) | copy-start | bytes 491524
  0.7 37.7 %copy-start.3 = (f32[512]{0:T(512)S(1)}, f32[512]{0:T(512)}, u32[]{:S(2)}) copy-start(f32[512]{0:T(512)} %param.21) | copy-start | bytes 6148
  1.8 10.8 %collective-permute-start = (bf16[176,512]{1,0:T(8,128)(2,1)S(1)}, bf16[176,512]{1,0:T(8,128)(2,1)S(1)}, u32[]{:S(2)}, u32[]{:S(2)}) collective-permute-start(bf16[176,512]{1,0:T(8,128)(2,1)S(1)} %pack.1.refs_0_), channel_id=1, source_target_pairs={{0,8},{4,12},{8,16},{12,20},{16,24},{20,28},{24,32},{28,36},{32,40... | collective-permute-start | bytes 540680 | tf_op jit(solution)/shard_map/ppermute | solution.py:355
  4.4 6.3 %collective-permute-start.1 = (bf16[160,512]{1,0:T(8,128)(2,1)}, bf16[160,512]{1,0:T(8,128)(2,1)S(1)}, u32[]{:S(2)}, u32[]{:S(2)}) collective-permute-start(bf16[160,512]{1,0:T(8,128)(2,1)} %nodes_ref.1), channel_id=1, source_target_pairs={{0,1},{1,2},{2,3},{3,0},{4,5},{5,6},{6,7},{7,4},{8,9},{9,10},{10,1... | collective-permute-start | bytes 491528 | tf_op jit(solution)/shard_map/ppermute | solution.py:383
  5.7 6.9 %collective-permute-start.2 = (bf16[176,512]{1,0:T(8,128)(2,1)S(1)}, bf16[176,512]{1,0:T(8,128)(2,1)S(1)}, u32[]{:S(2)}, u32[]{:S(2)}) collective-permute-start(bf16[176,512]{1,0:T(8,128)(2,1)S(1)} %pack.1.refs_0_), channel_id=1, source_target_pairs={{0,56},{4,60},{8,0},{12,4},{16,8},{20,12},{24,16},{28,20},{32,24},... | collective-permute-start | bytes 540680 | tf_op jit(solution)/shard_map/ppermute | solution.py:355
  12.6 6.0 %collective-permute-start.3 = (bf16[176,512]{1,0:T(8,128)(2,1)S(1)}, bf16[176,512]{1,0:T(8,128)(2,1)S(1)}, u32[]{:S(2)}, u32[]{:S(2)}) collective-permute-start(bf16[176,512]{1,0:T(8,128)(2,1)S(1)} %gate.2.refs_1_), channel_id=1, source_target_pairs={{0,8},{4,12},{8,16},{12,20},{16,24},{20,28},{24,32},{28,36},{32,40... | collective-permute-start | bytes 540680 | tf_op jit(solution)/shard_map/ppermute | solution.py:355
  12.6 11.3 %collective-permute-start.9 = (bf16[176,512]{1,0:T(8,128)(2,1)S(1)}, bf16[176,512]{1,0:T(8,128)(2,1)S(1)}, u32[]{:S(2)}, u32[]{:S(2)}) collective-permute-start(bf16[176,512]{1,0:T(8,128)(2,1)S(1)} %collective-permute-done.2.refs_2_), channel_id=1, source_target_pairs={{0,56},{4,60},{8,0},{12,4},{16,8},{20,12},{24,16},{28,20},{32,24},... | collective-permute-start | bytes 540680 | tf_op jit(solution)/shard_map/ppermute | solution.py:355
  18.6 8.0 %collective-permute-start.10 = (bf16[176,512]{1,0:T(8,128)(2,1)S(1)}, bf16[176,512]{1,0:T(8,128)(2,1)S(1)}, u32[]{:S(2)}, u32[]{:S(2)}) collective-permute-start(bf16[176,512]{1,0:T(8,128)(2,1)S(1)} %collective-permute-done.3.refs_3_), channel_id=1, source_target_pairs={{0,8},{4,12},{8,16},{12,20},{16,24},{20,28},{24,32},{28,36},{32,40... | collective-permute-start | bytes 540680 | tf_op jit(solution)/shard_map/ppermute | solution.py:355
  18.6 5.3 %collective-permute-start.8 = (bf16[160,512]{1,0:T(8,128)(2,1)}, bf16[160,512]{1,0:T(8,128)(2,1)S(1)}, u32[]{:S(2)}, u32[]{:S(2)}) collective-permute-start(bf16[160,512]{1,0:T(8,128)(2,1)} %nodes_ref.1), channel_id=1, source_target_pairs={{0,3},{1,0},{2,1},{3,2},{4,7},{5,4},{6,5},{7,6},{8,11},{9,8},{10,9... | collective-permute-start | bytes 491528 | tf_op jit(solution)/shard_map/ppermute | solution.py:383
  22.0 15.3 %collective-permute-start.4 = (bf16[192,512]{1,0:T(8,128)(2,1)S(1)}, bf16[192,512]{1,0:T(8,128)(2,1)S(1)}, u32[]{:S(2)}, u32[]{:S(2)}) collective-permute-start(bf16[192,512]{1,0:T(8,128)(2,1)S(1)} %get-tuple-element.16), channel_id=1, source_target_pairs={{0,64},{4,68},{8,72},{12,76},{16,80},{20,84},{24,88},{28,92},{32,9... | collective-permute-start | bytes 589832 | tf_op jit(solution)/shard_map/ppermute | solution.py:355
  24.0 10.9 %collective-permute-start.11 = (bf16[176,512]{1,0:T(8,128)(2,1)S(1)}, bf16[176,512]{1,0:T(8,128)(2,1)S(1)}, u32[]{:S(2)}, u32[]{:S(2)}) collective-permute-start(bf16[176,512]{1,0:T(8,128)(2,1)S(1)} %gate.3.refs_0_), channel_id=1, source_target_pairs={{0,56},{4,60},{8,0},{12,4},{16,8},{20,12},{24,16},{28,20},{32,24},... | collective-permute-start | bytes 540680 | tf_op jit(solution)/shard_map/ppermute | solution.py:355
  26.6 8.2 %collective-permute-start.12 = (bf16[176,512]{1,0:T(8,128)(2,1)S(1)}, bf16[176,512]{1,0:T(8,128)(2,1)S(1)}, u32[]{:S(2)}, u32[]{:S(2)}) collective-permute-start(bf16[176,512]{1,0:T(8,128)(2,1)S(1)} %collective-permute-done.10.refs_1_), channel_id=1, source_target_pairs={{0,8},{4,12},{8,16},{12,20},{16,24},{20,28},{24,32},{28,36},{32,40... | collective-permute-start | bytes 540680 | tf_op jit(solution)/shard_map/ppermute | solution.py:355
  26.6 5.7 %collective-permute-start.7 = (bf16[160,512]{1,0:T(8,128)(2,1)S(1)}, bf16[160,512]{1,0:T(8,128)(2,1)S(1)}, u32[]{:S(2)}, u32[]{:S(2)}) collective-permute-start(bf16[160,512]{1,0:T(8,128)(2,1)S(1)} %collective-permute-done.1.refs_1_.refs_4_), channel_id=1, source_target_pairs={{0,1},{1,2},{2,3},{3,0},{4,5},{5,6},{6,7},{7,4},{8,9},{9,10},{10,1... | collective-permute-start | bytes 491528 | tf_op jit(solution)/shard_map/ppermute | solution.py:383
  27.2 17.8 %collective-permute-start.5 = (bf16[192,512]{1,0:T(8,128)(2,1)S(1)}, bf16[192,512]{1,0:T(8,128)(2,1)S(1)}, u32[]{:S(2)}, u32[]{:S(2)}) collective-permute-start(bf16[192,512]{1,0:T(8,128)(2,1)S(1)} %get-tuple-element.17), channel_id=1, source_target_pairs={{0,128},{4,132},{8,136},{12,140},{16,144},{20,148},{24,152},{28,15... | collective-permute-start | bytes 589832 | tf_op jit(solution)/shard_map/ppermute | solution.py:355
  32.4 12.7 %collective-permute-start.6 = (bf16[192,512]{1,0:T(8,128)(2,1)S(1)}, bf16[192,512]{1,0:T(8,128)(2,1)S(1)}, u32[]{:S(2)}, u32[]{:S(2)}) collective-permute-start(bf16[192,512]{1,0:T(8,128)(2,1)S(1)} %get-tuple-element.18), channel_id=1, source_target_pairs={{0,192},{4,196},{8,200},{12,204},{16,208},{20,212},{24,216},{28,22... | collective-permute-start | bytes 589832 | tf_op jit(solution)/shard_map/ppermute | solution.py:355
  35.5 15.5 %collective-permute-start.14 = (bf16[192,512]{1,0:T(8,128)(2,1)S(1)}, bf16[192,512]{1,0:T(8,128)(2,1)S(1)}, u32[]{:S(2)}, u32[]{:S(2)}) collective-permute-start(bf16[192,512]{1,0:T(8,128)(2,1)S(1)} %get-tuple-element.20), channel_id=1, source_target_pairs={{0,64},{4,68},{8,72},{12,76},{16,80},{20,84},{24,88},{28,92},{32,9... | collective-permute-start | bytes 589832 | tf_op jit(solution)/shard_map/ppermute | solution.py:355
  35.5 15.4 %collective-permute-start.15 = (bf16[192,512]{1,0:T(8,128)(2,1)S(1)}, bf16[192,512]{1,0:T(8,128)(2,1)S(1)}, u32[]{:S(2)}, u32[]{:S(2)}) collective-permute-start(bf16[192,512]{1,0:T(8,128)(2,1)S(1)} %get-tuple-element.21), channel_id=1, source_target_pairs={{0,128},{4,132},{8,136},{12,140},{16,144},{20,148},{24,152},{28,15... | collective-permute-start | bytes 589832 | tf_op jit(solution)/shard_map/ppermute | solution.py:355
  37.3 13.7 %collective-permute-start.16 = (bf16[192,512]{1,0:T(8,128)(2,1)S(1)}, bf16[192,512]{1,0:T(8,128)(2,1)S(1)}, u32[]{:S(2)}, u32[]{:S(2)}) collective-permute-start(bf16[192,512]{1,0:T(8,128)(2,1)S(1)} %get-tuple-element.22), channel_id=1, source_target_pairs={{0,192},{4,196},{8,200},{12,204},{16,208},{20,212},{24,216},{28,22... | collective-permute-start | bytes 589832 | tf_op jit(solution)/shard_map/ppermute | solution.py:355
  45.1 7.8 %copy-start.4 = (f32[512]{0:T(512)S(1)}, f32[512]{0:T(512)}, u32[]{:S(2)}) copy-start(f32[512]{0:T(512)} %param.23) | copy-start | bytes 6148
  45.1 7.2 %collective-permute-start.13 = (bf16[384,512]{1,0:T(8,128)(2,1)S(1)}, bf16[384,512]{1,0:T(8,128)(2,1)S(1)}, u32[]{:S(2)}, u32[]{:S(2)}) collective-permute-start(bf16[384,512]{1,0:T(8,128)(2,1)S(1)} %crossing.2), channel_id=1, source_target_pairs={{0,4},{4,0},{8,12},{12,8},{16,20},{20,16},{24,28},{28,24},{32,36},... | collective-permute-start | bytes 1179656 | tf_op jit(solution)/shard_map/ppermute | solution.py:355
  51.0 1.9 %collective-permute-start.17 = (bf16[384,512]{1,0:T(8,128)(2,1)S(1)}, bf16[384,512]{1,0:T(8,128)(2,1)S(1)}, u32[]{:S(2)}, u32[]{:S(2)}) collective-permute-start(bf16[384,512]{1,0:T(8,128)(2,1)S(1)} %crossing.3), channel_id=1, source_target_pairs={{0,4},{4,0},{8,12},{12,8},{16,20},{20,16},{24,28},{28,24},{32,36},... | collective-permute-start | bytes 1179656 | tf_op jit(solution)/shard_map/ppermute | solution.py:355
  52.9 19.7 %copy-start.1 = (bf16[1024,512]{1,0:T(8,128)(2,1)S(1)}, bf16[1024,512]{1,0:T(8,128)(2,1)}, u32[]{:S(2)}) copy-start(bf16[1024,512]{1,0:T(8,128)(2,1)} %w1_ref.1) | copy-start | bytes 3145732
  52.9 19.7 %copy-start.2 = (bf16[512,512]{1,0:T(8,128)(2,1)S(1)}, bf16[512,512]{1,0:T(8,128)(2,1)}, u32[]{:S(2)}) copy-start(bf16[512,512]{1,0:T(8,128)(2,1)} %w2_ref.1) | copy-start | bytes 1572868
  52.9 19.7 %copy-start.5 = (f32[512]{0:T(512)S(1)}, f32[512]{0:T(512)}, u32[]{:S(2)}) copy-start(f32[512]{0:T(512)} %param.25) | copy-start | bytes 6148
  52.9 19.7 %copy-start.6 = (f32[512]{0:T(512)S(1)}, f32[512]{0:T(512)}, u32[]{:S(2)}) copy-start(f32[512]{0:T(512)} %param.27) | copy-start | bytes 6148
  59.3 9.2 %collective-permute-start.18 = (bf16[160,512]{1,0:T(8,128)(2,1)S(1)}, bf16[160,512]{1,0:T(8,128)(2,1)S(1)}, u32[]{:S(2)}, u32[]{:S(2)}) collective-permute-start(bf16[160,512]{1,0:T(8,128)(2,1)S(1)} %get-tuple-element.25), channel_id=1, source_target_pairs={{0,3},{1,0},{2,1},{3,2},{4,7},{5,4},{6,5},{7,6},{8,11},{9,8},{10,9... | collective-permute-start | bytes 491528 | tf_op jit(solution)/shard_map/ppermute | solution.py:383
  62.0 6.7 %collective-permute-start.19 = (bf16[160,512]{1,0:T(8,128)(2,1)S(1)}, bf16[160,512]{1,0:T(8,128)(2,1)S(1)}, u32[]{:S(2)}, u32[]{:S(2)}) collective-permute-start(bf16[160,512]{1,0:T(8,128)(2,1)S(1)} %get-tuple-element.26), channel_id=1, source_target_pairs={{0,2},{1,3},{2,0},{3,1},{4,6},{5,7},{6,4},{7,5},{8,10},{9,11},{10,... | collective-permute-start | bytes 491528 | tf_op jit(solution)/shard_map/ppermute | solution.py:383
  62.0 10.5 %collective-permute-start.20 = (bf16[160,512]{1,0:T(8,128)(2,1)S(1)}, bf16[160,512]{1,0:T(8,128)(2,1)S(1)}, u32[]{:S(2)}, u32[]{:S(2)}) collective-permute-start(bf16[160,512]{1,0:T(8,128)(2,1)S(1)} %get-tuple-element.27), channel_id=1, source_target_pairs={{0,1},{1,2},{2,3},{3,0},{4,5},{5,6},{6,7},{7,4},{8,9},{9,10},{10,1... | collective-permute-start | bytes 491528 | tf_op jit(solution)/shard_map/ppermute | solution.py:383
